TPU v7x, 32 devices: a whole 2x2x4 slice. The times are simulated.
32 devices in a mesh: gx: 8 (over y, x, core), gy: 4 (over z).
Axes of the slice: x: 2, y: 2, z: 4, core: 2. Of those that a mesh axis runs over, the one named last changes fastest.
Arguments:
- in_table: float32 [32768, 300], P(('gx', 'gy')), may hold values from -3 to 3
- out_table: float32 [32768, 300], P(('gx', 'gy')), may hold values from -3 to 3
- hot_table: float32 [2048, 300], replicated, may hold values from -3 to 3
- centre_owner: int32 [3, 4096, 1], P(None, ('gx', 'gy')), may hold values from 0 to 31; in each aligned block of 128 rows (0 to 127, 128 to 255, ..., all dimensions but the last counted through in order) at most 8 rows name the same one
- centre_row: int32 [3, 4096], P(None, ('gx', 'gy')), may hold values from 0 to 1023
- bag_owner: int32 [3, 4096, 6], P(None, ('gx', 'gy')), may hold values from 0 to 31, all different within a row; in each aligned block of 128 rows (0 to 127, 128 to 255, ..., all dimensions but the last counted through in order) at most 48 rows name the same one
- bag_row: int32 [3, 4096, 6], P(None, ('gx', 'gy')), may hold values from 0 to 1023
- bag_len: int32 [3, 4096], P(None, ('gx', 'gy')), may hold values from 1 to 6
- context_owner: int32 [3, 4096, 1], P(None, ('gx', 'gy')), may hold values from 0 to 31; in each aligned block of 128 rows (0 to 127, 128 to 255, ..., all dimensions but the last counted through in order) at most 8 rows name the same one
- context_row: int32 [3, 4096], P(None, ('gx', 'gy')), may hold values from 0 to 1023
- negative_ids: int32 [3, 32768], P(None, ('gx', 'gy')), may hold values from 0 to 2047
Outputs:
- new_in_table: float32 [32768, 300], P(('gx', 'gy'))
- new_out_table: float32 [32768, 300], P(('gx', 'gy'))
- new_hot_table: float32 [2048, 300], replicated
Inputs may be any that keep to these rules, and one draw needn't show every extreme that they name: `centre_owner`: in each step, the 128 centre words of one device name one owner at most 8 times, and some owner exactly that often. `bag_owner`: in each step, the bucket slots of one device's 128 centre words name one owner at most 48 times, and some owner exactly that often; the 6 slots of one word name distinct owners. Slots at positions bag_len and beyond are padding. `context_owner`: in each step, the 128 contexts of one device name one owner at most 8 times, and some owner exactly that often.
All inputs are finite; a program needn't handle non-finite values.
Results may differ from a plain program's by a relative error of at most 0.017.
Values sent between devices are 32-bit elements; how exact they have to be, the bound alone decides.
No kernel may reach another device: no remote copies, remote signals or barrier semaphores. Data moves between devices by JAX's collectives and lax.ppermute only.
A program may use at most 128 MiB of HBM per device.

v0:
```python
import jax
import jax.numpy as jnp
from jax import lax
from jax.sharding import PartitionSpec as P

learn_rate = 2.0
exact = lax.Precision.HIGHEST


def slot_ranks(owner_flat, owners):
    onehot = (owner_flat[:, None] == jnp.arange(owners, dtype=jnp.int32)[None, :]).astype(jnp.int32)
    running = jnp.cumsum(onehot, axis=0)
    return jnp.sum(running * onehot, axis=1) - 1


def swap_requests(requests):
    return lax.all_to_all(requests, ("gx", "gy"), split_axis=1, concat_axis=1, tiled=True)


def return_rows(in_rows, out_rows):
    return (
        lax.all_to_all(in_rows, ("gx", "gy"), split_axis=0, concat_axis=0, tiled=True),
        lax.all_to_all(out_rows, ("gx", "gy"), split_axis=0, concat_axis=0, tiled=True),
    )


def send_grads(in_grads, out_grads):
    return (
        lax.all_to_all(in_grads, ("gx", "gy"), split_axis=0, concat_axis=0, tiled=True),
        lax.all_to_all(out_grads, ("gx", "gy"), split_axis=0, concat_axis=0, tiled=True),
    )


def build_plan(
    step_index,
    centre_owner,
    centre_row,
    bag_owner,
    bag_row,
    context_owner,
    context_row,
    owners,
    cap_c,
    cap_b,
):
    cap_in = cap_c + cap_b
    centre_dest = centre_owner[step_index, :, 0]
    centre_slot = slot_ranks(centre_dest, owners)
    bag_dest = bag_owner[step_index].reshape(-1)
    bag_slot = slot_ranks(bag_dest, owners) + cap_c
    context_dest = context_owner[step_index, :, 0]
    context_slot = slot_ranks(context_dest, owners)
    requests = jnp.zeros((owners, cap_in + cap_c), jnp.int32)
    requests = requests.at[centre_dest, centre_slot].set(centre_row[step_index])
    requests = requests.at[bag_dest, bag_slot].set(bag_row[step_index].reshape(-1))
    requests = requests.at[context_dest, context_slot + cap_in].set(context_row[step_index])
    return (requests, centre_dest, centre_slot, bag_dest, bag_slot, context_dest, context_slot)


def body(
    in_table,
    out_table,
    hot_table,
    centre_owner,
    centre_row,
    bag_owner,
    bag_row,
    bag_len,
    context_owner,
    context_row,
    negative_ids,
):
    grid_x = lax.axis_size("gx")
    grid_y = lax.axis_size("gy")
    owners = grid_x * grid_y
    steps_total, tokens, bag_width = bag_row.shape
    feature_dim = in_table.shape[1]
    neg_count = negative_ids.shape[1]
    cap_c = max(2, 2 * tokens // owners)
    cap_b = max(2, 2 * tokens * bag_width // owners)
    cap_in = cap_c + cap_b
    plans = [
        build_plan(
            step_index,
            centre_owner,
            centre_row,
            bag_owner,
            bag_row,
            context_owner,
            context_row,
            owners,
            cap_c,
            cap_b,
        )
        for step_index in range(steps_total)
    ]
    for step_index in range(steps_total):
        requests, centre_dest, centre_slot, bag_dest, bag_slot, context_dest, context_slot = plans[
            step_index
        ]
        arrived = swap_requests(requests[None])[0]
        in_wanted = arrived[:, :cap_in]
        out_wanted = arrived[:, cap_in:]
        in_rows = in_table[in_wanted]
        out_rows = out_table[out_wanted]
        got_in, got_out = return_rows(in_rows, out_rows)
        word_vec = got_in[centre_dest, centre_slot]
        bag_vec = got_in[bag_dest, bag_slot].reshape(tokens, bag_width, feature_dim)
        context_vec = got_out[context_dest, context_slot]
        kept = (
            jnp.arange(bag_width, dtype=jnp.int32)[None, :] < bag_len[step_index][:, None]
        ).astype(jnp.float32)
        denom = 1.0 + bag_len[step_index].astype(jnp.float32)
        centre_vec = (word_vec + jnp.sum(bag_vec * kept[:, :, None], axis=1)) / denom[:, None]
        negatives = hot_table[negative_ids[step_index]]
        positive = jnp.sum(centre_vec * context_vec, axis=1)
        pos_grad = jax.nn.sigmoid(positive) - 1.0
        scores = jnp.dot(
            centre_vec, negatives.T, precision=exact, preferred_element_type=jnp.float32
        )
        neg_grad = 16.0 / neg_count * jax.nn.sigmoid(scores)
        toward_centre = jnp.dot(
            neg_grad, negatives, precision=exact, preferred_element_type=jnp.float32
        )
        toward_negative = jnp.dot(
            neg_grad.T, centre_vec, precision=exact, preferred_element_type=jnp.float32
        )
        hot_grad = (
            jnp.zeros(hot_table.shape, jnp.float32)
            .at[negative_ids[step_index]]
            .add(toward_negative)
        )
        hot_total = lax.psum(hot_grad, ("gx", "gy"))
        centre_grad = pos_grad[:, None] * context_vec + toward_centre
        word_grad = centre_grad / denom[:, None]
        bag_grad = kept[:, :, None] * centre_grad[:, None, :] / denom[:, None, None]
        context_grad = pos_grad[:, None] * centre_vec
        in_grads = jnp.zeros((owners, cap_in, feature_dim), jnp.float32)
        in_grads = in_grads.at[centre_dest, centre_slot].set(word_grad)
        in_grads = in_grads.at[bag_dest, bag_slot].set(bag_grad.reshape(-1, feature_dim))
        out_grads = (
            jnp.zeros((owners, cap_c, feature_dim), jnp.float32)
            .at[context_dest, context_slot]
            .set(context_grad)
        )
        recv_in, recv_out = send_grads(in_grads, out_grads)
        in_total = (
            jnp.zeros(in_table.shape, jnp.float32)
            .at[in_wanted.reshape(-1)]
            .add(recv_in.reshape(-1, feature_dim))
        )
        out_total = (
            jnp.zeros(out_table.shape, jnp.float32)
            .at[out_wanted.reshape(-1)]
            .add(recv_out.reshape(-1, feature_dim))
        )
        in_table = in_table - learn_rate * in_total
        out_table = out_table - learn_rate * out_total
        hot_table = hot_table - learn_rate * hot_total
    return (in_table, out_table, hot_table)


def solution(mesh):
    placed = (
        P(("gx", "gy"), None),
        P(("gx", "gy"), None),
        P(),
        P(None, ("gx", "gy"), None),
        P(None, ("gx", "gy")),
        P(None, ("gx", "gy"), None),
        P(None, ("gx", "gy"), None),
        P(None, ("gx", "gy")),
        P(None, ("gx", "gy"), None),
        P(None, ("gx", "gy")),
        P(None, ("gx", "gy")),
    )
    return jax.shard_map(
        body,
        mesh=mesh,
        in_specs=placed,
        out_specs=(P(("gx", "gy"), None), P(("gx", "gy"), None), P()),
        check_vma=False,
    )
```

profile of v0, /device:TPU:0, one launch (start us, length us, event | category | flops | bytes accessed | tf_op | source)
XLA Modules:
  0.0 1611.7 jit_solution(592823600968412349)
XLA Ops:
  19.5 17.3 %scatter_fusion = s32[32,64]{1,0:T(8,128)} fusion(s32[32,64]{1,0:T(8,128)} %broadcast.937.clone, s32[128]{0:T(128)S(1)} %get-tuple-element.97, s32[128]{0:T(128)S(1)} %get-tuple-element.76), kind=kCustom, calls=%fused_computation.18 | custom fusion | bytes 2560 | tf_op jit(solution)/shard_map/scatter | solution.py:54
  36.9 100.0 %scatter_fusion.1 = s32[32,64]{1,0:T(8,128)} fusion(s32[32,64]{1,0:T(8,128)} %scatter_fusion, s32[768]{0:T(1024)S(1)} %get-tuple-element.20, s32[768]{0:T(1024)S(1)} %reshape.1244), kind=kCustom, calls=%fused_computation.19 | custom fusion | bytes 15360 | tf_op jit(solution)/shard_map/scatter | solution.py:55
  137.4 17.3 %scatter_fusion.2 = s32[32,64]{1,0:T(8,128)} fusion(s32[32,64]{1,0:T(8,128)} %scatter_fusion.1, s32[128]{0:T(128)S(1)} %get-tuple-element.90, s32[128]{0:T(128)S(1)} %get-tuple-element.73), kind=kCustom, calls=%fused_computation.20 | custom fusion | bytes 2560 | tf_op jit(solution)/shard_map/scatter | solution.py:56
  154.7 7.1 all-to-all-start
  162.3 6.6 all-to-all-done
  175.9 5.5 gather_fusion
  195.1 6.9 gather_fusion.5
  202.6 17.5 %scatter_fusion.5 = s32[32,64]{1,0:T(8,128)} fusion(s32[32,64]{1,0:T(8,128)} %broadcast.937.clone.1, s32[128]{0:T(128)S(1)} %get-tuple-element.94, s32[128]{0:T(128)S(1)} %get-tuple-element.77), kind=kCustom, calls=%fused_computation.24 | custom fusion | bytes 2560 | tf_op jit(solution)/shard_map/scatter | solution.py:54
  220.1 99.6 %scatter_fusion.6 = s32[32,64]{1,0:T(8,128)} fusion(s32[32,64]{1,0:T(8,128)} %scatter_fusion.5, s32[768]{0:T(1024)S(1)} %get-tuple-element.111, s32[768]{0:T(1024)S(1)} %reshape.1282), kind=kCustom, calls=%fused_computation.25 | custom fusion | bytes 15360 | tf_op jit(solution)/shard_map/scatter | solution.py:55
  319.7 17.3 %scatter_fusion.7 = s32[32,64]{1,0:T(8,128)} fusion(s32[32,64]{1,0:T(8,128)} %scatter_fusion.6, s32[128]{0:T(128)S(1)} %get-tuple-element.87, s32[128]{0:T(128)S(1)} %get-tuple-element.74), kind=kCustom, calls=%fused_computation.26 | custom fusion | bytes 2560 | tf_op jit(solution)/shard_map/scatter | solution.py:56
  338.2 6.5 all-to-all-start.4
  344.7 9.2 gather_fusion.2
  361.3 15.8 scatter_fusion.8
  377.1 6.0 all-to-all-start.6
  392.5 15.5 scatter_fusion.3
  409.6 89.6 %scatter_fusion.4 = f32[32,56,300]{2,1,0:T(8,128)} fusion(f32[32,56,300]{2,1,0:T(8,128)} %scatter_fusion.3, s32[768]{0:T(1024)S(1)} %get-tuple-element.16, f32[768,300]{1,0:T(8,128)S(1)} %multiply_divide_fusion.2), kind=kCustom, calls=%fused_computation.22 | custom fusion | bytes 2770944 | tf_op jit(solution)/shard_map/scatter | solution.py:140
  499.1 6.3 all-to-all-start.3
  513.9 53.3 %all-to-all-done.3 = f32[32,56,300]{2,1,0:T(8,128)} async-done(((f32[32,56,300]{2,1,0:T(8,128)}), f32[32,56,300]{2,1,0:T(8,128)}, u32[]{:S(2)}, u32[]{:S(2)}) %all-to-all-start.3) | async-done | bytes 2150432 | tf_op jit(solution)/shard_map/all_to_all | solution.py:29
  574.7 14.6 scatter_custom_fusion.5
  590.9 5.8 gather_fusion.6
  596.7 6.3 all-to-all-start.5
  607.6 8.9 scatter_custom_fusion.11
  621.0 17.1 %scatter_fusion.11 = s32[32,64]{1,0:T(8,128)} fusion(s32[32,64]{1,0:T(8,128)} %broadcast.937.clone.2, s32[128]{0:T(128)S(1)} %get-tuple-element.64, s32[128]{0:T(128)S(1)} %copy-done.65), kind=kCustom, calls=%fused_computation.33 | custom fusion | bytes 2560 | tf_op jit(solution)/shard_map/scatter | solution.py:54
  638.3 98.1 %scatter_fusion.12 = s32[32,64]{1,0:T(8,128)} fusion(s32[32,64]{1,0:T(8,128)} %scatter_fusion.11, s32[768]{0:T(1024)S(1)} %get-tuple-element.18, s32[768]{0:T(1024)S(1)} %reshape.1342), kind=kCustom, calls=%fused_computation.34 | custom fusion | bytes 15360 | tf_op jit(solution)/shard_map/scatter | solution.py:55
  736.4 17.2 %scatter_fusion.13 = s32[32,64]{1,0:T(8,128)} fusion(s32[32,64]{1,0:T(8,128)} %scatter_fusion.12, s32[128]{0:T(128)S(1)} %copy-done.8, s32[128]{0:T(128)S(1)} %copy-done.64), kind=kCustom, calls=%fused_computation.35 | custom fusion | bytes 2560 | tf_op jit(solution)/shard_map/scatter | solution.py:56
  754.7 23.9 %all-reduce.4.cloned.1.call-done = f32[2048,300]{1,0:T(8,128)} async-done(((f32[2048,300]{1,0:T(8,128)}), f32[2048,300]{1,0:T(8,128)}) %all-reduce.4.cloned.1.call-update) | async-done | bytes 2457616 | tf_op jit(solution)/shard_map/psum | solution.py:133
  783.5 6.9 gather_fusion.11
  794.0 9.2 gather_fusion.8
  809.2 15.5 scatter_fusion.14
  825.2 5.9 all-to-all-start.11
  844.7 15.5 scatter_fusion.9
  861.7 89.6 %scatter_fusion.10 = f32[32,56,300]{2,1,0:T(8,128)} fusion(f32[32,56,300]{2,1,0:T(8,128)} %scatter_fusion.9, s32[768]{0:T(1024)S(1)} %get-tuple-element.113, f32[768,300]{1,0:T(8,128)S(1)} %multiply_divide_fusion.1), kind=kCustom, calls=%fused_computation.31 | custom fusion | bytes 2770944 | tf_op jit(solution)/shard_map/scatter | solution.py:140
  951.3 6.7 all-to-all-start.8
  971.8 48.0 %all-to-all-done.8 = f32[32,56,300]{2,1,0:T(8,128)} async-done(((f32[32,56,300]{2,1,0:T(8,128)}), f32[32,56,300]{2,1,0:T(8,128)}, u32[]{:S(2)}, u32[]{:S(2)}) %all-to-all-start.8) | async-done | bytes 2150432 | tf_op jit(solution)/shard_map/all_to_all | solution.py:29
  1025.9 14.6 scatter_custom_fusion.14
  1042.1 5.8 gather_fusion.12
  1047.9 6.3 all-to-all-start.10
  1057.4 8.9 scatter_custom_fusion.20
  1069.2 160.8 %all-reduce.6.cloned.1.call-done = f32[2048,300]{1,0:T(8,128)} async-done(((f32[2048,300]{1,0:T(8,128)}), f32[2048,300]{1,0:T(8,128)}) %all-reduce.6.cloned.1.call-update) | async-done | bytes 2457616 | tf_op jit(solution)/shard_map/psum | solution.py:133
  1234.8 6.9 gather_fusion.17
  1241.7 9.2 gather_fusion.14
  1257.6 15.5 scatter_fusion.17
  1289.6 15.5 scatter_fusion.15
  1306.7 89.7 %scatter_fusion.16 = f32[32,56,300]{2,1,0:T(8,128)} fusion(f32[32,56,300]{2,1,0:T(8,128)} %scatter_fusion.15, s32[768]{0:T(1024)S(1)} %get-tuple-element.12, f32[768,300]{1,0:T(8,128)S(1)} %multiply_divide_fusion), kind=kCustom, calls=%fused_computation.40 | custom fusion | bytes 2770944 | tf_op jit(solution)/shard_map/scatter | solution.py:140
  1396.4 6.4 all-to-all-start.13
  1405.9 9.2 scatter_custom_fusion.26
  1427.0 151.5 %all-reduce.8.cloned.1.call-done = f32[2048,300]{1,0:T(8,128)} async-done(((f32[2048,300]{1,0:T(8,128)}), f32[2048,300]{1,0:T(8,128)}) %all-reduce.8.cloned.1.call-update) | async-done | bytes 2457616 | tf_op jit(solution)/shard_map/psum | solution.py:133
  1586.7 13.9 scatter_custom_fusion.23
  (359 shorter events, 195.3 us)
Async XLA Ops:
  7.2 6.8 copy-start.56
  7.2 7.4 copy-start.67
  7.2 8.0 copy-start.49
  7.2 8.9 copy-start.57
  7.2 9.5 copy-start.68
  36.9 124.9 %copy-start.32 = (f32[1024,300]{0,1:T(8,128)S(1)}, f32[1024,300]{0,1:T(8,128)}, u32[]{:S(2)}) copy-start(f32[1024,300]{0,1:T(8,128)} %param.12) | copy-start | bytes 3686404
  154.7 14.2 all-to-all-start
  162.3 8.5 copy-start.3
  170.8 14.4 all-to-all-start.2
  185.2 152.9 %all-to-all-start.1 = ((f32[32,56,300]{2,1,0:T(8,128)}), f32[32,56,300]{2,1,0:T(8,128)}, u32[]{:S(2)}, u32[]{:S(2)}) async-start(f32[32,56,300]{2,1,0:T(8,128)} %bitcast.394), calls=%async_computation.1 | async-start | bytes 5505024 | tf_op jit(solution)/shard_map/all_to_all | solution.py:22
  195.1 6.9 copy-start.48
  338.2 38.9 %all-to-all-start.4 = ((s32[1,32,64]{2,0,1:T(1,128)}), s32[1,32,64]{2,0,1:T(1,128)S(1)}, u32[]{:S(2)}, u32[]{:S(2)}) async-start(s32[1,32,64]{2,0,1:T(1,128)} %bitcast.42), calls=%async_computation.4 | async-start | bytes 32768 | tf_op jit(solution)/shard_map/all_to_all | solution.py:17
  359.6 23.5 %copy-start.22 = (f32[128,300]{0,1:T(8,128)}, f32[128,300]{0,1:T(8,128)S(1)}, u32[]{:S(2)}) copy-start(f32[128,300]{0,1:T(8,128)S(1)} %get-tuple-element.26) | copy-start | bytes 460804
  361.3 21.9 %copy-start.13 = (f32[1024,300]{1,0:T(8,128)S(1)}, f32[1024,300]{1,0:T(8,128)}, u32[]{:S(2)}) copy-start(f32[1024,300]{1,0:T(8,128)} %gather_fusion.5) | copy-start | bytes 3686404
  377.1 128.5 %copy-start.38 = (s32[1,32,64]{2,0,1:T(1,128)}, s32[1,32,64]{2,0,1:T(1,128)S(1)}, u32[]{:S(2)}) copy-start(s32[1,32,64]{2,0,1:T(1,128)S(1)} %all-to-all-done.4) | copy-start | bytes 24580
  377.1 122.1 %all-to-all-start.6 = ((f32[32,8,300]{2,1,0:T(8,128)}), f32[32,8,300]{2,1,0:T(8,128)}, u32[]{:S(2)}, u32[]{:S(2)}) async-start(f32[32,8,300]{2,1,0:T(8,128)} %scatter_fusion.8), calls=%async_computation.6 | async-start | bytes 786432 | tf_op jit(solution)/shard_map/all_to_all | solution.py:30
  499.1 68.1 %all-to-all-start.3 = ((f32[32,56,300]{2,1,0:T(8,128)}), f32[32,56,300]{2,1,0:T(8,128)}, u32[]{:S(2)}, u32[]{:S(2)}) async-start(f32[32,56,300]{2,1,0:T(8,128)} %scatter_fusion.4), calls=%async_computation.3 | async-start | bytes 5505024 | tf_op jit(solution)/shard_map/all_to_all | solution.py:29
  567.3 29.4 %all-to-all-start.7 = ((f32[32,8,300]{2,1,0:T(8,128)}), f32[32,8,300]{2,1,0:T(8,128)S(1)}, u32[]{:S(2)}, u32[]{:S(2)}) async-start(f32[32,8,300]{2,1,0:T(8,128)} %bitcast.396), calls=%async_computation.7 | async-start | bytes 786432 | tf_op jit(solution)/shard_map/all_to_all | solution.py:23
  596.7 6.5 copy-start.44
  596.7 7.1 copy-start.54
  596.7 7.9 copy-start.17
  596.7 7.9 copy-start.23
  596.7 193.6 %all-to-all-start.5 = ((f32[32,56,300]{2,1,0:T(8,128)}), f32[32,56,300]{2,1,0:T(8,128)}, u32[]{:S(2)}, u32[]{:S(2)}) async-start(f32[32,56,300]{2,1,0:T(8,128)} %bitcast.393), calls=%async_computation.5 | async-start | bytes 5505024 | tf_op jit(solution)/shard_map/all_to_all | solution.py:22
  603.0 175.7 %all-reduce.4.cloned.1.call-start = ((), (), s32[]{:S(2)}) async-start(), calls=%async_computation.15 | async-start | bytes 6291456 | tf_op jit(solution)/shard_map/psum | solution.py:133
  638.3 98.1 %copy-start.8 = (s32[128]{0:T(128)S(1)}, s32[128]{0:T(128)}, u32[]{:S(2)}) copy-start(s32[128]{0:T(128)} %get-tuple-element.59) | copy-start | bytes 1540
  638.3 98.1 %copy-start.64 = (s32[128]{0:T(128)S(1)}, s32[128]{0:T(128)}, u32[]{:S(2)}) copy-start(s32[128]{0:T(128)} %get-tuple-element.72) | copy-start | bytes 1540
  638.3 115.3 %copy-start.47 = (s32[1024,1]{0,1:T(1,128)S(1)}, s32[1024,1]{0,1:T(1,128)}, u32[]{:S(2)}) copy-start(s32[1024,1]{0,1:T(1,128)} %get-tuple-element.31) | copy-start | bytes 12292
  638.3 115.3 %copy-start.7 = (s32[128]{0:T(128)S(1)}, s32[128]{0:T(128)}, u32[]{:S(2)}) copy-start(s32[128]{0:T(128)} %get-tuple-element.88) | copy-start | bytes 1540
  754.7 53.4 %copy-start.26 = (f32[128,300]{0,1:T(8,128)}, f32[128,300]{0,1:T(8,128)S(1)}, u32[]{:S(2)}) copy-start(f32[128,300]{0,1:T(8,128)S(1)} %copy.106) | copy-start | bytes 460804
  790.3 34.3 %all-to-all-start.9 = ((s32[1,32,64]{2,0,1:T(1,128)}), s32[1,32,64]{2,0,1:T(1,128)S(1)}, u32[]{:S(2)}, u32[]{:S(2)}) async-start(s32[1,32,64]{2,0,1:T(1,128)} %bitcast.73), calls=%async_computation.9 | async-start | bytes 32768 | tf_op jit(solution)/shard_map/all_to_all | solution.py:17
  824.6 9.9 copy-start.14
  825.2 126.1 %all-to-all-start.11 = ((f32[32,8,300]{2,1,0:T(8,128)}), f32[32,8,300]{2,1,0:T(8,128)S(1)}, u32[]{:S(2)}, u32[]{:S(2)}) async-start(f32[32,8,300]{2,1,0:T(8,128)} %scatter_fusion.14), calls=%async_computation.11 | async-start | bytes 786432 | tf_op jit(solution)/shard_map/all_to_all | solution.py:30
  844.7 15.5 copy-start.41
  844.7 15.5 copy-start.42
  951.3 68.5 %all-to-all-start.8 = ((f32[32,56,300]{2,1,0:T(8,128)}), f32[32,56,300]{2,1,0:T(8,128)}, u32[]{:S(2)}, u32[]{:S(2)}) async-start(f32[32,56,300]{2,1,0:T(8,128)} %scatter_fusion.10), calls=%async_computation.8 | async-start | bytes 5505024 | tf_op jit(solution)/shard_map/all_to_all | solution.py:29
  958.1 7.7 copy-start.1
  968.5 56.0 %copy-start.37 = (s32[1,32,64]{2,0,1:T(1,128)S(1)}, s32[1,32,64]{2,0,1:T(1,128)}, u32[]{:S(2)}) copy-start(s32[1,32,64]{2,0,1:T(1,128)} %copy-done.36) | copy-start | bytes 24580
  968.5 56.6 %copy-start.39 = (s32[32,56]{1,0:T(8,128)S(1)}, s32[32,56]{1,0:T(8,128)}, u32[]{:S(2)}) copy-start(s32[32,56]{1,0:T(8,128)} %get-tuple-element.37) | copy-start | bytes 21508
  1019.8 28.0 %all-to-all-start.12 = ((f32[32,8,300]{2,1,0:T(8,128)}), f32[32,8,300]{2,1,0:T(8,128)S(1)}, u32[]{:S(2)}, u32[]{:S(2)}) async-start(f32[32,8,300]{2,1,0:T(8,128)} %bitcast.83), calls=%async_computation.12 | async-start | bytes 786432 | tf_op jit(solution)/shard_map/all_to_all | solution.py:23
  1047.9 6.5 copy-start.25
  1047.9 193.8 %all-to-all-start.10 = ((f32[32,56,300]{2,1,0:T(8,128)}), f32[32,56,300]{2,1,0:T(8,128)}, u32[]{:S(2)}, u32[]{:S(2)}) async-start(f32[32,56,300]{2,1,0:T(8,128)} %bitcast.395), calls=%async_computation.10 | async-start | bytes 5505024 | tf_op jit(solution)/shard_map/all_to_all | solution.py:22
  1054.2 175.8 %all-reduce.6.cloned.1.call-start = ((), (), s32[]{:S(2)}) async-start(), calls=%async_computation.16 | async-start | bytes 6291456 | tf_op jit(solution)/shard_map/psum | solution.py:133
  1069.1 186.7 %copy-start.30 = (f32[128,300]{0,1:T(8,128)}, f32[128,300]{0,1:T(8,128)S(1)}, u32[]{:S(2)}) copy-start(f32[128,300]{0,1:T(8,128)S(1)} %copy.121) | copy-start | bytes 460804
  1257.6 19.1 %copy-start.15 = (f32[1024,300]{1,0:T(8,128)S(1)}, f32[1024,300]{1,0:T(8,128)}, u32[]{:S(2)}) copy-start(f32[1024,300]{1,0:T(8,128)} %gather_fusion.17) | copy-start | bytes 3686404
  1273.1 123.4 %all-to-all-start.14 = ((f32[32,8,300]{2,1,0:T(8,128)}), f32[32,8,300]{2,1,0:T(8,128)S(1)}, u32[]{:S(2)}, u32[]{:S(2)}) async-start(f32[32,8,300]{2,1,0:T(8,128)} %scatter_fusion.17), calls=%async_computation.14 | async-start | bytes 786432 | tf_op jit(solution)/shard_map/all_to_all | solution.py:30
  1289.6 15.5 copy-start.43
  1396.4 190.3 %all-to-all-start.13 = ((f32[32,56,300]{2,1,0:T(8,128)}), f32[32,56,300]{2,1,0:T(8,128)}, u32[]{:S(2)}, u32[]{:S(2)}) async-start(f32[32,56,300]{2,1,0:T(8,128)} %scatter_fusion.16), calls=%async_computation.13 | async-start | bytes 5505024 | tf_op jit(solution)/shard_map/all_to_all | solution.py:29
  1402.8 175.7 %all-reduce.8.cloned.1.call-start = ((), (), s32[]{:S(2)}) async-start(), calls=%async_computation.17 | async-start | bytes 6291456 | tf_op jit(solution)/shard_map/psum | solution.py:133
  (39 other events, 108.2 us)
Sparse Core Ops, SparseCore 0:
  616.7 161.9 all-reduce.3
  1066.5 163.3 all-reduce.5
  1415.2 163.2 all-reduce.7
where the time goes:
time: 1640 us; the launch traced here: 1610 us
  local copies, waits for them, and re-layouts  906 us (55%)
  waiting for transfers between devices  448 us (27%)
  other arithmetic  134 us (8%)
  starting transfers between devices  81 us (5%)
  matrix products  27 us (2%)
    psum x3, waiting for transfers between devices, body(): hot_total = lax.psum(hot_grad, ('gx', 'gy'))  336 us
    scatter x3, local copies, waits for them, and re-layouts, build_plan(): requests.at[bag_dest, bag_slot].set(bag_row[step_index].reshape(-1))  298 us
    scatter x3, local copies, waits for them, and re-layouts, body(): in_grads.at[bag_dest, bag_slot].set(bag_grad.reshape(-1, feature_dim))  269 us
    all_to_all x3, waiting for transfers between devices, send_grads(): lax.all_to_all(in_grads, ('gx', 'gy'), split_axis=0, concat_axis=0, tiled...  101 us
    scatter x3, local copies, waits for them, and re-layouts, build_plan(): requests = requests.at[centre_dest, centre_slot].set(centre_row[step_index])  51.9 us
    scatter x3, local copies, waits for them, and re-layouts, build_plan(): requests.at[context_dest, context_slot + cap_in]  51.8 us
    scatter x3, local copies, waits for them, and re-layouts, body(): out_grads = jnp.zeros((owners, cap_c, feature_dim), jnp.float32).at[conte...  46.7 us
    scatter x3, local copies, waits for them, and re-layouts, body(): in_grads = in_grads.at[centre_dest, centre_slot].set(word_grad)  46.5 us
  transfers between devices with their start and end apart: 18, of which 7 were waited for; matrix products, arithmetic and copies ran while one was open for 54% of the time, Pallas kernels for 0%

commit v1 on v0

v1 whole, which is shorter than its diff:
```python
import functools
import jax
import jax.numpy as jnp
from jax import lax
from jax.experimental import pallas as pl
from jax.experimental.pallas import tpu as pltpu
from jax.sharding import PartitionSpec as P

learn_rate = 2.0
exact = lax.Precision.HIGHEST
axes = ("gx", "gy")
LANES = 128
META = 16
SLOTS = 8
f32, bf16, i32 = jnp.float32, jnp.bfloat16, jnp.int32
NT = (((1,), (1,)), ((), ()))
TN = (((0,), (0,)), ((), ()))


def swap(x, bit, devices):
    return lax.ppermute(x, axes, [(d, d ^ bit) for d in range(devices)])


def split3(x):
    hi = x.astype(bf16)
    rest = x - hi.astype(f32)
    mid = rest.astype(bf16)
    return hi, mid, (rest - mid.astype(f32)).astype(bf16)


def split2(x):
    hi = x.astype(bf16)
    return hi, (x - hi.astype(f32)).astype(bf16)


class Tree:
    def __init__(self, gx, gy):
        self.gx, self.gy = gx, gy
        self.devices = gx * gy
        self.low = [1 << b for b in range(gy.bit_length() - 1)]
        self.high = [gy << b for b in range(1, gx.bit_length() - 1)]
        self.core = gy

    def widen(self, x, bits, descending):
        m = len(bits)
        x = x.reshape((1,) * m + x.shape)
        order = list(range(m))
        if descending:
            order.reverse()
        for b in order:
            x = jnp.concatenate([x, swap(x, bits[b], self.devices)], axis=m - 1 - b)
        return x.reshape((-1,) + x.shape[m + 1:])

    def gather(self, a, b):
        out = []
        for part, descending in ((a, False), (b, True)):
            x = self.widen(part[None], self.low, False)
            x = self.widen(x, self.high, descending)
            out += [x, swap(x, self.core, self.devices)]
        return out

    def gather_gx(self, a, b):
        out = []
        for part, descending in ((a, False), (b, True)):
            x = self.widen(part[None], self.high, descending)
            out += [x, swap(x, self.core, self.devices)]
        return out

    def gather_one(self, x):
        x = self.widen(x[None], self.low, False)
        x = self.widen(x, self.high, False)
        return jnp.concatenate([x, swap(x, self.core, self.devices)], axis=0)

    def reduce(self, keep, send, descending):
        x = keep + swap(send, self.core, self.devices)
        m = len(self.high)
        x = x.reshape((2,) * m + (self.gy,) + x.shape[1:])
        order = list(range(m))
        if descending:
            order.reverse()
        for b in order:
            axis = m - 1 - b
            near = lax.slice_in_dim(x, 0, 1, axis=axis)
            far = lax.slice_in_dim(x, 1, 2, axis=axis)
            x = near + swap(far, self.high[b], self.devices)
        x = x.reshape(x.shape[m:])
        for bit in reversed(self.low):
            half = x.shape[0] // 2
            x = x[:half] + swap(x[half:], bit, self.devices)
        return x[0]

    def place_of(self, mask):
        bits = self.devices.bit_length() - 1
        g, low = mask // self.gy, mask % self.gy
        return (g % 2) * (1 << (bits - 1)) + (g // 2) * self.gy + low

    def slice_mask(self, place):
        half = self.gx // 2
        return place // half + 2 * (place % half)


def params(*semantics):
    return pltpu.CompilerParams(dimension_semantics=semantics, vmem_limit_bytes=40 * 2**20)


def cost(flops, nbytes, trans=0):
    return pl.CostEstimate(flops=int(flops), bytes_accessed=int(nbytes), transcendentals=int(trans))


def lane_pair(ref0, ref1):
    return jnp.concatenate([ref0[0], ref1[0]], axis=1)


def count_kernel(width, offset_ref, ids_ref, out_ref):
    offset = offset_ref[pl.program_id(1)]
    ids = ids_ref[0, 0, SLOTS:, :] - offset
    hot = lax.broadcasted_iota(i32, (width, LANES), 0)
    total = jnp.zeros((8, width), f32)
    ones = jnp.ones((8, LANES), bf16)
    for k in range(META - SLOTS):
        same = (hot == ids[k:k + 1, :]).astype(f32).astype(bf16)
        total = total + lax.dot_general(ones, same, NT, preferred_element_type=f32)
    out_ref[0, 0] = total[0:1, :]


def count(meta, offsets, width, ids_index):
    steps = meta.shape[1]
    places = offsets.shape[0]
    return pl.pallas_call(
        functools.partial(count_kernel, width),
        out_shape=jax.ShapeDtypeStruct((steps, places, 1, width), f32),
        grid_spec=pltpu.PrefetchScalarGridSpec(
            num_scalar_prefetch=1,
            grid=(steps, places),
            in_specs=[pl.BlockSpec((1, 1, META, LANES), ids_index)],
            out_specs=pl.BlockSpec((1, 1, 1, width), lambda s, p, o: (s, p, 0, 0)),
        ),
        compiler_params=params("arbitrary", "arbitrary"),
        cost_estimate=cost(steps * places * 2 * 8 * width * 1024, steps * places * 8192),
        name="count",
    )(offsets, meta)


def couple_kernel(own_ref, other_ref, in_ref, out_ref, wide):
    @pl.when(pl.program_id(0) == 0)
    def _():
        for k in range(SLOTS):
            wide[k] = jnp.broadcast_to(own_ref[0, :, k:k + 1], wide.shape[1:])

    for c in range(2):
        total = jnp.zeros(wide.shape[1:], f32)
        for k in range(SLOTS - 1):
            row = other_ref[c, 0, 0, k:k + 1, :]
            in_bag = wide[1] == row
            for j in range(2, SLOTS - 1):
                in_bag = in_bag | (wide[j] == row)
            total = total + jnp.where(in_bag, 1.0, 0.0) + jnp.where(wide[0] == row, 1.0, 0.0)
        in_ref[c, 0] = total.astype(bf16)
        same = wide[SLOTS - 1] == other_ref[c, 0, 0, SLOTS - 1:SLOTS, :]
        out_ref[c, 0] = jnp.where(same, 1.0, 0.0).astype(bf16)


def couple(own, meta, later, earlier):
    half, n = meta.shape[1], own.shape[1]
    shape = jax.ShapeDtypeStruct((2, half, n, n), bf16)
    spec = pl.BlockSpec((2, 1, n, n), lambda p: (0, p, 0, 0))
    return pl.pallas_call(
        couple_kernel,
        out_shape=(shape, shape),
        grid=(half,),
        in_specs=[
            pl.BlockSpec((1, n, SLOTS), lambda p: (later, 0, 0)),
            pl.BlockSpec((2, 1, 1, META, LANES), lambda p: (0, p, earlier, 0, 0)),
        ],
        out_specs=(spec, spec),
        scratch_shapes=[pltpu.VMEM((SLOTS, n, n), i32)],
        compiler_params=params("arbitrary"),
        cost_estimate=cost(half * 2 * n * n * 150, half * n * n * 8),
        name="couple",
    )(own, meta)


def chosen(ref, base, rows, context):
    parts = []
    for c in range(2):
        ids = ref[c, 0, 0, :SLOTS, :] - base
        lane_iota = lax.broadcasted_iota(i32, (rows, LANES), 0)
        if context:
            parts.append(jnp.where(lane_iota == ids[SLOTS - 1:, :], 1.0, 0.0))
        else:
            ids = jnp.where((ids >= 0) & (ids < rows), ids, -1)
            bag = jnp.max(ids[1:SLOTS - 1, :], axis=0, keepdims=True)
            parts.append(jnp.where(lane_iota == ids[0:1, :], 1.0, 0.0) + jnp.where(lane_iota == bag, 1.0, 0.0))
    return jnp.concatenate(parts, axis=1).astype(bf16)


def base_kernel(rows, base_ref, meta_ref, table_ref, a0, a1, b0, b1, parts):
    @pl.when(pl.program_id(0) == 0)
    def _():
        for k, part in enumerate(split3(table_ref[...])):
            parts[k] = part

    pick = chosen(meta_ref, base_ref[0], rows, False)
    total = jnp.dot(parts[0], pick, preferred_element_type=f32)
    for k in (1, 2):
        total = total + jnp.dot(parts[k], pick, preferred_element_type=f32)
    h = a0.shape[1]
    a0[0] = total[:h, :LANES]
    a1[0] = total[:h, LANES:]
    b0[0] = total[h:, :LANES]
    b1[0] = total[h:, LANES:]


def base_sums(table_t, meta, base, step):
    half = meta.shape[1]
    feats, rows = table_t.shape
    shape = jax.ShapeDtypeStruct((half, feats // 2, LANES), f32)
    spec = pl.BlockSpec((1, feats // 2, LANES), lambda p, b: (p, 0, 0))
    return pl.pallas_call(
        functools.partial(base_kernel, rows),
        out_shape=(shape,) * 4,
        grid_spec=pltpu.PrefetchScalarGridSpec(
            num_scalar_prefetch=1,
            grid=(half,),
            in_specs=[
                pl.BlockSpec((2, 1, 1, META, LANES), lambda p, b: (0, p, step, 0, 0)),
                pl.BlockSpec((feats, rows), lambda p, b: (0, 0)),
            ],
            out_specs=(spec,) * 4,
            scratch_shapes=[pltpu.VMEM((3, feats, rows), bf16)],
        ),
        compiler_params=params("arbitrary"),
        cost_estimate=cost(2 * 3 * half * 256 * feats * rows, half * 2 * feats * 512 + feats * rows * 4),
        name="base_sums",
    )(base, meta, table_t)


def update_kernel(rows, context, base_ref, meta_ref, table_ref, *refs):
    out_ref = refs[-1]
    ga0, ga1, gb0, gb1 = refs[:4]

    @pl.when(pl.program_id(0) == 0)
    def _():
        out_ref[...] = table_ref[...]

    pick = chosen(meta_ref, base_ref[0], rows, context)
    h = ga0.shape[1]
    if context:
        ca0, ca1, cb0, cb1, pos_row = refs[4], refs[5], refs[6], refs[7], refs[8]
        del pos_row
    halves = [lane_pair(ga0, ga1), lane_pair(gb0, gb1)]
    if context:
        at = out_ref.shape[0] - 4 - h
        pos = halves[1][at:at + 1, :]
        halves = [lane_pair(ca0, ca1) * pos, lane_pair(cb0, cb1) * pos]
    for k in range(2):
        part = jnp.zeros((h, rows), f32)
        for piece in split2(halves[k] * learn_rate):
            part = part + lax.dot_general(piece, pick, NT, preferred_element_type=f32)
        out_ref[k * h:(k + 1) * h, :] = out_ref[k * h:(k + 1) * h, :] - part


def update(table_t, meta, base, step, g, c=None):
    half = meta.shape[1]
    feats, rows = table_t.shape
    piece = pl.BlockSpec((1, feats // 2, LANES), lambda p, b: (p, 0, 0))
    whole = pl.BlockSpec((feats, rows), lambda p, b: (0, 0))
    context = c is not None
    arrays = list(g) + (list(c) if context else [])
    kernel = functools.partial(context_update_kernel if context else update_kernel, rows, context)
    return pl.pallas_call(
        kernel,
        out_shape=jax.ShapeDtypeStruct((feats, rows), f32),
        grid_spec=pltpu.PrefetchScalarGridSpec(
            num_scalar_prefetch=1,
            grid=(half,),
            in_specs=[pl.BlockSpec((2, 1, 1, META, LANES), lambda p, b: (0, p, step, 0, 0)), whole]
            + [piece] * len(arrays),
            out_specs=whole,
        ),
        compiler_params=params("arbitrary"),
        cost_estimate=cost(2 * 2 * half * 256 * feats * rows, half * 2 * feats * 512 * len(arrays) // 4),
        name="context_update" if context else "update",
    )(base, meta, table_t, *arrays)


def context_update_kernel(rows, context, base_ref, meta_ref, table_ref, *refs):
    update_kernel(rows, context, base_ref, meta_ref, table_ref, *refs[:8], None, refs[8])


def absorb_kernel(width, ga0, ga1, gb0, gb1, ca0, ca1, cb0, cb1, in_ref, ctx_ref, c_out, x_out):
    @pl.when(pl.program_id(0) == 0)
    def _():
        c_out[...] = jnp.zeros_like(c_out)
        x_out[...] = jnp.zeros_like(x_out)

    h = ga0.shape[1]
    in_pair = jnp.concatenate([in_ref[0, 0], in_ref[1, 0]], axis=1)
    ctx_pair = jnp.concatenate([ctx_ref[0, 0], ctx_ref[1, 0]], axis=1)
    ga, gb = lane_pair(ga0, ga1), lane_pair(gb0, gb1)
    pos = gb[width - h:width - h + 1, :]
    for k, (grad, centre) in enumerate(((ga, lane_pair(ca0, ca1)), (gb, lane_pair(cb0, cb1)))):
        at = pl.ds(k * h, h)
        part = jnp.zeros((h, c_out.shape[1]), f32)
        for piece in split3(grad * learn_rate):
            part = part + lax.dot_general(piece, in_pair, NT, preferred_element_type=f32)
        c_out[at, :] += part
        part = jnp.zeros((h, c_out.shape[1]), f32)
        for piece in split3(centre * pos * learn_rate):
            part = part + lax.dot_general(piece, ctx_pair, NT, preferred_element_type=f32)
        x_out[at, :] += part


def absorb(width, g, c, in_pairs, ctx_pairs):
    half, feats_half, n = g[0].shape
    piece = pl.BlockSpec((1, feats_half, n), lambda p: (p, 0, 0))
    pair = pl.BlockSpec((2, 1, n, n), lambda p: (0, p, 0, 0))
    shape = jax.ShapeDtypeStruct((2 * feats_half, n), f32)
    spec = pl.BlockSpec((2 * feats_half, n), lambda p: (0, 0))
    return pl.pallas_call(
        functools.partial(absorb_kernel, width),
        out_shape=(shape, shape),
        grid=(half,),
        in_specs=[piece] * 8 + [pair] * 2,
        out_specs=(spec, spec),
        compiler_params=params("arbitrary"),
        cost_estimate=cost(2 * 2 * 3 * half * 256 * feats_half * 2 * n, half * 256 * feats_half * 16),
        name="absorb",
    )(*g, *c, in_pairs, ctx_pairs)


def own_kernel(width, scale, c_ref, x_ref, denom_ref, cnt_ref, a0, a1, b0, b1, out_ref, total):
    p = pl.program_id(0)

    @pl.when(p == 0)
    def _():
        total[...] = jnp.zeros_like(total)

    centre = c_ref[...]
    for c, (a, b) in enumerate(((a0, b0), (a1, b1))):
        hot = jnp.concatenate([a[0], b[0]], axis=0)
        scores = lax.dot_general(centre, hot, TN, precision=exact, preferred_element_type=f32)
        grad = (scale * cnt_ref[0, c, 0]) * jax.nn.sigmoid(scores)
        total[...] += lax.dot_general(hot, grad, NT, precision=exact, preferred_element_type=f32)

    @pl.when(p == pl.num_programs(0) - 1)
    def _():
        context = x_ref[...]
        positive = jnp.sum(centre * context, axis=0, keepdims=True)
        pos = jax.nn.sigmoid(positive) - 1.0
        grad = (pos * context + total[...]) / denom_ref[...]
        feature = lax.broadcasted_iota(i32, grad.shape, 0)
        out_ref[...] = jnp.where(feature == width, pos, grad)


def own_grads(width, scale, centre, context, denom, cnt, hot):
    feats, n = centre.shape
    half, feats_half, hot_slice = hot[0].shape
    whole = pl.BlockSpec((feats, n), lambda p: (0, 0))
    piece = pl.BlockSpec((1, feats_half, hot_slice), lambda p: (p, 0, 0))
    return pl.pallas_call(
        functools.partial(own_kernel, width, scale),
        out_shape=jax.ShapeDtypeStruct((feats, n), f32),
        grid=(half,),
        in_specs=[
            whole,
            whole,
            pl.BlockSpec((1, n), lambda p: (0, 0)),
            pl.BlockSpec((1, 2, 1, 1, hot_slice), lambda p: (0, 0, p, 0, 0)),
        ]
        + [piece] * 4,
        out_specs=whole,
        scratch_shapes=[pltpu.VMEM((feats, n), f32)],
        compiler_params=params("arbitrary"),
        cost_estimate=cost(2 * 2 * 6 * half * 2 * hot_slice * feats * n, half * 4 * feats_half * hot_slice * 4),
        name="own_grads",
    )(centre, context, denom, cnt, *hot)


def hot_kernel(scale, cnt_ref, hot_a, hot_b, a0, a1, b0, b1, out_a, out_b, total):
    p = pl.program_id(0)

    @pl.when(p == 0)
    def _():
        total[...] = jnp.zeros_like(total)

    hot = jnp.concatenate([hot_a[0], hot_b[0]], axis=0)
    for c, (a, b) in enumerate(((a0, b0), (a1, b1))):
        centre = jnp.concatenate([a[0], b[0]], axis=0)
        scores = lax.dot_general(centre, hot, TN, precision=exact, preferred_element_type=f32)
        grad = (scale * cnt_ref[0, c, 0]) * jax.nn.sigmoid(scores)
        total[...] += jnp.dot(centre, grad, precision=exact, preferred_element_type=f32)

    @pl.when(p == pl.num_programs(0) - 1)
    def _():
        h = out_a.shape[0]
        out_a[...] = hot_a[0] - learn_rate * total[:h, :]
        out_b[...] = hot_b[0] - learn_rate * total[h:, :]


def hot_update(scale, cnt, hot, c):
    half, feats_half, n = c[0].shape
    hot_slice = hot[0].shape[2]
    shape = jax.ShapeDtypeStruct((feats_half, hot_slice), f32)
    out = pl.BlockSpec((feats_half, hot_slice), lambda p: (0, 0))
    first = pl.BlockSpec((1, feats_half, hot_slice), lambda p: (0, 0, 0))
    piece = pl.BlockSpec((1, feats_half, n), lambda p: (p, 0, 0))
    return pl.pallas_call(
        functools.partial(hot_kernel, scale),
        out_shape=(shape, shape),
        grid=(half,),
        in_specs=[pl.BlockSpec((1, 2, 1, 1, hot_slice), lambda p: (0, 0, p, 0, 0)), first, first] + [piece] * 4,
        out_specs=(out, out),
        scratch_shapes=[pltpu.VMEM((2 * feats_half, hot_slice), f32)],
        compiler_params=params("arbitrary"),
        cost_estimate=cost(2 * 2 * 6 * half * 256 * hot_slice * feats_half * 2, half * 256 * feats_half * 8),
        name="hot_update",
    )(cnt, hot[0], hot[2], *c)


def fetch_contexts(tree, me, out_table, meta_flat, owner, cap):
    rows, width = out_table.shape
    devices, steps = meta_flat.shape[0], meta_flat.shape[1]
    n = owner.shape[1]
    ids = meta_flat[:, :, SLOTS - 1, :] - me * rows
    mine = (ids >= 0) & (ids < rows)
    before = jnp.triu(jnp.ones((n, n), bf16), 1)
    rank = jnp.dot(mine.astype(bf16), before, preferred_element_type=f32).astype(i32)
    slots = jnp.arange(cap, dtype=i32)
    hit = mine[:, :, None, :] & (rank[:, :, None, :] == slots[None, None, :, None])
    wanted = jnp.sum(jnp.where(hit, ids[:, :, None, :], 0), axis=3)
    order = tree.place_of(me ^ jnp.arange(devices, dtype=i32))
    wanted = wanted[order].reshape(devices, steps * cap)
    got = lax.all_to_all(out_table[wanted], axes, split_axis=0, concat_axis=0, tiled=True)
    same = (owner[:, :, None] == owner[:, None, :]) & (
        jnp.arange(n)[None, :, None] > jnp.arange(n)[None, None, :]
    )
    own_rank = jnp.sum(same.astype(i32), axis=2)
    at = (owner * steps + jnp.arange(steps, dtype=i32)[:, None]) * cap + own_rank
    return got.reshape(devices * steps * cap, width)[at]


def body(
    in_table,
    out_table,
    hot_table,
    centre_owner,
    centre_row,
    bag_owner,
    bag_row,
    bag_len,
    context_owner,
    context_row,
    negative_ids,
):
    gx, gy = lax.axis_size("gx"), lax.axis_size("gy")
    tree = Tree(gx, gy)
    devices = tree.devices
    me_x = lax.axis_index("gx").astype(i32)
    me = me_x * gy + lax.axis_index("gy").astype(i32)
    steps, n, bag = bag_row.shape
    rows, width = in_table.shape
    out_rows = out_table.shape[0]
    hot_rows = hot_table.shape[0]
    neg = negative_ids.shape[1]
    cap = max(2, 2 * n // devices)
    hot_slice = hot_rows // gx
    feats = -(-(width + 1) // 16) * 16
    h = feats // 2
    scale = 16.0 / neg

    kept = jnp.arange(bag, dtype=i32)[None, None, :] < bag_len[:, :, None]
    centre_ids = centre_owner * rows + centre_row[:, :, None]
    bag_ids = bag_owner * rows + bag_row
    context_ids = context_owner * out_rows + context_row[:, :, None]
    own = jnp.concatenate([centre_ids, jnp.where(kept, bag_ids, -2), context_ids], axis=2)
    sent = jnp.concatenate([centre_ids, jnp.where(kept, bag_ids, -1), context_ids], axis=2)
    meta = jnp.concatenate(
        [jnp.swapaxes(sent, 1, 2), negative_ids.reshape(steps, META - SLOTS, LANES)], axis=1
    )
    meta_flat = tree.gather_one(meta.reshape(steps * META, LANES)).reshape(devices, steps, META, LANES)
    meta_all = meta_flat.reshape(2, devices // 2, steps, META, LANES)

    in_base = (me * rows).reshape(1)
    out_base = (me * out_rows).reshape(1)
    spare = ((0, feats - width), (0, 0))
    in_t = jnp.pad(in_table.T, spare)
    out_t = jnp.pad(out_table.T, spare)
    slice_of = me_x ^ tree.slice_mask(jnp.arange(gx, dtype=i32))
    hot_t = jnp.pad(hot_table, ((0, 0), (0, feats - width))).reshape(gx, hot_slice, feats)
    hot_t = jnp.swapaxes(hot_t[slice_of], 1, 2)
    hot = [hot_t[: gx // 2, :h], hot_t[gx // 2:, :h], hot_t[: gx // 2, h:], hot_t[gx // 2:, h:]]

    own_cnt = count(meta[None], slice_of * hot_slice, hot_slice, lambda s, p, o: (0, s, 0, 0))
    all_cnt = count(
        meta_flat, jnp.full((devices,), 0, i32) + me_x * hot_slice, hot_slice, lambda s, p, o: (p, s, 0, 0)
    )
    own_cnt = own_cnt.reshape(steps, 2, gx // 2, 1, hot_slice)
    all_cnt = all_cnt.reshape(steps, 2, devices // 2, 1, hot_slice)

    denom = 1.0 + bag_len.astype(f32)
    base = []
    source = in_t
    for s in range(steps):
        a0, a1, b0, b1 = base_sums(source, meta_all, in_base, s)
        base.append(jnp.concatenate([tree.reduce(a0, a1, True), tree.reduce(b0, b1, False)], axis=0))
        if devices > 64:
            source, base[s] = lax.optimization_barrier((source, base[s]))
    context = fetch_contexts(tree, me, out_table, meta_flat, context_owner[:, :, 0], cap)
    context = [jnp.pad(context[s].T, spare) for s in range(steps)]
    pairs = {(s, e): couple(own, meta_all, s, e) for s in range(steps) for e in range(s)}

    if devices > 64:
        base, context = lax.optimization_barrier((base, context))
    real = jnp.arange(feats)[:, None] < width
    for s in range(steps):
        centre = jnp.where(real, base[s] / denom[s][None, :], 0.0)
        c = tree.gather(centre[:h], centre[h:])
        g = own_grads(width, scale, centre, context[s], denom[s][None, :], own_cnt[s:s + 1], hot)
        g = tree.gather(g[:h], g[h:])
        new_a, new_b = hot_update(scale, all_cnt[s:s + 1], hot, c)
        hot = tree.gather_gx(new_a, new_b)
        for later in range(s + 1, steps):
            centre_add, context_add = absorb(width, g, c, *pairs[(later, s)])
            base[later] = base[later] - centre_add
            context[later] = context[later] - context_add
        in_t = update(in_t, meta_all, in_base, s, g)
        out_t = update(out_t, meta_all, out_base, s, g, c)
        if devices > 64:
            in_t, out_t, hot, base, context = lax.optimization_barrier((in_t, out_t, hot, base, context))

    hot = jnp.concatenate([jnp.concatenate(hot[:2], axis=0), jnp.concatenate(hot[2:], axis=0)], axis=1)
    place = me_x ^ jnp.arange(gx, dtype=i32)
    hot = hot[place // 2 + (gx // 2) * (place % 2)]
    hot = jnp.swapaxes(hot, 1, 2).reshape(hot_rows, feats)[:, :width]
    return in_t[:width].T, out_t[:width].T, hot


def solution(mesh):
    placed = (
        P(axes, None),
        P(axes, None),
        P(),
        P(None, axes, None),
        P(None, axes),
        P(None, axes, None),
        P(None, axes, None),
        P(None, axes),
        P(None, axes, None),
        P(None, axes),
        P(None, axes),
    )
    return jax.shard_map(
        body,
        mesh=mesh,
        in_specs=placed,
        out_specs=(P(axes, None), P(axes, None), P()),
        check_vma=False,
    )
```

time: 1640 us -> 738 us (0.45); the launches traced: 1610 us -> 727 us
  local copies, waits for them, and re-layouts: 906 us -> 70 us
  Pallas kernels: 0 us -> 324 us
  waiting for transfers between devices: 448 us -> 175 us
  other arithmetic: 134 us -> 38.7 us
  starting transfers between devices: 81 us -> 116 us
  matrix products: 27 us -> 0.13 us
    scatter x18 -> x0, local copies, waits for them, and re-layouts: 764 us -> none  [the longest x3 298 us: build_plan(): requests.at[bag_dest, bag_slot].set(bag_row[step_index].reshape(-1))]
    psum x3 -> x0, waiting for transfers between devices: 336 us -> none  [body(): hot_total = lax.psum(hot_grad, ('gx', 'gy'))]
    pallas_call x0 -> x23, Pallas kernels: none -> 324 us  [the longest x6 90.4 us: update(): pl.pallas_call(kernel, out_shape=jax.ShapeDtypeStruct((feats, rows), f32)...]
    ppermute x0 -> x113, waiting for transfers between devices: none -> 175 us  [swap(): return lax.ppermute(x, axes, [(d, d ^ bit) for d in range(devices)])]
    ppermute x0 -> x113, starting transfers between devices: none -> 112 us  [swap(): return lax.ppermute(x, axes, [(d, d ^ bit) for d in range(devices)])]
    all_to_all x15 -> x1, waiting for transfers between devices: 112 us -> 0.01 us  [fetch_contexts(): lax.all_to_all(out_table[wanted], axes, split_axis=0, concat_axis=0, tile...]
    scatter-add x9 -> x0, other arithmetic: 80.6 us -> none  [the longest x3 43.1 us: body(): in_total = jnp.zeros(in_table.shape, jnp.float32).at[in_wanted.reshape(-1...]
    all_to_all x15 -> x1, starting transfers between devices: 80.5 us -> 3.78 us  [fetch_contexts(): lax.all_to_all(out_table[wanted], axes, split_axis=0, concat_axis=0, tile...]
  transfers between devices with their start and end apart: 18 -> 114, of which waited for: 7 -> 39; matrix products, arithmetic and copies ran while one was open for 54% -> 10% of each run, Pallas kernels for 0% -> 41%
where the time goes in v1:
time: 738 us; the launch traced here: 727 us
  Pallas kernels  324 us (44%)
  waiting for transfers between devices  175 us (24%)
  starting transfers between devices  116 us (16%)
  local copies, waits for them, and re-layouts  70 us (9%)
  other arithmetic  38.7 us (5%)
    ppermute x113, waiting for transfers between devices, swap(): return lax.ppermute(x, axes, [(d, d ^ bit) for d in range(devices)])  175 us
    ppermute x113, starting transfers between devices, swap(): return lax.ppermute(x, axes, [(d, d ^ bit) for d in range(devices)])  112 us
    pallas_call x6, Pallas kernels, update(): pl.pallas_call(kernel, out_shape=jax.ShapeDtypeStruct((feats, rows), f32)...  90.4 us
    pallas_call x3, Pallas kernels, hot_update(): pl.pallas_call(functools.partial(hot_kernel, scale), out_shape=(shape, sh...  80.8 us
    pallas_call x3, Pallas kernels, base_sums(): pl.pallas_call(functools.partial(base_kernel, rows), out_shape=(shape,) *...  40.3 us
    pallas_call x2, Pallas kernels, count(): pl.pallas_call(functools.partial(count_kernel, width), out_shape=jax.Shap...  32.8 us
    pallas_call x3, Pallas kernels, couple(): pl.pallas_call(couple_kernel, out_shape=(shape, shape), grid=(half,), in_...  30.8 us
    unnamed x218, local copies, waits for them, and re-layouts  29.9 us
  transfers between devices with their start and end apart: 114, of which 39 were waited for; matrix products, arithmetic and copies ran while one was open for 10% of the time, Pallas kernels for 41%

profile of v1, /device:TPU:0, one launch (start us, length us, event | category | flops | bytes accessed | tf_op | source)
XLA Modules:
  0.0 727.1 jit_solution(12156798428189527167)
XLA Ops:
  9.8 6.9 count.2
  38.0 4.3 gather_fusion.3
  48.3 13.4 %base_sums.5 = (f32[16,152,128]{2,1,0:T(8,128)S(1)}, f32[16,152,128]{2,1,0:T(8,128)S(1)}, f32[16,152,128]{2,1,0:T(8,128)S(1)}, f32[16,152,128]{2,1,0:T(8,128)}) custom-call(s32[1]{0:T(128)} %bitcast.base_ref, s32[2,16,3,16,128]{4,3,2,1,0:T(8,128)S(1)} %bitcast.196, f32[304,1024]{1,0:T(8,128)S(1)} %pad.20.table_ref), custom_call_target="tpu_custom_call" | custom-call | flops 7650410496 | bytes 6225920 | tf_op jit(solution)/shard_map/base_sums/pallas_call | solution.py:219
  63.8 13.5 %base_sums.4 = (f32[16,152,128]{2,1,0:T(8,128)S(1)}, f32[16,152,128]{2,1,0:T(8,128)}, f32[16,152,128]{2,1,0:T(8,128)S(1)}, f32[16,152,128]{2,1,0:T(8,128)}) custom-call(s32[1]{0:T(128)} %bitcast.base_ref, s32[2,16,3,16,128]{4,3,2,1,0:T(8,128)S(1)} %bitcast.197, f32[304,1024]{1,0:T(8,128)S(1)} %pad.20.table_ref), custom_call_target="tpu_custom_call" | custom-call | flops 7650410496 | bytes 6225920 | tf_op jit(solution)/shard_map/base_sums/pallas_call | solution.py:219
  81.7 4.7 gather_fusion.1
  86.3 3.8 all-to-all-start
  92.3 13.4 %base_sums.3 = (f32[16,152,128]{2,1,0:T(8,128)S(1)}, f32[16,152,128]{2,1,0:T(8,128)}, f32[16,152,128]{2,1,0:T(8,128)S(1)}, f32[16,152,128]{2,1,0:T(8,128)S(1)}) custom-call(s32[1]{0:T(128)} %bitcast.base_ref, s32[2,16,3,16,128]{4,3,2,1,0:T(8,128)S(1)} %bitcast.198, f32[304,1024]{1,0:T(8,128)S(1)} %copy-done.33), custom_call_target="tpu_custom_call" | custom-call | flops 7650410496 | bytes 6225920 | tf_op jit(solution)/shard_map/base_sums/pallas_call | solution.py:219
  115.2 25.9 %count.3 = f32[3,32,1,256]{3,2,1,0:T(1,128)S(1)} custom-call(s32[32]{0:T(128)S(1)} %add.357.offset_ref, s32[32,3,16,128]{3,2,1,0:T(8,128)S(1)} %pad_add_fusion.ids_ref), custom_call_target="tpu_custom_call" | custom-call | flops 402653184 | bytes 786432 | tf_op jit(solution)/shard_map/count/pallas_call | solution.py:129
  153.0 10.3 %couple.5 = (bf16[2,16,128,128]{3,2,1,0:T(8,128)(2,1)S(1)}, bf16[2,16,128,128]{3,2,1,0:T(8,128)(2,1)S(1)}) custom-call(s32[3,128,8]{2,1,0:T(8,128)S(1)} %pad_add_fusion.4.own_ref, s32[2,16,3,16,128]{4,3,2,1,0:T(8,128)S(1)} %bitcast.199), custom_call_target="tpu_custom_call" | custom-call | flops 78643200 | bytes 2097152 | tf_op jit(solution)/shard_map/couple/pallas_call | solution.py:167
  165.3 10.3 %couple.4 = (bf16[2,16,128,128]{3,2,1,0:T(8,128)(2,1)S(1)}, bf16[2,16,128,128]{3,2,1,0:T(8,128)(2,1)S(1)}) custom-call(s32[3,128,8]{2,1,0:T(8,128)S(1)} %pad_add_fusion.4.own_ref, s32[2,16,3,16,128]{4,3,2,1,0:T(8,128)S(1)} %bitcast.200), custom_call_target="tpu_custom_call" | custom-call | flops 78643200 | bytes 2097152 | tf_op jit(solution)/shard_map/couple/pallas_call | solution.py:167
  177.6 10.3 %couple.3 = (bf16[2,16,128,128]{3,2,1,0:T(8,128)(2,1)S(1)}, bf16[2,16,128,128]{3,2,1,0:T(8,128)(2,1)S(1)}) custom-call(s32[3,128,8]{2,1,0:T(8,128)S(1)} %pad_add_fusion.4.own_ref, s32[2,16,3,16,128]{4,3,2,1,0:T(8,128)S(1)} %bitcast.201), custom_call_target="tpu_custom_call" | custom-call | flops 78643200 | bytes 2097152 | tf_op jit(solution)/shard_map/couple/pallas_call | solution.py:167
  198.4 3.2 gather_fusion.2
  214.7 6.9 collective-permute-done.11
  224.3 10.5 %collective-permute-done.27 = f32[1,1,4,152,128]{4,3,2,1,0:T(8,128)S(1)} collective-permute-done((f32[1,1,4,152,128]{4,3,2,1,0:T(8,128)S(1)}, f32[1,1,4,152,128]{4,3,2,1,0:T(8,128)S(1)}, u32[]{:S(2)}, u32[]{:S(2)}) %collective-permute-start.27) | collective-permute-done | bytes 311328 | tf_op jit(solution)/shard_map/ppermute | solution.py:21
  243.6 10.3 %collective-permute-done.8 = f32[2,152,128]{2,1,0:T(8,128)S(1)} collective-permute-done((f32[2,152,128]{2,1,0:T(8,128)S(1)}, f32[2,152,128]{2,1,0:T(8,128)S(1)}, u32[]{:S(2)}, u32[]{:S(2)}) %collective-permute-start.8) | collective-permute-done | bytes 155680 | tf_op jit(solution)/shard_map/ppermute | solution.py:21
  261.0 7.0 own_grads.3
  275.0 3.9 collective-permute-start.21
  282.0 12.8 %collective-permute-done.41 = f32[1,2,1,152,128]{4,3,2,1,0:T(8,128)S(1)} collective-permute-done((f32[1,2,1,152,128]{4,3,2,1,0:T(8,128)S(1)}, f32[1,2,1,152,128]{4,3,2,1,0:T(8,128)S(1)}, u32[]{:S(2)}, u32[]{:S(2)}) %collective-permute-start.41) | collective-permute-done | bytes 155680 | tf_op jit(solution)/shard_map/ppermute | solution.py:21
  294.9 4.7 collective-permute-done.36
  305.1 4.2 collective-permute-done.42
  315.9 4.0 collective-permute-done.17
  322.6 10.6 %collective-permute-done.43 = f32[2,1,4,152,128]{4,3,2,1,0:T(8,128)S(1)} collective-permute-done((f32[2,1,4,152,128]{4,3,2,1,0:T(8,128)S(1)}, f32[2,1,4,152,128]{4,3,2,1,0:T(8,128)S(1)}, u32[]{:S(2)}, u32[]{:S(2)}) %collective-permute-start.43) | collective-permute-done | bytes 622624 | tf_op jit(solution)/shard_map/ppermute | solution.py:21
  334.2 7.8 %collective-permute-done.23 = f32[2,1,4,152,128]{4,3,2,1,0:T(8,128)S(1)} collective-permute-done((f32[2,1,4,152,128]{4,3,2,1,0:T(8,128)S(1)}, f32[2,1,4,152,128]{4,3,2,1,0:T(8,128)S(1)}, u32[]{:S(2)}, u32[]{:S(2)}) %collective-permute-start.23) | collective-permute-done | bytes 622624 | tf_op jit(solution)/shard_map/ppermute | solution.py:21
  352.5 26.5 %hot_update.3 = (f32[152,256]{1,0:T(8,128)S(1)}, f32[152,256]{1,0:T(8,128)S(1)}) custom-call(f32[1,2,16,1,256]{4,3,2,1,0:T(1,128)S(1)} %bitcast.288, f32[4,152,256]{2,1,0:T(8,128)S(1)} %copy-done.49, f32[4,152,256]{2,1,0:T(8,128)S(1)} %copy-done.48, f32[16,152,128]{2,1,0:T(8,128)S(1)} %bitcast.214, ...), custom_call_target="tpu_custom_call" | custom-call | flops 7650410496 | bytes 4980736 | tf_op jit(solution)/shard_map/hot_update/pallas_call | solution.py:408
  382.2 7.6 %absorb.3 = (f32[304,128]{1,0:T(8,128)S(1)}, f32[304,128]{1,0:T(8,128)S(1)}) custom-call(f32[16,152,128]{2,1,0:T(8,128)S(1)} %bitcast.224, f32[16,152,128]{2,1,0:T(8,128)S(1)} %collective-permute-done.19.refs_1_.ga1, f32[16,152,128]{2,1,0:T(8,128)S(1)} %bitcast.219, f32[16,152,128]{2,1,0:T(8,128)S(1)} %collective-permute-done.24.refs_3_.gb1, ...), custom_call_target="tpu_custom_call" | custom-call | flops 1912602624 | bytes 9961472 | tf_op jit(solution)/shard_map/absorb/pallas_call | solution.py:320
  400.3 3.4 collective-permute-start.77
  405.5 5.3 collective-permute-done.77
  415.0 6.8 own_grads.4
  433.7 10.4 %collective-permute-done.52 = f32[1,2,1,152,128]{4,3,2,1,0:T(8,128)S(1)} collective-permute-done((f32[1,2,1,152,128]{4,3,2,1,0:T(8,128)S(1)}, f32[1,2,1,152,128]{4,3,2,1,0:T(8,128)S(1)}, u32[]{:S(2)}, u32[]{:S(2)}) %collective-permute-start.52) | collective-permute-done | bytes 155680 | tf_op jit(solution)/shard_map/ppermute | solution.py:21
  447.6 4.8 collective-permute-done.53
  455.3 6.2 collective-permute-done.69
  461.5 6.5 collective-permute-done.59
  469.2 26.5 %hot_update.4 = (f32[152,256]{1,0:T(8,128)S(1)}, f32[152,256]{1,0:T(8,128)S(1)}) custom-call(f32[1,2,16,1,256]{4,3,2,1,0:T(1,128)S(1)} %bitcast.287, f32[4,152,256]{2,1,0:T(8,128)S(1)} %bitcast.264, f32[4,152,256]{2,1,0:T(8,128)S(1)} %bitcast.267, f32[16,152,128]{2,1,0:T(8,128)S(1)} %bitcast.233, f32[16,152,128]{2,1,0:T(8,128)S(1)} %collective-permute-done.75.ca1.a1.refs_5_, ...), custom_call_target="tpu_custom_call" | custom-call | flops 7650410496 | bytes 4980736 | tf_op jit(solution)/shard_map/hot_update/pallas_call | solution.py:408
  497.9 4.3 collective-permute-done.84
  505.1 7.8 %absorb.4 = (f32[304,128]{1,0:T(8,128)S(1)}, f32[304,128]{1,0:T(8,128)S(1)}) custom-call(f32[16,152,128]{2,1,0:T(8,128)S(1)} %bitcast.225, f32[16,152,128]{2,1,0:T(8,128)S(1)} %collective-permute-done.19.refs_1_.ga1, f32[16,152,128]{2,1,0:T(8,128)S(1)} %bitcast.220, f32[16,152,128]{2,1,0:T(8,128)S(1)} %collective-permute-done.24.refs_3_.gb1, ...), custom_call_target="tpu_custom_call" | custom-call | flops 1912602624 | bytes 9961472 | tf_op jit(solution)/shard_map/absorb/pallas_call | solution.py:320
  517.3 11.6 %absorb.5 = (f32[304,128]{1,0:T(8,128)S(1)}, f32[304,128]{1,0:T(8,128)S(1)}) custom-call(f32[16,152,128]{2,1,0:T(8,128)S(1)} %bitcast.241, f32[16,152,128]{2,1,0:T(8,128)} %collective-permute-done.55.refs_1_.ga1, f32[16,152,128]{2,1,0:T(8,128)S(1)} %bitcast.237, f32[16,152,128]{2,1,0:T(8,128)} %collective-permute-done.60.refs_3_.gb1, ...), custom_call_target="tpu_custom_call" | custom-call | flops 1912602624 | bytes 9961472 | tf_op jit(solution)/shard_map/absorb/pallas_call | solution.py:320
  533.2 7.8 %own_grads.5 = f32[304,128]{1,0:T(8,128)S(1)} custom-call(f32[304,128]{1,0:T(8,128)S(1)} %fusion.14.c_ref, f32[304,128]{1,0:T(8,128)S(1)} %subtract_subtract_fusion.x_ref, f32[1,128]{1,0:T(1,128)S(1)} %copy-done.56, f32[1,2,4,1,256]{4,3,2,1,0:T(1,128)S(1)} %bitcast.289, f32[4,152,256]{2,1,0:T(8,128)S(1)} %bitcast.257, ...), custom_call_target="tpu_custom_call" | custom-call | flops 1912602624 | bytes 2490368 | tf_op jit(solution)/shard_map/own_grads/pallas_call | solution.py:361
  548.7 12.1 %collective-permute-done.98 = f32[1,2,1,152,128]{4,3,2,1,0:T(8,128)S(1)} collective-permute-done((f32[1,2,1,152,128]{4,3,2,1,0:T(8,128)S(1)}, f32[1,2,1,152,128]{4,3,2,1,0:T(8,128)S(1)}, u32[]{:S(2)}, u32[]{:S(2)}) %collective-permute-start.98) | collective-permute-done | bytes 155680 | tf_op jit(solution)/shard_map/ppermute | solution.py:21
  565.1 5.6 collective-permute-done.88
  573.7 14.9 %update.3.table_ref = f32[304,1024]{1,0:T(8,128)S(1)} custom-call(s32[1]{0:T(128)} %bitcast.base_ref, s32[2,16,3,16,128]{4,3,2,1,0:T(8,128)S(1)} %bitcast.202, f32[304,1024]{1,0:T(8,128)S(1)} %copy-done.34, f32[16,152,128]{2,1,0:T(8,128)S(1)} %bitcast.226, f32[16,152,128]{2,1,0:T(8,128)S(1)} %collective-permute-done.19.refs_1_.ga1, ...), custom_call_target="tpu_custom_call" | custom-call | flops 5100273664 | bytes 4980736 | tf_op jit(solution)/shard_map/update/pallas_call | solution.py:271
  592.9 6.1 collective-permute-done.94
  601.9 13.9 %context_update.3.table_ref = f32[304,1024]{1,0:T(8,128)S(1)} custom-call(s32[1]{0:T(128)} %bitcast.base_ref, s32[2,16,3,16,128]{4,3,2,1,0:T(8,128)S(1)} %bitcast.203, f32[304,1024]{1,0:T(8,128)S(1)} %copy-done.35, f32[16,152,128]{2,1,0:T(8,128)S(1)} %bitcast.227, f32[16,152,128]{2,1,0:T(8,128)S(1)} %collective-permute-done.19.refs_1_.ga1, ...), custom_call_target="tpu_custom_call" | custom-call | flops 5100273664 | bytes 9961472 | tf_op jit(solution)/shard_map/context_update/pallas_call | solution.py:271
  615.9 16.3 %update.4.table_ref = f32[304,1024]{1,0:T(8,128)S(1)} custom-call(s32[1]{0:T(128)} %bitcast.base_ref, s32[2,16,3,16,128]{4,3,2,1,0:T(8,128)S(1)} %bitcast.204, f32[304,1024]{1,0:T(8,128)S(1)} %update.3.table_ref, f32[16,152,128]{2,1,0:T(8,128)S(1)} %bitcast.242, f32[16,152,128]{2,1,0:T(8,128)} %collective-permute-done.55.refs_1_.ga1, ...), custom_call_target="tpu_custom_call" | custom-call | flops 5100273664 | bytes 4980736 | tf_op jit(solution)/shard_map/update/pallas_call | solution.py:271
  635.8 27.8 %hot_update.5 = (f32[152,256]{1,0:T(8,128)S(1)}, f32[152,256]{1,0:T(8,128)S(1)}) custom-call(f32[1,2,16,1,256]{4,3,2,1,0:T(1,128)S(1)} %bitcast.286, f32[4,152,256]{2,1,0:T(8,128)S(1)} %bitcast.258, f32[4,152,256]{2,1,0:T(8,128)S(1)} %bitcast.261, f32[16,152,128]{2,1,0:T(8,128)S(1)} %bitcast.248, f32[16,152,128]{2,1,0:T(8,128)} %collective-permute-done.101.refs_5_.a1, ...), custom_call_target="tpu_custom_call" | custom-call | flops 7650410496 | bytes 4980736 | tf_op jit(solution)/shard_map/hot_update/pallas_call | solution.py:408
  667.3 15.4 %context_update.4.table_ref = f32[304,1024]{1,0:T(8,128)S(1)} custom-call(s32[1]{0:T(128)} %bitcast.base_ref, s32[2,16,3,16,128]{4,3,2,1,0:T(8,128)S(1)} %bitcast.205, f32[304,1024]{1,0:T(8,128)S(1)} %copy-done.66, f32[16,152,128]{2,1,0:T(8,128)S(1)} %bitcast.243, f32[16,152,128]{2,1,0:T(8,128)} %collective-permute-done.55.refs_1_.ga1, ...), custom_call_target="tpu_custom_call" | custom-call | flops 5100273664 | bytes 9961472 | tf_op jit(solution)/shard_map/context_update/pallas_call | solution.py:271
  687.1 14.9 %update.5 = f32[304,1024]{1,0:T(8,128)S(1)} custom-call(s32[1]{0:T(128)} %bitcast.base_ref, s32[2,16,3,16,128]{4,3,2,1,0:T(8,128)S(1)} %bitcast.206, f32[304,1024]{1,0:T(8,128)S(1)} %copy-done.68, f32[16,152,128]{2,1,0:T(8,128)S(1)} %bitcast.254, f32[16,152,128]{2,1,0:T(8,128)S(1)} %copy-done.63, f32[16,152,128]{2,1,0:T(8,128)S(1)} %bitcast.251, ...), custom_call_target="tpu_custom_call" | custom-call | flops 5100273664 | bytes 4980736 | tf_op jit(solution)/shard_map/update/pallas_call | solution.py:271
  703.3 15.0 %context_update.5 = f32[304,1024]{1,0:T(8,128)S(1)} custom-call(s32[1]{0:T(128)} %bitcast.base_ref, s32[2,16,3,16,128]{4,3,2,1,0:T(8,128)S(1)} %bitcast.207, f32[304,1024]{1,0:T(8,128)S(1)} %context_update.4.table_ref, f32[16,152,128]{2,1,0:T(8,128)S(1)} %bitcast.255, f32[16,152,128]{2,1,0:T(8,128)S(1)} %copy-done.63, f32[16,152,128]{2,1,0:T(8,128)S(1)} %bitcast.252, ...), custom_call_target="tpu_custom_call" | custom-call | flops 5100273664 | bytes 9961472 | tf_op jit(solution)/shard_map/context_update/pallas_call | solution.py:271
  723.2 3.5 copy.152
  (609 shorter events, 240.0 us)
Async XLA Ops:
  81.0 30.5 %collective-permute-start.61 = (f32[16,152,128]{2,1,0:T(8,128)}, f32[16,152,128]{2,1,0:T(8,128)}, u32[]{:S(2)}, u32[]{:S(2)}) collective-permute-start(f32[16,152,128]{2,1,0:T(8,128)} %copy-done.64), channel_id=1, source_target_pairs={{0,4},{1,5},{2,6},{3,7},{4,0},{5,1},{6,2},{7,3},{8,12},{9,13},{10,... | collective-permute-start | bytes 3735560 | tf_op jit(solution)/shard_map/ppermute | solution.py:21
  86.3 112.1 %all-to-all-start = ((f32[32,24,300]{2,1,0:T(8,128)}), f32[32,24,300]{2,1,0:T(8,128)}, u32[]{:S(2)}, u32[]{:S(2)}) async-start(f32[32,24,300]{2,1,0:T(8,128)} %bitcast.26), calls=%async_computation | async-start | bytes 2359296 | tf_op jit(solution)/shard_map/all_to_all | solution.py:434
  90.1 53.7 %collective-permute-start.66 = (f32[16,152,128]{2,1,0:T(8,128)}, f32[16,152,128]{2,1,0:T(8,128)}, u32[]{:S(2)}, u32[]{:S(2)}) collective-permute-start(f32[16,152,128]{2,1,0:T(8,128)} %get-tuple-element.50), channel_id=1, source_target_pairs={{0,4},{1,5},{2,6},{3,7},{4,0},{5,1},{6,2},{7,3},{8,12},{9,13},{10,... | collective-permute-start | bytes 3735560 | tf_op jit(solution)/shard_map/ppermute | solution.py:21
  90.5 57.3 %collective-permute-start.25 = (f32[16,152,128]{2,1,0:T(8,128)}, f32[16,152,128]{2,1,0:T(8,128)}, u32[]{:S(2)}, u32[]{:S(2)}) collective-permute-start(f32[16,152,128]{2,1,0:T(8,128)} %get-tuple-element.38), channel_id=1, source_target_pairs={{0,4},{1,5},{2,6},{3,7},{4,0},{5,1},{6,2},{7,3},{8,12},{9,13},{10,... | collective-permute-start | bytes 3735560 | tf_op jit(solution)/shard_map/ppermute | solution.py:21
  90.7 61.1 %collective-permute-start.30 = (f32[16,152,128]{2,1,0:T(8,128)}, f32[16,152,128]{2,1,0:T(8,128)}, u32[]{:S(2)}, u32[]{:S(2)}) collective-permute-start(f32[16,152,128]{2,1,0:T(8,128)} %get-tuple-element.40), channel_id=1, source_target_pairs={{0,4},{1,5},{2,6},{3,7},{4,0},{5,1},{6,2},{7,3},{8,12},{9,13},{10,... | collective-permute-start | bytes 3735560 | tf_op jit(solution)/shard_map/ppermute | solution.py:21
  107.9 83.1 %collective-permute-start.5 = (f32[16,152,128]{2,1,0:T(8,128)}, f32[16,152,128]{2,1,0:T(8,128)}, u32[]{:S(2)}, u32[]{:S(2)}) collective-permute-start(f32[16,152,128]{2,1,0:T(8,128)} %get-tuple-element.34), channel_id=1, source_target_pairs={{0,4},{1,5},{2,6},{3,7},{4,0},{5,1},{6,2},{7,3},{8,12},{9,13},{10,... | collective-permute-start | bytes 3735560 | tf_op jit(solution)/shard_map/ppermute | solution.py:21
  111.5 83.1 %collective-permute-start.10 = (f32[16,152,128]{2,1,0:T(8,128)}, f32[16,152,128]{2,1,0:T(8,128)}, u32[]{:S(2)}, u32[]{:S(2)}) collective-permute-start(f32[16,152,128]{2,1,0:T(8,128)} %copy-done.61), channel_id=1, source_target_pairs={{0,4},{1,5},{2,6},{3,7},{4,0},{5,1},{6,2},{7,3},{8,12},{9,13},{10,... | collective-permute-start | bytes 3735560 | tf_op jit(solution)/shard_map/ppermute | solution.py:21
  143.8 57.9 %collective-permute-start.62 = (f32[1,2,4,152,128]{4,3,2,1,0:T(8,128)}, f32[1,2,4,152,128]{4,3,2,1,0:T(8,128)}, u32[]{:S(2)}, u32[]{:S(2)}) collective-permute-start(f32[1,2,4,152,128]{4,3,2,1,0:T(8,128)} %bitcast.71), channel_id=1, source_target_pairs={{0,16},{1,17},{2,18},{3,19},{4,20},{5,21},{6,22},{7,23},{8,24},{9,... | collective-permute-start | bytes 1867784 | tf_op jit(solution)/shard_map/ppermute | solution.py:21
  147.8 60.4 %collective-permute-start.67 = (f32[2,1,4,152,128]{4,3,2,1,0:T(8,128)}, f32[2,1,4,152,128]{4,3,2,1,0:T(8,128)}, u32[]{:S(2)}, u32[]{:S(2)}) collective-permute-start(f32[2,1,4,152,128]{4,3,2,1,0:T(8,128)} %slice.490), channel_id=1, source_target_pairs={{0,8},{1,9},{2,10},{3,11},{4,12},{5,13},{6,14},{7,15},{8,0},{9,1},... | collective-permute-start | bytes 1867784 | tf_op jit(solution)/shard_map/ppermute | solution.py:21
  151.8 54.0 %collective-permute-start.26 = (f32[1,2,4,152,128]{4,3,2,1,0:T(8,128)}, f32[1,2,4,152,128]{4,3,2,1,0:T(8,128)}, u32[]{:S(2)}, u32[]{:S(2)}) collective-permute-start(f32[1,2,4,152,128]{4,3,2,1,0:T(8,128)} %bitcast.42), channel_id=1, source_target_pairs={{0,16},{1,17},{2,18},{3,19},{4,20},{5,21},{6,22},{7,23},{8,24},{9,... | collective-permute-start | bytes 1867784 | tf_op jit(solution)/shard_map/ppermute | solution.py:21
  191.0 19.5 %collective-permute-start.31 = (f32[2,1,4,152,128]{4,3,2,1,0:T(8,128)}, f32[2,1,4,152,128]{4,3,2,1,0:T(8,128)}, u32[]{:S(2)}, u32[]{:S(2)}) collective-permute-start(f32[2,1,4,152,128]{4,3,2,1,0:T(8,128)} %slice.467), channel_id=1, source_target_pairs={{0,8},{1,9},{2,10},{3,11},{4,12},{5,13},{6,14},{7,15},{8,0},{9,1},... | collective-permute-start | bytes 1867784 | tf_op jit(solution)/shard_map/ppermute | solution.py:21
  201.7 19.8 %collective-permute-start.11 = (f32[2,1,4,152,128]{4,3,2,1,0:T(8,128)}, f32[2,1,4,152,128]{4,3,2,1,0:T(8,128)}, u32[]{:S(2)}, u32[]{:S(2)}) collective-permute-start(f32[2,1,4,152,128]{4,3,2,1,0:T(8,128)} %slice.441), channel_id=1, source_target_pairs={{0,8},{1,9},{2,10},{3,11},{4,12},{5,13},{6,14},{7,15},{8,0},{9,1},... | collective-permute-start | bytes 1867784 | tf_op jit(solution)/shard_map/ppermute | solution.py:21
  205.8 37.6 %collective-permute-start.63 = (f32[1,1,4,152,128]{4,3,2,1,0:T(8,128)S(1)}, f32[1,1,4,152,128]{4,3,2,1,0:T(8,128)S(1)}, u32[]{:S(2)}, u32[]{:S(2)}) collective-permute-start(f32[1,1,4,152,128]{4,3,2,1,0:T(8,128)S(1)} %slice.484), channel_id=1, source_target_pairs={{0,8},{1,9},{2,10},{3,11},{4,12},{5,13},{6,14},{7,15},{8,0},{9,1},... | collective-permute-start | bytes 933896 | tf_op jit(solution)/shard_map/ppermute | solution.py:21
  208.2 26.6 %collective-permute-start.27 = (f32[1,1,4,152,128]{4,3,2,1,0:T(8,128)S(1)}, f32[1,1,4,152,128]{4,3,2,1,0:T(8,128)S(1)}, u32[]{:S(2)}, u32[]{:S(2)}) collective-permute-start(f32[1,1,4,152,128]{4,3,2,1,0:T(8,128)S(1)} %slice.461), channel_id=1, source_target_pairs={{0,8},{1,9},{2,10},{3,11},{4,12},{5,13},{6,14},{7,15},{8,0},{9,1},... | collective-permute-start | bytes 933896 | tf_op jit(solution)/shard_map/ppermute | solution.py:21
  211.7 103.2 %collective-permute-start.32 = (f32[1,1,4,152,128]{4,3,2,1,0:T(8,128)S(1)}, f32[1,1,4,152,128]{4,3,2,1,0:T(8,128)S(1)}, u32[]{:S(2)}, u32[]{:S(2)}) collective-permute-start(f32[1,1,4,152,128]{4,3,2,1,0:T(8,128)S(1)} %slice.469), channel_id=1, source_target_pairs={{0,16},{1,17},{2,18},{3,19},{4,20},{5,21},{6,22},{7,23},{8,24},{9,... | collective-permute-start | bytes 933896 | tf_op jit(solution)/shard_map/ppermute | solution.py:21
  213.7 26.6 %collective-permute-start.7 = (f32[1,1,4,152,128]{4,3,2,1,0:T(8,128)S(1)}, f32[1,1,4,152,128]{4,3,2,1,0:T(8,128)S(1)}, u32[]{:S(2)}, u32[]{:S(2)}) collective-permute-start(f32[1,1,4,152,128]{4,3,2,1,0:T(8,128)S(1)} %slice.435), channel_id=1, source_target_pairs={{0,8},{1,9},{2,10},{3,11},{4,12},{5,13},{6,14},{7,15},{8,0},{9,1},... | collective-permute-start | bytes 933896 | tf_op jit(solution)/shard_map/ppermute | solution.py:21
  222.7 20.1 %collective-permute-start.12 = (f32[1,1,4,152,128]{4,3,2,1,0:T(8,128)S(1)}, f32[1,1,4,152,128]{4,3,2,1,0:T(8,128)S(1)}, u32[]{:S(2)}, u32[]{:S(2)}) collective-permute-start(f32[1,1,4,152,128]{4,3,2,1,0:T(8,128)S(1)} %slice.443), channel_id=1, source_target_pairs={{0,16},{1,17},{2,18},{3,19},{4,20},{5,21},{6,22},{7,23},{8,24},{9,... | collective-permute-start | bytes 933896 | tf_op jit(solution)/shard_map/ppermute | solution.py:21
  234.9 99.2 %collective-permute-start.28 = (f32[2,152,128]{2,1,0:T(8,128)S(1)}, f32[2,152,128]{2,1,0:T(8,128)S(1)}, u32[]{:S(2)}, u32[]{:S(2)}) collective-permute-start(f32[2,152,128]{2,1,0:T(8,128)S(1)} %slice_bitcast_fusion.9), channel_id=1, source_target_pairs={{0,2},{1,3},{2,0},{3,1},{4,6},{5,7},{6,4},{7,5},{8,10},{9,11},{10,... | collective-permute-start | bytes 466952 | tf_op jit(solution)/shard_map/ppermute | solution.py:21
  275.0 29.7 %collective-permute-start.21 = (f32[1,2,1,152,128]{4,3,2,1,0:T(8,128)S(1)}, f32[1,2,1,152,128]{4,3,2,1,0:T(8,128)S(1)}, u32[]{:S(2)}, u32[]{:S(2)}) collective-permute-start(f32[1,2,1,152,128]{4,3,2,1,0:T(8,128)S(1)} %pad_maximum_fusion.49), channel_id=1, source_target_pairs={{0,2},{1,3},{2,0},{3,1},{4,6},{5,7},{6,4},{7,5},{8,10},{9,11},{10,... | collective-permute-start | bytes 466952 | tf_op jit(solution)/shard_map/ppermute | solution.py:21
  313.2 20.0 %collective-permute-start.43 = (f32[2,1,4,152,128]{4,3,2,1,0:T(8,128)S(1)}, f32[2,1,4,152,128]{4,3,2,1,0:T(8,128)S(1)}, u32[]{:S(2)}, u32[]{:S(2)}) collective-permute-start(f32[2,1,4,152,128]{4,3,2,1,0:T(8,128)S(1)} %pad_maximum_fusion.15), channel_id=1, source_target_pairs={{0,8},{1,9},{2,10},{3,11},{4,12},{5,13},{6,14},{7,15},{8,0},{9,1},... | collective-permute-start | bytes 1867784 | tf_op jit(solution)/shard_map/ppermute | solution.py:21
  319.9 24.8 %collective-permute-start.18 = (f32[1,2,4,152,128]{4,3,2,1,0:T(8,128)S(1)}, f32[1,2,4,152,128]{4,3,2,1,0:T(8,128)S(1)}, u32[]{:S(2)}, u32[]{:S(2)}) collective-permute-start(f32[1,2,4,152,128]{4,3,2,1,0:T(8,128)S(1)} %pad_maximum_fusion.12), channel_id=1, source_target_pairs={{0,16},{1,17},{2,18},{3,19},{4,20},{5,21},{6,22},{7,23},{8,24},{9,... | collective-permute-start | bytes 1867784 | tf_op jit(solution)/shard_map/ppermute | solution.py:21
  321.7 20.4 %collective-permute-start.23 = (f32[2,1,4,152,128]{4,3,2,1,0:T(8,128)S(1)}, f32[2,1,4,152,128]{4,3,2,1,0:T(8,128)S(1)}, u32[]{:S(2)}, u32[]{:S(2)}) collective-permute-start(f32[2,1,4,152,128]{4,3,2,1,0:T(8,128)S(1)} %pad_maximum_fusion.13), channel_id=1, source_target_pairs={{0,8},{1,9},{2,10},{3,11},{4,12},{5,13},{6,14},{7,15},{8,0},{9,1},... | collective-permute-start | bytes 1867784 | tf_op jit(solution)/shard_map/ppermute | solution.py:21
  344.7 37.5 %collective-permute-start.24 = (f32[16,152,128]{2,1,0:T(8,128)S(1)}, f32[16,152,128]{2,1,0:T(8,128)S(1)}, u32[]{:S(2)}, u32[]{:S(2)}) collective-permute-start(f32[16,152,128]{2,1,0:T(8,128)S(1)} %bitcast.218), channel_id=1, source_target_pairs={{0,4},{1,5},{2,6},{3,7},{4,0},{5,1},{6,2},{7,3},{8,12},{9,13},{10,... | collective-permute-start | bytes 3735560 | tf_op jit(solution)/shard_map/ppermute | solution.py:21
  344.9 37.3 %collective-permute-start.19 = (f32[16,152,128]{2,1,0:T(8,128)S(1)}, f32[16,152,128]{2,1,0:T(8,128)S(1)}, u32[]{:S(2)}, u32[]{:S(2)}) collective-permute-start(f32[16,152,128]{2,1,0:T(8,128)S(1)} %bitcast.223), channel_id=1, source_target_pairs={{0,4},{1,5},{2,6},{3,7},{4,0},{5,1},{6,2},{7,3},{8,12},{9,13},{10,... | collective-permute-start | bytes 3735560 | tf_op jit(solution)/shard_map/ppermute | solution.py:21
  351.9 79.9 %collective-permute-start.68 = (f32[1,1,4,152,128]{4,3,2,1,0:T(8,128)S(1)}, f32[1,1,4,152,128]{4,3,2,1,0:T(8,128)S(1)}, u32[]{:S(2)}, u32[]{:S(2)}) collective-permute-start(f32[1,1,4,152,128]{4,3,2,1,0:T(8,128)S(1)} %slice.492), channel_id=1, source_target_pairs={{0,16},{1,17},{2,18},{3,19},{4,20},{5,21},{6,22},{7,23},{8,24},{9,... | collective-permute-start | bytes 933896 | tf_op jit(solution)/shard_map/ppermute | solution.py:21
  410.9 44.3 %collective-permute-start.64 = (f32[2,152,128]{2,1,0:T(8,128)S(1)}, f32[2,152,128]{2,1,0:T(8,128)S(1)}, u32[]{:S(2)}, u32[]{:S(2)}) collective-permute-start(f32[2,152,128]{2,1,0:T(8,128)S(1)} %slice_bitcast_fusion.5), channel_id=1, source_target_pairs={{0,2},{1,3},{2,0},{3,1},{4,6},{5,7},{6,4},{7,5},{8,10},{9,11},{10,... | collective-permute-start | bytes 466952 | tf_op jit(solution)/shard_map/ppermute | solution.py:21
  413.7 33.3 %collective-permute-start.74 = (f32[1,2,4,152,128]{4,3,2,1,0:T(8,128)S(1)}, f32[1,2,4,152,128]{4,3,2,1,0:T(8,128)S(1)}, u32[]{:S(2)}, u32[]{:S(2)}) collective-permute-start(f32[1,2,4,152,128]{4,3,2,1,0:T(8,128)S(1)} %pad_maximum_fusion.20), channel_id=1, source_target_pairs={{0,16},{1,17},{2,18},{3,19},{4,20},{5,21},{6,22},{7,23},{8,24},{9,... | collective-permute-start | bytes 1867784 | tf_op jit(solution)/shard_map/ppermute | solution.py:21
  423.2 23.6 %collective-permute-start.79 = (f32[2,1,4,152,128]{4,3,2,1,0:T(8,128)S(1)}, f32[2,1,4,152,128]{4,3,2,1,0:T(8,128)S(1)}, u32[]{:S(2)}, u32[]{:S(2)}) collective-permute-start(f32[2,1,4,152,128]{4,3,2,1,0:T(8,128)S(1)} %pad_maximum_fusion.21), channel_id=1, source_target_pairs={{0,8},{1,9},{2,10},{3,11},{4,12},{5,13},{6,14},{7,15},{8,0},{9,1},... | collective-permute-start | bytes 1867784 | tf_op jit(solution)/shard_map/ppermute | solution.py:21
  446.9 22.3 %collective-permute-start.80 = (f32[16,152,128]{2,1,0:T(8,128)S(1)}, f32[16,152,128]{2,1,0:T(8,128)S(1)}, u32[]{:S(2)}, u32[]{:S(2)}) collective-permute-start(f32[16,152,128]{2,1,0:T(8,128)S(1)} %bitcast.228), channel_id=1, source_target_pairs={{0,4},{1,5},{2,6},{3,7},{4,0},{5,1},{6,2},{7,3},{8,12},{9,13},{10,... | collective-permute-start | bytes 3735560 | tf_op jit(solution)/shard_map/ppermute | solution.py:21
  447.1 22.1 %collective-permute-start.75 = (f32[16,152,128]{2,1,0:T(8,128)S(1)}, f32[16,152,128]{2,1,0:T(8,128)S(1)}, u32[]{:S(2)}, u32[]{:S(2)}) collective-permute-start(f32[16,152,128]{2,1,0:T(8,128)S(1)} %bitcast.232), channel_id=1, source_target_pairs={{0,4},{1,5},{2,6},{3,7},{4,0},{5,1},{6,2},{7,3},{8,12},{9,13},{10,... | collective-permute-start | bytes 3735560 | tf_op jit(solution)/shard_map/ppermute | solution.py:21
  461.5 34.9 %collective-permute-start.65 = (f32[1,152,128]{2,1,0:T(8,128)S(1)}, f32[1,152,128]{2,1,0:T(8,128)S(1)}, u32[]{:S(2)}, u32[]{:S(2)}) collective-permute-start(f32[1,152,128]{2,1,0:T(8,128)S(1)} %slice.488), channel_id=1, source_target_pairs={{0,1},{1,0},{2,3},{3,2},{4,5},{5,4},{6,7},{7,6},{8,9},{9,8},{10,11... | collective-permute-start | bytes 233480 | tf_op jit(solution)/shard_map/ppermute | solution.py:21
  468.0 36.4 %collective-permute-start.70 = (f32[1,152,128]{2,1,0:T(8,128)S(1)}, f32[1,152,128]{2,1,0:T(8,128)S(1)}, u32[]{:S(2)}, u32[]{:S(2)}) collective-permute-start(f32[1,152,128]{2,1,0:T(8,128)S(1)} %slice.496), channel_id=1, source_target_pairs={{0,1},{1,0},{2,3},{3,2},{4,5},{5,4},{6,7},{7,6},{8,9},{9,8},{10,11... | collective-permute-start | bytes 233480 | tf_op jit(solution)/shard_map/ppermute | solution.py:21
  468.1 46.5 %collective-permute-start.60 = (f32[16,152,128]{2,1,0:T(8,128)S(1)}, f32[16,152,128]{2,1,0:T(8,128)}, u32[]{:S(2)}, u32[]{:S(2)}) collective-permute-start(f32[16,152,128]{2,1,0:T(8,128)S(1)} %bitcast.236), channel_id=1, source_target_pairs={{0,4},{1,5},{2,6},{3,7},{4,0},{5,1},{6,2},{7,3},{8,12},{9,13},{10,... | collective-permute-start | bytes 3735560 | tf_op jit(solution)/shard_map/ppermute | solution.py:21
  469.2 45.5 %collective-permute-start.55 = (f32[16,152,128]{2,1,0:T(8,128)S(1)}, f32[16,152,128]{2,1,0:T(8,128)}, u32[]{:S(2)}, u32[]{:S(2)}) collective-permute-start(f32[16,152,128]{2,1,0:T(8,128)S(1)} %bitcast.240), channel_id=1, source_target_pairs={{0,4},{1,5},{2,6},{3,7},{4,0},{5,1},{6,2},{7,3},{8,12},{9,13},{10,... | collective-permute-start | bytes 3735560 | tf_op jit(solution)/shard_map/ppermute | solution.py:21
  513.0 20.1 %collective-permute-start.83 = (f32[4,152,256]{2,1,0:T(8,128)S(1)}, f32[4,152,256]{2,1,0:T(8,128)}, u32[]{:S(2)}, u32[]{:S(2)}) collective-permute-start(f32[4,152,256]{2,1,0:T(8,128)S(1)} %bitcast.256), channel_id=1, source_target_pairs={{0,4},{1,5},{2,6},{3,7},{4,0},{5,1},{6,2},{7,3},{8,12},{9,13},{10,... | collective-permute-start | bytes 1867784 | tf_op jit(solution)/shard_map/ppermute | solution.py:21
  541.0 24.1 %collective-permute-start.92 = (f32[1,1,1,152,128]{4,3,2,1,0:T(8,128)S(1)}, f32[1,1,1,152,128]{4,3,2,1,0:T(8,128)S(1)}, u32[]{:S(2)}, u32[]{:S(2)}) collective-permute-start(f32[1,1,1,152,128]{4,3,2,1,0:T(8,128)S(1)} %get-tuple-element.82), channel_id=1, source_target_pairs={{0,1},{1,0},{2,3},{3,2},{4,5},{5,4},{6,7},{7,6},{8,9},{9,8},{10,11... | collective-permute-start | bytes 233480 | tf_op jit(solution)/shard_map/ppermute | solution.py:21
  544.6 19.5 %collective-permute-start.103 = (f32[1,2,1,152,128]{4,3,2,1,0:T(8,128)S(1)}, f32[1,2,1,152,128]{4,3,2,1,0:T(8,128)S(1)}, u32[]{:S(2)}, u32[]{:S(2)}) collective-permute-start(f32[1,2,1,152,128]{4,3,2,1,0:T(8,128)S(1)} %pad_maximum_fusion.59), channel_id=1, source_target_pairs={{0,2},{1,3},{2,0},{3,1},{4,6},{5,7},{6,4},{7,5},{8,10},{9,11},{10,... | collective-permute-start | bytes 466952 | tf_op jit(solution)/shard_map/ppermute | solution.py:21
  548.6 22.2 %collective-permute-start.88 = (f32[1,2,1,152,128]{4,3,2,1,0:T(8,128)S(1)}, f32[1,2,1,152,128]{4,3,2,1,0:T(8,128)S(1)}, u32[]{:S(2)}, u32[]{:S(2)}) collective-permute-start(f32[1,2,1,152,128]{4,3,2,1,0:T(8,128)S(1)} %pad_maximum_fusion.56), channel_id=1, source_target_pairs={{0,2},{1,3},{2,0},{3,1},{4,6},{5,7},{6,4},{7,5},{8,10},{9,11},{10,... | collective-permute-start | bytes 466952 | tf_op jit(solution)/shard_map/ppermute | solution.py:21
  565.1 23.5 %collective-permute-start.93 = (f32[1,2,1,152,128]{4,3,2,1,0:T(8,128)S(1)}, f32[1,2,1,152,128]{4,3,2,1,0:T(8,128)S(1)}, u32[]{:S(2)}, u32[]{:S(2)}) collective-permute-start(f32[1,2,1,152,128]{4,3,2,1,0:T(8,128)S(1)} %pad_maximum_fusion.57), channel_id=1, source_target_pairs={{0,2},{1,3},{2,0},{3,1},{4,6},{5,7},{6,4},{7,5},{8,10},{9,11},{10,... | collective-permute-start | bytes 466952 | tf_op jit(solution)/shard_map/ppermute | solution.py:21
  570.8 19.4 %collective-permute-start.89 = (f32[1,1,4,152,128]{4,3,2,1,0:T(8,128)S(1)}, f32[1,1,4,152,128]{4,3,2,1,0:T(8,128)S(1)}, u32[]{:S(2)}, u32[]{:S(2)}) collective-permute-start(f32[1,1,4,152,128]{4,3,2,1,0:T(8,128)S(1)} %bitcast.313), channel_id=1, source_target_pairs={{0,8},{1,9},{2,10},{3,11},{4,12},{5,13},{6,14},{7,15},{8,0},{9,1},... | collective-permute-start | bytes 933896 | tf_op jit(solution)/shard_map/ppermute | solution.py:21
  571.0 20.9 %collective-permute-start.100 = (f32[1,2,4,152,128]{4,3,2,1,0:T(8,128)S(1)}, f32[1,2,4,152,128]{4,3,2,1,0:T(8,128)S(1)}, u32[]{:S(2)}, u32[]{:S(2)}) collective-permute-start(f32[1,2,4,152,128]{4,3,2,1,0:T(8,128)S(1)} %pad_maximum_fusion.26), channel_id=1, source_target_pairs={{0,16},{1,17},{2,18},{3,19},{4,20},{5,21},{6,22},{7,23},{8,24},{9,... | collective-permute-start | bytes 1867784 | tf_op jit(solution)/shard_map/ppermute | solution.py:21
  591.1 42.9 %collective-permute-start.90 = (f32[1,2,4,152,128]{4,3,2,1,0:T(8,128)}, f32[1,2,4,152,128]{4,3,2,1,0:T(8,128)}, u32[]{:S(2)}, u32[]{:S(2)}) collective-permute-start(f32[1,2,4,152,128]{4,3,2,1,0:T(8,128)} %pad_maximum_fusion.24), channel_id=1, source_target_pairs={{0,16},{1,17},{2,18},{3,19},{4,20},{5,21},{6,22},{7,23},{8,24},{9,... | collective-permute-start | bytes 1867784 | tf_op jit(solution)/shard_map/ppermute | solution.py:21
  591.8 44.0 %collective-permute-start.106 = (f32[16,152,128]{2,1,0:T(8,128)S(1)}, f32[16,152,128]{2,1,0:T(8,128)S(1)}, u32[]{:S(2)}, u32[]{:S(2)}) collective-permute-start(f32[16,152,128]{2,1,0:T(8,128)S(1)} %bitcast.244), channel_id=1, source_target_pairs={{0,4},{1,5},{2,6},{3,7},{4,0},{5,1},{6,2},{7,3},{8,12},{9,13},{10,... | collective-permute-start | bytes 3735560 | tf_op jit(solution)/shard_map/ppermute | solution.py:21
  592.9 42.9 %collective-permute-start.101 = (f32[16,152,128]{2,1,0:T(8,128)S(1)}, f32[16,152,128]{2,1,0:T(8,128)}, u32[]{:S(2)}, u32[]{:S(2)}) collective-permute-start(f32[16,152,128]{2,1,0:T(8,128)S(1)} %bitcast.247), channel_id=1, source_target_pairs={{0,4},{1,5},{2,6},{3,7},{4,0},{5,1},{6,2},{7,3},{8,12},{9,13},{10,... | collective-permute-start | bytes 3735560 | tf_op jit(solution)/shard_map/ppermute | solution.py:21
  600.6 31.6 %collective-permute-start.95 = (f32[2,1,4,152,128]{4,3,2,1,0:T(8,128)}, f32[2,1,4,152,128]{4,3,2,1,0:T(8,128)}, u32[]{:S(2)}, u32[]{:S(2)}) collective-permute-start(f32[2,1,4,152,128]{4,3,2,1,0:T(8,128)} %pad_maximum_fusion.25), channel_id=1, source_target_pairs={{0,8},{1,9},{2,10},{3,11},{4,12},{5,13},{6,14},{7,15},{8,0},{9,1},... | collective-permute-start | bytes 1867784 | tf_op jit(solution)/shard_map/ppermute | solution.py:21
  633.9 50.9 %collective-permute-start.96 = (f32[16,152,128]{2,1,0:T(8,128)S(1)}, f32[16,152,128]{2,1,0:T(8,128)S(1)}, u32[]{:S(2)}, u32[]{:S(2)}) collective-permute-start(f32[16,152,128]{2,1,0:T(8,128)S(1)} %bitcast.250), channel_id=1, source_target_pairs={{0,4},{1,5},{2,6},{3,7},{4,0},{5,1},{6,2},{7,3},{8,12},{9,13},{10,... | collective-permute-start | bytes 3735560 | tf_op jit(solution)/shard_map/ppermute | solution.py:21
  635.3 49.5 %collective-permute-start.91 = (f32[16,152,128]{2,1,0:T(8,128)S(1)}, f32[16,152,128]{2,1,0:T(8,128)S(1)}, u32[]{:S(2)}, u32[]{:S(2)}) collective-permute-start(f32[16,152,128]{2,1,0:T(8,128)S(1)} %bitcast.253), channel_id=1, source_target_pairs={{0,4},{1,5},{2,6},{3,7},{4,0},{5,1},{6,2},{7,3},{8,12},{9,13},{10,... | collective-permute-start | bytes 3735560 | tf_op jit(solution)/shard_map/ppermute | solution.py:21
  682.8 19.4 %collective-permute-start.111 = (f32[2,1,1,152,256]{4,3,2,1,0:T(8,128)S(1)}, f32[2,1,1,152,256]{4,3,2,1,0:T(8,128)S(1)}, u32[]{:S(2)}, u32[]{:S(2)}) collective-permute-start(f32[2,1,1,152,256]{4,3,2,1,0:T(8,128)S(1)} %pad_maximum_fusion.47), channel_id=1, source_target_pairs={{0,8},{1,9},{2,10},{3,11},{4,12},{5,13},{6,14},{7,15},{8,0},{9,1},... | collective-permute-start | bytes 933896 | tf_op jit(solution)/shard_map/ppermute | solution.py:21
  (171 other events, 1774.6 us)

commit v2 on v1

v2 whole, which is shorter than its diff:
```python
import functools
import jax
import jax.numpy as jnp
from jax import lax
from jax.experimental import pallas as pl
from jax.experimental.pallas import tpu as pltpu
from jax.sharding import PartitionSpec as P

learn_rate = 2.0
exact = lax.Precision.HIGHEST
axes = ("gx", "gy")
LANES = 128
SLOTS = 8
META = SLOTS + 16
GROUP = 4
f32, bf16, i32 = jnp.float32, jnp.bfloat16, jnp.int32
NN = (((1,), (0,)), ((), ()))
NT = (((1,), (1,)), ((), ()))
TN = (((0,), (0,)), ((), ()))


def swap(x, bit, devices):
    return lax.ppermute(x, axes, [(d, d ^ bit) for d in range(devices)])


def split3(x):
    hi = x.astype(bf16)
    rest = x - hi.astype(f32)
    mid = rest.astype(bf16)
    return hi, mid, (rest - mid.astype(f32)).astype(bf16)


def split2(x):
    hi = x.astype(bf16)
    return hi, (x - hi.astype(f32)).astype(bf16)


class Tree:
    def __init__(self, gx, gy):
        self.gx, self.gy = gx, gy
        self.devices = gx * gy
        self.low = [1 << b for b in range(gy.bit_length() - 1)]
        self.high = [gy << b for b in range(1, gx.bit_length() - 1)]
        self.core = gy

    def widen(self, x, bits, descending):
        m = len(bits)
        x = x.reshape((1,) * m + x.shape)
        order = list(range(m))
        if descending:
            order.reverse()
        for b in order:
            x = jnp.concatenate([x, swap(x, bits[b], self.devices)], axis=m - 1 - b)
        return x.reshape((-1,) + x.shape[m + 1:])

    def gather(self, a, b):
        out = []
        for part, descending in ((a, False), (b, True)):
            x = self.widen(part[None], self.low, False)
            x = self.widen(x, self.high, descending)
            out += [x, swap(x, self.core, self.devices)]
        return out

    def gather_gx(self, a, b):
        out = []
        for part, descending in ((a, False), (b, True)):
            x = self.widen(part[None], self.high, descending)
            out += [x, swap(x, self.core, self.devices)]
        return out

    def gather_one(self, x):
        x = self.widen(x[None], self.low, False)
        x = self.widen(x, self.high, False)
        return jnp.concatenate([x, swap(x, self.core, self.devices)], axis=0)

    def reduce(self, keep, send, descending):
        x = keep + swap(send, self.core, self.devices)
        m = len(self.high)
        x = x.reshape((2,) * m + (self.gy,) + x.shape[1:])
        order = list(range(m))
        if descending:
            order.reverse()
        for b in order:
            axis = m - 1 - b
            near = lax.slice_in_dim(x, 0, 1, axis=axis)
            far = lax.slice_in_dim(x, 1, 2, axis=axis)
            x = near + swap(far, self.high[b], self.devices)
        x = x.reshape(x.shape[m:])
        for bit in reversed(self.low):
            half = x.shape[0] // 2
            x = x[:half] + swap(x[half:], bit, self.devices)
        return x[0]

    def place_of(self, mask):
        bits = self.devices.bit_length() - 1
        g, low = mask // self.gy, mask % self.gy
        return (g % 2) * (1 << (bits - 1)) + (g // 2) * self.gy + low

    def slice_mask(self, place):
        half = self.gx // 2
        return place // half + 2 * (place % half)


def params(*semantics):
    return pltpu.CompilerParams(dimension_semantics=semantics, vmem_limit_bytes=40 * 2**20)


def cost(flops, nbytes, trans=0):
    return pl.CostEstimate(flops=int(flops), bytes_accessed=int(nbytes), transcendentals=int(trans))


def after(x, *earlier):
    return lax.optimization_barrier((x, earlier))[0]


def count_kernel(ids_ref, out_ref):
    groups = out_ref.shape[1]
    for s in range(out_ref.shape[0]):
        ids = ids_ref[s:s + 1, :]
        n = ids.shape[1]
        high = jnp.where(lax.broadcasted_iota(i32, (groups, n), 0) == ids // LANES, 1.0, 0.0)
        low = jnp.where(lax.broadcasted_iota(i32, (LANES, n), 0) == ids % LANES, 1.0, 0.0)
        total = lax.dot_general(high.astype(bf16), low.astype(bf16), NT, preferred_element_type=f32)
        out_ref[s] = total.astype(i32)


def count(ids, hot_rows):
    return pl.pallas_call(
        count_kernel,
        out_shape=jax.ShapeDtypeStruct((ids.shape[0], hot_rows // LANES, LANES), i32),
        compiler_params=pltpu.CompilerParams(vmem_limit_bytes=40 * 2**20),
        cost_estimate=cost(1e6, 1e5),
        name="count",
    )(ids)


def count_row(rows_ref, slice_at, width):
    at = SLOTS + slice_at * (width // LANES)
    rows = [rows_ref[pl.ds(at + q, 1), :] for q in range(width // LANES)]
    return jnp.concatenate(rows, axis=1).astype(f32)


def couple_kernel(own_ref, other_ref, in_ref, out_ref, wide):
    @pl.when(pl.program_id(0) == 0)
    def _():
        for k in range(SLOTS):
            wide[k] = jnp.broadcast_to(own_ref[0, :, k:k + 1], wide.shape[1:])

    for c in range(2):
        total = jnp.zeros(wide.shape[1:], f32)
        for k in range(SLOTS - 1):
            row = other_ref[c, 0, 0, k:k + 1, :]
            in_bag = wide[1] == row
            for j in range(2, SLOTS - 1):
                in_bag = in_bag | (wide[j] == row)
            total = total + jnp.where(in_bag, 1.0, 0.0) + jnp.where(wide[0] == row, 1.0, 0.0)
        in_ref[c, 0] = total.astype(bf16)
        same = wide[SLOTS - 1] == other_ref[c, 0, 0, SLOTS - 1:SLOTS, :]
        out_ref[c, 0] = jnp.where(same, 1.0, 0.0).astype(bf16)


def couple(own, meta, later, earlier):
    half, n = meta.shape[1], own.shape[1]
    shape = jax.ShapeDtypeStruct((2, half, n, n), bf16)
    spec = pl.BlockSpec((2, 1, n, n), lambda p: (0, p, 0, 0))
    return pl.pallas_call(
        couple_kernel,
        out_shape=(shape, shape),
        grid=(half,),
        in_specs=[
            pl.BlockSpec((1, n, SLOTS), lambda p: (later, 0, 0)),
            pl.BlockSpec((2, 1, 1, META, LANES), lambda p: (0, p, earlier, 0, 0)),
        ],
        out_specs=(spec, spec),
        scratch_shapes=[pltpu.VMEM((SLOTS, n, n), i32)],
        compiler_params=params("arbitrary"),
        cost_estimate=cost(half * 2 * n * n * 150, half * n * n * 8),
        name="couple",
    )(own, meta)


def local_rows(ids, rows, context):
    if context:
        return [ids[SLOTS - 1:SLOTS, :]]
    ids = jnp.where((ids >= 0) & (ids < rows), ids, -1)
    return [ids[0:1, :], jnp.max(ids[1:SLOTS - 1, :], axis=0, keepdims=True)]


def base_kernel(rows, base_ref, meta_ref, table_ref, a0, a1, b0, b1, parts):
    feats = table_ref.shape[0]

    @pl.when(pl.program_id(0) == 0)
    def _():
        for k, part in enumerate(split3(table_ref[...])):
            parts[k * feats:(k + 1) * feats, :] = part

    h = a0.shape[1]
    iota = lax.broadcasted_iota(i32, (rows, LANES), 0)
    for p in range(a0.shape[0]):
        picks = []
        for c in range(2):
            one, two = local_rows(meta_ref[c, p, 0, :SLOTS, :] - base_ref[0], rows, False)
            picks.append(jnp.where(iota == one, 1.0, 0.0) + jnp.where(iota == two, 1.0, 0.0))
        pick = jnp.concatenate(picks, axis=1).astype(bf16)
        total = jnp.dot(parts[...], pick, preferred_element_type=f32)
        total = total[:feats] + total[feats:2 * feats] + total[2 * feats:]
        a0[p] = total[:h, :LANES]
        a1[p] = total[:h, LANES:]
        b0[p] = total[h:, :LANES]
        b1[p] = total[h:, LANES:]


def base_sums(table_t, meta, base, step):
    half = meta.shape[1]
    feats, rows = table_t.shape
    shape = jax.ShapeDtypeStruct((half, feats // 2, LANES), f32)
    spec = pl.BlockSpec((GROUP, feats // 2, LANES), lambda p, b: (p, 0, 0))
    return pl.pallas_call(
        functools.partial(base_kernel, rows),
        out_shape=(shape,) * 4,
        grid_spec=pltpu.PrefetchScalarGridSpec(
            num_scalar_prefetch=1,
            grid=(half // GROUP,),
            in_specs=[
                pl.BlockSpec((2, GROUP, 1, META, LANES), lambda p, b: (0, p, step, 0, 0)),
                pl.BlockSpec((feats, rows), lambda p, b: (0, 0)),
            ],
            out_specs=(spec,) * 4,
            scratch_shapes=[pltpu.VMEM((3 * feats, rows), bf16)],
        ),
        compiler_params=params("arbitrary"),
        cost_estimate=cost(2 * 3 * half * 256 * feats * rows, half * 2 * feats * 512 + feats * rows * 4),
        name="base_sums",
    )(base, meta, table_t)


def tokens_of(r0, r1):
    return jnp.concatenate([r[p] for p in range(r0.shape[0]) for r in (r0, r1)], axis=1)


def update_kernel(rows, width, base_ref, meta_ref, table_ref, *refs):
    pick, out_ref = refs[-1], refs[-2]
    ga0, ga1, gb0, gb1 = refs[:4]
    context = len(refs) == 8

    @pl.when(pl.program_id(0) == 0)
    def _():
        out_ref[...] = table_ref[...]

    iota = lax.broadcasted_iota(i32, (LANES, rows), 1)
    for p in range(ga0.shape[0]):
        for c in range(2):
            ids = meta_ref[c, p, 0, :SLOTS, :] - base_ref[0]
            found = local_rows(ids, rows, context)
            found = jnp.concatenate(found + [found[0]] * (SLOTS - len(found)), axis=0).T
            hits = jnp.where(iota == found[:, 0:1], 1.0, 0.0)
            if not context:
                hits = hits + jnp.where(iota == found[:, 1:2], 1.0, 0.0)
            at = (2 * p + c) * LANES
            pick[at:at + LANES, :] = hits.astype(bf16)
    ga, gb = tokens_of(ga0, ga1), tokens_of(gb0, gb1)
    if context:
        pos0, pos1 = refs[4], refs[5]
        row = width - gb.shape[0]
        pos = jnp.concatenate(
            [r[p, row:row + 1, :] for p in range(pos0.shape[0]) for r in (pos0, pos1)], axis=1
        )
        ga, gb = ga * pos, gb * pos
    grad = jnp.concatenate([ga, gb], axis=0) * learn_rate
    feats = grad.shape[0]
    both = jnp.concatenate(split2(grad), axis=0)
    total = jnp.dot(both, pick[...], preferred_element_type=f32)
    out_ref[...] = out_ref[...] - (total[:feats] + total[feats:])


def update(table_t, meta, base, step, width, g, pos=()):
    half = meta.shape[1]
    feats, rows = table_t.shape
    piece = pl.BlockSpec((GROUP, feats // 2, LANES), lambda p, b: (p, 0, 0))
    whole = pl.BlockSpec((feats, rows), lambda p, b: (0, 0))
    arrays = list(g) + list(pos)
    return pl.pallas_call(
        functools.partial(update_kernel, rows, width),
        out_shape=jax.ShapeDtypeStruct((feats, rows), f32),
        grid_spec=pltpu.PrefetchScalarGridSpec(
            num_scalar_prefetch=1,
            grid=(half // GROUP,),
            in_specs=[pl.BlockSpec((2, GROUP, 1, META, LANES), lambda p, b: (0, p, step, 0, 0)), whole]
            + [piece] * len(arrays),
            out_specs=whole,
            scratch_shapes=[pltpu.VMEM((GROUP * 2 * LANES, rows), bf16)],
        ),
        compiler_params=params("arbitrary"),
        cost_estimate=cost(2 * 2 * half * 256 * feats * rows, half * 2 * feats * 512 * len(arrays) // 4),
        name="context_update" if pos else "update",
    )(base, meta, table_t, *arrays)


def absorb_kernel(width, ga0, ga1, gb0, gb1, ca0, ca1, cb0, cb1, in_ref, ctx_ref, c_out, x_out):
    @pl.when(pl.program_id(0) == 0)
    def _():
        c_out[...] = jnp.zeros_like(c_out)
        x_out[...] = jnp.zeros_like(x_out)

    group = ga0.shape[0]
    ga, gb = tokens_of(ga0, ga1), tokens_of(gb0, gb1)
    row = width - gb.shape[0]
    pos = gb[row:row + 1, :]
    grad = jnp.concatenate([ga, gb], axis=0)
    centre = jnp.concatenate([tokens_of(ca0, ca1), tokens_of(cb0, cb1)], axis=0) * pos
    feats = grad.shape[0]
    for value, ref, out in ((grad, in_ref, c_out), (centre, ctx_ref, x_out)):
        pairs = jnp.concatenate([ref[c, p] for p in range(group) for c in range(2)], axis=1)
        parts = jnp.concatenate(split3(value * learn_rate), axis=0)
        total = lax.dot_general(parts, pairs, NT, preferred_element_type=f32)
        out[...] += total[:feats] + total[feats:2 * feats] + total[2 * feats:]


def absorb(width, g, c, in_pairs, ctx_pairs):
    half, feats_half, n = g[0].shape
    piece = pl.BlockSpec((GROUP, feats_half, n), lambda p: (p, 0, 0))
    pair = pl.BlockSpec((2, GROUP, n, n), lambda p: (0, p, 0, 0))
    shape = jax.ShapeDtypeStruct((2 * feats_half, n), f32)
    spec = pl.BlockSpec((2 * feats_half, n), lambda p: (0, 0))
    return pl.pallas_call(
        functools.partial(absorb_kernel, width),
        out_shape=(shape, shape),
        grid=(half // GROUP,),
        in_specs=[piece] * 8 + [pair] * 2,
        out_specs=(spec, spec),
        compiler_params=params("arbitrary"),
        cost_estimate=cost(2 * 2 * 3 * half * 256 * feats_half * 2 * n, half * 256 * feats_half * 16),
        name="absorb",
    )(*g, *c, in_pairs, ctx_pairs)


def dot6(left, right, dims):
    m = left[0].shape[0]
    one = lax.dot_general(jnp.concatenate(left, axis=0), right[0], dims, preferred_element_type=f32)
    two = lax.dot_general(jnp.concatenate(left[:2], axis=0), right[1], dims, preferred_element_type=f32)
    three = lax.dot_general(left[0], right[2], dims, preferred_element_type=f32)
    return one[:m] + (one[m:2 * m] + two[:m]) + ((one[2 * m:] + two[m:]) + three)


def own_kernel(width, scale, slice_ref, c_ref, x_ref, denom_ref, meta_ref, a0, a1, b0, b1, out_ref, total):
    p = pl.program_id(0)

    @pl.when(p == 0)
    def _():
        total[...] = jnp.zeros_like(total)

    centre = c_ref[...]
    group, hot_slice = a0.shape[0], a0.shape[2]
    hot = jnp.concatenate([tokens_of(a0, a1), tokens_of(b0, b1)], axis=0)
    half = pl.num_programs(0) * group
    counts = [
        count_row(meta_ref.at[0], slice_ref[c * half + p * group + q], hot_slice)
        for q in range(group)
        for c in range(2)
    ]
    counts = jnp.concatenate(counts, axis=1)
    parts = split3(hot)
    scores = dot6(split3(centre.T), parts, NN)
    grad = (scale * counts) * jax.nn.sigmoid(scores)
    total[...] += dot6(parts, split3(grad), NT)

    @pl.when(p == pl.num_programs(0) - 1)
    def _():
        context = x_ref[...]
        positive = jnp.sum(centre * context, axis=0, keepdims=True)
        pos = jax.nn.sigmoid(positive) - 1.0
        grad = (pos * context + total[...]) / denom_ref[...]
        feature = lax.broadcasted_iota(i32, grad.shape, 0)
        out_ref[...] = jnp.where(feature == width, pos, grad)


def own_grads(width, scale, centre, context, denom, slice_of, meta, step, hot):
    feats, n = centre.shape
    half, feats_half, hot_slice = hot[0].shape
    group = max(1, 512 // hot_slice)
    whole = pl.BlockSpec((feats, n), lambda p, o: (0, 0))
    piece = pl.BlockSpec((group, feats_half, hot_slice), lambda p, o: (p, 0, 0))
    return pl.pallas_call(
        functools.partial(own_kernel, width, scale),
        out_shape=jax.ShapeDtypeStruct((feats, n), f32),
        grid_spec=pltpu.PrefetchScalarGridSpec(
            num_scalar_prefetch=1,
            grid=(half // group,),
            in_specs=[
                whole,
                whole,
                pl.BlockSpec((1, n), lambda p, o: (0, 0)),
                pl.BlockSpec((1, META, LANES), lambda p, o: (step, 0, 0)),
            ]
            + [piece] * 4,
            out_specs=whole,
            scratch_shapes=[pltpu.VMEM((feats, n), f32)],
        ),
        compiler_params=params("arbitrary"),
        cost_estimate=cost(2 * 2 * 6 * half * 2 * hot_slice * feats * n, half * 4 * feats_half * hot_slice * 4),
        name="own_grads",
    )(slice_of, centre, context, denom, meta, *hot)


def hot_kernel(scale, slice_ref, meta_ref, hot_a, hot_b, a0, a1, b0, b1, out_a, out_b, total, parts):
    p = pl.program_id(0)

    @pl.when(p == 0)
    def _():
        total[...] = jnp.zeros_like(total)
        hot = jnp.concatenate([hot_a[0], hot_b[0]], axis=0)
        for k, part in enumerate(split3(hot)):
            parts[k] = part

    group, n = a0.shape[0], a0.shape[2]
    hot_slice = hot_a.shape[2]
    centre = jnp.concatenate([tokens_of(a0, a1), tokens_of(b0, b1)], axis=0)
    scores = dot6(split3(centre.T), [parts[0], parts[1], parts[2]], NN)
    sums = []
    for q in range(group):
        grads = []
        for c in range(2):
            at = (2 * q + c) * n
            counts = count_row(meta_ref.at[c, q, 0], slice_ref[0], hot_slice)
            grads.append((scale * counts) * jax.nn.sigmoid(scores[at:at + n]))
        at = 2 * q * n
        sums.append(dot6(split3(centre[:, at:at + 2 * n]), split3(jnp.concatenate(grads, axis=0)), NN))
    while len(sums) > 1:
        sums = [a + b for a, b in zip(sums[::2], sums[1::2])]
    total[...] += sums[0]

    @pl.when(p == pl.num_programs(0) - 1)
    def _():
        h = out_a.shape[0]
        out_a[...] = hot_a[0] - learn_rate * total[:h, :]
        out_b[...] = hot_b[0] - learn_rate * total[h:, :]


def hot_update(scale, me_x, meta, step, hot, c):
    half, feats_half, n = c[0].shape
    hot_slice = hot[0].shape[2]
    shape = jax.ShapeDtypeStruct((feats_half, hot_slice), f32)
    out = pl.BlockSpec((feats_half, hot_slice), lambda p, o: (0, 0))
    first = pl.BlockSpec((1, feats_half, hot_slice), lambda p, o: (0, 0, 0))
    piece = pl.BlockSpec((GROUP, feats_half, n), lambda p, o: (p, 0, 0))
    return pl.pallas_call(
        functools.partial(hot_kernel, scale),
        out_shape=(shape, shape),
        grid_spec=pltpu.PrefetchScalarGridSpec(
            num_scalar_prefetch=1,
            grid=(half // GROUP,),
            in_specs=[
                pl.BlockSpec((2, GROUP, 1, META, LANES), lambda p, o: (0, p, step, 0, 0)),
                first,
                first,
            ]
            + [piece] * 4,
            out_specs=(out, out),
            scratch_shapes=[
                pltpu.VMEM((2 * feats_half, hot_slice), f32),
                pltpu.VMEM((3, 2 * feats_half, hot_slice), bf16),
            ],
        ),
        compiler_params=params("arbitrary"),
        cost_estimate=cost(2 * 2 * 6 * half * 256 * hot_slice * feats_half * 2, half * 256 * feats_half * 8),
        name="hot_update",
    )(me_x, meta, hot[0], hot[2], *c)


def fetch_contexts(tree, me, out_table, ids, owner, cap):
    rows, width = out_table.shape
    devices, steps, n = ids.shape
    ids = ids - me * rows
    mine = (ids >= 0) & (ids < rows)
    before = jnp.triu(jnp.ones((n, n), bf16), 1)
    rank = jnp.dot(mine.astype(bf16), before, preferred_element_type=f32).astype(i32)
    slots = jnp.arange(cap, dtype=i32)
    hit = mine[:, :, None, :] & (rank[:, :, None, :] == slots[None, None, :, None])
    wanted = jnp.sum(jnp.where(hit, ids[:, :, None, :], 0), axis=3)
    order = tree.place_of(me ^ jnp.arange(devices, dtype=i32))
    wanted = wanted[order].reshape(devices, steps * cap)
    got = lax.all_to_all(out_table[wanted], axes, split_axis=0, concat_axis=0, tiled=True)
    same = (owner[:, :, None] == owner[:, None, :]) & (
        jnp.arange(n)[None, :, None] > jnp.arange(n)[None, None, :]
    )
    own_rank = jnp.sum(same.astype(i32), axis=2)
    at = (owner * steps + jnp.arange(steps, dtype=i32)[:, None]) * cap + own_rank
    return got.reshape(devices * steps * cap, width)[at]


def body(
    in_table,
    out_table,
    hot_table,
    centre_owner,
    centre_row,
    bag_owner,
    bag_row,
    bag_len,
    context_owner,
    context_row,
    negative_ids,
):
    gx, gy = lax.axis_size("gx"), lax.axis_size("gy")
    tree = Tree(gx, gy)
    devices = tree.devices
    me_x = lax.axis_index("gx").astype(i32)
    me = me_x * gy + lax.axis_index("gy").astype(i32)
    steps, n, bag = bag_row.shape
    rows, width = in_table.shape
    out_rows = out_table.shape[0]
    hot_rows = hot_table.shape[0]
    neg = negative_ids.shape[1]
    cap = max(2, 2 * n // devices)
    hot_slice = hot_rows // gx
    feats = -(-(width + 1) // 16) * 16
    h = feats // 2
    scale = 16.0 / neg

    kept = jnp.arange(bag, dtype=i32)[None, None, :] < bag_len[:, :, None]
    centre_ids = centre_owner * rows + centre_row[:, :, None]
    bag_ids = bag_owner * rows + bag_row
    context_ids = context_owner * out_rows + context_row[:, :, None]
    own = jnp.concatenate([centre_ids, jnp.where(kept, bag_ids, -2), context_ids], axis=2)
    sent = jnp.concatenate([centre_ids, jnp.where(kept, bag_ids, -1), context_ids], axis=2)
    meta = jnp.concatenate([jnp.swapaxes(sent, 1, 2), count(negative_ids, hot_rows)], axis=1)
    meta_flat = tree.gather_one(meta.reshape(steps * META, LANES)).reshape(devices, steps, META, LANES)
    meta_all = meta_flat.reshape(2, devices // 2, steps, META, LANES)

    in_base = (me * rows).reshape(1)
    out_base = (me * out_rows).reshape(1)
    spare = ((0, feats - width), (0, 0))
    in_t = jnp.pad(in_table.T, spare)
    out_t = jnp.pad(out_table.T, spare)
    slice_of = me_x ^ tree.slice_mask(jnp.arange(gx, dtype=i32))
    hot_t = jnp.pad(hot_table, ((0, 0), (0, feats - width))).reshape(gx, hot_slice, feats)
    hot_t = jnp.swapaxes(hot_t[slice_of], 1, 2)
    hot = [hot_t[: gx // 2, :h], hot_t[gx // 2:, :h], hot_t[: gx // 2, h:], hot_t[gx // 2:, h:]]

    denom = 1.0 + bag_len.astype(f32)
    context_all = meta_flat[:, :, SLOTS - 1, :]
    owner = context_owner[:, :, 0]

    def base_of(s, table):
        a0, a1, b0, b1 = base_sums(table, meta_all, in_base, s)
        return jnp.concatenate([tree.reduce(a0, a1, True), tree.reduce(b0, b1, False)], axis=0)

    def contexts_of(first, last, table):
        got = fetch_contexts(tree, me, table, context_all[:, first:last], owner[first:last], cap)
        return [jnp.pad(got[k].T, spare) for k in range(last - first)]

    small = devices > 64
    base = [base_of(0, in_t)] + [None] * (steps - 1)
    context = contexts_of(0, 1, out_table)
    base_source = in_t
    real = jnp.arange(feats)[:, None] < width
    held = []
    added = [[] for _ in range(steps)]
    for s in range(steps):
        centre = jnp.where(real, base[s] / denom[s][None, :], 0.0)
        c = tree.gather(centre[:h], centre[h:])
        g = own_grads(width, scale, centre, context[s], denom[s][None, :], slice_of, meta, s, hot)
        g = tree.gather(g[:h], g[h:])
        if s == 0:
            context += contexts_of(1, steps, after(out_table, base[0], context[0]))
        if s + 1 < steps:
            base[s + 1] = base_of(s + 1, after(base_source, g if small else base[s]))
        due = [(later, s) for later in range(s + 1, steps)] if small else [(s + 1, e) for e in range(s + 1)]
        due = [] if s + 1 == steps else due
        pairs = [couple(after(own, base[s]), meta_all, later, e) for later, e in due]
        if s > 0:
            c[0], in_t, out_t = lax.optimization_barrier((c[0], in_t, out_t))
        new_a, new_b = hot_update(scale, me_x.reshape(1), meta_all, s, hot, c)
        hot = tree.gather_gx(new_a, new_b)
        held.append((g, c))
        for (later, e), pair in zip(due, pairs):
            added[later].append(absorb(width, *held[e], *pair))
        in_t = update(in_t, meta_all, in_base, s, width, g)
        out_t = update(out_t, meta_all, out_base, s, width, c, g[2:])
        if s + 1 < steps:
            for centre_add, context_add in added[s + 1]:
                base[s + 1] = base[s + 1] - centre_add
                context[s + 1] = context[s + 1] - context_add
            if small:
                in_t, out_t, hot, base, context, added = lax.optimization_barrier(
                    (in_t, out_t, hot, base, context, added)
                )

    hot = jnp.concatenate([jnp.concatenate(hot[:2], axis=0), jnp.concatenate(hot[2:], axis=0)], axis=1)
    place = me_x ^ jnp.arange(gx, dtype=i32)
    hot = hot[place // 2 + (gx // 2) * (place % 2)]
    hot = jnp.swapaxes(hot, 1, 2).reshape(hot_rows, feats)[:, :width]
    return in_t[:width].T, out_t[:width].T, hot


def solution(mesh):
    placed = (
        P(axes, None),
        P(axes, None),
        P(),
        P(None, axes, None),
        P(None, axes),
        P(None, axes, None),
        P(None, axes, None),
        P(None, axes),
        P(None, axes, None),
        P(None, axes),
        P(None, axes),
    )
    return jax.shard_map(
        body,
        mesh=mesh,
        in_specs=placed,
        out_specs=(P(axes, None), P(axes, None), P()),
        check_vma=False,
    )
```

time: 738 us -> 689 us (0.934)
  Pallas kernels: 324 us -> 206 us
  waiting for transfers between devices: 175 us -> 235 us
    pallas_call x8 -> x7, Pallas kernels: 123 us -> 54.8 us  [the longest x6 54.5 us: update(): pl.pallas_call(functools.partial(update_kernel, rows, width), out_shape=j...]
    ppermute x113, waiting for transfers between devices: 175 us -> 235 us  [swap(): return lax.ppermute(x, axes, [(d, d ^ bit) for d in range(devices)])]
    pallas_call x3, Pallas kernels: 80.8 us -> 57.6 us  [hot_update(): pl.pallas_call(functools.partial(hot_kernel, scale), out_shape=(shape, sh...]
    pallas_call x3, Pallas kernels: 40.3 us -> 29.6 us  [base_sums(): pl.pallas_call(functools.partial(base_kernel, rows), out_shape=(shape,) *...]
    concatenate x64, other arithmetic: 9.9 us -> 19.5 us  [widen(): x = jnp.concatenate([x, swap(x, bits[b], self.devices)], axis=m - 1 - b)]
    pallas_call x3, Pallas kernels: 27 us -> 17.9 us  [absorb(): pl.pallas_call(functools.partial(absorb_kernel, width), out_shape=(shape,...]
    unnamed x218 -> x160, local copies, waits for them, and re-layouts: 29.9 us -> 20.9 us
  transfers between devices with their start and end apart: 114 -> 115, of which waited for: 39 -> 48; matrix products, arithmetic and copies ran while one was open for 10% -> 14% of each run, Pallas kernels for 41% -> 27%
where the time goes in v2:
time: 689 us; the launch traced here: 681 us
  waiting for transfers between devices  235 us (34%)
  Pallas kernels  206 us (30%)
  starting transfers between devices  120 us (17%)
  local copies, waits for them, and re-layouts  71.9 us (10%)
  other arithmetic  44.7 us (6%)
    ppermute x113, waiting for transfers between devices, swap(): return lax.ppermute(x, axes, [(d, d ^ bit) for d in range(devices)])  235 us
    ppermute x113, starting transfers between devices, swap(): return lax.ppermute(x, axes, [(d, d ^ bit) for d in range(devices)])  111 us
    pallas_call x3, Pallas kernels, hot_update(): pl.pallas_call(functools.partial(hot_kernel, scale), out_shape=(shape, sh...  57.6 us
    pallas_call x6, Pallas kernels, update(): pl.pallas_call(functools.partial(update_kernel, rows, width), out_shape=j...  54.5 us
    pallas_call x3, Pallas kernels, couple(): pl.pallas_call(couple_kernel, out_shape=(shape, shape), grid=(half,), in_...  30.9 us
    pallas_call x3, Pallas kernels, base_sums(): pl.pallas_call(functools.partial(base_kernel, rows), out_shape=(shape,) *...  29.6 us
    unnamed x160, local copies, waits for them, and re-layouts  20.9 us
    concatenate x64, other arithmetic, widen(): x = jnp.concatenate([x, swap(x, bits[b], self.devices)], axis=m - 1 - b)  19.5 us
  transfers between devices with their start and end apart: 115, of which 48 were waited for; matrix products, arithmetic and copies ran while one was open for 14% of the time, Pallas kernels for 27%

profile of v2, /device:TPU:0, one launch (start us, length us, event | category | flops | bytes accessed | tf_op | source)
XLA Modules:
  0.0 680.7 jit_solution(9403301081457319322)
XLA Ops:
  13.7 4.0 copy.57
  36.3 6.0 collective-permute-done.3
  46.8 9.8 %base_sums.3 = (f32[16,152,128]{2,1,0:T(8,128)S(1)}, f32[16,152,128]{2,1,0:T(8,128)}, f32[16,152,128]{2,1,0:T(8,128)S(1)}, f32[16,152,128]{2,1,0:T(8,128)S(1)}) custom-call(s32[1]{0:T(128)} %bitcast.base_ref, s32[2,16,3,24,128]{4,3,2,1,0:T(8,128)S(1)} %bitcast.201, f32[304,1024]{1,0:T(8,128)S(1)} %copy-done.11), custom_call_target="tpu_custom_call" | custom-call | flops 7650410496 | bytes 6225920 | tf_op jit(solution)/shard_map/base_sums/pallas_call | solution.py:218
  84.0 9.6 %collective-permute-done.6 = f32[1,2,4,152,128]{4,3,2,1,0:T(8,128)} collective-permute-done((f32[1,2,4,152,128]{4,3,2,1,0:T(8,128)}, f32[1,2,4,152,128]{4,3,2,1,0:T(8,128)}, u32[]{:S(2)}, u32[]{:S(2)}) %collective-permute-start.6) | collective-permute-done | bytes 622624 | tf_op jit(solution)/shard_map/ppermute | solution.py:23
  112.6 7.5 %collective-permute-done.8 = f32[2,152,128]{2,1,0:T(8,128)S(1)} collective-permute-done((f32[2,152,128]{2,1,0:T(8,128)S(1)}, f32[2,152,128]{2,1,0:T(8,128)S(1)}, u32[]{:S(2)}, u32[]{:S(2)}) %collective-permute-start.8) | collective-permute-done | bytes 155680 | tf_op jit(solution)/shard_map/ppermute | solution.py:23
  127.4 10.0 %base_sums.4 = (f32[16,152,128]{2,1,0:T(8,128)S(1)}, f32[16,152,128]{2,1,0:T(8,128)}, f32[16,152,128]{2,1,0:T(8,128)S(1)}, f32[16,152,128]{2,1,0:T(8,128)}) custom-call(s32[1]{0:T(128)} %bitcast.base_ref, s32[2,16,3,24,128]{4,3,2,1,0:T(8,128)S(1)} %bitcast.202, f32[304,1024]{1,0:T(8,128)S(1)} %copy-done.12), custom_call_target="tpu_custom_call" | custom-call | flops 7650410496 | bytes 6225920 | tf_op jit(solution)/shard_map/base_sums/pallas_call | solution.py:218
  140.1 4.9 own_grads.3
  152.0 5.2 all-to-all-start.1
  163.2 9.3 %collective-permute-done.25 = f32[1,1,1,152,128]{4,3,2,1,0:T(8,128)S(1)} collective-permute-done((f32[1,1,1,152,128]{4,3,2,1,0:T(8,128)S(1)}, f32[1,1,1,152,128]{4,3,2,1,0:T(8,128)S(1)}, u32[]{:S(2)}, u32[]{:S(2)}) %collective-permute-start.25) | collective-permute-done | bytes 77856 | tf_op jit(solution)/shard_map/ppermute | solution.py:23
  172.5 4.7 collective-permute-start.31
  177.2 14.4 %collective-permute-done.41 = f32[1,2,1,152,128]{4,3,2,1,0:T(8,128)S(1)} collective-permute-done((f32[1,2,1,152,128]{4,3,2,1,0:T(8,128)S(1)}, f32[1,2,1,152,128]{4,3,2,1,0:T(8,128)S(1)}, u32[]{:S(2)}, u32[]{:S(2)}) %collective-permute-start.41) | collective-permute-done | bytes 155680 | tf_op jit(solution)/shard_map/ppermute | solution.py:23
  192.5 5.7 collective-permute-done.36
  225.1 6.8 %collective-permute-done.43 = f32[2,1,4,152,128]{4,3,2,1,0:T(8,128)S(1)} collective-permute-done((f32[2,1,4,152,128]{4,3,2,1,0:T(8,128)S(1)}, f32[2,1,4,152,128]{4,3,2,1,0:T(8,128)S(1)}, u32[]{:S(2)}, u32[]{:S(2)}) %collective-permute-start.43) | collective-permute-done | bytes 622624 | tf_op jit(solution)/shard_map/ppermute | solution.py:23
  234.6 10.3 %couple.3 = (bf16[2,16,128,128]{3,2,1,0:T(8,128)(2,1)S(1)}, bf16[2,16,128,128]{3,2,1,0:T(8,128)(2,1)S(1)}) custom-call(s32[3,128,8]{2,1,0:T(8,128)S(1)} %copy.58.own_ref, s32[2,16,3,24,128]{4,3,2,1,0:T(8,128)S(1)} %bitcast.203), custom_call_target="tpu_custom_call" | custom-call | flops 78643200 | bytes 2097152 | tf_op jit(solution)/shard_map/couple/pallas_call | solution.py:166
  275.4 6.9 %collective-permute-done.22 = f32[1,1,4,152,128]{4,3,2,1,0:T(8,128)S(1)} collective-permute-done((f32[1,1,4,152,128]{4,3,2,1,0:T(8,128)S(1)}, f32[1,1,4,152,128]{4,3,2,1,0:T(8,128)S(1)}, u32[]{:S(2)}, u32[]{:S(2)}) %collective-permute-start.22) | collective-permute-done | bytes 311328 | tf_op jit(solution)/shard_map/ppermute | solution.py:23
  282.4 7.0 %collective-permute-done.18 = f32[2,152,128]{2,1,0:T(8,128)S(1)} collective-permute-done((f32[2,152,128]{2,1,0:T(8,128)S(1)}, f32[2,152,128]{2,1,0:T(8,128)S(1)}, u32[]{:S(2)}, u32[]{:S(2)}) %collective-permute-start.18) | collective-permute-done | bytes 155680 | tf_op jit(solution)/shard_map/ppermute | solution.py:23
  289.5 9.4 %collective-permute-done.23 = f32[2,152,128]{2,1,0:T(8,128)S(1)} collective-permute-done((f32[2,152,128]{2,1,0:T(8,128)S(1)}, f32[2,152,128]{2,1,0:T(8,128)S(1)}, u32[]{:S(2)}, u32[]{:S(2)}) %collective-permute-start.23) | collective-permute-done | bytes 155680 | tf_op jit(solution)/shard_map/ppermute | solution.py:23
  301.0 20.0 %hot_update.3 = (f32[152,256]{1,0:T(8,128)S(1)}, f32[152,256]{1,0:T(8,128)S(1)}) custom-call(s32[1]{0:T(128)} %bitcast.71.slice_ref, s32[2,16,3,24,128]{4,3,2,1,0:T(8,128)S(1)} %bitcast.204, f32[4,152,256]{2,1,0:T(8,128)S(1)} %copy-done.20, f32[4,152,256]{2,1,0:T(8,128)S(1)} %copy-done.18, f32[16,152,128]{2,1,0:T(8,128)} %bitcast.49.ca0.a0.refs_0_, ...), custom_call_target="tpu_custom_call" | custom-call | flops 7650410496 | bytes 4980736 | tf_op jit(solution)/shard_map/hot_update/pallas_call | solution.py:446
  323.4 9.1 %context_update.3.table_ref = f32[304,1024]{1,0:T(8,128)S(1)} custom-call(s32[1]{0:T(128)} %bitcast.base_ref, s32[2,16,3,24,128]{4,3,2,1,0:T(8,128)S(1)} %bitcast.205, f32[304,1024]{1,0:T(8,128)S(1)} %copy-done.14, f32[16,152,128]{2,1,0:T(8,128)} %bitcast.49.ca0.a0.refs_0_, f32[16,152,128]{2,1,0:T(8,128)} %collective-permute-done.39.ca1.a1.refs_1_, ...), custom_call_target="tpu_custom_call" | custom-call | flops 5100273664 | bytes 7471104 | tf_op jit(solution)/shard_map/context_update/pallas_call | solution.py:282
  332.6 11.4 %update.3.table_ref = f32[304,1024]{1,0:T(8,128)S(1)} custom-call(s32[1]{0:T(128)} %bitcast.base_ref, s32[2,16,3,24,128]{4,3,2,1,0:T(8,128)S(1)} %bitcast.206, f32[304,1024]{1,0:T(8,128)S(1)} %copy-done.13, f32[16,152,128]{2,1,0:T(8,128)S(1)} %bitcast.222, f32[16,152,128]{2,1,0:T(8,128)S(1)} %collective-permute-done.29.ga1.refs_1_, ...), custom_call_target="tpu_custom_call" | custom-call | flops 5100273664 | bytes 4980736 | tf_op jit(solution)/shard_map/update/pallas_call | solution.py:282
  345.1 6.4 absorb.3
  355.3 9.8 %base_sums.5 = (f32[16,152,128]{2,1,0:T(8,128)S(1)}, f32[16,152,128]{2,1,0:T(8,128)}, f32[16,152,128]{2,1,0:T(8,128)S(1)}, f32[16,152,128]{2,1,0:T(8,128)S(1)}) custom-call(s32[1]{0:T(128)} %bitcast.base_ref, s32[2,16,3,24,128]{4,3,2,1,0:T(8,128)S(1)} %bitcast.207, f32[304,1024]{1,0:T(8,128)S(1)} %copy-done.13), custom_call_target="tpu_custom_call" | custom-call | flops 7650410496 | bytes 6225920 | tf_op jit(solution)/shard_map/base_sums/pallas_call | solution.py:218
  370.6 10.3 %couple.4 = (bf16[2,16,128,128]{3,2,1,0:T(8,128)(2,1)S(1)}, bf16[2,16,128,128]{3,2,1,0:T(8,128)(2,1)S(1)}) custom-call(s32[3,128,8]{2,1,0:T(8,128)S(1)} %copy.59.own_ref, s32[2,16,3,24,128]{4,3,2,1,0:T(8,128)S(1)} %bitcast.208), custom_call_target="tpu_custom_call" | custom-call | flops 78643200 | bytes 2097152 | tf_op jit(solution)/shard_map/couple/pallas_call | solution.py:166
  380.9 10.3 %couple.5 = (bf16[2,16,128,128]{3,2,1,0:T(8,128)(2,1)S(1)}, bf16[2,16,128,128]{3,2,1,0:T(8,128)(2,1)S(1)}) custom-call(s32[3,128,8]{2,1,0:T(8,128)S(1)} %copy.59.own_ref, s32[2,16,3,24,128]{4,3,2,1,0:T(8,128)S(1)} %bitcast.209), custom_call_target="tpu_custom_call" | custom-call | flops 78643200 | bytes 2097152 | tf_op jit(solution)/shard_map/couple/pallas_call | solution.py:166
  393.2 8.2 %collective-permute-done.77 = f32[1,2,1,152,128]{4,3,2,1,0:T(8,128)S(1)} collective-permute-done((f32[1,2,1,152,128]{4,3,2,1,0:T(8,128)S(1)}, f32[1,2,1,152,128]{4,3,2,1,0:T(8,128)S(1)}, u32[]{:S(2)}, u32[]{:S(2)}) %collective-permute-start.77) | collective-permute-done | bytes 155680 | tf_op jit(solution)/shard_map/ppermute | solution.py:23
  402.2 6.5 absorb.4
  413.1 5.1 own_grads.4
  422.8 4.4 collective-permute-done.61
  433.5 6.0 collective-permute-done.67
  445.6 11.0 %collective-permute-done.68 = f32[1,1,4,152,128]{4,3,2,1,0:T(8,128)S(1)} collective-permute-done((f32[1,1,4,152,128]{4,3,2,1,0:T(8,128)S(1)}, f32[1,1,4,152,128]{4,3,2,1,0:T(8,128)S(1)}, u32[]{:S(2)}, u32[]{:S(2)}) %collective-permute-start.68) | collective-permute-done | bytes 311328 | tf_op jit(solution)/shard_map/ppermute | solution.py:23
  464.6 15.9 %collective-permute-done.47 = f32[1,1,4,152,128]{4,3,2,1,0:T(8,128)S(1)} collective-permute-done((f32[1,1,4,152,128]{4,3,2,1,0:T(8,128)S(1)}, f32[1,1,4,152,128]{4,3,2,1,0:T(8,128)S(1)}, u32[]{:S(2)}, u32[]{:S(2)}) %collective-permute-start.47) | collective-permute-done | bytes 311328 | tf_op jit(solution)/shard_map/ppermute | solution.py:23
  482.1 7.1 %collective-permute-done.52 = f32[1,1,4,152,128]{4,3,2,1,0:T(8,128)S(1)} collective-permute-done((f32[1,1,4,152,128]{4,3,2,1,0:T(8,128)S(1)}, f32[1,1,4,152,128]{4,3,2,1,0:T(8,128)S(1)}, u32[]{:S(2)}, u32[]{:S(2)}) %collective-permute-start.52) | collective-permute-done | bytes 311328 | tf_op jit(solution)/shard_map/ppermute | solution.py:23
  492.5 9.5 %collective-permute-done.48 = f32[2,152,128]{2,1,0:T(8,128)S(1)} collective-permute-done((f32[2,152,128]{2,1,0:T(8,128)S(1)}, f32[2,152,128]{2,1,0:T(8,128)S(1)}, u32[]{:S(2)}, u32[]{:S(2)}) %collective-permute-start.48) | collective-permute-done | bytes 155680 | tf_op jit(solution)/shard_map/ppermute | solution.py:23
  506.5 18.8 %hot_update.4 = (f32[152,256]{1,0:T(8,128)S(1)}, f32[152,256]{1,0:T(8,128)S(1)}) custom-call(s32[1]{0:T(128)} %bitcast.71.slice_ref, s32[2,16,3,24,128]{4,3,2,1,0:T(8,128)S(1)} %bitcast.210, f32[4,152,256]{2,1,0:T(8,128)S(1)} %bitcast.256, f32[4,152,256]{2,1,0:T(8,128)S(1)} %bitcast.253, f32[16,152,128]{2,1,0:T(8,128)S(1)} %bitcast.226, ...), custom_call_target="tpu_custom_call" | custom-call | flops 7650410496 | bytes 4980736 | tf_op jit(solution)/shard_map/hot_update/pallas_call | solution.py:446
  534.0 4.8 collective-permute-done.89
  540.6 5.0 absorb.5
  548.0 4.8 own_grads.5
  556.1 10.1 %collective-permute-done.103 = f32[1,2,1,152,128]{4,3,2,1,0:T(8,128)S(1)} collective-permute-done((f32[1,2,1,152,128]{4,3,2,1,0:T(8,128)S(1)}, f32[1,2,1,152,128]{4,3,2,1,0:T(8,128)S(1)}, u32[]{:S(2)}, u32[]{:S(2)}) %collective-permute-start.103) | collective-permute-done | bytes 155680 | tf_op jit(solution)/shard_map/ppermute | solution.py:23
  566.8 6.1 collective-permute-done.82
  579.0 4.2 collective-permute-done.83
  583.5 6.1 collective-permute-done.92
  591.8 4.8 collective-permute-done.105
  599.0 4.2 collective-permute-done.93
  603.4 7.9 %context_update.4.table_ref = f32[304,1024]{1,0:T(8,128)S(1)} custom-call(s32[1]{0:T(128)} %bitcast.base_ref, s32[2,16,3,24,128]{4,3,2,1,0:T(8,128)S(1)} %bitcast.211, f32[304,1024]{1,0:T(8,128)S(1)} %copy-done.32, f32[16,152,128]{2,1,0:T(8,128)S(1)} %bitcast.228, f32[16,152,128]{2,1,0:T(8,128)S(1)} %collective-permute-done.75.ca1.refs_1_.a1, ...), custom_call_target="tpu_custom_call" | custom-call | flops 5100273664 | bytes 7471104 | tf_op jit(solution)/shard_map/context_update/pallas_call | solution.py:282
  611.4 9.2 %update.4.table_ref = f32[304,1024]{1,0:T(8,128)S(1)} custom-call(s32[1]{0:T(128)} %bitcast.base_ref, s32[2,16,3,24,128]{4,3,2,1,0:T(8,128)S(1)} %bitcast.212, f32[304,1024]{1,0:T(8,128)S(1)} %copy-done.34, f32[16,152,128]{2,1,0:T(8,128)S(1)} %bitcast.239, f32[16,152,128]{2,1,0:T(8,128)S(1)} %collective-permute-done.65.ga1.refs_1_, ...), custom_call_target="tpu_custom_call" | custom-call | flops 5100273664 | bytes 4980736 | tf_op jit(solution)/shard_map/update/pallas_call | solution.py:282
  622.5 18.8 %hot_update.5 = (f32[152,256]{1,0:T(8,128)S(1)}, f32[152,256]{1,0:T(8,128)S(1)}) custom-call(s32[1]{0:T(128)} %bitcast.71.slice_ref, s32[2,16,3,24,128]{4,3,2,1,0:T(8,128)S(1)} %bitcast.213, f32[4,152,256]{2,1,0:T(8,128)S(1)} %bitcast.262, f32[4,152,256]{2,1,0:T(8,128)S(1)} %bitcast.259, f32[16,152,128]{2,1,0:T(8,128)S(1)} %bitcast.247, ...), custom_call_target="tpu_custom_call" | custom-call | flops 7650410496 | bytes 4980736 | tf_op jit(solution)/shard_map/hot_update/pallas_call | solution.py:446
  651.2 7.7 %context_update.5 = f32[304,1024]{1,0:T(8,128)S(1)} custom-call(s32[1]{0:T(128)} %bitcast.base_ref, s32[2,16,3,24,128]{4,3,2,1,0:T(8,128)S(1)} %bitcast.214, f32[304,1024]{1,0:T(8,128)S(1)} %context_update.4.table_ref, f32[16,152,128]{2,1,0:T(8,128)S(1)} %bitcast.248, f32[16,152,128]{2,1,0:T(8,128)S(1)} %collective-permute-done.101.refs_1_.a1, ...), custom_call_target="tpu_custom_call" | custom-call | flops 5100273664 | bytes 7471104 | tf_op jit(solution)/shard_map/context_update/pallas_call | solution.py:282
  659.7 9.2 %update.5 = f32[304,1024]{1,0:T(8,128)S(1)} custom-call(s32[1]{0:T(128)} %bitcast.base_ref, s32[2,16,3,24,128]{4,3,2,1,0:T(8,128)S(1)} %bitcast.215, f32[304,1024]{1,0:T(8,128)S(1)} %update.4.table_ref, f32[16,152,128]{2,1,0:T(8,128)S(1)} %bitcast.250, f32[16,152,128]{2,1,0:T(8,128)S(1)} %collective-permute-done.95.refs_1_, f32[16,152,128]{2,1,0:T(8,128)S(1)} %bitcast.245, ...), custom_call_target="tpu_custom_call" | custom-call | flops 5100273664 | bytes 4980736 | tf_op jit(solution)/shard_map/update/pallas_call | solution.py:282
  (561 shorter events, 273.4 us)
Async XLA Ops:
  67.9 29.9 %all-to-all-start = ((f32[32,8,300]{2,1,0:T(8,128)}), f32[32,8,300]{2,1,0:T(8,128)S(1)}, u32[]{:S(2)}, u32[]{:S(2)}) async-start(f32[32,8,300]{2,1,0:T(8,128)} %bitcast.344), calls=%async_computation | async-start | bytes 786432 | tf_op jit(solution)/shard_map/all_to_all | solution.py:482
  80.0 20.4 %collective-permute-start.11 = (f32[2,1,4,152,128]{4,3,2,1,0:T(8,128)}, f32[2,1,4,152,128]{4,3,2,1,0:T(8,128)}, u32[]{:S(2)}, u32[]{:S(2)}) collective-permute-start(f32[2,1,4,152,128]{4,3,2,1,0:T(8,128)} %slice.412), channel_id=1, source_target_pairs={{0,8},{1,9},{2,10},{3,11},{4,12},{5,13},{6,14},{7,15},{8,0},{9,1},... | collective-permute-start | bytes 1867784 | tf_op jit(solution)/shard_map/ppermute | solution.py:23
  137.4 83.5 %collective-permute-start.15 = (f32[16,152,128]{2,1,0:T(8,128)}, f32[16,152,128]{2,1,0:T(8,128)}, u32[]{:S(2)}, u32[]{:S(2)}) collective-permute-start(f32[16,152,128]{2,1,0:T(8,128)} %get-tuple-element.50), channel_id=1, source_target_pairs={{0,4},{1,5},{2,6},{3,7},{4,0},{5,1},{6,2},{7,3},{8,12},{9,13},{10,... | collective-permute-start | bytes 3735560 | tf_op jit(solution)/shard_map/ppermute | solution.py:23
  137.4 109.2 %collective-permute-start.20 = (f32[16,152,128]{2,1,0:T(8,128)}, f32[16,152,128]{2,1,0:T(8,128)}, u32[]{:S(2)}, u32[]{:S(2)}) collective-permute-start(f32[16,152,128]{2,1,0:T(8,128)} %get-tuple-element.52), channel_id=1, source_target_pairs={{0,4},{1,5},{2,6},{3,7},{4,0},{5,1},{6,2},{7,3},{8,12},{9,13},{10,... | collective-permute-start | bytes 3735560 | tf_op jit(solution)/shard_map/ppermute | solution.py:23
  138.1 22.0 %collective-permute-start.35 = (f32[1,1,1,152,128]{4,3,2,1,0:T(8,128)S(1)}, f32[1,1,1,152,128]{4,3,2,1,0:T(8,128)S(1)}, u32[]{:S(2)}, u32[]{:S(2)}) collective-permute-start(f32[1,1,1,152,128]{4,3,2,1,0:T(8,128)S(1)} %get-tuple-element.110), channel_id=1, source_target_pairs={{0,1},{1,0},{2,3},{3,2},{4,5},{5,4},{6,7},{7,6},{8,9},{9,8},{10,11... | collective-permute-start | bytes 233480 | tf_op jit(solution)/shard_map/ppermute | solution.py:23
  152.0 106.1 %all-to-all-start.1 = ((f32[32,16,300]{2,1,0:T(8,128)}), f32[32,16,300]{2,1,0:T(8,128)}, u32[]{:S(2)}, u32[]{:S(2)}) async-start(f32[32,16,300]{2,1,0:T(8,128)} %bitcast.297), calls=%async_computation.1 | async-start | bytes 1572864 | tf_op jit(solution)/shard_map/all_to_all | solution.py:482
  160.1 31.4 %collective-permute-start.41 = (f32[1,2,1,152,128]{4,3,2,1,0:T(8,128)S(1)}, f32[1,2,1,152,128]{4,3,2,1,0:T(8,128)S(1)}, u32[]{:S(2)}, u32[]{:S(2)}) collective-permute-start(f32[1,2,1,152,128]{4,3,2,1,0:T(8,128)S(1)} %pad_maximum_fusion.52), channel_id=1, source_target_pairs={{0,2},{1,3},{2,0},{3,1},{4,6},{5,7},{6,4},{7,5},{8,10},{9,11},{10,... | collective-permute-start | bytes 466952 | tf_op jit(solution)/shard_map/ppermute | solution.py:23
  162.6 35.6 %collective-permute-start.36 = (f32[1,2,1,152,128]{4,3,2,1,0:T(8,128)S(1)}, f32[1,2,1,152,128]{4,3,2,1,0:T(8,128)S(1)}, u32[]{:S(2)}, u32[]{:S(2)}) collective-permute-start(f32[1,2,1,152,128]{4,3,2,1,0:T(8,128)S(1)} %pad_maximum_fusion.51), channel_id=1, source_target_pairs={{0,2},{1,3},{2,0},{3,1},{4,6},{5,7},{6,4},{7,5},{8,10},{9,11},{10,... | collective-permute-start | bytes 466952 | tf_op jit(solution)/shard_map/ppermute | solution.py:23
  172.5 29.1 %collective-permute-start.31 = (f32[1,2,1,152,128]{4,3,2,1,0:T(8,128)S(1)}, f32[1,2,1,152,128]{4,3,2,1,0:T(8,128)S(1)}, u32[]{:S(2)}, u32[]{:S(2)}) collective-permute-start(f32[1,2,1,152,128]{4,3,2,1,0:T(8,128)S(1)} %pad_maximum_fusion.50), channel_id=1, source_target_pairs={{0,2},{1,3},{2,0},{3,1},{4,6},{5,7},{6,4},{7,5},{8,10},{9,11},{10,... | collective-permute-start | bytes 466952 | tf_op jit(solution)/shard_map/ppermute | solution.py:23
  211.9 20.0 %collective-permute-start.43 = (f32[2,1,4,152,128]{4,3,2,1,0:T(8,128)S(1)}, f32[2,1,4,152,128]{4,3,2,1,0:T(8,128)S(1)}, u32[]{:S(2)}, u32[]{:S(2)}) collective-permute-start(f32[2,1,4,152,128]{4,3,2,1,0:T(8,128)S(1)} %pad_maximum_fusion.15), channel_id=1, source_target_pairs={{0,8},{1,9},{2,10},{3,11},{4,12},{5,13},{6,14},{7,15},{8,0},{9,1},... | collective-permute-start | bytes 1867784 | tf_op jit(solution)/shard_map/ppermute | solution.py:23
  214.2 35.0 %collective-permute-start.38 = (f32[1,2,4,152,128]{4,3,2,1,0:T(8,128)}, f32[1,2,4,152,128]{4,3,2,1,0:T(8,128)}, u32[]{:S(2)}, u32[]{:S(2)}) collective-permute-start(f32[1,2,4,152,128]{4,3,2,1,0:T(8,128)} %pad_maximum_fusion.14), channel_id=1, source_target_pairs={{0,16},{1,17},{2,18},{3,19},{4,20},{5,21},{6,22},{7,23},{8,24},{9,... | collective-permute-start | bytes 1867784 | tf_op jit(solution)/shard_map/ppermute | solution.py:23
  218.5 34.5 %collective-permute-start.33 = (f32[2,1,4,152,128]{4,3,2,1,0:T(8,128)}, f32[2,1,4,152,128]{4,3,2,1,0:T(8,128)}, u32[]{:S(2)}, u32[]{:S(2)}) collective-permute-start(f32[2,1,4,152,128]{4,3,2,1,0:T(8,128)} %pad_maximum_fusion.13), channel_id=1, source_target_pairs={{0,8},{1,9},{2,10},{3,11},{4,12},{5,13},{6,14},{7,15},{8,0},{9,1},... | collective-permute-start | bytes 1867784 | tf_op jit(solution)/shard_map/ppermute | solution.py:23
  220.9 34.5 %collective-permute-start.28 = (f32[1,2,4,152,128]{4,3,2,1,0:T(8,128)}, f32[1,2,4,152,128]{4,3,2,1,0:T(8,128)}, u32[]{:S(2)}, u32[]{:S(2)}) collective-permute-start(f32[1,2,4,152,128]{4,3,2,1,0:T(8,128)} %pad_maximum_fusion.12), channel_id=1, source_target_pairs={{0,16},{1,17},{2,18},{3,19},{4,20},{5,21},{6,22},{7,23},{8,24},{9,... | collective-permute-start | bytes 1867784 | tf_op jit(solution)/shard_map/ppermute | solution.py:23
  231.9 29.2 %collective-permute-start.16 = (f32[1,2,4,152,128]{4,3,2,1,0:T(8,128)}, f32[1,2,4,152,128]{4,3,2,1,0:T(8,128)}, u32[]{:S(2)}, u32[]{:S(2)}) collective-permute-start(f32[1,2,4,152,128]{4,3,2,1,0:T(8,128)} %bitcast.17), channel_id=1, source_target_pairs={{0,16},{1,17},{2,18},{3,19},{4,20},{5,21},{6,22},{7,23},{8,24},{9,... | collective-permute-start | bytes 1867784 | tf_op jit(solution)/shard_map/ppermute | solution.py:23
  246.6 52.2 %collective-permute-start.44 = (f32[16,152,128]{2,1,0:T(8,128)S(1)}, f32[16,152,128]{2,1,0:T(8,128)}, u32[]{:S(2)}, u32[]{:S(2)}) collective-permute-start(f32[16,152,128]{2,1,0:T(8,128)S(1)} %bitcast.216), channel_id=1, source_target_pairs={{0,4},{1,5},{2,6},{3,7},{4,0},{5,1},{6,2},{7,3},{8,12},{9,13},{10,... | collective-permute-start | bytes 3735560 | tf_op jit(solution)/shard_map/ppermute | solution.py:23
  249.2 19.7 %collective-permute-start.21 = (f32[2,1,4,152,128]{4,3,2,1,0:T(8,128)}, f32[2,1,4,152,128]{4,3,2,1,0:T(8,128)}, u32[]{:S(2)}, u32[]{:S(2)}) collective-permute-start(f32[2,1,4,152,128]{4,3,2,1,0:T(8,128)} %slice.428), channel_id=1, source_target_pairs={{0,8},{1,9},{2,10},{3,11},{4,12},{5,13},{6,14},{7,15},{8,0},{9,1},... | collective-permute-start | bytes 1867784 | tf_op jit(solution)/shard_map/ppermute | solution.py:23
  253.0 48.0 %collective-permute-start.39 = (f32[16,152,128]{2,1,0:T(8,128)}, f32[16,152,128]{2,1,0:T(8,128)}, u32[]{:S(2)}, u32[]{:S(2)}) collective-permute-start(f32[16,152,128]{2,1,0:T(8,128)} %bitcast.49.ca0.a0.refs_0_), channel_id=1, source_target_pairs={{0,4},{1,5},{2,6},{3,7},{4,0},{5,1},{6,2},{7,3},{8,12},{9,13},{10,... | collective-permute-start | bytes 3735560 | tf_op jit(solution)/shard_map/ppermute | solution.py:23
  255.4 66.2 %collective-permute-start.34 = (f32[16,152,128]{2,1,0:T(8,128)}, f32[16,152,128]{2,1,0:T(8,128)}, u32[]{:S(2)}, u32[]{:S(2)}) collective-permute-start(f32[16,152,128]{2,1,0:T(8,128)} %bitcast.46.gb0.refs_2_.refs_4_), channel_id=1, source_target_pairs={{0,4},{1,5},{2,6},{3,7},{4,0},{5,1},{6,2},{7,3},{8,12},{9,13},{10,... | collective-permute-start | bytes 3735560 | tf_op jit(solution)/shard_map/ppermute | solution.py:23
  268.9 63.7 %collective-permute-start.29 = (f32[16,152,128]{2,1,0:T(8,128)}, f32[16,152,128]{2,1,0:T(8,128)S(1)}, u32[]{:S(2)}, u32[]{:S(2)}) collective-permute-start(f32[16,152,128]{2,1,0:T(8,128)} %bitcast.221), channel_id=1, source_target_pairs={{0,4},{1,5},{2,6},{3,7},{4,0},{5,1},{6,2},{7,3},{8,12},{9,13},{10,... | collective-permute-start | bytes 3735560 | tf_op jit(solution)/shard_map/ppermute | solution.py:23
  298.8 52.7 %collective-permute-start.19 = (f32[1,152,128]{2,1,0:T(8,128)S(1)}, f32[1,152,128]{2,1,0:T(8,128)S(1)}, u32[]{:S(2)}, u32[]{:S(2)}) collective-permute-start(f32[1,152,128]{2,1,0:T(8,128)S(1)} %slice.426), channel_id=1, source_target_pairs={{0,1},{1,0},{2,3},{3,2},{4,5},{5,4},{6,7},{7,6},{8,9},{9,8},{10,11... | collective-permute-start | bytes 233480 | tf_op jit(solution)/shard_map/ppermute | solution.py:23
  298.9 52.7 %collective-permute-start.24 = (f32[1,152,128]{2,1,0:T(8,128)S(1)}, f32[1,152,128]{2,1,0:T(8,128)S(1)}, u32[]{:S(2)}, u32[]{:S(2)}) collective-permute-start(f32[1,152,128]{2,1,0:T(8,128)S(1)} %slice.434), channel_id=1, source_target_pairs={{0,1},{1,0},{2,3},{3,2},{4,5},{5,4},{6,7},{7,6},{8,9},{9,8},{10,11... | collective-permute-start | bytes 233480 | tf_op jit(solution)/shard_map/ppermute | solution.py:23
  321.0 30.8 %collective-permute-start.58 = (f32[1,1,1,152,256]{4,3,2,1,0:T(8,128)S(1)}, f32[1,1,1,152,256]{4,3,2,1,0:T(8,128)S(1)}, u32[]{:S(2)}, u32[]{:S(2)}) collective-permute-start(f32[1,1,1,152,256]{4,3,2,1,0:T(8,128)S(1)} %bitcast.266), channel_id=1, source_target_pairs={{0,16},{1,17},{2,18},{3,19},{4,20},{5,21},{6,22},{7,23},{8,24},{9,... | collective-permute-start | bytes 466952 | tf_op jit(solution)/shard_map/ppermute | solution.py:23
  321.6 31.3 %collective-permute-start.55 = (f32[1,1,1,152,256]{4,3,2,1,0:T(8,128)S(1)}, f32[1,1,1,152,256]{4,3,2,1,0:T(8,128)S(1)}, u32[]{:S(2)}, u32[]{:S(2)}) collective-permute-start(f32[1,1,1,152,256]{4,3,2,1,0:T(8,128)S(1)} %bitcast.263), channel_id=1, source_target_pairs={{0,8},{1,9},{2,10},{3,11},{4,12},{5,13},{6,14},{7,15},{8,0},{9,1},... | collective-permute-start | bytes 466952 | tf_op jit(solution)/shard_map/ppermute | solution.py:23
  351.7 39.5 %collective-permute-start.76 = (f32[1,1,1,152,128]{4,3,2,1,0:T(8,128)S(1)}, f32[1,1,1,152,128]{4,3,2,1,0:T(8,128)S(1)}, u32[]{:S(2)}, u32[]{:S(2)}) collective-permute-start(f32[1,1,1,152,128]{4,3,2,1,0:T(8,128)S(1)} %get-tuple-element.105), channel_id=1, source_target_pairs={{0,1},{1,0},{2,3},{3,2},{4,5},{5,4},{6,7},{7,6},{8,9},{9,8},{10,11... | collective-permute-start | bytes 233480 | tf_op jit(solution)/shard_map/ppermute | solution.py:23
  352.6 38.7 %collective-permute-start.59 = (f32[2,1,1,152,256]{4,3,2,1,0:T(8,128)}, f32[2,1,1,152,256]{4,3,2,1,0:T(8,128)}, u32[]{:S(2)}, u32[]{:S(2)}) collective-permute-start(f32[2,1,1,152,256]{4,3,2,1,0:T(8,128)} %pad_maximum_fusion.35), channel_id=1, source_target_pairs={{0,8},{1,9},{2,10},{3,11},{4,12},{5,13},{6,14},{7,15},{8,0},{9,1},... | collective-permute-start | bytes 933896 | tf_op jit(solution)/shard_map/ppermute | solution.py:23
  353.8 39.0 %collective-permute-start.56 = (f32[1,2,1,152,256]{4,3,2,1,0:T(8,128)}, f32[1,2,1,152,256]{4,3,2,1,0:T(8,128)S(1)}, u32[]{:S(2)}, u32[]{:S(2)}) collective-permute-start(f32[1,2,1,152,256]{4,3,2,1,0:T(8,128)} %pad_maximum_fusion.34), channel_id=1, source_target_pairs={{0,16},{1,17},{2,18},{3,19},{4,20},{5,21},{6,22},{7,23},{8,24},{9,... | collective-permute-start | bytes 933896 | tf_op jit(solution)/shard_map/ppermute | solution.py:23
  368.4 59.8 %collective-permute-start.45 = (f32[16,152,128]{2,1,0:T(8,128)}, f32[16,152,128]{2,1,0:T(8,128)}, u32[]{:S(2)}, u32[]{:S(2)}) collective-permute-start(f32[16,152,128]{2,1,0:T(8,128)} %get-tuple-element.59), channel_id=1, source_target_pairs={{0,4},{1,5},{2,6},{3,7},{4,0},{5,1},{6,2},{7,3},{8,12},{9,13},{10,... | collective-permute-start | bytes 3735560 | tf_op jit(solution)/shard_map/ppermute | solution.py:23
  368.5 33.6 %collective-permute-start.71 = (f32[1,1,1,152,128]{4,3,2,1,0:T(8,128)S(1)}, f32[1,1,1,152,128]{4,3,2,1,0:T(8,128)S(1)}, u32[]{:S(2)}, u32[]{:S(2)}) collective-permute-start(f32[1,1,1,152,128]{4,3,2,1,0:T(8,128)S(1)} %get-tuple-element.106), channel_id=1, source_target_pairs={{0,1},{1,0},{2,3},{3,2},{4,5},{5,4},{6,7},{7,6},{8,9},{9,8},{10,11... | collective-permute-start | bytes 233480 | tf_op jit(solution)/shard_map/ppermute | solution.py:23
  392.5 20.2 %collective-permute-start.60 = (f32[4,152,256]{2,1,0:T(8,128)S(1)}, f32[4,152,256]{2,1,0:T(8,128)S(1)}, u32[]{:S(2)}, u32[]{:S(2)}) collective-permute-start(f32[4,152,256]{2,1,0:T(8,128)S(1)} %bitcast.251), channel_id=1, source_target_pairs={{0,4},{1,5},{2,6},{3,7},{4,0},{5,1},{6,2},{7,3},{8,12},{9,13},{10,... | collective-permute-start | bytes 1867784 | tf_op jit(solution)/shard_map/ppermute | solution.py:23
  392.9 20.3 %collective-permute-start.57 = (f32[4,152,256]{2,1,0:T(8,128)S(1)}, f32[4,152,256]{2,1,0:T(8,128)S(1)}, u32[]{:S(2)}, u32[]{:S(2)}) collective-permute-start(f32[4,152,256]{2,1,0:T(8,128)S(1)} %bitcast.254), channel_id=1, source_target_pairs={{0,4},{1,5},{2,6},{3,7},{4,0},{5,1},{6,2},{7,3},{8,12},{9,13},{10,... | collective-permute-start | bytes 1867784 | tf_op jit(solution)/shard_map/ppermute | solution.py:23
  410.9 20.9 %collective-permute-start.50 = (f32[16,152,128]{2,1,0:T(8,128)S(1)}, f32[16,152,128]{2,1,0:T(8,128)S(1)}, u32[]{:S(2)}, u32[]{:S(2)}) collective-permute-start(f32[16,152,128]{2,1,0:T(8,128)S(1)} %copy-done.29), channel_id=1, source_target_pairs={{0,4},{1,5},{2,6},{3,7},{4,0},{5,1},{6,2},{7,3},{8,12},{9,13},{10,... | collective-permute-start | bytes 3735560 | tf_op jit(solution)/shard_map/ppermute | solution.py:23
  412.7 32.6 %collective-permute-start.79 = (f32[2,1,4,152,128]{4,3,2,1,0:T(8,128)S(1)}, f32[2,1,4,152,128]{4,3,2,1,0:T(8,128)S(1)}, u32[]{:S(2)}, u32[]{:S(2)}) collective-permute-start(f32[2,1,4,152,128]{4,3,2,1,0:T(8,128)S(1)} %pad_maximum_fusion.21), channel_id=1, source_target_pairs={{0,8},{1,9},{2,10},{3,11},{4,12},{5,13},{6,14},{7,15},{8,0},{9,1},... | collective-permute-start | bytes 1867784 | tf_op jit(solution)/shard_map/ppermute | solution.py:23
  421.2 22.3 %collective-permute-start.74 = (f32[1,2,4,152,128]{4,3,2,1,0:T(8,128)S(1)}, f32[1,2,4,152,128]{4,3,2,1,0:T(8,128)S(1)}, u32[]{:S(2)}, u32[]{:S(2)}) collective-permute-start(f32[1,2,4,152,128]{4,3,2,1,0:T(8,128)S(1)} %pad_maximum_fusion.20), channel_id=1, source_target_pairs={{0,16},{1,17},{2,18},{3,19},{4,20},{5,21},{6,22},{7,23},{8,24},{9,... | collective-permute-start | bytes 1867784 | tf_op jit(solution)/shard_map/ppermute | solution.py:23
  431.8 24.8 %collective-permute-start.46 = (f32[1,2,4,152,128]{4,3,2,1,0:T(8,128)S(1)}, f32[1,2,4,152,128]{4,3,2,1,0:T(8,128)S(1)}, u32[]{:S(2)}, u32[]{:S(2)}) collective-permute-start(f32[1,2,4,152,128]{4,3,2,1,0:T(8,128)S(1)} %bitcast.349), channel_id=1, source_target_pairs={{0,16},{1,17},{2,18},{3,19},{4,20},{5,21},{6,22},{7,23},{8,24},{9,... | collective-permute-start | bytes 1867784 | tf_op jit(solution)/shard_map/ppermute | solution.py:23
  439.6 23.4 %collective-permute-start.51 = (f32[2,1,4,152,128]{4,3,2,1,0:T(8,128)S(1)}, f32[2,1,4,152,128]{4,3,2,1,0:T(8,128)S(1)}, u32[]{:S(2)}, u32[]{:S(2)}) collective-permute-start(f32[2,1,4,152,128]{4,3,2,1,0:T(8,128)S(1)} %slice.453), channel_id=1, source_target_pairs={{0,8},{1,9},{2,10},{3,11},{4,12},{5,13},{6,14},{7,15},{8,0},{9,1},... | collective-permute-start | bytes 1867784 | tf_op jit(solution)/shard_map/ppermute | solution.py:23
  445.4 61.1 %collective-permute-start.75 = (f32[16,152,128]{2,1,0:T(8,128)S(1)}, f32[16,152,128]{2,1,0:T(8,128)S(1)}, u32[]{:S(2)}, u32[]{:S(2)}) collective-permute-start(f32[16,152,128]{2,1,0:T(8,128)S(1)} %bitcast.225), channel_id=1, source_target_pairs={{0,4},{1,5},{2,6},{3,7},{4,0},{5,1},{6,2},{7,3},{8,12},{9,13},{10,... | collective-permute-start | bytes 3735560 | tf_op jit(solution)/shard_map/ppermute | solution.py:23
  456.5 47.9 %collective-permute-start.80 = (f32[16,152,128]{2,1,0:T(8,128)S(1)}, f32[16,152,128]{2,1,0:T(8,128)S(1)}, u32[]{:S(2)}, u32[]{:S(2)}) collective-permute-start(f32[16,152,128]{2,1,0:T(8,128)S(1)} %bitcast.229), channel_id=1, source_target_pairs={{0,4},{1,5},{2,6},{3,7},{4,0},{5,1},{6,2},{7,3},{8,12},{9,13},{10,... | collective-permute-start | bytes 3735560 | tf_op jit(solution)/shard_map/ppermute | solution.py:23
  456.6 33.0 %collective-permute-start.69 = (f32[2,1,4,152,128]{4,3,2,1,0:T(8,128)S(1)}, f32[2,1,4,152,128]{4,3,2,1,0:T(8,128)S(1)}, u32[]{:S(2)}, u32[]{:S(2)}) collective-permute-start(f32[2,1,4,152,128]{4,3,2,1,0:T(8,128)S(1)} %pad_maximum_fusion.19), channel_id=1, source_target_pairs={{0,8},{1,9},{2,10},{3,11},{4,12},{5,13},{6,14},{7,15},{8,0},{9,1},... | collective-permute-start | bytes 1867784 | tf_op jit(solution)/shard_map/ppermute | solution.py:23
  463.0 29.4 %collective-permute-start.64 = (f32[1,2,4,152,128]{4,3,2,1,0:T(8,128)S(1)}, f32[1,2,4,152,128]{4,3,2,1,0:T(8,128)S(1)}, u32[]{:S(2)}, u32[]{:S(2)}) collective-permute-start(f32[1,2,4,152,128]{4,3,2,1,0:T(8,128)S(1)} %pad_maximum_fusion.18), channel_id=1, source_target_pairs={{0,16},{1,17},{2,18},{3,19},{4,20},{5,21},{6,22},{7,23},{8,24},{9,... | collective-permute-start | bytes 1867784 | tf_op jit(solution)/shard_map/ppermute | solution.py:23
  492.4 48.2 %collective-permute-start.70 = (f32[16,152,128]{2,1,0:T(8,128)S(1)}, f32[16,152,128]{2,1,0:T(8,128)S(1)}, u32[]{:S(2)}, u32[]{:S(2)}) collective-permute-start(f32[16,152,128]{2,1,0:T(8,128)S(1)} %bitcast.233), channel_id=1, source_target_pairs={{0,4},{1,5},{2,6},{3,7},{4,0},{5,1},{6,2},{7,3},{8,12},{9,13},{10,... | collective-permute-start | bytes 3735560 | tf_op jit(solution)/shard_map/ppermute | solution.py:23
  502.0 38.6 %collective-permute-start.65 = (f32[16,152,128]{2,1,0:T(8,128)S(1)}, f32[16,152,128]{2,1,0:T(8,128)S(1)}, u32[]{:S(2)}, u32[]{:S(2)}) collective-permute-start(f32[16,152,128]{2,1,0:T(8,128)S(1)} %bitcast.237), channel_id=1, source_target_pairs={{0,4},{1,5},{2,6},{3,7},{4,0},{5,1},{6,2},{7,3},{8,12},{9,13},{10,... | collective-permute-start | bytes 3735560 | tf_op jit(solution)/shard_map/ppermute | solution.py:23
  504.4 22.5 %collective-permute-start.49 = (f32[1,152,128]{2,1,0:T(8,128)S(1)}, f32[1,152,128]{2,1,0:T(8,128)S(1)}, u32[]{:S(2)}, u32[]{:S(2)}) collective-permute-start(f32[1,152,128]{2,1,0:T(8,128)S(1)} %slice.451), channel_id=1, source_target_pairs={{0,1},{1,0},{2,3},{3,2},{4,5},{5,4},{6,7},{7,6},{8,9},{9,8},{10,11... | collective-permute-start | bytes 233480 | tf_op jit(solution)/shard_map/ppermute | solution.py:23
  504.4 29.5 %collective-permute-start.54 = (f32[1,152,128]{2,1,0:T(8,128)S(1)}, f32[1,152,128]{2,1,0:T(8,128)S(1)}, u32[]{:S(2)}, u32[]{:S(2)}) collective-permute-start(f32[1,152,128]{2,1,0:T(8,128)S(1)} %slice.459), channel_id=1, source_target_pairs={{0,1},{1,0},{2,3},{3,2},{4,5},{5,4},{6,7},{7,6},{8,9},{9,8},{10,11... | collective-permute-start | bytes 233480 | tf_op jit(solution)/shard_map/ppermute | solution.py:23
  591.4 29.2 %collective-permute-start.99 = (f32[2,1,4,152,128]{4,3,2,1,0:T(8,128)S(1)}, f32[2,1,4,152,128]{4,3,2,1,0:T(8,128)S(1)}, u32[]{:S(2)}, u32[]{:S(2)}) collective-permute-start(f32[2,1,4,152,128]{4,3,2,1,0:T(8,128)S(1)} %pad_maximum_fusion.26), channel_id=1, source_target_pairs={{0,8},{1,9},{2,10},{3,11},{4,12},{5,13},{6,14},{7,15},{8,0},{9,1},... | collective-permute-start | bytes 1867784 | tf_op jit(solution)/shard_map/ppermute | solution.py:23
  596.7 25.9 %collective-permute-start.106 = (f32[16,152,128]{2,1,0:T(8,128)S(1)}, f32[16,152,128]{2,1,0:T(8,128)S(1)}, u32[]{:S(2)}, u32[]{:S(2)}) collective-permute-start(f32[16,152,128]{2,1,0:T(8,128)S(1)} %bitcast.240), channel_id=1, source_target_pairs={{0,4},{1,5},{2,6},{3,7},{4,0},{5,1},{6,2},{7,3},{8,12},{9,13},{10,... | collective-permute-start | bytes 3735560 | tf_op jit(solution)/shard_map/ppermute | solution.py:23
  599.0 23.6 %collective-permute-start.101 = (f32[16,152,128]{2,1,0:T(8,128)S(1)}, f32[16,152,128]{2,1,0:T(8,128)S(1)}, u32[]{:S(2)}, u32[]{:S(2)}) collective-permute-start(f32[16,152,128]{2,1,0:T(8,128)S(1)} %bitcast.246), channel_id=1, source_target_pairs={{0,4},{1,5},{2,6},{3,7},{4,0},{5,1},{6,2},{7,3},{8,12},{9,13},{10,... | collective-permute-start | bytes 3735560 | tf_op jit(solution)/shard_map/ppermute | solution.py:23
  620.7 30.5 %collective-permute-start.100 = (f32[16,152,128]{2,1,0:T(8,128)S(1)}, f32[16,152,128]{2,1,0:T(8,128)S(1)}, u32[]{:S(2)}, u32[]{:S(2)}) collective-permute-start(f32[16,152,128]{2,1,0:T(8,128)S(1)} %bitcast.243), channel_id=1, source_target_pairs={{0,4},{1,5},{2,6},{3,7},{4,0},{5,1},{6,2},{7,3},{8,12},{9,13},{10,... | collective-permute-start | bytes 3735560 | tf_op jit(solution)/shard_map/ppermute | solution.py:23
  622.0 37.7 %collective-permute-start.95 = (f32[16,152,128]{2,1,0:T(8,128)S(1)}, f32[16,152,128]{2,1,0:T(8,128)S(1)}, u32[]{:S(2)}, u32[]{:S(2)}) collective-permute-start(f32[16,152,128]{2,1,0:T(8,128)S(1)} %bitcast.249), channel_id=1, source_target_pairs={{0,4},{1,5},{2,6},{3,7},{4,0},{5,1},{6,2},{7,3},{8,12},{9,13},{10,... | collective-permute-start | bytes 3735560 | tf_op jit(solution)/shard_map/ppermute | solution.py:23
  (145 other events, 1555.9 us)

commit v3 on v2

--- a/solution.py
+++ b/solution.py
@@ -43,53 +43,42 @@
         self.high = [gy << b for b in range(1, gx.bit_length() - 1)]
         self.core = gy
 
-    def widen(self, x, bits, descending):
-        m = len(bits)
-        x = x.reshape((1,) * m + x.shape)
-        order = list(range(m))
-        if descending:
-            order.reverse()
-        for b in order:
-            x = jnp.concatenate([x, swap(x, bits[b], self.devices)], axis=m - 1 - b)
-        return x.reshape((-1,) + x.shape[m + 1:])
-
-    def gather(self, a, b):
-        out = []
-        for part, descending in ((a, False), (b, True)):
-            x = self.widen(part[None], self.low, False)
-            x = self.widen(x, self.high, descending)
-            out += [x, swap(x, self.core, self.devices)]
-        return out
-
-    def gather_gx(self, a, b):
-        out = []
-        for part, descending in ((a, False), (b, True)):
-            x = self.widen(part[None], self.high, descending)
-            out += [x, swap(x, self.core, self.devices)]
-        return out
+    def widen(self, parts, plans):
+        m = len(plans[0])
+        tails = [p.shape for p in parts]
+        parts = [p.reshape((1,) * m + p.shape) for p in parts]
+        for k in range(m):
+            got = yield parts, [swap(p, plan[k][0], self.devices) for p, plan in zip(parts, plans)]
+            parts = [jnp.concatenate([p, g], axis=plan[k][1]) for p, g, plan in zip(parts, got, plans)]
+        return [p.reshape((-1,) + t) for p, t in zip(parts, tails)]
+
+    def plans(self, with_low):
+        mh, ml = len(self.high), len(self.low) if with_low else 0
+        low = [(self.low[b], mh + ml - 1 - b) for b in reversed(range(ml))]
+        high = [(self.high[b], mh - 1 - b) for b in range(mh)]
+        return [low + high, low + high[::-1]]
+
+    def gather(self, a, b, with_low=True):
+        x, y = yield from self.widen([a, b], self.plans(with_low))
+        got = yield [x, y], [swap(x, self.core, self.devices), swap(y, self.core, self.devices)]
+        return [x, got[0], y, got[1]]
 
     def gather_one(self, x):
-        x = self.widen(x[None], self.low, False)
-        x = self.widen(x, self.high, False)
-        return jnp.concatenate([x, swap(x, self.core, self.devices)], axis=0)
-
-    def reduce(self, keep, send, descending):
-        x = keep + swap(send, self.core, self.devices)
-        m = len(self.high)
-        x = x.reshape((2,) * m + (self.gy,) + x.shape[1:])
-        order = list(range(m))
-        if descending:
-            order.reverse()
-        for b in order:
-            axis = m - 1 - b
-            near = lax.slice_in_dim(x, 0, 1, axis=axis)
-            far = lax.slice_in_dim(x, 1, 2, axis=axis)
-            x = near + swap(far, self.high[b], self.devices)
-        x = x.reshape(x.shape[m:])
-        for bit in reversed(self.low):
-            half = x.shape[0] // 2
-            x = x[:half] + swap(x[half:], bit, self.devices)
-        return x[0]
+        (x,) = yield from self.widen([x], self.plans(True)[:1])
+        got = yield [x], [swap(x, self.core, self.devices)]
+        return jnp.concatenate([x, got[0]], axis=0)
+
+    def reduce(self, a0, a1, b0, b1):
+        got = yield [a1, b1], [swap(a1, self.core, self.devices), swap(b1, self.core, self.devices)]
+        shape = (2,) * (len(self.high) + len(self.low)) + a0.shape[1:]
+        parts = [(a0 + got[0]).reshape(shape), (b0 + got[1]).reshape(shape)]
+        plans = [plan[::-1] for plan in self.plans(True)]
+        for k in range(len(plans[0])):
+            near = [lax.slice_in_dim(p, 0, 1, axis=plan[k][1]) for p, plan in zip(parts, plans)]
+            far = [lax.slice_in_dim(p, 1, 2, axis=plan[k][1]) for p, plan in zip(parts, plans)]
+            got = yield far, [swap(p, plan[k][0], self.devices) for p, plan in zip(far, plans)]
+            parts = [p + g for p, g in zip(near, got)]
+        return jnp.concatenate([p.reshape(p.shape[-2:]) for p in parts], axis=0)
 
     def place_of(self, mask):
         bits = self.devices.bit_length() - 1
@@ -111,6 +100,26 @@
 
 def after(x, *earlier):
     return lax.optimization_barrier((x, earlier))[0]
+
+
+class Lane:
+    def __init__(self, chain, stages):
+        self.chain, self.left = chain, stages
+        self.sent, self.got = next(chain)
+
+
+def stage(lanes, fill=None):
+    lanes = [lane for lane in lanes if lane is not None and lane.left > 0]
+    sent = [lane.sent for lane in lanes]
+    beside = fill(lambda x: after(x, sent)) if fill is not None else ()
+    got, beside = lax.optimization_barrier(([lane.got for lane in lanes], beside))
+    for lane, arrived in zip(lanes, got):
+        lane.left -= 1
+        try:
+            lane.sent, lane.got = lane.chain.send(arrived)
+        except StopIteration as end:
+            lane.result = end.value
+    return beside
 
 
 def count_kernel(ids_ref, out_ref):
@@ -524,67 +533,145 @@
     own = jnp.concatenate([centre_ids, jnp.where(kept, bag_ids, -2), context_ids], axis=2)
     sent = jnp.concatenate([centre_ids, jnp.where(kept, bag_ids, -1), context_ids], axis=2)
     meta = jnp.concatenate([jnp.swapaxes(sent, 1, 2), count(negative_ids, hot_rows)], axis=1)
-    meta_flat = tree.gather_one(meta.reshape(steps * META, LANES)).reshape(devices, steps, META, LANES)
+    span = len(tree.low) + len(tree.high) + 1
+    short = len(tree.high) + 1
+    lane = Lane(tree.gather_one(meta.reshape(steps * META, LANES)), span)
+    while lane.left:
+        stage([lane])
+    meta_flat = lane.result.reshape(devices, steps, META, LANES)
     meta_all = meta_flat.reshape(2, devices // 2, steps, META, LANES)
 
+    small = devices > 64
     in_base = (me * rows).reshape(1)
     out_base = (me * out_rows).reshape(1)
     spare = ((0, feats - width), (0, 0))
     in_t = jnp.pad(in_table.T, spare)
-    out_t = jnp.pad(out_table.T, spare)
+    source = in_t
+    part = base_sums(source, meta_all, in_base, 0)
+    hot_t, out_late = after((hot_table, out_table), part[0])
+    out_t = jnp.pad(out_late.T, spare)
     slice_of = me_x ^ tree.slice_mask(jnp.arange(gx, dtype=i32))
-    hot_t = jnp.pad(hot_table, ((0, 0), (0, feats - width))).reshape(gx, hot_slice, feats)
+    hot_t = jnp.pad(hot_t, ((0, 0), (0, feats - width))).reshape(gx, hot_slice, feats)
     hot_t = jnp.swapaxes(hot_t[slice_of], 1, 2)
     hot = [hot_t[: gx // 2, :h], hot_t[gx // 2:, :h], hot_t[: gx // 2, h:], hot_t[gx // 2:, h:]]
-
     denom = 1.0 + bag_len.astype(f32)
-    context_all = meta_flat[:, :, SLOTS - 1, :]
-    owner = context_owner[:, :, 0]
-
-    def base_of(s, table):
-        a0, a1, b0, b1 = base_sums(table, meta_all, in_base, s)
-        return jnp.concatenate([tree.reduce(a0, a1, True), tree.reduce(b0, b1, False)], axis=0)
-
-    def contexts_of(first, last, table):
-        got = fetch_contexts(tree, me, table, context_all[:, first:last], owner[first:last], cap)
-        return [jnp.pad(got[k].T, spare) for k in range(last - first)]
-
-    small = devices > 64
-    base = [base_of(0, in_t)] + [None] * (steps - 1)
-    context = contexts_of(0, 1, out_table)
-    base_source = in_t
+    got = fetch_contexts(tree, me, out_table, meta_flat[:, :, SLOTS - 1, :], context_owner[:, :, 0], cap)
+    context = [jnp.pad(got[k].T, spare) for k in range(steps)]
+
+    def sums(s):
+        return lambda gate: base_sums(gate(source), meta_all, in_base, s)
+
+    def pair(later, e):
+        return lambda gate: couple(gate(own), meta_all, later, e)
+
+    def run(lanes, fills, kept, until):
+        while until.left:
+            name, fill = fills.pop(0) if fills else (None, None)
+            beside = stage(lanes, fill)
+            if name is not None:
+                kept[name] = beside
+
+    kept = {}
+    lane = Lane(tree.reduce(*part), span)
+    fills = [] if small else [(None, None), (("sums", 1), sums(1)), (("pair", 1, 0), pair(1, 0))]
+    run([lane], fills[: span] if steps > 1 else [], kept, lane)
+    base = [lane.result] + [None] * (steps - 1)
     real = jnp.arange(feats)[:, None] < width
     held = []
     added = [[] for _ in range(steps)]
+    tables = [in_t, out_t]
+
+    def grow(s, which):
+        def fill(gate):
+            g, c = held[s]
+            if which == 0:
+                return update(gate(tables[0]), meta_all, in_base, s, width, g)
+            return update(gate(tables[1]), meta_all, out_base, s, width, c, g[2:])
+
+        return fill
+
+    def soak(later, e):
+        def fill(gate):
+            g, c = held[e]
+            return absorb(width, [gate(g[0])] + g[1:], c, *kept[("pair", later, e)])
+
+        return fill
+
     for s in range(steps):
+        last = s + 1 == steps
         centre = jnp.where(real, base[s] / denom[s][None, :], 0.0)
-        c = tree.gather(centre[:h], centre[h:])
-        g = own_grads(width, scale, centre, context[s], denom[s][None, :], slice_of, meta, s, hot)
-        g = tree.gather(g[:h], g[h:])
-        if s == 0:
-            context += contexts_of(1, steps, after(out_table, base[0], context[0]))
-        if s + 1 < steps:
-            base[s + 1] = base_of(s + 1, after(base_source, g if small else base[s]))
-        due = [(later, s) for later in range(s + 1, steps)] if small else [(s + 1, e) for e in range(s + 1)]
-        due = [] if s + 1 == steps else due
-        pairs = [couple(after(own, base[s]), meta_all, later, e) for later, e in due]
-        if s > 0:
-            c[0], in_t, out_t = lax.optimization_barrier((c[0], in_t, out_t))
-        new_a, new_b = hot_update(scale, me_x.reshape(1), meta_all, s, hot, c)
-        hot = tree.gather_gx(new_a, new_b)
-        held.append((g, c))
-        for (later, e), pair in zip(due, pairs):
-            added[later].append(absorb(width, *held[e], *pair))
-        in_t = update(in_t, meta_all, in_base, s, width, g)
-        out_t = update(out_t, meta_all, out_base, s, width, c, g[2:])
-        if s + 1 < steps:
+        c_lane = Lane(tree.gather(centre[:h], centre[h:]), span)
+        g = stage(
+            [c_lane],
+            lambda gate: own_grads(
+                width, scale, gate(centre), context[s], denom[s][None, :], slice_of, meta, s, hot
+            ),
+        )
+        g_lane = Lane(tree.gather(g[:h], g[h:]), span)
+        fills = []
+        if not small:
+            if s > 0:
+                fills.append((("table", 1), grow(s - 1, 1)))
+            for e in range(s + 1 if not last else 0):
+                if ("pair", s + 1, e) not in kept:
+                    fills.append((("pair", s + 1, e), pair(s + 1, e)))
+            if s > 0:
+                fills.append((("table", 0), grow(s - 1, 0)))
+            if s + 2 < steps:
+                fills.append((("sums", s + 2), sums(s + 2)))
+                fills.append((("pair", s + 2, s), pair(s + 2, s)))
+        r_lane = None
+        while c_lane.left:
+            if c_lane.left == 1 and not small and not last:
+                if ("sums", s + 1) not in kept:
+                    kept[("sums", s + 1)] = base_sums(source, meta_all, in_base, s + 1)
+                r_lane = Lane(tree.reduce(*kept[("sums", s + 1)]), span)
+            name, fill = fills.pop(0) if fills else (None, None)
+            beside = stage([c_lane, g_lane, r_lane], fill)
+            if name is not None:
+                kept[name] = beside
+        for name, fill in fills:
+            kept[name] = fill(lambda x: x)
+        for which in (0, 1):
+            tables[which] = kept.pop(("table", which), tables[which])
+        c = c_lane.result
+        new_a, new_b = stage(
+            [g_lane, r_lane],
+            lambda gate: hot_update(scale, me_x.reshape(1), meta_all, s, hot, [gate(c[0])] + c[1:]),
+        )
+        while g_lane.left:
+            stage([g_lane, r_lane])
+        held.append((g_lane.result, c))
+        h_lane = Lane(tree.gather(new_a, new_b, False), short)
+        due = [(later, s) for later in range(s + 1, steps)] if small else [(s + 1, e) for e in range(s, -1, -1)]
+        due = [] if last else due
+        if small:
+            for later, e in due:
+                kept[("pair", later, e)] = couple(own, meta_all, later, e)
+        fills = [(("soak", later, e), soak(later, e)) for later, e in due]
+        if last or small:
+            fills += [(("table", 1), grow(s, 1)), (("table", 0), grow(s, 0))]
+        run([h_lane, r_lane], fills, kept, h_lane)
+        for name, fill in fills:
+            kept[name] = fill(lambda x: x)
+        for which in (0, 1):
+            tables[which] = kept.pop(("table", which), tables[which])
+        for later, e in due:
+            added[later].append(kept.pop(("soak", later, e)))
+        hot = h_lane.result
+        if not last:
+            if small:
+                source, tables, hot, context, added = lax.optimization_barrier(
+                    (source, tables, hot, context, added)
+                )
+                r_lane = Lane(tree.reduce(*base_sums(source, meta_all, in_base, s + 1)), span)
+            while r_lane.left:
+                stage([r_lane])
+            base[s + 1] = r_lane.result
             for centre_add, context_add in added[s + 1]:
                 base[s + 1] = base[s + 1] - centre_add
                 context[s + 1] = context[s + 1] - context_add
-            if small:
-                in_t, out_t, hot, base, context, added = lax.optimization_barrier(
-                    (in_t, out_t, hot, base, context, added)
-                )
+    in_t, out_t = tables
 
     hot = jnp.concatenate([jnp.concatenate(hot[:2], axis=0), jnp.concatenate(hot[2:], axis=0)], axis=1)
     place = me_x ^ jnp.arange(gx, dtype=i32)

time: 689 us -> 598 us (0.87)
  waiting for transfers between devices: 235 us -> 136 us
  local copies, waits for them, and re-layouts: 71.9 us -> 83.1 us
  Pallas kernels: 206 us -> 198 us
    ppermute x113, waiting for transfers between devices: 235 us -> 136 us  [swap(): return lax.ppermute(x, axes, [(d, d ^ bit) for d in range(devices)])]
    unnamed x160 -> x362, local copies, waits for them, and re-layouts: 20.9 us -> 38.4 us
    concatenate x66 -> x65, other arithmetic: 20.7 us -> 29.4 us  [the longest x64 28.1 us: widen(): jnp.concatenate([p, g], axis=plan[k][1])]
  transfers between devices with their start and end apart: 115 -> 114, of which waited for: 48 -> 32; matrix products, arithmetic and copies ran while one was open for 14% -> 12% of each run, Pallas kernels for 27% -> 32%
where the time goes in v3:
time: 598 us; the launch traced here: 591 us
  Pallas kernels  198 us (33%)
  waiting for transfers between devices  136 us (23%)
  starting transfers between devices  119 us (20%)
  local copies, waits for them, and re-layouts  83.1 us (14%)
  other arithmetic  51.2 us (9%)
    ppermute x113, waiting for transfers between devices, swap(): return lax.ppermute(x, axes, [(d, d ^ bit) for d in range(devices)])  136 us
    ppermute x113, starting transfers between devices, swap(): return lax.ppermute(x, axes, [(d, d ^ bit) for d in range(devices)])  113 us
    pallas_call x3, Pallas kernels, hot_update(): pl.pallas_call(functools.partial(hot_kernel, scale), out_shape=(shape, sh...  56.5 us
    pallas_call x6, Pallas kernels, update(): pl.pallas_call(functools.partial(update_kernel, rows, width), out_shape=j...  51 us
    unnamed x362, local copies, waits for them, and re-layouts  38.4 us
    pallas_call x3, Pallas kernels, couple(): pl.pallas_call(couple_kernel, out_shape=(shape, shape), grid=(half,), in_...  30.9 us
    pallas_call x3, Pallas kernels, base_sums(): pl.pallas_call(functools.partial(base_kernel, rows), out_shape=(shape,) *...  29.2 us
    concatenate x64, other arithmetic, widen(): jnp.concatenate([p, g], axis=plan[k][1])  28.1 us
  transfers between devices with their start and end apart: 114, of which 32 were waited for; matrix products, arithmetic and copies ran while one was open for 12% of the time, Pallas kernels for 32%

profile of v3, /device:TPU:0, one launch (start us, length us, event | category | flops | bytes accessed | tf_op | source)
XLA Modules:
  0.0 591.0 jit_solution(5319774479999663299)
XLA Ops:
  3.2 4.1 collective-permute-start
  16.4 2.9 collective-permute-done.2
  21.1 4.9 collective-permute-done.3
  30.9 9.9 %base_sums.3 = (f32[16,152,128]{2,1,0:T(8,128)S(1)}, f32[16,152,128]{2,1,0:T(8,128)}, f32[16,152,128]{2,1,0:T(8,128)S(1)}, f32[16,152,128]{2,1,0:T(8,128)}) custom-call(s32[1]{0:T(128)} %bitcast.base_ref, s32[2,16,3,24,128]{4,3,2,1,0:T(8,128)S(1)} %bitcast.131, f32[304,1024]{1,0:T(8,128)S(1)} %pad.20.table_ref), custom_call_target="tpu_custom_call" | custom-call | flops 7650410496 | bytes 6225920 | tf_op jit(solution)/shard_map/base_sums/pallas_call | solution.py:227
  45.6 4.6 gather_fusion.1
  50.2 6.4 %all-to-all-start = ((f32[32,24,300]{2,1,0:T(8,128)}), f32[32,24,300]{2,1,0:T(8,128)}, u32[]{:S(2)}, u32[]{:S(2)}) async-start(f32[32,24,300]{2,1,0:T(8,128)} %bitcast.238), calls=%async_computation | async-start | bytes 2359296 | tf_op jit(solution)/shard_map/all_to_all | solution.py:491
  56.7 2.9 copy.91
  66.0 9.1 %base_sums.4 = (f32[16,152,128]{2,1,0:T(8,128)S(1)}, f32[16,152,128]{2,1,0:T(8,128)S(1)}, f32[16,152,128]{2,1,0:T(8,128)S(1)}, f32[16,152,128]{2,1,0:T(8,128)S(1)}) custom-call(s32[1]{0:T(128)} %bitcast.base_ref, s32[2,16,3,24,128]{4,3,2,1,0:T(8,128)S(1)} %bitcast.132, f32[304,1024]{1,0:T(8,128)S(1)} %copy-done.58), custom_call_target="tpu_custom_call" | custom-call | flops 7650410496 | bytes 6225920 | tf_op jit(solution)/shard_map/base_sums/pallas_call | solution.py:227
  77.2 8.0 %collective-permute-done.8 = f32[2,1,2,2,152,128]{5,4,3,2,1,0:T(8,128)S(1)} collective-permute-done((f32[2,1,2,2,152,128]{5,4,3,2,1,0:T(8,128)S(1)}, f32[2,1,2,2,152,128]{5,4,3,2,1,0:T(8,128)S(1)}, u32[]{:S(2)}, u32[]{:S(2)}) %collective-permute-start.8) | collective-permute-done | bytes 622624 | tf_op jit(solution)/shard_map/ppermute | solution.py:23
  93.2 3.9 gather_fusion.3
  97.1 3.3 pad_bitcast_fusion
  100.6 10.3 %couple.3 = (bf16[2,16,128,128]{3,2,1,0:T(8,128)(2,1)S(1)}, bf16[2,16,128,128]{3,2,1,0:T(8,128)(2,1)S(1)}) custom-call(s32[3,128,8]{2,1,0:T(8,128)S(1)} %copy.69.own_ref, s32[2,16,3,24,128]{4,3,2,1,0:T(8,128)S(1)} %bitcast.133), custom_call_target="tpu_custom_call" | custom-call | flops 78643200 | bytes 2097152 | tf_op jit(solution)/shard_map/couple/pallas_call | solution.py:175
  118.2 4.0 gather_fusion.2
  138.3 2.9 collective-permute-start.15
  142.3 4.9 own_grads.3
  147.5 2.8 collective-permute-start.19
  152.4 10.2 %base_sums.5 = (f32[16,152,128]{2,1,0:T(8,128)S(1)}, f32[16,152,128]{2,1,0:T(8,128)}, f32[16,152,128]{2,1,0:T(8,128)S(1)}, f32[16,152,128]{2,1,0:T(8,128)S(1)}) custom-call(s32[1]{0:T(128)} %bitcast.base_ref, s32[2,16,3,24,128]{4,3,2,1,0:T(8,128)S(1)} %bitcast.134, f32[304,1024]{1,0:T(8,128)S(1)} %copy-done.58), custom_call_target="tpu_custom_call" | custom-call | flops 7650410496 | bytes 6225920 | tf_op jit(solution)/shard_map/base_sums/pallas_call | solution.py:227
  171.2 10.3 %couple.4 = (bf16[2,16,128,128]{3,2,1,0:T(8,128)(2,1)S(1)}, bf16[2,16,128,128]{3,2,1,0:T(8,128)(2,1)S(1)}) custom-call(s32[3,128,8]{2,1,0:T(8,128)S(1)} %copy.81.own_ref, s32[2,16,3,24,128]{4,3,2,1,0:T(8,128)S(1)} %bitcast.135), custom_call_target="tpu_custom_call" | custom-call | flops 78643200 | bytes 2097152 | tf_op jit(solution)/shard_map/couple/pallas_call | solution.py:175
  188.7 15.6 %collective-permute-done.28 = f32[1,1,2,2,152,128]{5,4,3,2,1,0:T(8,128)S(1)} collective-permute-done((f32[1,1,2,2,152,128]{5,4,3,2,1,0:T(8,128)S(1)}, f32[1,1,2,2,152,128]{5,4,3,2,1,0:T(8,128)S(1)}, u32[]{:S(2)}, u32[]{:S(2)}) %collective-permute-start.28) | collective-permute-done | bytes 311328 | tf_op jit(solution)/shard_map/ppermute | solution.py:23
  209.8 14.1 %collective-permute-done.32 = f32[2,1,2,2,152,128]{5,4,3,2,1,0:T(8,128)S(1)} collective-permute-done((f32[2,1,2,2,152,128]{5,4,3,2,1,0:T(8,128)S(1)}, f32[2,1,2,2,152,128]{5,4,3,2,1,0:T(8,128)S(1)}, u32[]{:S(2)}, u32[]{:S(2)}) %collective-permute-start.32) | collective-permute-done | bytes 622624 | tf_op jit(solution)/shard_map/ppermute | solution.py:23
  230.4 18.8 %hot_update.3 = (f32[152,256]{1,0:T(8,128)S(1)}, f32[152,256]{1,0:T(8,128)S(1)}) custom-call(s32[1]{0:T(128)} %bitcast.37.slice_ref, s32[2,16,3,24,128]{4,3,2,1,0:T(8,128)S(1)} %bitcast.136, f32[4,152,256]{2,1,0:T(8,128)S(1)} %copy-done.75, f32[4,152,256]{2,1,0:T(8,128)S(1)} %copy-done.73, f32[16,152,128]{2,1,0:T(8,128)S(1)} %bitcast.147, ...), custom_call_target="tpu_custom_call" | custom-call | flops 7650410496 | bytes 4980736 | tf_op jit(solution)/shard_map/hot_update/pallas_call | solution.py:455
  253.7 5.2 absorb.3
  258.9 3.6 collective-permute-done.39
  283.3 5.5 collective-permute-done.50
  290.6 2.9 collective-permute-start.51
  293.6 4.8 own_grads.4
  300.3 2.9 collective-permute-start.55
  305.4 7.7 %context_update.3.table_ref = f32[304,1024]{1,0:T(8,128)S(1)} custom-call(s32[1]{0:T(128)} %bitcast.base_ref, s32[2,16,3,24,128]{4,3,2,1,0:T(8,128)S(1)} %bitcast.137, f32[304,1024]{1,0:T(8,128)S(1)} %copy-done.60, f32[16,152,128]{2,1,0:T(8,128)S(1)} %bitcast.149, f32[16,152,128]{2,1,0:T(8,128)S(1)} %copy-done.14, f32[16,152,128]{2,1,0:T(8,128)S(1)} %bitcast.154, ...), custom_call_target="tpu_custom_call" | custom-call | flops 5100273664 | bytes 7471104 | tf_op jit(solution)/shard_map/context_update/pallas_call | solution.py:291
  324.0 10.3 %couple.5 = (bf16[2,16,128,128]{3,2,1,0:T(8,128)(2,1)S(1)}, bf16[2,16,128,128]{3,2,1,0:T(8,128)(2,1)S(1)}) custom-call(s32[3,128,8]{2,1,0:T(8,128)S(1)} %copy-done.71, s32[2,16,3,24,128]{4,3,2,1,0:T(8,128)S(1)} %bitcast.138), custom_call_target="tpu_custom_call" | custom-call | flops 78643200 | bytes 2097152 | tf_op jit(solution)/shard_map/couple/pallas_call | solution.py:175
  345.1 9.2 %update.3.table_ref = f32[304,1024]{1,0:T(8,128)S(1)} custom-call(s32[1]{0:T(128)} %bitcast.base_ref, s32[2,16,3,24,128]{4,3,2,1,0:T(8,128)S(1)} %bitcast.139, f32[304,1024]{1,0:T(8,128)S(1)} %copy-done.59, f32[16,152,128]{2,1,0:T(8,128)S(1)} %bitcast.158, f32[16,152,128]{2,1,0:T(8,128)S(1)} %copy-done.21, f32[16,152,128]{2,1,0:T(8,128)S(1)} %bitcast.163, ...), custom_call_target="tpu_custom_call" | custom-call | flops 5100273664 | bytes 4980736 | tf_op jit(solution)/shard_map/update/pallas_call | solution.py:291
  355.4 5.7 collective-permute-done.64
  368.3 13.5 %collective-permute-done.68 = f32[2,1,2,2,152,128]{5,4,3,2,1,0:T(8,128)S(1)} collective-permute-done((f32[2,1,2,2,152,128]{5,4,3,2,1,0:T(8,128)S(1)}, f32[2,1,2,2,152,128]{5,4,3,2,1,0:T(8,128)S(1)}, u32[]{:S(2)}, u32[]{:S(2)}) %collective-permute-start.68) | collective-permute-done | bytes 622624 | tf_op jit(solution)/shard_map/ppermute | solution.py:23
  391.5 19.0 %hot_update.4 = (f32[152,256]{1,0:T(8,128)S(1)}, f32[152,256]{1,0:T(8,128)S(1)}) custom-call(s32[1]{0:T(128)} %bitcast.37.slice_ref, s32[2,16,3,24,128]{4,3,2,1,0:T(8,128)S(1)} %bitcast.140, f32[4,152,256]{2,1,0:T(8,128)S(1)} %bitcast.198, f32[4,152,256]{2,1,0:T(8,128)S(1)} %bitcast.201, f32[16,152,128]{2,1,0:T(8,128)S(1)} %bitcast.166, ...), custom_call_target="tpu_custom_call" | custom-call | flops 7650410496 | bytes 4980736 | tf_op jit(solution)/shard_map/hot_update/pallas_call | solution.py:455
  432.3 5.0 absorb.4
  443.7 5.0 absorb.5
  453.4 5.2 collective-permute-done.86
  460.5 2.9 collective-permute-start.87
  463.5 4.9 own_grads.5
  470.2 2.9 collective-permute-start.91
  475.3 7.7 %context_update.4.table_ref = f32[304,1024]{1,0:T(8,128)S(1)} custom-call(s32[1]{0:T(128)} %bitcast.base_ref, s32[2,16,3,24,128]{4,3,2,1,0:T(8,128)S(1)} %bitcast.141, f32[304,1024]{1,0:T(8,128)S(1)} %copy-done.101, f32[16,152,128]{2,1,0:T(8,128)S(1)} %bitcast.168, f32[16,152,128]{2,1,0:T(8,128)S(1)} %copy-done.48, f32[16,152,128]{2,1,0:T(8,128)S(1)} %bitcast.172, ...), custom_call_target="tpu_custom_call" | custom-call | flops 5100273664 | bytes 7471104 | tf_op jit(solution)/shard_map/context_update/pallas_call | solution.py:291
  489.0 9.5 %update.4.table_ref = f32[304,1024]{1,0:T(8,128)S(1)} custom-call(s32[1]{0:T(128)} %bitcast.base_ref, s32[2,16,3,24,128]{4,3,2,1,0:T(8,128)S(1)} %bitcast.142, f32[304,1024]{1,0:T(8,128)S(1)} %copy-done.103, f32[16,152,128]{2,1,0:T(8,128)S(1)} %bitcast.175, f32[16,152,128]{2,1,0:T(8,128)S(1)} %copy-done.54, f32[16,152,128]{2,1,0:T(8,128)S(1)} %bitcast.179, ...), custom_call_target="tpu_custom_call" | custom-call | flops 5100273664 | bytes 4980736 | tf_op jit(solution)/shard_map/update/pallas_call | solution.py:291
  502.8 16.9 %collective-permute-done.100 = f32[1,1,2,2,152,128]{5,4,3,2,1,0:T(8,128)S(1)} collective-permute-done((f32[1,1,2,2,152,128]{5,4,3,2,1,0:T(8,128)S(1)}, f32[1,1,2,2,152,128]{5,4,3,2,1,0:T(8,128)S(1)}, u32[]{:S(2)}, u32[]{:S(2)}) %collective-permute-start.100) | collective-permute-done | bytes 311328 | tf_op jit(solution)/shard_map/ppermute | solution.py:23
  522.9 13.8 %collective-permute-done.104 = f32[2,1,2,2,152,128]{5,4,3,2,1,0:T(8,128)S(1)} collective-permute-done((f32[2,1,2,2,152,128]{5,4,3,2,1,0:T(8,128)S(1)}, f32[2,1,2,2,152,128]{5,4,3,2,1,0:T(8,128)S(1)}, u32[]{:S(2)}, u32[]{:S(2)}) %collective-permute-start.104) | collective-permute-done | bytes 622624 | tf_op jit(solution)/shard_map/ppermute | solution.py:23
  538.4 18.8 %hot_update.5 = (f32[152,256]{1,0:T(8,128)S(1)}, f32[152,256]{1,0:T(8,128)S(1)}) custom-call(s32[1]{0:T(128)} %bitcast.37.slice_ref, s32[2,16,3,24,128]{4,3,2,1,0:T(8,128)S(1)} %bitcast.143, f32[4,152,256]{2,1,0:T(8,128)S(1)} %bitcast.204, f32[4,152,256]{2,1,0:T(8,128)S(1)} %bitcast.207, f32[16,152,128]{2,1,0:T(8,128)S(1)} %bitcast.181, ...), custom_call_target="tpu_custom_call" | custom-call | flops 7650410496 | bytes 4980736 | tf_op jit(solution)/shard_map/hot_update/pallas_call | solution.py:455
  559.1 7.7 %context_update.5 = f32[304,1024]{1,0:T(8,128)S(1)} custom-call(s32[1]{0:T(128)} %bitcast.base_ref, s32[2,16,3,24,128]{4,3,2,1,0:T(8,128)S(1)} %bitcast.144, f32[304,1024]{1,0:T(8,128)S(1)} %context_update.4.table_ref, f32[16,152,128]{2,1,0:T(8,128)S(1)} %bitcast.182, f32[16,152,128]{2,1,0:T(8,128)S(1)} %collective-permute-done.101.a1.refs_1_, ...), custom_call_target="tpu_custom_call" | custom-call | flops 5100273664 | bytes 7471104 | tf_op jit(solution)/shard_map/context_update/pallas_call | solution.py:291
  569.1 9.2 %update.5 = f32[304,1024]{1,0:T(8,128)S(1)} custom-call(s32[1]{0:T(128)} %bitcast.base_ref, s32[2,16,3,24,128]{4,3,2,1,0:T(8,128)S(1)} %bitcast.145, f32[304,1024]{1,0:T(8,128)S(1)} %update.4.table_ref, f32[16,152,128]{2,1,0:T(8,128)S(1)} %bitcast.187, f32[16,152,128]{2,1,0:T(8,128)S(1)} %collective-permute-done.105.refs_1_, f32[16,152,128]{2,1,0:T(8,128)S(1)} %bitcast.190, ...), custom_call_target="tpu_custom_call" | custom-call | flops 5100273664 | bytes 4980736 | tf_op jit(solution)/shard_map/update/pallas_call | solution.py:291
  583.2 3.9 gather_fusion.4
  587.1 3.5 copy.90
  (744 shorter events, 225.6 us)
Async XLA Ops:
  40.8 18.8 %collective-permute-start.5 = (f32[16,152,128]{2,1,0:T(8,128)}, f32[16,152,128]{2,1,0:T(8,128)}, u32[]{:S(2)}, u32[]{:S(2)}) collective-permute-start(f32[16,152,128]{2,1,0:T(8,128)} %get-tuple-element.199), channel_id=1, source_target_pairs={{0,4},{1,5},{2,6},{3,7},{4,0},{5,1},{6,2},{7,3},{8,12},{9,13},{10,... | collective-permute-start | bytes 3735560 | tf_op jit(solution)/shard_map/ppermute | solution.py:23
  41.3 18.3 %collective-permute-start.6 = (f32[16,152,128]{2,1,0:T(8,128)}, f32[16,152,128]{2,1,0:T(8,128)}, u32[]{:S(2)}, u32[]{:S(2)}) collective-permute-start(f32[16,152,128]{2,1,0:T(8,128)} %get-tuple-element.200), channel_id=1, source_target_pairs={{0,4},{1,5},{2,6},{3,7},{4,0},{5,1},{6,2},{7,3},{8,12},{9,13},{10,... | collective-permute-start | bytes 3735560 | tf_op jit(solution)/shard_map/ppermute | solution.py:23
  50.2 67.9 %all-to-all-start = ((f32[32,24,300]{2,1,0:T(8,128)}), f32[32,24,300]{2,1,0:T(8,128)}, u32[]{:S(2)}, u32[]{:S(2)}) async-start(f32[32,24,300]{2,1,0:T(8,128)} %bitcast.238), calls=%async_computation | async-start | bytes 2359296 | tf_op jit(solution)/shard_map/all_to_all | solution.py:491
  62.6 22.6 %collective-permute-start.8 = (f32[2,1,2,2,152,128]{5,4,3,2,1,0:T(8,128)S(1)}, f32[2,1,2,2,152,128]{5,4,3,2,1,0:T(8,128)S(1)}, u32[]{:S(2)}, u32[]{:S(2)}) collective-permute-start(f32[2,1,2,2,152,128]{5,4,3,2,1,0:T(8,128)S(1)} %slice.338), channel_id=1, source_target_pairs={{0,8},{1,9},{2,10},{3,11},{4,12},{5,13},{6,14},{7,15},{8,0},{9,1},... | collective-permute-start | bytes 1867784 | tf_op jit(solution)/shard_map/ppermute | solution.py:23
  64.5 21.4 %collective-permute-start.7 = (f32[1,2,2,2,152,128]{5,4,3,2,1,0:T(8,128)S(1)}, f32[1,2,2,2,152,128]{5,4,3,2,1,0:T(8,128)S(1)}, u32[]{:S(2)}, u32[]{:S(2)}) collective-permute-start(f32[1,2,2,2,152,128]{5,4,3,2,1,0:T(8,128)S(1)} %bitcast.249), channel_id=1, source_target_pairs={{0,16},{1,17},{2,18},{3,19},{4,20},{5,21},{6,22},{7,23},{8,24},{9,... | collective-permute-start | bytes 1867784 | tf_op jit(solution)/shard_map/ppermute | solution.py:23
  87.6 23.3 %collective-permute-start.10 = (f32[1,1,2,2,152,128]{5,4,3,2,1,0:T(8,128)}, f32[1,1,2,2,152,128]{5,4,3,2,1,0:T(8,128)}, u32[]{:S(2)}, u32[]{:S(2)}) collective-permute-start(f32[1,1,2,2,152,128]{5,4,3,2,1,0:T(8,128)} %slice.342), channel_id=1, source_target_pairs={{0,16},{1,17},{2,18},{3,19},{4,20},{5,21},{6,22},{7,23},{8,24},{9,... | collective-permute-start | bytes 933896 | tf_op jit(solution)/shard_map/ppermute | solution.py:23
  88.5 22.5 %collective-permute-start.9 = (f32[1,1,2,2,152,128]{5,4,3,2,1,0:T(8,128)}, f32[1,1,2,2,152,128]{5,4,3,2,1,0:T(8,128)}, u32[]{:S(2)}, u32[]{:S(2)}) collective-permute-start(f32[1,1,2,2,152,128]{5,4,3,2,1,0:T(8,128)} %slice.340), channel_id=1, source_target_pairs={{0,8},{1,9},{2,10},{3,11},{4,12},{5,13},{6,14},{7,15},{8,0},{9,1},... | collective-permute-start | bytes 933896 | tf_op jit(solution)/shard_map/ppermute | solution.py:23
  147.3 17.5 %collective-permute-start.20 = (f32[1,1,1,1,152,128]{5,4,3,2,1,0:T(8,128)S(1)}, f32[1,1,1,1,152,128]{5,4,3,2,1,0:T(8,128)S(1)}, u32[]{:S(2)}, u32[]{:S(2)}) collective-permute-start(f32[1,1,1,1,152,128]{5,4,3,2,1,0:T(8,128)S(1)} %get-tuple-element.416), channel_id=1, source_target_pairs={{0,2},{1,3},{2,0},{3,1},{4,6},{5,7},{6,4},{7,5},{8,10},{9,11},{10,... | collective-permute-start | bytes 233480 | tf_op jit(solution)/shard_map/ppermute | solution.py:23
  147.5 17.3 %collective-permute-start.19 = (f32[1,1,1,1,152,128]{5,4,3,2,1,0:T(8,128)S(1)}, f32[1,1,1,1,152,128]{5,4,3,2,1,0:T(8,128)S(1)}, u32[]{:S(2)}, u32[]{:S(2)}) collective-permute-start(f32[1,1,1,1,152,128]{5,4,3,2,1,0:T(8,128)S(1)} %get-tuple-element.417), channel_id=1, source_target_pairs={{0,2},{1,3},{2,0},{3,1},{4,6},{5,7},{6,4},{7,5},{8,10},{9,11},{10,... | collective-permute-start | bytes 233480 | tf_op jit(solution)/shard_map/ppermute | solution.py:23
  184.3 20.0 %collective-permute-start.26 = (f32[2,1,2,2,152,128]{5,4,3,2,1,0:T(8,128)S(1)}, f32[2,1,2,2,152,128]{5,4,3,2,1,0:T(8,128)S(1)}, u32[]{:S(2)}, u32[]{:S(2)}) collective-permute-start(f32[2,1,2,2,152,128]{5,4,3,2,1,0:T(8,128)S(1)} %pad_maximum_fusion.13), channel_id=1, source_target_pairs={{0,8},{1,9},{2,10},{3,11},{4,12},{5,13},{6,14},{7,15},{8,0},{9,1},... | collective-permute-start | bytes 1867784 | tf_op jit(solution)/shard_map/ppermute | solution.py:23
  185.9 18.5 %collective-permute-start.25 = (f32[1,2,2,2,152,128]{5,4,3,2,1,0:T(8,128)S(1)}, f32[1,2,2,2,152,128]{5,4,3,2,1,0:T(8,128)S(1)}, u32[]{:S(2)}, u32[]{:S(2)}) collective-permute-start(f32[1,2,2,2,152,128]{5,4,3,2,1,0:T(8,128)S(1)} %pad_maximum_fusion.12), channel_id=1, source_target_pairs={{0,16},{1,17},{2,18},{3,19},{4,20},{5,21},{6,22},{7,23},{8,24},{9,... | collective-permute-start | bytes 1867784 | tf_op jit(solution)/shard_map/ppermute | solution.py:23
  187.3 20.7 %collective-permute-start.33 = (f32[16,152,128]{2,1,0:T(8,128)S(1)}, f32[16,152,128]{2,1,0:T(8,128)S(1)}, u32[]{:S(2)}, u32[]{:S(2)}) collective-permute-start(f32[16,152,128]{2,1,0:T(8,128)S(1)} %copy-done.99), channel_id=1, source_target_pairs={{0,4},{1,5},{2,6},{3,7},{4,0},{5,1},{6,2},{7,3},{8,12},{9,13},{10,... | collective-permute-start | bytes 3735560 | tf_op jit(solution)/shard_map/ppermute | solution.py:23
  187.3 17.0 %collective-permute-start.28 = (f32[1,1,2,2,152,128]{5,4,3,2,1,0:T(8,128)S(1)}, f32[1,1,2,2,152,128]{5,4,3,2,1,0:T(8,128)S(1)}, u32[]{:S(2)}, u32[]{:S(2)}) collective-permute-start(f32[1,1,2,2,152,128]{5,4,3,2,1,0:T(8,128)S(1)} %pad_maximum_fusion.33), channel_id=1, source_target_pairs={{0,16},{1,17},{2,18},{3,19},{4,20},{5,21},{6,22},{7,23},{8,24},{9,... | collective-permute-start | bytes 933896 | tf_op jit(solution)/shard_map/ppermute | solution.py:23
  188.1 16.3 %collective-permute-start.27 = (f32[1,1,2,2,152,128]{5,4,3,2,1,0:T(8,128)S(1)}, f32[1,1,2,2,152,128]{5,4,3,2,1,0:T(8,128)S(1)}, u32[]{:S(2)}, u32[]{:S(2)}) collective-permute-start(f32[1,1,2,2,152,128]{5,4,3,2,1,0:T(8,128)S(1)} %pad_maximum_fusion.32), channel_id=1, source_target_pairs={{0,8},{1,9},{2,10},{3,11},{4,12},{5,13},{6,14},{7,15},{8,0},{9,1},... | collective-permute-start | bytes 933896 | tf_op jit(solution)/shard_map/ppermute | solution.py:23
  206.7 17.8 %collective-permute-start.30 = (f32[16,152,128]{2,1,0:T(8,128)S(1)}, f32[16,152,128]{2,1,0:T(8,128)S(1)}, u32[]{:S(2)}, u32[]{:S(2)}) collective-permute-start(f32[16,152,128]{2,1,0:T(8,128)S(1)} %bitcast.151), channel_id=1, source_target_pairs={{0,4},{1,5},{2,6},{3,7},{4,0},{5,1},{6,2},{7,3},{8,12},{9,13},{10,... | collective-permute-start | bytes 3735560 | tf_op jit(solution)/shard_map/ppermute | solution.py:23
  207.3 17.2 %collective-permute-start.29 = (f32[16,152,128]{2,1,0:T(8,128)S(1)}, f32[16,152,128]{2,1,0:T(8,128)S(1)}, u32[]{:S(2)}, u32[]{:S(2)}) collective-permute-start(f32[16,152,128]{2,1,0:T(8,128)S(1)} %bitcast.146), channel_id=1, source_target_pairs={{0,4},{1,5},{2,6},{3,7},{4,0},{5,1},{6,2},{7,3},{8,12},{9,13},{10,... | collective-permute-start | bytes 3735560 | tf_op jit(solution)/shard_map/ppermute | solution.py:23
  207.4 16.4 %collective-permute-start.32 = (f32[2,1,2,2,152,128]{5,4,3,2,1,0:T(8,128)S(1)}, f32[2,1,2,2,152,128]{5,4,3,2,1,0:T(8,128)S(1)}, u32[]{:S(2)}, u32[]{:S(2)}) collective-permute-start(f32[2,1,2,2,152,128]{5,4,3,2,1,0:T(8,128)S(1)} %pad_maximum_fusion.15), channel_id=1, source_target_pairs={{0,8},{1,9},{2,10},{3,11},{4,12},{5,13},{6,14},{7,15},{8,0},{9,1},... | collective-permute-start | bytes 1867784 | tf_op jit(solution)/shard_map/ppermute | solution.py:23
  208.0 16.5 %collective-permute-start.31 = (f32[1,2,2,2,152,128]{5,4,3,2,1,0:T(8,128)S(1)}, f32[1,2,2,2,152,128]{5,4,3,2,1,0:T(8,128)S(1)}, u32[]{:S(2)}, u32[]{:S(2)}) collective-permute-start(f32[1,2,2,2,152,128]{5,4,3,2,1,0:T(8,128)S(1)} %pad_maximum_fusion.14), channel_id=1, source_target_pairs={{0,16},{1,17},{2,18},{3,19},{4,20},{5,21},{6,22},{7,23},{8,24},{9,... | collective-permute-start | bytes 1867784 | tf_op jit(solution)/shard_map/ppermute | solution.py:23
  224.7 24.6 %collective-permute-start.36 = (f32[16,152,128]{2,1,0:T(8,128)S(1)}, f32[16,152,128]{2,1,0:T(8,128)S(1)}, u32[]{:S(2)}, u32[]{:S(2)}) collective-permute-start(f32[16,152,128]{2,1,0:T(8,128)S(1)} %bitcast.160), channel_id=1, source_target_pairs={{0,4},{1,5},{2,6},{3,7},{4,0},{5,1},{6,2},{7,3},{8,12},{9,13},{10,... | collective-permute-start | bytes 3735560 | tf_op jit(solution)/shard_map/ppermute | solution.py:23
  224.8 24.5 %collective-permute-start.35 = (f32[16,152,128]{2,1,0:T(8,128)S(1)}, f32[16,152,128]{2,1,0:T(8,128)S(1)}, u32[]{:S(2)}, u32[]{:S(2)}) collective-permute-start(f32[16,152,128]{2,1,0:T(8,128)S(1)} %bitcast.156), channel_id=1, source_target_pairs={{0,4},{1,5},{2,6},{3,7},{4,0},{5,1},{6,2},{7,3},{8,12},{9,13},{10,... | collective-permute-start | bytes 3735560 | tf_op jit(solution)/shard_map/ppermute | solution.py:23
  227.0 22.2 %collective-permute-start.38 = (f32[2,1,2,2,152,128]{5,4,3,2,1,0:T(8,128)S(1)}, f32[2,1,2,2,152,128]{5,4,3,2,1,0:T(8,128)S(1)}, u32[]{:S(2)}, u32[]{:S(2)}) collective-permute-start(f32[2,1,2,2,152,128]{5,4,3,2,1,0:T(8,128)S(1)} %slice.361), channel_id=1, source_target_pairs={{0,8},{1,9},{2,10},{3,11},{4,12},{5,13},{6,14},{7,15},{8,0},{9,1},... | collective-permute-start | bytes 1867784 | tf_op jit(solution)/shard_map/ppermute | solution.py:23
  228.6 20.6 %collective-permute-start.37 = (f32[1,2,2,2,152,128]{5,4,3,2,1,0:T(8,128)S(1)}, f32[1,2,2,2,152,128]{5,4,3,2,1,0:T(8,128)S(1)}, u32[]{:S(2)}, u32[]{:S(2)}) collective-permute-start(f32[1,2,2,2,152,128]{5,4,3,2,1,0:T(8,128)S(1)} %bitcast.250), channel_id=1, source_target_pairs={{0,16},{1,17},{2,18},{3,19},{4,20},{5,21},{6,22},{7,23},{8,24},{9,... | collective-permute-start | bytes 1867784 | tf_op jit(solution)/shard_map/ppermute | solution.py:23
  316.2 18.2 %collective-permute-start.58 = (f32[1,1,2,2,152,128]{5,4,3,2,1,0:T(8,128)}, f32[1,1,2,2,152,128]{5,4,3,2,1,0:T(8,128)}, u32[]{:S(2)}, u32[]{:S(2)}) collective-permute-start(f32[1,1,2,2,152,128]{5,4,3,2,1,0:T(8,128)} %pad_maximum_fusion.37), channel_id=1, source_target_pairs={{0,16},{1,17},{2,18},{3,19},{4,20},{5,21},{6,22},{7,23},{8,24},{9,... | collective-permute-start | bytes 933896 | tf_op jit(solution)/shard_map/ppermute | solution.py:23
  317.6 16.8 %collective-permute-start.57 = (f32[1,1,2,2,152,128]{5,4,3,2,1,0:T(8,128)}, f32[1,1,2,2,152,128]{5,4,3,2,1,0:T(8,128)}, u32[]{:S(2)}, u32[]{:S(2)}) collective-permute-start(f32[1,1,2,2,152,128]{5,4,3,2,1,0:T(8,128)} %pad_maximum_fusion.36), channel_id=1, source_target_pairs={{0,8},{1,9},{2,10},{3,11},{4,12},{5,13},{6,14},{7,15},{8,0},{9,1},... | collective-permute-start | bytes 933896 | tf_op jit(solution)/shard_map/ppermute | solution.py:23
  322.3 45.4 %collective-permute-start.69 = (f32[16,152,128]{2,1,0:T(8,128)}, f32[16,152,128]{2,1,0:T(8,128)}, u32[]{:S(2)}, u32[]{:S(2)}) collective-permute-start(f32[16,152,128]{2,1,0:T(8,128)} %get-tuple-element.306), channel_id=1, source_target_pairs={{0,4},{1,5},{2,6},{3,7},{4,0},{5,1},{6,2},{7,3},{8,12},{9,13},{10,... | collective-permute-start | bytes 3735560 | tf_op jit(solution)/shard_map/ppermute | solution.py:23
  337.6 23.6 %collective-permute-start.62 = (f32[2,1,2,2,152,128]{5,4,3,2,1,0:T(8,128)S(1)}, f32[2,1,2,2,152,128]{5,4,3,2,1,0:T(8,128)S(1)}, u32[]{:S(2)}, u32[]{:S(2)}) collective-permute-start(f32[2,1,2,2,152,128]{5,4,3,2,1,0:T(8,128)S(1)} %pad_maximum_fusion.19), channel_id=1, source_target_pairs={{0,8},{1,9},{2,10},{3,11},{4,12},{5,13},{6,14},{7,15},{8,0},{9,1},... | collective-permute-start | bytes 1867784 | tf_op jit(solution)/shard_map/ppermute | solution.py:23
  338.3 22.9 %collective-permute-start.61 = (f32[1,2,2,2,152,128]{5,4,3,2,1,0:T(8,128)S(1)}, f32[1,2,2,2,152,128]{5,4,3,2,1,0:T(8,128)S(1)}, u32[]{:S(2)}, u32[]{:S(2)}) collective-permute-start(f32[1,2,2,2,152,128]{5,4,3,2,1,0:T(8,128)S(1)} %pad_maximum_fusion.18), channel_id=1, source_target_pairs={{0,16},{1,17},{2,18},{3,19},{4,20},{5,21},{6,22},{7,23},{8,24},{9,... | collective-permute-start | bytes 1867784 | tf_op jit(solution)/shard_map/ppermute | solution.py:23
  340.0 21.2 %collective-permute-start.64 = (f32[1,1,2,2,152,128]{5,4,3,2,1,0:T(8,128)S(1)}, f32[1,1,2,2,152,128]{5,4,3,2,1,0:T(8,128)S(1)}, u32[]{:S(2)}, u32[]{:S(2)}) collective-permute-start(f32[1,1,2,2,152,128]{5,4,3,2,1,0:T(8,128)S(1)} %pad_maximum_fusion.39), channel_id=1, source_target_pairs={{0,16},{1,17},{2,18},{3,19},{4,20},{5,21},{6,22},{7,23},{8,24},{9,... | collective-permute-start | bytes 933896 | tf_op jit(solution)/shard_map/ppermute | solution.py:23
  342.4 18.7 %collective-permute-start.63 = (f32[1,1,2,2,152,128]{5,4,3,2,1,0:T(8,128)S(1)}, f32[1,1,2,2,152,128]{5,4,3,2,1,0:T(8,128)S(1)}, u32[]{:S(2)}, u32[]{:S(2)}) collective-permute-start(f32[1,1,2,2,152,128]{5,4,3,2,1,0:T(8,128)S(1)} %pad_maximum_fusion.38), channel_id=1, source_target_pairs={{0,8},{1,9},{2,10},{3,11},{4,12},{5,13},{6,14},{7,15},{8,0},{9,1},... | collective-permute-start | bytes 933896 | tf_op jit(solution)/shard_map/ppermute | solution.py:23
  363.7 20.1 %collective-permute-start.66 = (f32[16,152,128]{2,1,0:T(8,128)S(1)}, f32[16,152,128]{2,1,0:T(8,128)S(1)}, u32[]{:S(2)}, u32[]{:S(2)}) collective-permute-start(f32[16,152,128]{2,1,0:T(8,128)S(1)} %bitcast.169), channel_id=1, source_target_pairs={{0,4},{1,5},{2,6},{3,7},{4,0},{5,1},{6,2},{7,3},{8,12},{9,13},{10,... | collective-permute-start | bytes 3735560 | tf_op jit(solution)/shard_map/ppermute | solution.py:23
  364.3 19.6 %collective-permute-start.65 = (f32[16,152,128]{2,1,0:T(8,128)S(1)}, f32[16,152,128]{2,1,0:T(8,128)S(1)}, u32[]{:S(2)}, u32[]{:S(2)}) collective-permute-start(f32[16,152,128]{2,1,0:T(8,128)S(1)} %bitcast.165), channel_id=1, source_target_pairs={{0,4},{1,5},{2,6},{3,7},{4,0},{5,1},{6,2},{7,3},{8,12},{9,13},{10,... | collective-permute-start | bytes 3735560 | tf_op jit(solution)/shard_map/ppermute | solution.py:23
  365.3 16.4 %collective-permute-start.68 = (f32[2,1,2,2,152,128]{5,4,3,2,1,0:T(8,128)S(1)}, f32[2,1,2,2,152,128]{5,4,3,2,1,0:T(8,128)S(1)}, u32[]{:S(2)}, u32[]{:S(2)}) collective-permute-start(f32[2,1,2,2,152,128]{5,4,3,2,1,0:T(8,128)S(1)} %pad_maximum_fusion.21), channel_id=1, source_target_pairs={{0,8},{1,9},{2,10},{3,11},{4,12},{5,13},{6,14},{7,15},{8,0},{9,1},... | collective-permute-start | bytes 1867784 | tf_op jit(solution)/shard_map/ppermute | solution.py:23
  386.4 24.1 %collective-permute-start.72 = (f32[16,152,128]{2,1,0:T(8,128)S(1)}, f32[16,152,128]{2,1,0:T(8,128)S(1)}, u32[]{:S(2)}, u32[]{:S(2)}) collective-permute-start(f32[16,152,128]{2,1,0:T(8,128)S(1)} %bitcast.176), channel_id=1, source_target_pairs={{0,4},{1,5},{2,6},{3,7},{4,0},{5,1},{6,2},{7,3},{8,12},{9,13},{10,... | collective-permute-start | bytes 3735560 | tf_op jit(solution)/shard_map/ppermute | solution.py:23
  386.5 24.1 %collective-permute-start.71 = (f32[16,152,128]{2,1,0:T(8,128)S(1)}, f32[16,152,128]{2,1,0:T(8,128)S(1)}, u32[]{:S(2)}, u32[]{:S(2)}) collective-permute-start(f32[16,152,128]{2,1,0:T(8,128)S(1)} %bitcast.173), channel_id=1, source_target_pairs={{0,4},{1,5},{2,6},{3,7},{4,0},{5,1},{6,2},{7,3},{8,12},{9,13},{10,... | collective-permute-start | bytes 3735560 | tf_op jit(solution)/shard_map/ppermute | solution.py:23
  387.5 23.0 %collective-permute-start.74 = (f32[2,1,2,2,152,128]{5,4,3,2,1,0:T(8,128)S(1)}, f32[2,1,2,2,152,128]{5,4,3,2,1,0:T(8,128)S(1)}, u32[]{:S(2)}, u32[]{:S(2)}) collective-permute-start(f32[2,1,2,2,152,128]{5,4,3,2,1,0:T(8,128)S(1)} %slice.380), channel_id=1, source_target_pairs={{0,8},{1,9},{2,10},{3,11},{4,12},{5,13},{6,14},{7,15},{8,0},{9,1},... | collective-permute-start | bytes 1867784 | tf_op jit(solution)/shard_map/ppermute | solution.py:23
  390.4 20.2 %collective-permute-start.73 = (f32[1,2,2,2,152,128]{5,4,3,2,1,0:T(8,128)S(1)}, f32[1,2,2,2,152,128]{5,4,3,2,1,0:T(8,128)S(1)}, u32[]{:S(2)}, u32[]{:S(2)}) collective-permute-start(f32[1,2,2,2,152,128]{5,4,3,2,1,0:T(8,128)S(1)} %bitcast.251), channel_id=1, source_target_pairs={{0,16},{1,17},{2,18},{3,19},{4,20},{5,21},{6,22},{7,23},{8,24},{9,... | collective-permute-start | bytes 1867784 | tf_op jit(solution)/shard_map/ppermute | solution.py:23
  413.7 23.7 %collective-permute-start.78 = (f32[1,1,2,2,152,128]{5,4,3,2,1,0:T(8,128)}, f32[1,1,2,2,152,128]{5,4,3,2,1,0:T(8,128)}, u32[]{:S(2)}, u32[]{:S(2)}) collective-permute-start(f32[1,1,2,2,152,128]{5,4,3,2,1,0:T(8,128)} %slice.384), channel_id=1, source_target_pairs={{0,16},{1,17},{2,18},{3,19},{4,20},{5,21},{6,22},{7,23},{8,24},{9,... | collective-permute-start | bytes 933896 | tf_op jit(solution)/shard_map/ppermute | solution.py:23
  414.7 22.7 %collective-permute-start.77 = (f32[1,1,2,2,152,128]{5,4,3,2,1,0:T(8,128)}, f32[1,1,2,2,152,128]{5,4,3,2,1,0:T(8,128)}, u32[]{:S(2)}, u32[]{:S(2)}) collective-permute-start(f32[1,1,2,2,152,128]{5,4,3,2,1,0:T(8,128)} %slice.382), channel_id=1, source_target_pairs={{0,8},{1,9},{2,10},{3,11},{4,12},{5,13},{6,14},{7,15},{8,0},{9,1},... | collective-permute-start | bytes 933896 | tf_op jit(solution)/shard_map/ppermute | solution.py:23
  417.2 20.1 %collective-permute-start.75 = (f32[1,1,152,256]{3,2,1,0:T(8,128)}, f32[1,1,152,256]{3,2,1,0:T(8,128)S(1)}, u32[]{:S(2)}, u32[]{:S(2)}) collective-permute-start(f32[1,1,152,256]{3,2,1,0:T(8,128)} %bitcast.211), channel_id=1, source_target_pairs={{0,8},{1,9},{2,10},{3,11},{4,12},{5,13},{6,14},{7,15},{8,0},{9,1},... | collective-permute-start | bytes 466952 | tf_op jit(solution)/shard_map/ppermute | solution.py:23
  418.4 18.9 %collective-permute-start.76 = (f32[1,1,152,256]{3,2,1,0:T(8,128)}, f32[1,1,152,256]{3,2,1,0:T(8,128)S(1)}, u32[]{:S(2)}, u32[]{:S(2)}) collective-permute-start(f32[1,1,152,256]{3,2,1,0:T(8,128)} %bitcast.208), channel_id=1, source_target_pairs={{0,16},{1,17},{2,18},{3,19},{4,20},{5,21},{6,22},{7,23},{8,24},{9,... | collective-permute-start | bytes 466952 | tf_op jit(solution)/shard_map/ppermute | solution.py:23
  498.6 21.2 %collective-permute-start.98 = (f32[2,1,2,2,152,128]{5,4,3,2,1,0:T(8,128)S(1)}, f32[2,1,2,2,152,128]{5,4,3,2,1,0:T(8,128)S(1)}, u32[]{:S(2)}, u32[]{:S(2)}) collective-permute-start(f32[2,1,2,2,152,128]{5,4,3,2,1,0:T(8,128)S(1)} %pad_maximum_fusion.25), channel_id=1, source_target_pairs={{0,8},{1,9},{2,10},{3,11},{4,12},{5,13},{6,14},{7,15},{8,0},{9,1},... | collective-permute-start | bytes 1867784 | tf_op jit(solution)/shard_map/ppermute | solution.py:23
  499.5 20.3 %collective-permute-start.97 = (f32[1,2,2,2,152,128]{5,4,3,2,1,0:T(8,128)S(1)}, f32[1,2,2,2,152,128]{5,4,3,2,1,0:T(8,128)S(1)}, u32[]{:S(2)}, u32[]{:S(2)}) collective-permute-start(f32[1,2,2,2,152,128]{5,4,3,2,1,0:T(8,128)S(1)} %pad_maximum_fusion.24), channel_id=1, source_target_pairs={{0,16},{1,17},{2,18},{3,19},{4,20},{5,21},{6,22},{7,23},{8,24},{9,... | collective-permute-start | bytes 1867784 | tf_op jit(solution)/shard_map/ppermute | solution.py:23
  500.5 19.2 %collective-permute-start.100 = (f32[1,1,2,2,152,128]{5,4,3,2,1,0:T(8,128)S(1)}, f32[1,1,2,2,152,128]{5,4,3,2,1,0:T(8,128)S(1)}, u32[]{:S(2)}, u32[]{:S(2)}) collective-permute-start(f32[1,1,2,2,152,128]{5,4,3,2,1,0:T(8,128)S(1)} %pad_maximum_fusion.45), channel_id=1, source_target_pairs={{0,16},{1,17},{2,18},{3,19},{4,20},{5,21},{6,22},{7,23},{8,24},{9,... | collective-permute-start | bytes 933896 | tf_op jit(solution)/shard_map/ppermute | solution.py:23
  501.6 18.1 %collective-permute-start.99 = (f32[1,1,2,2,152,128]{5,4,3,2,1,0:T(8,128)S(1)}, f32[1,1,2,2,152,128]{5,4,3,2,1,0:T(8,128)S(1)}, u32[]{:S(2)}, u32[]{:S(2)}) collective-permute-start(f32[1,1,2,2,152,128]{5,4,3,2,1,0:T(8,128)S(1)} %pad_maximum_fusion.44), channel_id=1, source_target_pairs={{0,8},{1,9},{2,10},{3,11},{4,12},{5,13},{6,14},{7,15},{8,0},{9,1},... | collective-permute-start | bytes 933896 | tf_op jit(solution)/shard_map/ppermute | solution.py:23
  520.0 17.7 %collective-permute-start.102 = (f32[16,152,128]{2,1,0:T(8,128)S(1)}, f32[16,152,128]{2,1,0:T(8,128)S(1)}, u32[]{:S(2)}, u32[]{:S(2)}) collective-permute-start(f32[16,152,128]{2,1,0:T(8,128)S(1)} %bitcast.183), channel_id=1, source_target_pairs={{0,4},{1,5},{2,6},{3,7},{4,0},{5,1},{6,2},{7,3},{8,12},{9,13},{10,... | collective-permute-start | bytes 3735560 | tf_op jit(solution)/shard_map/ppermute | solution.py:23
  520.0 17.6 %collective-permute-start.101 = (f32[16,152,128]{2,1,0:T(8,128)S(1)}, f32[16,152,128]{2,1,0:T(8,128)S(1)}, u32[]{:S(2)}, u32[]{:S(2)}) collective-permute-start(f32[16,152,128]{2,1,0:T(8,128)S(1)} %bitcast.180), channel_id=1, source_target_pairs={{0,4},{1,5},{2,6},{3,7},{4,0},{5,1},{6,2},{7,3},{8,12},{9,13},{10,... | collective-permute-start | bytes 3735560 | tf_op jit(solution)/shard_map/ppermute | solution.py:23
  537.8 19.3 %collective-permute-start.106 = (f32[16,152,128]{2,1,0:T(8,128)S(1)}, f32[16,152,128]{2,1,0:T(8,128)S(1)}, u32[]{:S(2)}, u32[]{:S(2)}) collective-permute-start(f32[16,152,128]{2,1,0:T(8,128)S(1)} %bitcast.188), channel_id=1, source_target_pairs={{0,4},{1,5},{2,6},{3,7},{4,0},{5,1},{6,2},{7,3},{8,12},{9,13},{10,... | collective-permute-start | bytes 3735560 | tf_op jit(solution)/shard_map/ppermute | solution.py:23
  537.9 19.3 %collective-permute-start.105 = (f32[16,152,128]{2,1,0:T(8,128)S(1)}, f32[16,152,128]{2,1,0:T(8,128)S(1)}, u32[]{:S(2)}, u32[]{:S(2)}) collective-permute-start(f32[16,152,128]{2,1,0:T(8,128)S(1)} %bitcast.186), channel_id=1, source_target_pairs={{0,4},{1,5},{2,6},{3,7},{4,0},{5,1},{6,2},{7,3},{8,12},{9,13},{10,... | collective-permute-start | bytes 3735560 | tf_op jit(solution)/shard_map/ppermute | solution.py:23
  (244 other events, 2341.7 us)

commit v4 on v3

--- a/solution.py
+++ b/solution.py
@@ -52,33 +52,50 @@
             parts = [jnp.concatenate([p, g], axis=plan[k][1]) for p, g, plan in zip(parts, got, plans)]
         return [p.reshape((-1,) + t) for p, t in zip(parts, tails)]
 
-    def plans(self, with_low):
-        mh, ml = len(self.high), len(self.low) if with_low else 0
-        low = [(self.low[b], mh + ml - 1 - b) for b in reversed(range(ml))]
+    def plans(self):
+        mh, ml = len(self.high), len(self.low)
+        low = [(self.low[b], ml - 1 - b) for b in reversed(range(ml))]
         high = [(self.high[b], mh - 1 - b) for b in range(mh)]
-        return [low + high, low + high[::-1]]
-
-    def gather(self, a, b, with_low=True):
-        x, y = yield from self.widen([a, b], self.plans(with_low))
+        return low, [high, high[::-1]]
+
+    def gather(self, x):
+        low, _ = self.plans()
+        (x,) = yield from self.widen([x], [low])
+        h = x.shape[1] // 2
+        return (yield from self.gather_gx(x[:, :h], x[:, h:]))
+
+    def gather_gx(self, a, b):
+        _, high = self.plans()
+        x, y = yield from self.widen([a, b], high)
+        x, y = [v.reshape((-1,) + v.shape[2:]) for v in (x, y)]
         got = yield [x, y], [swap(x, self.core, self.devices), swap(y, self.core, self.devices)]
         return [x, got[0], y, got[1]]
 
     def gather_one(self, x):
-        (x,) = yield from self.widen([x], self.plans(True)[:1])
+        low, high = self.plans()
+        (x,) = yield from self.widen([x], [low])
+        (x,) = yield from self.widen([x], high[:1])
+        x = x.reshape((-1,) + x.shape[2:])
         got = yield [x], [swap(x, self.core, self.devices)]
         return jnp.concatenate([x, got[0]], axis=0)
 
     def reduce(self, a0, a1, b0, b1):
         got = yield [a1, b1], [swap(a1, self.core, self.devices), swap(b1, self.core, self.devices)]
-        shape = (2,) * (len(self.high) + len(self.low)) + a0.shape[1:]
+        low, high = self.plans()
+        shape = (2,) * len(high[0]) + (self.gy,) + a0.shape[1:]
         parts = [(a0 + got[0]).reshape(shape), (b0 + got[1]).reshape(shape)]
-        plans = [plan[::-1] for plan in self.plans(True)]
+        parts = yield from self.fold(parts, [plan[::-1] for plan in high])
+        x = jnp.concatenate([p.reshape(p.shape[-3:]) for p in parts], axis=1)
+        (x,) = yield from self.fold([x.reshape((2,) * len(low) + x.shape[1:])], [low[::-1]])
+        return x.reshape(x.shape[-2:])
+
+    def fold(self, parts, plans):
         for k in range(len(plans[0])):
             near = [lax.slice_in_dim(p, 0, 1, axis=plan[k][1]) for p, plan in zip(parts, plans)]
             far = [lax.slice_in_dim(p, 1, 2, axis=plan[k][1]) for p, plan in zip(parts, plans)]
             got = yield far, [swap(p, plan[k][0], self.devices) for p, plan in zip(far, plans)]
             parts = [p + g for p, g in zip(near, got)]
-        return jnp.concatenate([p.reshape(p.shape[-2:]) for p in parts], axis=0)
+        return parts
 
     def place_of(self, mask):
         bits = self.devices.bit_length() - 1
@@ -247,10 +264,12 @@
     return jnp.concatenate([r[p] for p in range(r0.shape[0]) for r in (r0, r1)], axis=1)
 
 
-def update_kernel(rows, width, base_ref, meta_ref, table_ref, *refs):
-    pick, out_ref = refs[-1], refs[-2]
+def update_kernel(rows, width, context, final, base_ref, meta_ref, table_ref, *refs):
+    if final:
+        result, pick, out_ref = refs[-3:]
+    else:
+        out_ref, pick = refs[-2:]
     ga0, ga1, gb0, gb1 = refs[:4]
-    context = len(refs) == 8
 
     @pl.when(pl.program_id(0) == 0)
     def _():
@@ -280,24 +299,30 @@
     both = jnp.concatenate(split2(grad), axis=0)
     total = jnp.dot(both, pick[...], preferred_element_type=f32)
     out_ref[...] = out_ref[...] - (total[:feats] + total[feats:])
-
-
-def update(table_t, meta, base, step, width, g, pos=()):
+    if final:
+
+        @pl.when(pl.program_id(0) == pl.num_programs(0) - 1)
+        def _():
+            result[...] = out_ref[...].T[:, :width]
+
+
+def update(table_t, meta, base, step, width, g, pos=(), final=False):
     half = meta.shape[1]
     feats, rows = table_t.shape
     piece = pl.BlockSpec((GROUP, feats // 2, LANES), lambda p, b: (p, 0, 0))
     whole = pl.BlockSpec((feats, rows), lambda p, b: (0, 0))
     arrays = list(g) + list(pos)
     return pl.pallas_call(
-        functools.partial(update_kernel, rows, width),
-        out_shape=jax.ShapeDtypeStruct((feats, rows), f32),
+        functools.partial(update_kernel, rows, width, bool(pos), final),
+        out_shape=jax.ShapeDtypeStruct((rows, width) if final else (feats, rows), f32),
         grid_spec=pltpu.PrefetchScalarGridSpec(
             num_scalar_prefetch=1,
             grid=(half // GROUP,),
             in_specs=[pl.BlockSpec((2, GROUP, 1, META, LANES), lambda p, b: (0, p, step, 0, 0)), whole]
             + [piece] * len(arrays),
-            out_specs=whole,
-            scratch_shapes=[pltpu.VMEM((GROUP * 2 * LANES, rows), bf16)],
+            out_specs=pl.BlockSpec((rows, width), lambda p, b: (0, 0)) if final else whole,
+            scratch_shapes=[pltpu.VMEM((GROUP * 2 * LANES, rows), bf16)]
+            + ([pltpu.VMEM((feats, rows), f32)] if final else []),
         ),
         compiler_params=params("arbitrary"),
         cost_estimate=cost(2 * 2 * half * 256 * feats * rows, half * 2 * feats * 512 * len(arrays) // 4),
@@ -411,73 +436,145 @@
     )(slice_of, centre, context, denom, meta, *hot)
 
 
-def hot_kernel(scale, slice_ref, meta_ref, hot_a, hot_b, a0, a1, b0, b1, out_a, out_b, total, parts):
+def hot_kernel(scale, slice_ref, meta_ref, hot_a, hot_b, a, b, *refs):
     p = pl.program_id(0)
+    total, parts = refs[-2:]
+    first = len(refs) == 3
 
     @pl.when(p == 0)
     def _():
-        total[...] = jnp.zeros_like(total)
+        total[...] = jnp.zeros_like(total) if first else refs[0][...]
         hot = jnp.concatenate([hot_a[0], hot_b[0]], axis=0)
         for k, part in enumerate(split3(hot)):
             parts[k] = part
 
-    group, n = a0.shape[0], a0.shape[2]
+    group, n = a.shape[0], a.shape[2]
     hot_slice = hot_a.shape[2]
-    centre = jnp.concatenate([tokens_of(a0, a1), tokens_of(b0, b1)], axis=0)
+    centre = jnp.concatenate(
+        [jnp.concatenate([r[q] for q in range(group)], axis=1) for r in (a, b)], axis=0
+    )
     scores = dot6(split3(centre.T), [parts[0], parts[1], parts[2]], NN)
     sums = []
-    for q in range(group):
+    for q in range(0, group, 2):
         grads = []
-        for c in range(2):
-            at = (2 * q + c) * n
-            counts = count_row(meta_ref.at[c, q, 0], slice_ref[0], hot_slice)
-            grads.append((scale * counts) * jax.nn.sigmoid(scores[at:at + n]))
-        at = 2 * q * n
-        sums.append(dot6(split3(centre[:, at:at + 2 * n]), split3(jnp.concatenate(grads, axis=0)), NN))
+        for r in (q, q + 1):
+            counts = count_row(meta_ref.at[0, r, 0], slice_ref[0], hot_slice)
+            grads.append((scale * counts) * jax.nn.sigmoid(scores[r * n:(r + 1) * n]))
+        sums.append(dot6(split3(centre[:, q * n:(q + 2) * n]), split3(jnp.concatenate(grads, axis=0)), NN))
     while len(sums) > 1:
-        sums = [a + b for a, b in zip(sums[::2], sums[1::2])]
+        sums = [x + y for x, y in zip(sums[::2], sums[1::2])]
     total[...] += sums[0]
 
     @pl.when(p == pl.num_programs(0) - 1)
     def _():
-        h = out_a.shape[0]
-        out_a[...] = hot_a[0] - learn_rate * total[:h, :]
-        out_b[...] = hot_b[0] - learn_rate * total[h:, :]
-
-
-def hot_update(scale, me_x, meta, step, hot, c):
-    half, feats_half, n = c[0].shape
+        if first:
+            refs[0][...] = total[...]
+        else:
+            out_a, out_b = refs[1:3]
+            h = out_a.shape[0]
+            out_a[...] = hot_a[0] - learn_rate * total[:h, :]
+            out_b[...] = hot_b[0] - learn_rate * total[h:, :]
+
+
+def hot_update(scale, me_x, meta, step, hot, core, a, b, partial=None):
+    half, feats_half, n = a.shape
     hot_slice = hot[0].shape[2]
-    shape = jax.ShapeDtypeStruct((feats_half, hot_slice), f32)
+    group = 2 * GROUP
+    whole = pl.BlockSpec((2 * feats_half, hot_slice), lambda p, o: (0, 0))
     out = pl.BlockSpec((feats_half, hot_slice), lambda p, o: (0, 0))
     first = pl.BlockSpec((1, feats_half, hot_slice), lambda p, o: (0, 0, 0))
-    piece = pl.BlockSpec((GROUP, feats_half, n), lambda p, o: (p, 0, 0))
+    piece = pl.BlockSpec((group, feats_half, n), lambda p, o: (p, 0, 0))
+    sum_shape = jax.ShapeDtypeStruct((2 * feats_half, hot_slice), f32)
+    half_shape = jax.ShapeDtypeStruct((feats_half, hot_slice), f32)
     return pl.pallas_call(
         functools.partial(hot_kernel, scale),
-        out_shape=(shape, shape),
+        out_shape=sum_shape if partial is None else (half_shape, half_shape),
         grid_spec=pltpu.PrefetchScalarGridSpec(
             num_scalar_prefetch=1,
-            grid=(half // GROUP,),
+            grid=(half // group,),
             in_specs=[
-                pl.BlockSpec((2, GROUP, 1, META, LANES), lambda p, o: (0, p, step, 0, 0)),
+                pl.BlockSpec((1, group, 1, META, LANES), lambda p, o: (core, p, step, 0, 0)),
                 first,
                 first,
+                piece,
+                piece,
             ]
-            + [piece] * 4,
-            out_specs=(out, out),
+            + ([] if partial is None else [whole]),
+            out_specs=whole if partial is None else (out, out),
             scratch_shapes=[
                 pltpu.VMEM((2 * feats_half, hot_slice), f32),
                 pltpu.VMEM((3, 2 * feats_half, hot_slice), bf16),
             ],
         ),
         compiler_params=params("arbitrary"),
-        cost_estimate=cost(2 * 2 * 6 * half * 256 * hot_slice * feats_half * 2, half * 256 * feats_half * 8),
+        cost_estimate=cost(2 * 2 * 6 * half * 128 * hot_slice * feats_half * 2, half * 128 * feats_half * 8),
         name="hot_update",
-    )(me_x, meta, hot[0], hot[2], *c)
-
-
-def fetch_contexts(tree, me, out_table, ids, owner, cap):
-    rows, width = out_table.shape
+    )(me_x, meta, hot[0], hot[2], a, b, *([] if partial is None else [partial]))
+
+
+def spread_kernel(slice_ref, row0, row1, a0, a1, b0, b1):
+    h = a0.shape[1]
+    for row, a, b in ((row0, a0, b0), (row1, a1, b1)):
+        turned = row[...].T
+        a[0] = turned[:h]
+        b[...] = jnp.zeros_like(b)
+        b[0, :turned.shape[0] - h, :] = turned[h:]
+
+
+def spread(hot_table, slice_of, feats):
+    hot_rows, width = hot_table.shape
+    count_of = slice_of.shape[0]
+    half, hot_slice = count_of // 2, hot_rows // count_of
+    shape = jax.ShapeDtypeStruct((half, feats // 2, hot_slice), f32)
+    piece = pl.BlockSpec((1, feats // 2, hot_slice), lambda p, o: (p, 0, 0))
+    return list(
+        pl.pallas_call(
+            spread_kernel,
+            out_shape=(shape,) * 4,
+            grid_spec=pltpu.PrefetchScalarGridSpec(
+                num_scalar_prefetch=1,
+                grid=(half,),
+                in_specs=[
+                    pl.BlockSpec((hot_slice, width), lambda p, o: (o[p], 0)),
+                    pl.BlockSpec((hot_slice, width), lambda p, o: (o[half + p], 0)),
+                ],
+                out_specs=(piece,) * 4,
+            ),
+            compiler_params=params("arbitrary"),
+            cost_estimate=cost(1e6, 2 * hot_rows * feats * 4),
+            name="spread",
+        )(slice_of, hot_table, hot_table)
+    )
+
+
+def collect_kernel(width, slice_ref, a0, a1, b0, b1, out):
+    for c, (a, b) in enumerate(((a0, b0), (a1, b1))):
+
+        @pl.when(pl.program_id(0) == c)
+        def _():
+            out[...] = jnp.concatenate([a[0], b[0]], axis=0).T[:, :width]
+
+
+def collect(pieces, slice_of, width):
+    half, feats_half, hot_slice = pieces[0].shape
+    piece = pl.BlockSpec((1, feats_half, hot_slice), lambda c, p, o: (p, 0, 0))
+    return pl.pallas_call(
+        functools.partial(collect_kernel, width),
+        out_shape=jax.ShapeDtypeStruct((2 * half * hot_slice, width), f32),
+        grid_spec=pltpu.PrefetchScalarGridSpec(
+            num_scalar_prefetch=1,
+            grid=(2, half),
+            in_specs=[piece] * 4,
+            out_specs=pl.BlockSpec((hot_slice, width), lambda c, p, o: (o[c * half + p], 0)),
+        ),
+        compiler_params=params("arbitrary", "arbitrary"),
+        cost_estimate=cost(1e6, 4 * half * feats_half * hot_slice * 8),
+        name="collect",
+    )(slice_of, *pieces)
+
+
+def rows_to_send(tree, me, out_table, ids, cap):
+    rows = out_table.shape[0]
     devices, steps, n = ids.shape
     ids = ids - me * rows
     mine = (ids >= 0) & (ids < rows)
@@ -487,14 +584,17 @@
     hit = mine[:, :, None, :] & (rank[:, :, None, :] == slots[None, None, :, None])
     wanted = jnp.sum(jnp.where(hit, ids[:, :, None, :], 0), axis=3)
     order = tree.place_of(me ^ jnp.arange(devices, dtype=i32))
-    wanted = wanted[order].reshape(devices, steps * cap)
-    got = lax.all_to_all(out_table[wanted], axes, split_axis=0, concat_axis=0, tiled=True)
+    return out_table[wanted[order].reshape(devices, steps * cap)]
+
+
+def rows_that_came(got, owner, cap):
+    steps, n = owner.shape
     same = (owner[:, :, None] == owner[:, None, :]) & (
         jnp.arange(n)[None, :, None] > jnp.arange(n)[None, None, :]
     )
     own_rank = jnp.sum(same.astype(i32), axis=2)
     at = (owner * steps + jnp.arange(steps, dtype=i32)[:, None]) * cap + own_rank
-    return got.reshape(devices * steps * cap, width)[at]
+    return got.reshape(-1, got.shape[2])[at]
 
 
 def body(
@@ -548,15 +648,11 @@
     in_t = jnp.pad(in_table.T, spare)
     source = in_t
     part = base_sums(source, meta_all, in_base, 0)
-    hot_t, out_late = after((hot_table, out_table), part[0])
+    hot_late, out_late = after((hot_table, out_table), part[0])
     out_t = jnp.pad(out_late.T, spare)
     slice_of = me_x ^ tree.slice_mask(jnp.arange(gx, dtype=i32))
-    hot_t = jnp.pad(hot_t, ((0, 0), (0, feats - width))).reshape(gx, hot_slice, feats)
-    hot_t = jnp.swapaxes(hot_t[slice_of], 1, 2)
-    hot = [hot_t[: gx // 2, :h], hot_t[gx // 2:, :h], hot_t[: gx // 2, h:], hot_t[gx // 2:, h:]]
+    hot = spread(hot_late, slice_of, feats)
     denom = 1.0 + bag_len.astype(f32)
-    got = fetch_contexts(tree, me, out_table, meta_flat[:, :, SLOTS - 1, :], context_owner[:, :, 0], cap)
-    context = [jnp.pad(got[k].T, spare) for k in range(steps)]
 
     def sums(s):
         return lambda gate: base_sums(gate(source), meta_all, in_base, s)
@@ -571,11 +667,19 @@
             if name is not None:
                 kept[name] = beside
 
+    def requests(gate):
+        return rows_to_send(tree, me, gate(out_table), meta_flat[:, :, SLOTS - 1, :], cap)
+
     kept = {}
     lane = Lane(tree.reduce(*part), span)
-    fills = [] if small else [(None, None), (("sums", 1), sums(1)), (("pair", 1, 0), pair(1, 0))]
-    run([lane], fills[: span] if steps > 1 else [], kept, lane)
+    fills = [(("rows",), requests)]
+    if not small and steps > 1:
+        fills.insert(0, (("sums", 1), sums(1)))
+    run([lane], fills, kept, lane)
     base = [lane.result] + [None] * (steps - 1)
+    got = lax.all_to_all(kept.pop(("rows",)), axes, split_axis=0, concat_axis=0, tiled=True)
+    got = rows_that_came(got, context_owner[:, :, 0], cap)
+    context = [jnp.pad(got[k].T, spare) for k in range(steps)]
     real = jnp.arange(feats)[:, None] < width
     held = []
     added = [[] for _ in range(steps)]
@@ -584,9 +688,10 @@
     def grow(s, which):
         def fill(gate):
             g, c = held[s]
+            final = s + 1 == steps
             if which == 0:
-                return update(gate(tables[0]), meta_all, in_base, s, width, g)
-            return update(gate(tables[1]), meta_all, out_base, s, width, c, g[2:])
+                return update(gate(tables[0]), meta_all, in_base, s, width, g, (), final)
+            return update(gate(tables[1]), meta_all, out_base, s, width, c, g[2:], final)
 
         return fill
 
@@ -600,49 +705,57 @@
     for s in range(steps):
         last = s + 1 == steps
         centre = jnp.where(real, base[s] / denom[s][None, :], 0.0)
-        c_lane = Lane(tree.gather(centre[:h], centre[h:]), span)
+        c_lane = Lane(tree.gather(centre), span)
         g = stage(
             [c_lane],
             lambda gate: own_grads(
                 width, scale, gate(centre), context[s], denom[s][None, :], slice_of, meta, s, hot
             ),
         )
-        g_lane = Lane(tree.gather(g[:h], g[h:]), span)
+        g_lane = Lane(tree.gather(g), span)
         fills = []
         if not small:
             if s > 0:
                 fills.append((("table", 1), grow(s - 1, 1)))
-            for e in range(s + 1 if not last else 0):
-                if ("pair", s + 1, e) not in kept:
-                    fills.append((("pair", s + 1, e), pair(s + 1, e)))
+            if not last:
+                fills.append((("pair", s + 1, s), pair(s + 1, s)))
+            for later in range(s + 2, steps):
+                fills.append((("sums", later), sums(later)) if later == s + 2 else (None, None))
             if s > 0:
                 fills.append((("table", 0), grow(s - 1, 0)))
-            if s + 2 < steps:
-                fills.append((("sums", s + 2), sums(s + 2)))
-                fills.append((("pair", s + 2, s), pair(s + 2, s)))
+        if len(fills) == 2:
+            fills.insert(1, (None, None))
         r_lane = None
         while c_lane.left:
-            if c_lane.left == 1 and not small and not last:
-                if ("sums", s + 1) not in kept:
-                    kept[("sums", s + 1)] = base_sums(source, meta_all, in_base, s + 1)
-                r_lane = Lane(tree.reduce(*kept[("sums", s + 1)]), span)
+            if c_lane.left == 1:
+                kept.update((name, fill(lambda x: x)) for name, fill in fills if name is not None)
+                for e in range(s):
+                    if not small and not last:
+                        kept[("pair", s + 1, e)] = couple(after(own, c_lane.sent[0]), meta_all, s + 1, e)
+                if not small and not last:
+                    r_lane = Lane(tree.reduce(*kept.pop(("sums", s + 1))), span)
+                half_sum = stage(
+                    [c_lane, g_lane, r_lane],
+                    lambda gate: hot_update(
+                        scale, me_x.reshape(1), meta_all, s, hot, 0, gate(c_lane.sent[0]), c_lane.sent[1]
+                    ),
+                )
+                continue
             name, fill = fills.pop(0) if fills else (None, None)
             beside = stage([c_lane, g_lane, r_lane], fill)
             if name is not None:
                 kept[name] = beside
-        for name, fill in fills:
-            kept[name] = fill(lambda x: x)
         for which in (0, 1):
             tables[which] = kept.pop(("table", which), tables[which])
         c = c_lane.result
         new_a, new_b = stage(
             [g_lane, r_lane],
-            lambda gate: hot_update(scale, me_x.reshape(1), meta_all, s, hot, [gate(c[0])] + c[1:]),
+            lambda gate: hot_update(scale, me_x.reshape(1), meta_all, s, hot, 1, gate(c[1]), c[3], half_sum),
         )
         while g_lane.left:
             stage([g_lane, r_lane])
         held.append((g_lane.result, c))
-        h_lane = Lane(tree.gather(new_a, new_b, False), short)
+        h_lane = Lane(tree.gather_gx(new_a[None], new_b[None]), short)
         due = [(later, s) for later in range(s + 1, steps)] if small else [(s + 1, e) for e in range(s, -1, -1)]
         due = [] if last else due
         if small:
@@ -671,13 +784,7 @@
             for centre_add, context_add in added[s + 1]:
                 base[s + 1] = base[s + 1] - centre_add
                 context[s + 1] = context[s + 1] - context_add
-    in_t, out_t = tables
-
-    hot = jnp.concatenate([jnp.concatenate(hot[:2], axis=0), jnp.concatenate(hot[2:], axis=0)], axis=1)
-    place = me_x ^ jnp.arange(gx, dtype=i32)
-    hot = hot[place // 2 + (gx // 2) * (place % 2)]
-    hot = jnp.swapaxes(hot, 1, 2).reshape(hot_rows, feats)[:, :width]
-    return in_t[:width].T, out_t[:width].T, hot
+    return tables[0], tables[1], collect(hot, slice_of, width)
 
 
 def solution(mesh):

time: 598 us -> 549 us (0.918)
  starting transfers between devices: 119 us -> 92.6 us
  local copies, waits for them, and re-layouts: 83.1 us -> 59.5 us
  other arithmetic: 51.2 us -> 29.8 us
  Pallas kernels: 198 us -> 209 us
  waiting for transfers between devices: 136 us -> 145 us
    ppermute x113 -> x95, starting transfers between devices: 113 us -> 87.4 us  [swap(): return lax.ppermute(x, axes, [(d, d ^ bit) for d in range(devices)])]
    gather x8 -> x4, local copies, waits for them, and re-layouts: 19.4 us -> 6.96 us  [the longest x3 3.73 us: rows_to_send(): return out_table[wanted[order].reshape(devices, steps * cap)]]
    concatenate x64 -> x52, other arithmetic: 28.1 us -> 15.7 us  [widen(): jnp.concatenate([p, g], axis=plan[k][1])]
    pallas_call x9 -> x14, Pallas kernels: 107 us -> 117 us  [the longest x6 59.1 us: hot_update(): pl.pallas_call(functools.partial(hot_kernel, scale), out_shape=sum_shape...]
    ppermute x113 -> x95, waiting for transfers between devices: 136 us -> 145 us  [swap(): return lax.ppermute(x, axes, [(d, d ^ bit) for d in range(devices)])]
    unnamed x362 -> x235, local copies, waits for them, and re-layouts: 38.4 us -> 39.3 us
  transfers between devices with their start and end apart: 114 -> 96, of which waited for: 32 -> 45; matrix products, arithmetic and copies ran while one was open for 12% -> 8% of each run, Pallas kernels for 32% -> 36%
where the time goes in v4:
time: 549 us; the launch traced here: 540 us
  Pallas kernels  209 us (38%)
  waiting for transfers between devices  145 us (26%)
  starting transfers between devices  92.6 us (17%)
  local copies, waits for them, and re-layouts  59.5 us (11%)
  other arithmetic  29.8 us (5%)
    ppermute x95, waiting for transfers between devices, swap(): return lax.ppermute(x, axes, [(d, d ^ bit) for d in range(devices)])  145 us
    ppermute x95, starting transfers between devices, swap(): return lax.ppermute(x, axes, [(d, d ^ bit) for d in range(devices)])  87.4 us
    pallas_call x6, Pallas kernels, hot_update(): pl.pallas_call(functools.partial(hot_kernel, scale), out_shape=sum_shape...  59.1 us
    pallas_call x6, Pallas kernels, update(): pl.pallas_call(functools.partial(update_kernel, rows, width, bool(pos), f...  51.5 us
    unnamed x235, local copies, waits for them, and re-layouts  39.3 us
    pallas_call x3, Pallas kernels, couple(): pl.pallas_call(couple_kernel, out_shape=(shape, shape), grid=(half,), in_...  31.1 us
    pallas_call x3, Pallas kernels, base_sums(): pl.pallas_call(functools.partial(base_kernel, rows), out_shape=(shape,) *...  28 us
    pallas_call x3, Pallas kernels, own_grads(): pl.pallas_call(functools.partial(own_kernel, width, scale), out_shape=jax...  17.4 us
  transfers between devices with their start and end apart: 96, of which 45 were waited for; matrix products, arithmetic and copies ran while one was open for 8% of the time, Pallas kernels for 36%

profile of v4, /device:TPU:0, one launch (start us, length us, event | category | flops | bytes accessed | tf_op | source)
XLA Modules:
  0.0 540.0 jit_solution(307599868720772303)
XLA Ops:
  3.3 4.1 collective-permute-start
  11.2 2.8 collective-permute-done.1
  15.8 3.4 collective-permute-done.2
  21.1 5.0 collective-permute-done.3
  28.3 9.1 %base_sums.3 = (f32[16,152,128]{2,1,0:T(8,128)S(1)}, f32[16,152,128]{2,1,0:T(8,128)S(1)}, f32[16,152,128]{2,1,0:T(8,128)S(1)}, f32[16,152,128]{2,1,0:T(8,128)S(1)}) custom-call(s32[1]{0:T(128)} %bitcast.base_ref, s32[2,16,3,24,128]{4,3,2,1,0:T(8,128)S(1)} %bitcast.139, f32[304,1024]{1,0:T(8,128)S(1)} %pad.17.table_ref), custom_call_target="tpu_custom_call" | custom-call | flops 7650410496 | bytes 6225920 | tf_op jit(solution)/shard_map/base_sums/pallas_call | solution.py:244
  38.3 9.1 %base_sums.4 = (f32[16,152,128]{2,1,0:T(8,128)S(1)}, f32[16,152,128]{2,1,0:T(8,128)S(1)}, f32[16,152,128]{2,1,0:T(8,128)S(1)}, f32[16,152,128]{2,1,0:T(8,128)S(1)}) custom-call(s32[1]{0:T(128)} %bitcast.base_ref, s32[2,16,3,24,128]{4,3,2,1,0:T(8,128)S(1)} %bitcast.140, f32[304,1024]{1,0:T(8,128)S(1)} %pad.17.table_ref), custom_call_target="tpu_custom_call" | custom-call | flops 7650410496 | bytes 6225920 | tf_op jit(solution)/shard_map/base_sums/pallas_call | solution.py:244
  60.5 3.0 gather_fusion.1
  63.5 5.4 %collective-permute-done.8 = f32[2,1,4,152,128]{4,3,2,1,0:T(8,128)} collective-permute-done((f32[2,1,4,152,128]{4,3,2,1,0:T(8,128)}, f32[2,1,4,152,128]{4,3,2,1,0:T(8,128)}, u32[]{:S(2)}, u32[]{:S(2)}) %collective-permute-start.8) | collective-permute-done | bytes 622624 | tf_op jit(solution)/shard_map/ppermute | solution.py:23
  75.8 5.2 all-to-all-start
  83.9 25.3 %collective-permute-done.11 = f32[2,1,304,128]{3,2,1,0:T(8,128)S(1)} collective-permute-done((f32[2,1,304,128]{3,2,1,0:T(8,128)S(1)}, f32[2,1,304,128]{3,2,1,0:T(8,128)S(1)}, u32[]{:S(2)}, u32[]{:S(2)}) %collective-permute-start.11) | collective-permute-done | bytes 311328 | tf_op jit(solution)/shard_map/ppermute | solution.py:23
  122.9 3.2 gather_fusion.2
  129.7 4.9 own_grads.3
  135.4 3.2 collective-permute-start.14
  138.7 10.3 %couple.3 = (bf16[2,16,128,128]{3,2,1,0:T(8,128)(2,1)S(1)}, bf16[2,16,128,128]{3,2,1,0:T(8,128)(2,1)S(1)}) custom-call(s32[3,128,8]{2,1,0:T(8,128)S(1)} %copy.95.own_ref, s32[2,16,3,24,128]{4,3,2,1,0:T(8,128)S(1)} %bitcast.141), custom_call_target="tpu_custom_call" | custom-call | flops 78643200 | bytes 2097152 | tf_op jit(solution)/shard_map/couple/pallas_call | solution.py:192
  165.9 9.8 %base_sums.5 = (f32[16,152,128]{2,1,0:T(8,128)S(1)}, f32[16,152,128]{2,1,0:T(8,128)}, f32[16,152,128]{2,1,0:T(8,128)S(1)}, f32[16,152,128]{2,1,0:T(8,128)S(1)}) custom-call(s32[1]{0:T(128)} %bitcast.base_ref, s32[2,16,3,24,128]{4,3,2,1,0:T(8,128)S(1)} %bitcast.142, f32[304,1024]{1,0:T(8,128)S(1)} %copy-done.55), custom_call_target="tpu_custom_call" | custom-call | flops 7650410496 | bytes 6225920 | tf_op jit(solution)/shard_map/base_sums/pallas_call | solution.py:244
  176.9 4.9 collective-permute-done.20
  186.2 9.8 %hot_update.6.refs_0_ = f32[304,256]{1,0:T(8,128)S(1)} custom-call(s32[1]{0:T(128)} %bitcast.35.slice_ref, s32[2,16,3,24,128]{4,3,2,1,0:T(8,128)S(1)} %bitcast.143, f32[4,152,256]{2,1,0:T(8,128)S(1)} %copy-done.75, f32[4,152,256]{2,1,0:T(8,128)S(1)} %copy-done.79, f32[16,152,128]{2,1,0:T(8,128)S(1)} %bitcast.163, f32[16,152,128]{2,1,0:T(8,128)S(1)} %bitcast.158), custom_call_target="tpu_custom_call" | custom-call | flops 3825205248 | bytes 2490368 | tf_op jit(solution)/shard_map/hot_update/pallas_call | solution.py:489
  196.0 3.1 collective-permute-done.26
  206.0 9.4 %hot_update.7 = (f32[152,256]{1,0:T(8,128)S(1)}, f32[152,256]{1,0:T(8,128)S(1)}) custom-call(s32[1]{0:T(128)} %bitcast.35.slice_ref, s32[2,16,3,24,128]{4,3,2,1,0:T(8,128)S(1)} %bitcast.144, f32[4,152,256]{2,1,0:T(8,128)S(1)} %copy-done.76, f32[4,152,256]{2,1,0:T(8,128)S(1)} %copy-done.79, f32[16,152,128]{2,1,0:T(8,128)S(1)} %collective-permute-done.23.a.ca1.refs_1_, ...), custom_call_target="tpu_custom_call" | custom-call | flops 3825205248 | bytes 2490368 | tf_op jit(solution)/shard_map/hot_update/pallas_call | solution.py:489
  223.7 5.0 absorb.3
  228.7 2.8 collective-permute-done.33
  233.3 5.4 collective-permute-done.39
  247.4 8.3 %collective-permute-done.42 = f32[1,1,304,128]{3,2,1,0:T(8,128)S(1)} collective-permute-done((f32[1,1,304,128]{3,2,1,0:T(8,128)S(1)}, f32[1,1,304,128]{3,2,1,0:T(8,128)S(1)}, u32[]{:S(2)}, u32[]{:S(2)}) %collective-permute-start.42) | collective-permute-done | bytes 155680 | tf_op jit(solution)/shard_map/ppermute | solution.py:23
  256.0 6.3 %own_grads.4 = f32[304,128]{1,0:T(8,128)S(1)} custom-call(s32[8]{0:T(128)S(1)} %fusion.33.slice_ref, f32[304,128]{1,0:T(8,128)S(1)} %fusion.15.c_ref, f32[304,128]{1,0:T(8,128)S(1)} %pad_subtract_fusion.x_ref, f32[1,128]{1,0:T(1,128)S(1)} %get-tuple-element.419.denom_ref, s32[3,24,128]{2,1,0:T(8,128)S(1)} %pad_add_fusion.6.meta_ref, ...), custom_call_target="tpu_custom_call" | custom-call | flops 1912602624 | bytes 2490368 | tf_op jit(solution)/shard_map/own_grads/pallas_call | solution.py:417
  267.1 7.7 %context_update.3.table_ref = f32[304,1024]{1,0:T(8,128)S(1)} custom-call(s32[1]{0:T(128)} %bitcast.base_ref, s32[2,16,3,24,128]{4,3,2,1,0:T(8,128)S(1)} %bitcast.145, f32[304,1024]{1,0:T(8,128)S(1)} %copy-done.57, f32[16,152,128]{2,1,0:T(8,128)S(1)} %bitcast.165, f32[16,152,128]{2,1,0:T(8,128)S(1)} %copy-done.16, f32[16,152,128]{2,1,0:T(8,128)S(1)} %bitcast.160, ...), custom_call_target="tpu_custom_call" | custom-call | flops 5100273664 | bytes 7471104 | tf_op jit(solution)/shard_map/context_update/pallas_call | solution.py:315
  282.4 10.5 %couple.4 = (bf16[2,16,128,128]{3,2,1,0:T(8,128)(2,1)S(1)}, bf16[2,16,128,128]{3,2,1,0:T(8,128)(2,1)S(1)}) custom-call(s32[3,128,8]{2,1,0:T(8,128)S(1)} %copy.97.own_ref, s32[2,16,3,24,128]{4,3,2,1,0:T(8,128)S(1)} %bitcast.146), custom_call_target="tpu_custom_call" | custom-call | flops 78643200 | bytes 2097152 | tf_op jit(solution)/shard_map/couple/pallas_call | solution.py:192
  300.8 9.2 %update.3.table_ref = f32[304,1024]{1,0:T(8,128)S(1)} custom-call(s32[1]{0:T(128)} %bitcast.base_ref, s32[2,16,3,24,128]{4,3,2,1,0:T(8,128)S(1)} %bitcast.147, f32[304,1024]{1,0:T(8,128)S(1)} %copy-done.56, f32[16,152,128]{2,1,0:T(8,128)S(1)} %bitcast.174, f32[16,152,128]{2,1,0:T(8,128)S(1)} %copy-done.23, f32[16,152,128]{2,1,0:T(8,128)S(1)} %bitcast.170, ...), custom_call_target="tpu_custom_call" | custom-call | flops 5100273664 | bytes 4980736 | tf_op jit(solution)/shard_map/update/pallas_call | solution.py:315
  310.0 9.7 %collective-permute-done.51 = f32[1,1,4,152,128]{4,3,2,1,0:T(8,128)S(1)} collective-permute-done((f32[1,1,4,152,128]{4,3,2,1,0:T(8,128)S(1)}, f32[1,1,4,152,128]{4,3,2,1,0:T(8,128)S(1)}, u32[]{:S(2)}, u32[]{:S(2)}) %collective-permute-start.51) | collective-permute-done | bytes 311328 | tf_op jit(solution)/shard_map/ppermute | solution.py:23
  326.7 10.3 %hot_update.8.refs_0_ = f32[304,256]{1,0:T(8,128)S(1)} custom-call(s32[1]{0:T(128)} %bitcast.35.slice_ref, s32[2,16,3,24,128]{4,3,2,1,0:T(8,128)S(1)} %bitcast.148, f32[4,152,256]{2,1,0:T(8,128)} %bitcast.45.a0.hot_a, f32[4,152,256]{2,1,0:T(8,128)S(1)} %bitcast.214, f32[16,152,128]{2,1,0:T(8,128)S(1)} %bitcast.188, f32[16,152,128]{2,1,0:T(8,128)S(1)} %bitcast.184), custom_call_target="tpu_custom_call" | custom-call | flops 3825205248 | bytes 2490368 | tf_op jit(solution)/shard_map/hot_update/pallas_call | solution.py:489
  347.8 10.4 %hot_update.9 = (f32[152,256]{1,0:T(8,128)S(1)}, f32[152,256]{1,0:T(8,128)S(1)}) custom-call(s32[1]{0:T(128)} %bitcast.35.slice_ref, s32[2,16,3,24,128]{4,3,2,1,0:T(8,128)S(1)} %bitcast.149, f32[4,152,256]{2,1,0:T(8,128)} %bitcast.45.a0.hot_a, f32[4,152,256]{2,1,0:T(8,128)S(1)} %bitcast.215, f32[16,152,128]{2,1,0:T(8,128)S(1)} %collective-permute-done.53.a.ca1.refs_1_, ...), custom_call_target="tpu_custom_call" | custom-call | flops 3825205248 | bytes 2490368 | tf_op jit(solution)/shard_map/hot_update/pallas_call | solution.py:489
  358.4 2.7 collective-permute-done.61
  365.6 5.2 absorb.4
  379.5 10.3 %couple.5 = (bf16[2,16,128,128]{3,2,1,0:T(8,128)(2,1)S(1)}, bf16[2,16,128,128]{3,2,1,0:T(8,128)(2,1)S(1)}) custom-call(s32[3,128,8]{2,1,0:T(8,128)S(1)} %copy.98.own_ref, s32[2,16,3,24,128]{4,3,2,1,0:T(8,128)S(1)} %bitcast.150), custom_call_target="tpu_custom_call" | custom-call | flops 78643200 | bytes 2097152 | tf_op jit(solution)/shard_map/couple/pallas_call | solution.py:192
  397.6 4.9 absorb.5
  409.5 9.0 %collective-permute-done.72 = f32[1,1,304,128]{3,2,1,0:T(8,128)S(1)} collective-permute-done((f32[1,1,304,128]{3,2,1,0:T(8,128)S(1)}, f32[1,1,304,128]{3,2,1,0:T(8,128)S(1)}, u32[]{:S(2)}, u32[]{:S(2)}) %collective-permute-start.72) | collective-permute-done | bytes 155680 | tf_op jit(solution)/shard_map/ppermute | solution.py:23
  418.8 6.2 %own_grads.5 = f32[304,128]{1,0:T(8,128)S(1)} custom-call(s32[8]{0:T(128)S(1)} %copy-done.66, f32[304,128]{1,0:T(8,128)S(1)} %fusion.11.c_ref, f32[304,128]{1,0:T(8,128)S(1)} %subtract_subtract_fusion.x_ref, f32[1,128]{1,0:T(1,128)S(1)} %copy-done.67, s32[3,24,128]{2,1,0:T(8,128)S(1)} %copy-done.61, f32[4,152,256]{2,1,0:T(8,128)S(1)} %bitcast.221, ...), custom_call_target="tpu_custom_call" | custom-call | flops 1912602624 | bytes 2490368 | tf_op jit(solution)/shard_map/own_grads/pallas_call | solution.py:417
  425.1 3.3 collective-permute-done.73
  430.4 7.7 %context_update.4.table_ref = f32[304,1024]{1,0:T(8,128)S(1)} custom-call(s32[1]{0:T(128)} %bitcast.base_ref, s32[2,16,3,24,128]{4,3,2,1,0:T(8,128)S(1)} %bitcast.151, f32[304,1024]{1,0:T(8,128)S(1)} %copy-done.85, f32[16,152,128]{2,1,0:T(8,128)S(1)} %bitcast.190, f32[16,152,128]{2,1,0:T(8,128)S(1)} %copy-done.53, f32[16,152,128]{2,1,0:T(8,128)S(1)} %bitcast.186, ...), custom_call_target="tpu_custom_call" | custom-call | flops 5100273664 | bytes 7471104 | tf_op jit(solution)/shard_map/context_update/pallas_call | solution.py:315
  443.8 5.9 %collective-permute-done.78 = f32[2,1,304,128]{3,2,1,0:T(8,128)S(1)} collective-permute-done((f32[2,1,304,128]{3,2,1,0:T(8,128)S(1)}, f32[2,1,304,128]{3,2,1,0:T(8,128)S(1)}, u32[]{:S(2)}, u32[]{:S(2)}) %collective-permute-start.78) | collective-permute-done | bytes 311328 | tf_op jit(solution)/shard_map/ppermute | solution.py:23
  455.5 9.2 %update.4.table_ref = f32[304,1024]{1,0:T(8,128)S(1)} custom-call(s32[1]{0:T(128)} %bitcast.base_ref, s32[2,16,3,24,128]{4,3,2,1,0:T(8,128)S(1)} %bitcast.152, f32[304,1024]{1,0:T(8,128)S(1)} %copy-done.87, f32[16,152,128]{2,1,0:T(8,128)S(1)} %bitcast.182, f32[16,152,128]{2,1,0:T(8,128)S(1)} %copy-done.49, f32[16,152,128]{2,1,0:T(8,128)S(1)} %bitcast.179, ...), custom_call_target="tpu_custom_call" | custom-call | flops 5100273664 | bytes 4980736 | tf_op jit(solution)/shard_map/update/pallas_call | solution.py:315
  464.8 7.2 %collective-permute-done.81 = f32[1,1,4,152,128]{4,3,2,1,0:T(8,128)S(1)} collective-permute-done((f32[1,1,4,152,128]{4,3,2,1,0:T(8,128)S(1)}, f32[1,1,4,152,128]{4,3,2,1,0:T(8,128)S(1)}, u32[]{:S(2)}, u32[]{:S(2)}) %collective-permute-start.81) | collective-permute-done | bytes 311328 | tf_op jit(solution)/shard_map/ppermute | solution.py:23
  475.5 9.7 %hot_update.10.refs_0_ = f32[304,256]{1,0:T(8,128)S(1)} custom-call(s32[1]{0:T(128)} %bitcast.35.slice_ref, s32[2,16,3,24,128]{4,3,2,1,0:T(8,128)S(1)} %bitcast.153, f32[4,152,256]{2,1,0:T(8,128)S(1)} %bitcast.222, f32[4,152,256]{2,1,0:T(8,128)S(1)} %bitcast.218, f32[16,152,128]{2,1,0:T(8,128)S(1)} %bitcast.205, f32[16,152,128]{2,1,0:T(8,128)S(1)} %bitcast.202), custom_call_target="tpu_custom_call" | custom-call | flops 3825205248 | bytes 2490368 | tf_op jit(solution)/shard_map/hot_update/pallas_call | solution.py:489
  485.2 4.1 collective-permute-done.86
  491.2 9.4 %hot_update.11 = (f32[152,256]{1,0:T(8,128)S(1)}, f32[152,256]{1,0:T(8,128)S(1)}) custom-call(s32[1]{0:T(128)} %bitcast.35.slice_ref, s32[2,16,3,24,128]{4,3,2,1,0:T(8,128)S(1)} %bitcast.154, f32[4,152,256]{2,1,0:T(8,128)S(1)} %bitcast.223, f32[4,152,256]{2,1,0:T(8,128)S(1)} %bitcast.219, f32[16,152,128]{2,1,0:T(8,128)S(1)} %collective-permute-done.83.a.refs_1_, ...), custom_call_target="tpu_custom_call" | custom-call | flops 3825205248 | bytes 2490368 | tf_op jit(solution)/shard_map/hot_update/pallas_call | solution.py:489
  502.2 8.1 %context_update.5 = f32[1024,300]{1,0:T(8,128)S(1)} custom-call(s32[1]{0:T(128)} %bitcast.base_ref, s32[2,16,3,24,128]{4,3,2,1,0:T(8,128)S(1)} %bitcast.155, f32[304,1024]{1,0:T(8,128)S(1)} %context_update.4.table_ref, f32[16,152,128]{2,1,0:T(8,128)S(1)} %bitcast.206, f32[16,152,128]{2,1,0:T(8,128)S(1)} %collective-permute-done.83.a.refs_1_, ...), custom_call_target="tpu_custom_call" | custom-call | flops 5100273664 | bytes 7471104 | tf_op jit(solution)/shard_map/context_update/pallas_call | solution.py:315
  513.1 9.6 %update.5 = f32[1024,300]{1,0:T(8,128)S(1)} custom-call(s32[1]{0:T(128)} %bitcast.base_ref, s32[2,16,3,24,128]{4,3,2,1,0:T(8,128)S(1)} %bitcast.156, f32[304,1024]{1,0:T(8,128)S(1)} %update.4.table_ref, f32[16,152,128]{2,1,0:T(8,128)S(1)} %bitcast.211, f32[16,152,128]{2,1,0:T(8,128)S(1)} %collective-permute-done.87.refs_1_, f32[16,152,128]{2,1,0:T(8,128)S(1)} %bitcast.209, ...), custom_call_target="tpu_custom_call" | custom-call | flops 5100273664 | bytes 4980736 | tf_op jit(solution)/shard_map/update/pallas_call | solution.py:315
  525.3 2.9 copy.100
  532.3 5.1 collect.1
  (549 shorter events, 199.4 us)
Async XLA Ops:
  52.6 16.4 %collective-permute-start.8 = (f32[2,1,4,152,128]{4,3,2,1,0:T(8,128)}, f32[2,1,4,152,128]{4,3,2,1,0:T(8,128)}, u32[]{:S(2)}, u32[]{:S(2)}) collective-permute-start(f32[2,1,4,152,128]{4,3,2,1,0:T(8,128)} %slice.258), channel_id=1, source_target_pairs={{0,8},{1,9},{2,10},{3,11},{4,12},{5,13},{6,14},{7,15},{8,0},{9,1},... | collective-permute-start | bytes 1867784 | tf_op jit(solution)/shard_map/ppermute | solution.py:23
  54.3 16.1 %collective-permute-start.7 = (f32[1,2,4,152,128]{4,3,2,1,0:T(8,128)}, f32[1,2,4,152,128]{4,3,2,1,0:T(8,128)}, u32[]{:S(2)}, u32[]{:S(2)}) collective-permute-start(f32[1,2,4,152,128]{4,3,2,1,0:T(8,128)} %bitcast.8), channel_id=1, source_target_pairs={{0,16},{1,17},{2,18},{3,19},{4,20},{5,21},{6,22},{7,23},{8,24},{9,... | collective-permute-start | bytes 1867784 | tf_op jit(solution)/shard_map/ppermute | solution.py:23
  75.8 47.1 %all-to-all-start = ((f32[32,24,300]{2,1,0:T(8,128)}), f32[32,24,300]{2,1,0:T(8,128)}, u32[]{:S(2)}, u32[]{:S(2)}) async-start(f32[32,24,300]{2,1,0:T(8,128)} %bitcast.17), calls=%async_computation | async-start | bytes 2359296 | tf_op jit(solution)/shard_map/all_to_all | solution.py:680
  82.5 26.7 %collective-permute-start.11 = (f32[2,1,304,128]{3,2,1,0:T(8,128)S(1)}, f32[2,1,304,128]{3,2,1,0:T(8,128)S(1)}, u32[]{:S(2)}, u32[]{:S(2)}) collective-permute-start(f32[2,1,304,128]{3,2,1,0:T(8,128)S(1)} %pad_maximum_fusion.38), channel_id=1, source_target_pairs={{0,1},{1,0},{2,3},{3,2},{4,5},{5,4},{6,7},{7,6},{8,9},{9,8},{10,11... | collective-permute-start | bytes 933896 | tf_op jit(solution)/shard_map/ppermute | solution.py:23
  135.4 13.7 %collective-permute-start.14 = (f32[2,1,304,128]{3,2,1,0:T(8,128)}, f32[2,1,304,128]{3,2,1,0:T(8,128)S(1)}, u32[]{:S(2)}, u32[]{:S(2)}) collective-permute-start(f32[2,1,304,128]{3,2,1,0:T(8,128)} %pad_maximum_fusion.39), channel_id=1, source_target_pairs={{0,1},{1,0},{2,3},{3,2},{4,5},{5,4},{6,7},{7,6},{8,9},{9,8},{10,11... | collective-permute-start | bytes 933896 | tf_op jit(solution)/shard_map/ppermute | solution.py:23
  155.6 29.0 %collective-permute-start.27 = (f32[16,152,128]{2,1,0:T(8,128)S(1)}, f32[16,152,128]{2,1,0:T(8,128)S(1)}, u32[]{:S(2)}, u32[]{:S(2)}) collective-permute-start(f32[16,152,128]{2,1,0:T(8,128)S(1)} %copy-done.73), channel_id=1, source_target_pairs={{0,4},{1,5},{2,6},{3,7},{4,0},{5,1},{6,2},{7,3},{8,12},{9,13},{10,... | collective-permute-start | bytes 3735560 | tf_op jit(solution)/shard_map/ppermute | solution.py:23
  161.8 15.0 %collective-permute-start.21 = (f32[1,1,4,152,128]{4,3,2,1,0:T(8,128)S(1)}, f32[1,1,4,152,128]{4,3,2,1,0:T(8,128)S(1)}, u32[]{:S(2)}, u32[]{:S(2)}) collective-permute-start(f32[1,1,4,152,128]{4,3,2,1,0:T(8,128)S(1)} %get-tuple-element.405), channel_id=1, source_target_pairs={{0,8},{1,9},{2,10},{3,11},{4,12},{5,13},{6,14},{7,15},{8,0},{9,1},... | collective-permute-start | bytes 933896 | tf_op jit(solution)/shard_map/ppermute | solution.py:23
  162.5 14.4 %collective-permute-start.22 = (f32[1,1,4,152,128]{4,3,2,1,0:T(8,128)S(1)}, f32[1,1,4,152,128]{4,3,2,1,0:T(8,128)S(1)}, u32[]{:S(2)}, u32[]{:S(2)}) collective-permute-start(f32[1,1,4,152,128]{4,3,2,1,0:T(8,128)S(1)} %get-tuple-element.404), channel_id=1, source_target_pairs={{0,16},{1,17},{2,18},{3,19},{4,20},{5,21},{6,22},{7,23},{8,24},{9,... | collective-permute-start | bytes 933896 | tf_op jit(solution)/shard_map/ppermute | solution.py:23
  164.0 17.8 %collective-permute-start.20 = (f32[2,1,4,152,128]{4,3,2,1,0:T(8,128)S(1)}, f32[2,1,4,152,128]{4,3,2,1,0:T(8,128)S(1)}, u32[]{:S(2)}, u32[]{:S(2)}) collective-permute-start(f32[2,1,4,152,128]{4,3,2,1,0:T(8,128)S(1)} %pad_maximum_fusion.14), channel_id=1, source_target_pairs={{0,8},{1,9},{2,10},{3,11},{4,12},{5,13},{6,14},{7,15},{8,0},{9,1},... | collective-permute-start | bytes 1867784 | tf_op jit(solution)/shard_map/ppermute | solution.py:23
  165.4 16.7 %collective-permute-start.19 = (f32[1,2,4,152,128]{4,3,2,1,0:T(8,128)S(1)}, f32[1,2,4,152,128]{4,3,2,1,0:T(8,128)S(1)}, u32[]{:S(2)}, u32[]{:S(2)}) collective-permute-start(f32[1,2,4,152,128]{4,3,2,1,0:T(8,128)S(1)} %pad_maximum_fusion.13), channel_id=1, source_target_pairs={{0,16},{1,17},{2,18},{3,19},{4,20},{5,21},{6,22},{7,23},{8,24},{9,... | collective-permute-start | bytes 1867784 | tf_op jit(solution)/shard_map/ppermute | solution.py:23
  176.8 19.3 %collective-permute-start.28 = (f32[16,152,128]{2,1,0:T(8,128)S(1)}, f32[16,152,128]{2,1,0:T(8,128)S(1)}, u32[]{:S(2)}, u32[]{:S(2)}) collective-permute-start(f32[16,152,128]{2,1,0:T(8,128)S(1)} %copy-done.71), channel_id=1, source_target_pairs={{0,4},{1,5},{2,6},{3,7},{4,0},{5,1},{6,2},{7,3},{8,12},{9,13},{10,... | collective-permute-start | bytes 3735560 | tf_op jit(solution)/shard_map/ppermute | solution.py:23
  182.4 17.9 %collective-permute-start.24 = (f32[16,152,128]{2,1,0:T(8,128)S(1)}, f32[16,152,128]{2,1,0:T(8,128)S(1)}, u32[]{:S(2)}, u32[]{:S(2)}) collective-permute-start(f32[16,152,128]{2,1,0:T(8,128)S(1)} %bitcast.157), channel_id=1, source_target_pairs={{0,4},{1,5},{2,6},{3,7},{4,0},{5,1},{6,2},{7,3},{8,12},{9,13},{10,... | collective-permute-start | bytes 3735560 | tf_op jit(solution)/shard_map/ppermute | solution.py:23
  182.5 17.9 %collective-permute-start.23 = (f32[16,152,128]{2,1,0:T(8,128)S(1)}, f32[16,152,128]{2,1,0:T(8,128)S(1)}, u32[]{:S(2)}, u32[]{:S(2)}) collective-permute-start(f32[16,152,128]{2,1,0:T(8,128)S(1)} %bitcast.162), channel_id=1, source_target_pairs={{0,4},{1,5},{2,6},{3,7},{4,0},{5,1},{6,2},{7,3},{8,12},{9,13},{10,... | collective-permute-start | bytes 3735560 | tf_op jit(solution)/shard_map/ppermute | solution.py:23
  183.0 16.1 %collective-permute-start.26 = (f32[2,1,4,152,128]{4,3,2,1,0:T(8,128)S(1)}, f32[2,1,4,152,128]{4,3,2,1,0:T(8,128)S(1)}, u32[]{:S(2)}, u32[]{:S(2)}) collective-permute-start(f32[2,1,4,152,128]{4,3,2,1,0:T(8,128)S(1)} %pad_maximum_fusion.17), channel_id=1, source_target_pairs={{0,8},{1,9},{2,10},{3,11},{4,12},{5,13},{6,14},{7,15},{8,0},{9,1},... | collective-permute-start | bytes 1867784 | tf_op jit(solution)/shard_map/ppermute | solution.py:23
  184.5 15.8 %collective-permute-start.25 = (f32[1,2,4,152,128]{4,3,2,1,0:T(8,128)S(1)}, f32[1,2,4,152,128]{4,3,2,1,0:T(8,128)S(1)}, u32[]{:S(2)}, u32[]{:S(2)}) collective-permute-start(f32[1,2,4,152,128]{4,3,2,1,0:T(8,128)S(1)} %pad_maximum_fusion.16), channel_id=1, source_target_pairs={{0,16},{1,17},{2,18},{3,19},{4,20},{5,21},{6,22},{7,23},{8,24},{9,... | collective-permute-start | bytes 1867784 | tf_op jit(solution)/shard_map/ppermute | solution.py:23
  200.6 18.7 %collective-permute-start.30 = (f32[16,152,128]{2,1,0:T(8,128)S(1)}, f32[16,152,128]{2,1,0:T(8,128)S(1)}, u32[]{:S(2)}, u32[]{:S(2)}) collective-permute-start(f32[16,152,128]{2,1,0:T(8,128)S(1)} %bitcast.167), channel_id=1, source_target_pairs={{0,4},{1,5},{2,6},{3,7},{4,0},{5,1},{6,2},{7,3},{8,12},{9,13},{10,... | collective-permute-start | bytes 3735560 | tf_op jit(solution)/shard_map/ppermute | solution.py:23
  200.7 18.6 %collective-permute-start.29 = (f32[16,152,128]{2,1,0:T(8,128)S(1)}, f32[16,152,128]{2,1,0:T(8,128)S(1)}, u32[]{:S(2)}, u32[]{:S(2)}) collective-permute-start(f32[16,152,128]{2,1,0:T(8,128)S(1)} %bitcast.172), channel_id=1, source_target_pairs={{0,4},{1,5},{2,6},{3,7},{4,0},{5,1},{6,2},{7,3},{8,12},{9,13},{10,... | collective-permute-start | bytes 3735560 | tf_op jit(solution)/shard_map/ppermute | solution.py:23
  202.9 14.9 %collective-permute-start.32 = (f32[2,1,4,152,128]{4,3,2,1,0:T(8,128)S(1)}, f32[2,1,4,152,128]{4,3,2,1,0:T(8,128)S(1)}, u32[]{:S(2)}, u32[]{:S(2)}) collective-permute-start(f32[2,1,4,152,128]{4,3,2,1,0:T(8,128)S(1)} %slice.275), channel_id=1, source_target_pairs={{0,8},{1,9},{2,10},{3,11},{4,12},{5,13},{6,14},{7,15},{8,0},{9,1},... | collective-permute-start | bytes 1867784 | tf_op jit(solution)/shard_map/ppermute | solution.py:23
  204.3 14.9 %collective-permute-start.31 = (f32[1,2,4,152,128]{4,3,2,1,0:T(8,128)S(1)}, f32[1,2,4,152,128]{4,3,2,1,0:T(8,128)S(1)}, u32[]{:S(2)}, u32[]{:S(2)}) collective-permute-start(f32[1,2,4,152,128]{4,3,2,1,0:T(8,128)S(1)} %bitcast.290), channel_id=1, source_target_pairs={{0,16},{1,17},{2,18},{3,19},{4,20},{5,21},{6,22},{7,23},{8,24},{9,... | collective-permute-start | bytes 1867784 | tf_op jit(solution)/shard_map/ppermute | solution.py:23
  239.9 15.8 %collective-permute-start.41 = (f32[4,152,256]{2,1,0:T(8,128)S(1)}, f32[4,152,256]{2,1,0:T(8,128)}, u32[]{:S(2)}, u32[]{:S(2)}) collective-permute-start(f32[4,152,256]{2,1,0:T(8,128)S(1)} %bitcast.212), channel_id=1, source_target_pairs={{0,4},{1,5},{2,6},{3,7},{4,0},{5,1},{6,2},{7,3},{8,12},{9,13},{10,... | collective-permute-start | bytes 1867784 | tf_op jit(solution)/shard_map/ppermute | solution.py:23
  240.8 14.9 %collective-permute-start.40 = (f32[4,152,256]{2,1,0:T(8,128)}, f32[4,152,256]{2,1,0:T(8,128)}, u32[]{:S(2)}, u32[]{:S(2)}) collective-permute-start(f32[4,152,256]{2,1,0:T(8,128)} %bitcast.45.a0.hot_a), channel_id=1, source_target_pairs={{0,4},{1,5},{2,6},{3,7},{4,0},{5,1},{6,2},{7,3},{8,12},{9,13},{10,... | collective-permute-start | bytes 1867784 | tf_op jit(solution)/shard_map/ppermute | solution.py:23
  278.9 14.0 %collective-permute-start.48 = (f32[2,1,304,128]{3,2,1,0:T(8,128)}, f32[2,1,304,128]{3,2,1,0:T(8,128)}, u32[]{:S(2)}, u32[]{:S(2)}) collective-permute-start(f32[2,1,304,128]{3,2,1,0:T(8,128)} %pad_maximum_fusion.44), channel_id=1, source_target_pairs={{0,1},{1,0},{2,3},{3,2},{4,5},{5,4},{6,7},{7,6},{8,9},{9,8},{10,11... | collective-permute-start | bytes 933896 | tf_op jit(solution)/shard_map/ppermute | solution.py:23
  281.6 43.5 %collective-permute-start.57 = (f32[16,152,128]{2,1,0:T(8,128)}, f32[16,152,128]{2,1,0:T(8,128)}, u32[]{:S(2)}, u32[]{:S(2)}) collective-permute-start(f32[16,152,128]{2,1,0:T(8,128)} %get-tuple-element.287), channel_id=1, source_target_pairs={{0,4},{1,5},{2,6},{3,7},{4,0},{5,1},{6,2},{7,3},{8,12},{9,13},{10,... | collective-permute-start | bytes 3735560 | tf_op jit(solution)/shard_map/ppermute | solution.py:23
  296.6 23.3 %collective-permute-start.50 = (f32[2,1,4,152,128]{4,3,2,1,0:T(8,128)S(1)}, f32[2,1,4,152,128]{4,3,2,1,0:T(8,128)S(1)}, u32[]{:S(2)}, u32[]{:S(2)}) collective-permute-start(f32[2,1,4,152,128]{4,3,2,1,0:T(8,128)S(1)} %pad_maximum_fusion.22), channel_id=1, source_target_pairs={{0,8},{1,9},{2,10},{3,11},{4,12},{5,13},{6,14},{7,15},{8,0},{9,1},... | collective-permute-start | bytes 1867784 | tf_op jit(solution)/shard_map/ppermute | solution.py:23
  297.1 22.8 %collective-permute-start.49 = (f32[1,2,4,152,128]{4,3,2,1,0:T(8,128)S(1)}, f32[1,2,4,152,128]{4,3,2,1,0:T(8,128)S(1)}, u32[]{:S(2)}, u32[]{:S(2)}) collective-permute-start(f32[1,2,4,152,128]{4,3,2,1,0:T(8,128)S(1)} %pad_maximum_fusion.21), channel_id=1, source_target_pairs={{0,16},{1,17},{2,18},{3,19},{4,20},{5,21},{6,22},{7,23},{8,24},{9,... | collective-permute-start | bytes 1867784 | tf_op jit(solution)/shard_map/ppermute | solution.py:23
  298.8 21.0 %collective-permute-start.51 = (f32[1,1,4,152,128]{4,3,2,1,0:T(8,128)S(1)}, f32[1,1,4,152,128]{4,3,2,1,0:T(8,128)S(1)}, u32[]{:S(2)}, u32[]{:S(2)}) collective-permute-start(f32[1,1,4,152,128]{4,3,2,1,0:T(8,128)S(1)} %get-tuple-element.401), channel_id=1, source_target_pairs={{0,8},{1,9},{2,10},{3,11},{4,12},{5,13},{6,14},{7,15},{8,0},{9,1},... | collective-permute-start | bytes 933896 | tf_op jit(solution)/shard_map/ppermute | solution.py:23
  300.4 19.5 %collective-permute-start.52 = (f32[1,1,4,152,128]{4,3,2,1,0:T(8,128)S(1)}, f32[1,1,4,152,128]{4,3,2,1,0:T(8,128)S(1)}, u32[]{:S(2)}, u32[]{:S(2)}) collective-permute-start(f32[1,1,4,152,128]{4,3,2,1,0:T(8,128)S(1)} %get-tuple-element.400), channel_id=1, source_target_pairs={{0,16},{1,17},{2,18},{3,19},{4,20},{5,21},{6,22},{7,23},{8,24},{9,... | collective-permute-start | bytes 933896 | tf_op jit(solution)/shard_map/ppermute | solution.py:23
  319.8 17.3 %collective-permute-start.58 = (f32[16,152,128]{2,1,0:T(8,128)S(1)}, f32[16,152,128]{2,1,0:T(8,128)S(1)}, u32[]{:S(2)}, u32[]{:S(2)}) collective-permute-start(f32[16,152,128]{2,1,0:T(8,128)S(1)} %copy-done.69), channel_id=1, source_target_pairs={{0,4},{1,5},{2,6},{3,7},{4,0},{5,1},{6,2},{7,3},{8,12},{9,13},{10,... | collective-permute-start | bytes 3735560 | tf_op jit(solution)/shard_map/ppermute | solution.py:23
  322.7 18.2 %collective-permute-start.54 = (f32[16,152,128]{2,1,0:T(8,128)S(1)}, f32[16,152,128]{2,1,0:T(8,128)S(1)}, u32[]{:S(2)}, u32[]{:S(2)}) collective-permute-start(f32[16,152,128]{2,1,0:T(8,128)S(1)} %bitcast.183), channel_id=1, source_target_pairs={{0,4},{1,5},{2,6},{3,7},{4,0},{5,1},{6,2},{7,3},{8,12},{9,13},{10,... | collective-permute-start | bytes 3735560 | tf_op jit(solution)/shard_map/ppermute | solution.py:23
  323.1 17.7 %collective-permute-start.53 = (f32[16,152,128]{2,1,0:T(8,128)S(1)}, f32[16,152,128]{2,1,0:T(8,128)S(1)}, u32[]{:S(2)}, u32[]{:S(2)}) collective-permute-start(f32[16,152,128]{2,1,0:T(8,128)S(1)} %bitcast.187), channel_id=1, source_target_pairs={{0,4},{1,5},{2,6},{3,7},{4,0},{5,1},{6,2},{7,3},{8,12},{9,13},{10,... | collective-permute-start | bytes 3735560 | tf_op jit(solution)/shard_map/ppermute | solution.py:23
  323.3 16.4 %collective-permute-start.56 = (f32[2,1,4,152,128]{4,3,2,1,0:T(8,128)S(1)}, f32[2,1,4,152,128]{4,3,2,1,0:T(8,128)S(1)}, u32[]{:S(2)}, u32[]{:S(2)}) collective-permute-start(f32[2,1,4,152,128]{4,3,2,1,0:T(8,128)S(1)} %pad_maximum_fusion.25), channel_id=1, source_target_pairs={{0,8},{1,9},{2,10},{3,11},{4,12},{5,13},{6,14},{7,15},{8,0},{9,1},... | collective-permute-start | bytes 1867784 | tf_op jit(solution)/shard_map/ppermute | solution.py:23
  325.1 15.8 %collective-permute-start.55 = (f32[1,2,4,152,128]{4,3,2,1,0:T(8,128)S(1)}, f32[1,2,4,152,128]{4,3,2,1,0:T(8,128)S(1)}, u32[]{:S(2)}, u32[]{:S(2)}) collective-permute-start(f32[1,2,4,152,128]{4,3,2,1,0:T(8,128)S(1)} %pad_maximum_fusion.24), channel_id=1, source_target_pairs={{0,16},{1,17},{2,18},{3,19},{4,20},{5,21},{6,22},{7,23},{8,24},{9,... | collective-permute-start | bytes 1867784 | tf_op jit(solution)/shard_map/ppermute | solution.py:23
  341.1 20.0 %collective-permute-start.60 = (f32[16,152,128]{2,1,0:T(8,128)S(1)}, f32[16,152,128]{2,1,0:T(8,128)S(1)}, u32[]{:S(2)}, u32[]{:S(2)}) collective-permute-start(f32[16,152,128]{2,1,0:T(8,128)S(1)} %bitcast.176), channel_id=1, source_target_pairs={{0,4},{1,5},{2,6},{3,7},{4,0},{5,1},{6,2},{7,3},{8,12},{9,13},{10,... | collective-permute-start | bytes 3735560 | tf_op jit(solution)/shard_map/ppermute | solution.py:23
  341.2 19.9 %collective-permute-start.59 = (f32[16,152,128]{2,1,0:T(8,128)S(1)}, f32[16,152,128]{2,1,0:T(8,128)S(1)}, u32[]{:S(2)}, u32[]{:S(2)}) collective-permute-start(f32[16,152,128]{2,1,0:T(8,128)S(1)} %bitcast.180), channel_id=1, source_target_pairs={{0,4},{1,5},{2,6},{3,7},{4,0},{5,1},{6,2},{7,3},{8,12},{9,13},{10,... | collective-permute-start | bytes 3735560 | tf_op jit(solution)/shard_map/ppermute | solution.py:23
  343.4 14.9 %collective-permute-start.62 = (f32[2,1,4,152,128]{4,3,2,1,0:T(8,128)S(1)}, f32[2,1,4,152,128]{4,3,2,1,0:T(8,128)S(1)}, u32[]{:S(2)}, u32[]{:S(2)}) collective-permute-start(f32[2,1,4,152,128]{4,3,2,1,0:T(8,128)S(1)} %slice.292), channel_id=1, source_target_pairs={{0,8},{1,9},{2,10},{3,11},{4,12},{5,13},{6,14},{7,15},{8,0},{9,1},... | collective-permute-start | bytes 1867784 | tf_op jit(solution)/shard_map/ppermute | solution.py:23
  346.2 14.9 %collective-permute-start.61 = (f32[1,2,4,152,128]{4,3,2,1,0:T(8,128)S(1)}, f32[1,2,4,152,128]{4,3,2,1,0:T(8,128)S(1)}, u32[]{:S(2)}, u32[]{:S(2)}) collective-permute-start(f32[1,2,4,152,128]{4,3,2,1,0:T(8,128)S(1)} %bitcast.291), channel_id=1, source_target_pairs={{0,16},{1,17},{2,18},{3,19},{4,20},{5,21},{6,22},{7,23},{8,24},{9,... | collective-permute-start | bytes 1867784 | tf_op jit(solution)/shard_map/ppermute | solution.py:23
  376.0 26.6 %collective-permute-start.69 = (f32[2,1,304,128]{3,2,1,0:T(8,128)}, f32[2,1,304,128]{3,2,1,0:T(8,128)}, u32[]{:S(2)}, u32[]{:S(2)}) collective-permute-start(f32[2,1,304,128]{3,2,1,0:T(8,128)} %pad_maximum_fusion.36), channel_id=1, source_target_pairs={{0,1},{1,0},{2,3},{3,2},{4,5},{5,4},{6,7},{7,6},{8,9},{9,8},{10,11... | collective-permute-start | bytes 933896 | tf_op jit(solution)/shard_map/ppermute | solution.py:23
  376.9 25.7 %collective-permute-start.68 = (f32[2,1,1,152,256]{4,3,2,1,0:T(8,128)}, f32[2,1,1,152,256]{4,3,2,1,0:T(8,128)}, u32[]{:S(2)}, u32[]{:S(2)}) collective-permute-start(f32[2,1,1,152,256]{4,3,2,1,0:T(8,128)} %pad_maximum_fusion.46), channel_id=1, source_target_pairs={{0,8},{1,9},{2,10},{3,11},{4,12},{5,13},{6,14},{7,15},{8,0},{9,1},... | collective-permute-start | bytes 933896 | tf_op jit(solution)/shard_map/ppermute | solution.py:23
  377.8 24.8 %collective-permute-start.67 = (f32[1,2,1,152,256]{4,3,2,1,0:T(8,128)}, f32[1,2,1,152,256]{4,3,2,1,0:T(8,128)}, u32[]{:S(2)}, u32[]{:S(2)}) collective-permute-start(f32[1,2,1,152,256]{4,3,2,1,0:T(8,128)} %pad_maximum_fusion.45), channel_id=1, source_target_pairs={{0,16},{1,17},{2,18},{3,19},{4,20},{5,21},{6,22},{7,23},{8,24},{9,... | collective-permute-start | bytes 933896 | tf_op jit(solution)/shard_map/ppermute | solution.py:23
  403.7 14.8 %collective-permute-start.71 = (f32[4,152,256]{2,1,0:T(8,128)S(1)}, f32[4,152,256]{2,1,0:T(8,128)}, u32[]{:S(2)}, u32[]{:S(2)}) collective-permute-start(f32[4,152,256]{2,1,0:T(8,128)S(1)} %bitcast.216), channel_id=1, source_target_pairs={{0,4},{1,5},{2,6},{3,7},{4,0},{5,1},{6,2},{7,3},{8,12},{9,13},{10,... | collective-permute-start | bytes 1867784 | tf_op jit(solution)/shard_map/ppermute | solution.py:23
  451.3 21.1 %collective-permute-start.80 = (f32[2,1,4,152,128]{4,3,2,1,0:T(8,128)S(1)}, f32[2,1,4,152,128]{4,3,2,1,0:T(8,128)S(1)}, u32[]{:S(2)}, u32[]{:S(2)}) collective-permute-start(f32[2,1,4,152,128]{4,3,2,1,0:T(8,128)S(1)} %pad_maximum_fusion.31), channel_id=1, source_target_pairs={{0,8},{1,9},{2,10},{3,11},{4,12},{5,13},{6,14},{7,15},{8,0},{9,1},... | collective-permute-start | bytes 1867784 | tf_op jit(solution)/shard_map/ppermute | solution.py:23
  452.0 20.3 %collective-permute-start.79 = (f32[1,2,4,152,128]{4,3,2,1,0:T(8,128)S(1)}, f32[1,2,4,152,128]{4,3,2,1,0:T(8,128)S(1)}, u32[]{:S(2)}, u32[]{:S(2)}) collective-permute-start(f32[1,2,4,152,128]{4,3,2,1,0:T(8,128)S(1)} %pad_maximum_fusion.30), channel_id=1, source_target_pairs={{0,16},{1,17},{2,18},{3,19},{4,20},{5,21},{6,22},{7,23},{8,24},{9,... | collective-permute-start | bytes 1867784 | tf_op jit(solution)/shard_map/ppermute | solution.py:23
  452.9 19.1 %collective-permute-start.81 = (f32[1,1,4,152,128]{4,3,2,1,0:T(8,128)S(1)}, f32[1,1,4,152,128]{4,3,2,1,0:T(8,128)S(1)}, u32[]{:S(2)}, u32[]{:S(2)}) collective-permute-start(f32[1,1,4,152,128]{4,3,2,1,0:T(8,128)S(1)} %get-tuple-element.397), channel_id=1, source_target_pairs={{0,8},{1,9},{2,10},{3,11},{4,12},{5,13},{6,14},{7,15},{8,0},{9,1},... | collective-permute-start | bytes 933896 | tf_op jit(solution)/shard_map/ppermute | solution.py:23
  454.4 18.0 %collective-permute-start.82 = (f32[1,1,4,152,128]{4,3,2,1,0:T(8,128)S(1)}, f32[1,1,4,152,128]{4,3,2,1,0:T(8,128)S(1)}, u32[]{:S(2)}, u32[]{:S(2)}) collective-permute-start(f32[1,1,4,152,128]{4,3,2,1,0:T(8,128)S(1)} %get-tuple-element.396), channel_id=1, source_target_pairs={{0,16},{1,17},{2,18},{3,19},{4,20},{5,21},{6,22},{7,23},{8,24},{9,... | collective-permute-start | bytes 933896 | tf_op jit(solution)/shard_map/ppermute | solution.py:23
  472.5 17.9 %collective-permute-start.84 = (f32[16,152,128]{2,1,0:T(8,128)S(1)}, f32[16,152,128]{2,1,0:T(8,128)S(1)}, u32[]{:S(2)}, u32[]{:S(2)}) collective-permute-start(f32[16,152,128]{2,1,0:T(8,128)S(1)} %bitcast.201), channel_id=1, source_target_pairs={{0,4},{1,5},{2,6},{3,7},{4,0},{5,1},{6,2},{7,3},{8,12},{9,13},{10,... | collective-permute-start | bytes 3735560 | tf_op jit(solution)/shard_map/ppermute | solution.py:23
  472.6 17.8 %collective-permute-start.83 = (f32[16,152,128]{2,1,0:T(8,128)S(1)}, f32[16,152,128]{2,1,0:T(8,128)S(1)}, u32[]{:S(2)}, u32[]{:S(2)}) collective-permute-start(f32[16,152,128]{2,1,0:T(8,128)S(1)} %bitcast.204), channel_id=1, source_target_pairs={{0,4},{1,5},{2,6},{3,7},{4,0},{5,1},{6,2},{7,3},{8,12},{9,13},{10,... | collective-permute-start | bytes 3735560 | tf_op jit(solution)/shard_map/ppermute | solution.py:23
  473.2 16.1 %collective-permute-start.86 = (f32[2,1,4,152,128]{4,3,2,1,0:T(8,128)S(1)}, f32[2,1,4,152,128]{4,3,2,1,0:T(8,128)S(1)}, u32[]{:S(2)}, u32[]{:S(2)}) collective-permute-start(f32[2,1,4,152,128]{4,3,2,1,0:T(8,128)S(1)} %pad_maximum_fusion.33), channel_id=1, source_target_pairs={{0,8},{1,9},{2,10},{3,11},{4,12},{5,13},{6,14},{7,15},{8,0},{9,1},... | collective-permute-start | bytes 1867784 | tf_op jit(solution)/shard_map/ppermute | solution.py:23
  474.7 15.7 %collective-permute-start.85 = (f32[1,2,4,152,128]{4,3,2,1,0:T(8,128)S(1)}, f32[1,2,4,152,128]{4,3,2,1,0:T(8,128)S(1)}, u32[]{:S(2)}, u32[]{:S(2)}) collective-permute-start(f32[1,2,4,152,128]{4,3,2,1,0:T(8,128)S(1)} %pad_maximum_fusion.32), channel_id=1, source_target_pairs={{0,16},{1,17},{2,18},{3,19},{4,20},{5,21},{6,22},{7,23},{8,24},{9,... | collective-permute-start | bytes 1867784 | tf_op jit(solution)/shard_map/ppermute | solution.py:23
  (162 other events, 2060.7 us)

commit v5 on v4

--- a/solution.py
+++ b/solution.py
@@ -567,7 +567,9 @@
             in_specs=[piece] * 4,
             out_specs=pl.BlockSpec((hot_slice, width), lambda c, p, o: (o[c * half + p], 0)),
         ),
-        compiler_params=params("arbitrary", "arbitrary"),
+        compiler_params=pltpu.CompilerParams(
+            dimension_semantics=("arbitrary", "arbitrary"), vmem_limit_bytes=62 * 2**20
+        ),
         cost_estimate=cost(1e6, 4 * half * feats_half * hot_slice * 8),
         name="collect",
     )(slice_of, *pieces)
@@ -677,9 +679,15 @@
         fills.insert(0, (("sums", 1), sums(1)))
     run([lane], fills, kept, lane)
     base = [lane.result] + [None] * (steps - 1)
-    got = lax.all_to_all(kept.pop(("rows",)), axes, split_axis=0, concat_axis=0, tiled=True)
-    got = rows_that_came(got, context_owner[:, :, 0], cap)
-    context = [jnp.pad(got[k].T, spare) for k in range(steps)]
+    send_rows = kept.pop(("rows",))
+    owner = context_owner[:, :, 0]
+
+    def exchange(rows, owner):
+        got = lax.all_to_all(rows, axes, split_axis=0, concat_axis=0, tiled=True)
+        got = rows_that_came(got, owner, cap)
+        return [jnp.pad(got[k].T, spare) for k in range(owner.shape[0])]
+
+    context = exchange(send_rows[:, :cap], owner[:1])
     real = jnp.arange(feats)[:, None] < width
     held = []
     added = [[] for _ in range(steps)]
@@ -720,7 +728,9 @@
             if not last:
                 fills.append((("pair", s + 1, s), pair(s + 1, s)))
             for later in range(s + 2, steps):
-                fills.append((("sums", later), sums(later)) if later == s + 2 else (None, None))
+                fills.append((("pair", later, s), pair(later, s)))
+            if s + 2 < steps:
+                fills.append((("sums", s + 2), sums(s + 2)))
             if s > 0:
                 fills.append((("table", 0), grow(s - 1, 0)))
         if len(fills) == 2:
@@ -729,9 +739,6 @@
         while c_lane.left:
             if c_lane.left == 1:
                 kept.update((name, fill(lambda x: x)) for name, fill in fills if name is not None)
-                for e in range(s):
-                    if not small and not last:
-                        kept[("pair", s + 1, e)] = couple(after(own, c_lane.sent[0]), meta_all, s + 1, e)
                 if not small and not last:
                     r_lane = Lane(tree.reduce(*kept.pop(("sums", s + 1))), span)
                 half_sum = stage(
@@ -741,6 +748,8 @@
                     ),
                 )
                 continue
+            if c_lane.left == 2 and s == 0 and not last:
+                context += exchange(after(send_rows[:, cap:], c_lane.sent), owner[1:])
             name, fill = fills.pop(0) if fills else (None, None)
             beside = stage([c_lane, g_lane, r_lane], fill)
             if name is not None:
@@ -756,8 +765,7 @@
             stage([g_lane, r_lane])
         held.append((g_lane.result, c))
         h_lane = Lane(tree.gather_gx(new_a[None], new_b[None]), short)
-        due = [(later, s) for later in range(s + 1, steps)] if small else [(s + 1, e) for e in range(s, -1, -1)]
-        due = [] if last else due
+        due = [(later, s) for later in range(s + 1, steps)]
         if small:
             for later, e in due:
                 kept[("pair", later, e)] = couple(own, meta_all, later, e)

time: 549 us -> 566 us (1.031)
  waiting for transfers between devices: 145 us -> 128 us
  local copies, waits for them, and re-layouts: 59.5 us -> 73.8 us
  other arithmetic: 29.8 us -> 39.4 us
  Pallas kernels: 209 us -> 215 us
    ppermute x95, waiting for transfers between devices: 145 us -> 128 us  [swap(): return lax.ppermute(x, axes, [(d, d ^ bit) for d in range(devices)])]
    unnamed x235 -> x271, local copies, waits for them, and re-layouts: 39.3 us -> 49 us
    concatenate x52, other arithmetic: 15.7 us -> 21.6 us  [widen(): jnp.concatenate([p, g], axis=plan[k][1])]
  transfers between devices with their start and end apart: 96 -> 97, of which waited for: 45 -> 42; matrix products, arithmetic and copies ran while one was open for 8% -> 10% of each run, Pallas kernels for 36% -> 36%
where the time goes in v5:
time: 566 us; the launch traced here: 557 us
  Pallas kernels  215 us (38%)
  waiting for transfers between devices  128 us (23%)
  starting transfers between devices  97.6 us (17%)
  local copies, waits for them, and re-layouts  73.8 us (13%)
  other arithmetic  39.4 us (7%)
    ppermute x95, waiting for transfers between devices, swap(): return lax.ppermute(x, axes, [(d, d ^ bit) for d in range(devices)])  128 us
    ppermute x95, starting transfers between devices, swap(): return lax.ppermute(x, axes, [(d, d ^ bit) for d in range(devices)])  87.4 us
    pallas_call x6, Pallas kernels, hot_update(): pl.pallas_call(functools.partial(hot_kernel, scale), out_shape=sum_shape...  60.9 us
    pallas_call x6, Pallas kernels, update(): pl.pallas_call(functools.partial(update_kernel, rows, width, bool(pos), f...  51.7 us
    unnamed x271, local copies, waits for them, and re-layouts  49 us
    pallas_call x3, Pallas kernels, couple(): pl.pallas_call(couple_kernel, out_shape=(shape, shape), grid=(half,), in_...  31 us
    pallas_call x3, Pallas kernels, base_sums(): pl.pallas_call(functools.partial(base_kernel, rows), out_shape=(shape,) *...  28.7 us
    concatenate x52, other arithmetic, widen(): jnp.concatenate([p, g], axis=plan[k][1])  21.6 us
  transfers between devices with their start and end apart: 97, of which 42 were waited for; matrix products, arithmetic and copies ran while one was open for 10% of the time, Pallas kernels for 36%

profile of v5, /device:TPU:0, one launch (start us, length us, event | category | flops | bytes accessed | tf_op | source)
XLA Modules:
  0.0 556.5 jit_solution(4365700952838269975)
XLA Ops:
  3.2 4.1 collective-permute-start
  15.8 3.4 collective-permute-done.2
  21.1 5.0 collective-permute-done.3
  28.3 9.1 %base_sums.3 = (f32[16,152,128]{2,1,0:T(8,128)S(1)}, f32[16,152,128]{2,1,0:T(8,128)S(1)}, f32[16,152,128]{2,1,0:T(8,128)S(1)}, f32[16,152,128]{2,1,0:T(8,128)S(1)}) custom-call(s32[1]{0:T(128)} %bitcast.base_ref, s32[2,16,3,24,128]{4,3,2,1,0:T(8,128)S(1)} %bitcast.150, f32[304,1024]{1,0:T(8,128)S(1)} %pad.17.table_ref), custom_call_target="tpu_custom_call" | custom-call | flops 7650410496 | bytes 6225920 | tf_op jit(solution)/shard_map/base_sums/pallas_call | solution.py:244
  38.3 9.8 %base_sums.4 = (f32[16,152,128]{2,1,0:T(8,128)S(1)}, f32[16,152,128]{2,1,0:T(8,128)}, f32[16,152,128]{2,1,0:T(8,128)S(1)}, f32[16,152,128]{2,1,0:T(8,128)S(1)}) custom-call(s32[1]{0:T(128)} %bitcast.base_ref, s32[2,16,3,24,128]{4,3,2,1,0:T(8,128)S(1)} %bitcast.151, f32[304,1024]{1,0:T(8,128)S(1)} %pad.17.table_ref), custom_call_target="tpu_custom_call" | custom-call | flops 7650410496 | bytes 6225920 | tf_op jit(solution)/shard_map/base_sums/pallas_call | solution.py:244
  59.8 3.0 gather_fusion.1
  62.8 5.5 collective-permute-done.8
  76.2 5.3 all-to-all-start
  83.6 13.6 %collective-permute-done.11 = f32[2,1,304,128]{3,2,1,0:T(8,128)S(1)} collective-permute-done((f32[2,1,304,128]{3,2,1,0:T(8,128)S(1)}, f32[2,1,304,128]{3,2,1,0:T(8,128)S(1)}, u32[]{:S(2)}, u32[]{:S(2)}) %collective-permute-start.11) | collective-permute-done | bytes 311328 | tf_op jit(solution)/shard_map/ppermute | solution.py:23
  114.7 4.9 own_grads.3
  122.9 10.3 %couple.3 = (bf16[2,16,128,128]{3,2,1,0:T(8,128)(2,1)S(1)}, bf16[2,16,128,128]{3,2,1,0:T(8,128)(2,1)S(1)}) custom-call(s32[3,128,8]{2,1,0:T(8,128)S(1)} %copy.94.own_ref, s32[2,16,3,24,128]{4,3,2,1,0:T(8,128)S(1)} %bitcast.152), custom_call_target="tpu_custom_call" | custom-call | flops 78643200 | bytes 2097152 | tf_op jit(solution)/shard_map/couple/pallas_call | solution.py:192
  139.6 10.3 %couple.4 = (bf16[2,16,128,128]{3,2,1,0:T(8,128)(2,1)S(1)}, bf16[2,16,128,128]{3,2,1,0:T(8,128)(2,1)S(1)}) custom-call(s32[3,128,8]{2,1,0:T(8,128)S(1)} %copy.95.own_ref, s32[2,16,3,24,128]{4,3,2,1,0:T(8,128)S(1)} %bitcast.153), custom_call_target="tpu_custom_call" | custom-call | flops 78643200 | bytes 2097152 | tf_op jit(solution)/shard_map/couple/pallas_call | solution.py:192
  157.9 9.8 %base_sums.5 = (f32[16,152,128]{2,1,0:T(8,128)S(1)}, f32[16,152,128]{2,1,0:T(8,128)}, f32[16,152,128]{2,1,0:T(8,128)S(1)}, f32[16,152,128]{2,1,0:T(8,128)S(1)}) custom-call(s32[1]{0:T(128)} %bitcast.base_ref, s32[2,16,3,24,128]{4,3,2,1,0:T(8,128)S(1)} %bitcast.154, f32[304,1024]{1,0:T(8,128)S(1)} %copy-done.55), custom_call_target="tpu_custom_call" | custom-call | flops 7650410496 | bytes 6225920 | tf_op jit(solution)/shard_map/base_sums/pallas_call | solution.py:244
  168.8 8.2 %collective-permute-done.20 = f32[2,1,4,152,128]{4,3,2,1,0:T(8,128)S(1)} collective-permute-done((f32[2,1,4,152,128]{4,3,2,1,0:T(8,128)S(1)}, f32[2,1,4,152,128]{4,3,2,1,0:T(8,128)S(1)}, u32[]{:S(2)}, u32[]{:S(2)}) %collective-permute-start.20) | collective-permute-done | bytes 622624 | tf_op jit(solution)/shard_map/ppermute | solution.py:23
  182.9 10.0 %hot_update.6.refs_0_ = f32[304,256]{1,0:T(8,128)S(1)} custom-call(s32[1]{0:T(128)} %bitcast.36.slice_ref, s32[2,16,3,24,128]{4,3,2,1,0:T(8,128)S(1)} %bitcast.155, f32[4,152,256]{2,1,0:T(8,128)S(1)} %copy-done.92, f32[4,152,256]{2,1,0:T(8,128)S(1)} %copy-done.95, f32[16,152,128]{2,1,0:T(8,128)S(1)} %bitcast.183, f32[16,152,128]{2,1,0:T(8,128)S(1)} %bitcast.178), custom_call_target="tpu_custom_call" | custom-call | flops 3825205248 | bytes 2490368 | tf_op jit(solution)/shard_map/hot_update/pallas_call | solution.py:489
  192.8 3.9 collective-permute-done.26
  204.0 9.5 %hot_update.7 = (f32[152,256]{1,0:T(8,128)S(1)}, f32[152,256]{1,0:T(8,128)S(1)}) custom-call(s32[1]{0:T(128)} %bitcast.36.slice_ref, s32[2,16,3,24,128]{4,3,2,1,0:T(8,128)S(1)} %bitcast.156, f32[4,152,256]{2,1,0:T(8,128)S(1)} %copy-done.92, f32[4,152,256]{2,1,0:T(8,128)S(1)} %copy-done.95, f32[16,152,128]{2,1,0:T(8,128)S(1)} %collective-permute-done.23.a.ca1.refs_1_, ...), custom_call_target="tpu_custom_call" | custom-call | flops 3825205248 | bytes 2490368 | tf_op jit(solution)/shard_map/hot_update/pallas_call | solution.py:489
  224.0 4.9 all-to-all-start.1
  243.9 4.9 absorb.3
  257.3 3.0 gather_fusion.3
  270.7 5.0 absorb.4
  285.7 7.5 %collective-permute-done.42 = f32[1,1,304,128]{3,2,1,0:T(8,128)S(1)} collective-permute-done((f32[1,1,304,128]{3,2,1,0:T(8,128)S(1)}, f32[1,1,304,128]{3,2,1,0:T(8,128)S(1)}, u32[]{:S(2)}, u32[]{:S(2)}) %collective-permute-start.42) | collective-permute-done | bytes 155680 | tf_op jit(solution)/shard_map/ppermute | solution.py:23
  293.4 6.3 %own_grads.4 = f32[304,128]{1,0:T(8,128)S(1)} custom-call(s32[8]{0:T(128)S(1)} %fusion.31.slice_ref, f32[304,128]{1,0:T(8,128)S(1)} %fusion.15.c_ref, f32[304,128]{1,0:T(8,128)S(1)} %pad_subtract_fusion.x_ref, f32[1,128]{1,0:T(1,128)S(1)} %get-tuple-element.424.denom_ref, s32[3,24,128]{2,1,0:T(8,128)S(1)} %pad_add_fusion.6.meta_ref, ...), custom_call_target="tpu_custom_call" | custom-call | flops 1912602624 | bytes 2490368 | tf_op jit(solution)/shard_map/own_grads/pallas_call | solution.py:417
  299.7 3.0 collective-permute-done.43
  305.4 7.7 %context_update.3.table_ref = f32[304,1024]{1,0:T(8,128)S(1)} custom-call(s32[1]{0:T(128)} %bitcast.base_ref, s32[2,16,3,24,128]{4,3,2,1,0:T(8,128)S(1)} %bitcast.157, f32[304,1024]{1,0:T(8,128)S(1)} %copy-done.57, f32[16,152,128]{2,1,0:T(8,128)S(1)} %bitcast.186, f32[16,152,128]{2,1,0:T(8,128)S(1)} %copy-done.32, f32[16,152,128]{2,1,0:T(8,128)S(1)} %bitcast.181, ...), custom_call_target="tpu_custom_call" | custom-call | flops 5100273664 | bytes 7471104 | tf_op jit(solution)/shard_map/context_update/pallas_call | solution.py:315
  321.3 10.3 %couple.5 = (bf16[2,16,128,128]{3,2,1,0:T(8,128)(2,1)S(1)}, bf16[2,16,128,128]{3,2,1,0:T(8,128)(2,1)S(1)}) custom-call(s32[3,128,8]{2,1,0:T(8,128)S(1)} %copy.98.own_ref, s32[2,16,3,24,128]{4,3,2,1,0:T(8,128)S(1)} %bitcast.158), custom_call_target="tpu_custom_call" | custom-call | flops 78643200 | bytes 2097152 | tf_op jit(solution)/shard_map/couple/pallas_call | solution.py:192
  339.6 9.4 %update.3.table_ref = f32[304,1024]{1,0:T(8,128)S(1)} custom-call(s32[1]{0:T(128)} %bitcast.base_ref, s32[2,16,3,24,128]{4,3,2,1,0:T(8,128)S(1)} %bitcast.159, f32[304,1024]{1,0:T(8,128)S(1)} %copy-done.56, f32[16,152,128]{2,1,0:T(8,128)S(1)} %bitcast.176, f32[16,152,128]{2,1,0:T(8,128)S(1)} %copy-done.22, f32[16,152,128]{2,1,0:T(8,128)S(1)} %bitcast.172, ...), custom_call_target="tpu_custom_call" | custom-call | flops 5100273664 | bytes 4980736 | tf_op jit(solution)/shard_map/update/pallas_call | solution.py:315
  348.9 9.6 %collective-permute-done.51 = f32[1,1,4,152,128]{4,3,2,1,0:T(8,128)S(1)} collective-permute-done((f32[1,1,4,152,128]{4,3,2,1,0:T(8,128)S(1)}, f32[1,1,4,152,128]{4,3,2,1,0:T(8,128)S(1)}, u32[]{:S(2)}, u32[]{:S(2)}) %collective-permute-start.51) | collective-permute-done | bytes 311328 | tf_op jit(solution)/shard_map/ppermute | solution.py:23
  364.4 10.3 %hot_update.8.refs_0_ = f32[304,256]{1,0:T(8,128)S(1)} custom-call(s32[1]{0:T(128)} %bitcast.36.slice_ref, s32[2,16,3,24,128]{4,3,2,1,0:T(8,128)S(1)} %bitcast.160, f32[4,152,256]{2,1,0:T(8,128)} %bitcast.46.a0.hot_a, f32[4,152,256]{2,1,0:T(8,128)S(1)} %bitcast.221, f32[16,152,128]{2,1,0:T(8,128)S(1)} %bitcast.199, f32[16,152,128]{2,1,0:T(8,128)S(1)} %bitcast.195), custom_call_target="tpu_custom_call" | custom-call | flops 3825205248 | bytes 2490368 | tf_op jit(solution)/shard_map/hot_update/pallas_call | solution.py:489
  374.8 3.7 collective-permute-done.56
  385.5 10.3 %hot_update.9 = (f32[152,256]{1,0:T(8,128)S(1)}, f32[152,256]{1,0:T(8,128)S(1)}) custom-call(s32[1]{0:T(128)} %bitcast.36.slice_ref, s32[2,16,3,24,128]{4,3,2,1,0:T(8,128)S(1)} %bitcast.161, f32[4,152,256]{2,1,0:T(8,128)} %bitcast.46.a0.hot_a, f32[4,152,256]{2,1,0:T(8,128)S(1)} %bitcast.222, f32[16,152,128]{2,1,0:T(8,128)S(1)} %collective-permute-done.53.a.ca1.refs_1_, ...), custom_call_target="tpu_custom_call" | custom-call | flops 3825205248 | bytes 2490368 | tf_op jit(solution)/shard_map/hot_update/pallas_call | solution.py:489
  404.2 5.4 absorb.5
  414.8 3.4 collective-permute-done.69
  426.5 8.4 %collective-permute-done.72 = f32[1,1,304,128]{3,2,1,0:T(8,128)S(1)} collective-permute-done((f32[1,1,304,128]{3,2,1,0:T(8,128)S(1)}, f32[1,1,304,128]{3,2,1,0:T(8,128)S(1)}, u32[]{:S(2)}, u32[]{:S(2)}) %collective-permute-start.72) | collective-permute-done | bytes 155680 | tf_op jit(solution)/shard_map/ppermute | solution.py:23
  435.2 6.3 %own_grads.5 = f32[304,128]{1,0:T(8,128)S(1)} custom-call(s32[8]{0:T(128)S(1)} %fusion.31.slice_ref, f32[304,128]{1,0:T(8,128)S(1)} %fusion.11.c_ref, f32[304,128]{1,0:T(8,128)S(1)} %subtract_subtract_fusion.x_ref, f32[1,128]{1,0:T(1,128)S(1)} %get-tuple-element.420.denom_ref, s32[3,24,128]{2,1,0:T(8,128)S(1)} %pad_add_fusion.6.meta_ref, ...), custom_call_target="tpu_custom_call" | custom-call | flops 1912602624 | bytes 2490368 | tf_op jit(solution)/shard_map/own_grads/pallas_call | solution.py:417
  441.6 2.9 collective-permute-done.73
  446.4 7.7 %context_update.4.table_ref = f32[304,1024]{1,0:T(8,128)S(1)} custom-call(s32[1]{0:T(128)} %bitcast.base_ref, s32[2,16,3,24,128]{4,3,2,1,0:T(8,128)S(1)} %bitcast.162, f32[304,1024]{1,0:T(8,128)S(1)} %copy-done.101, f32[16,152,128]{2,1,0:T(8,128)S(1)} %bitcast.201, f32[16,152,128]{2,1,0:T(8,128)S(1)} %copy-done.53, f32[16,152,128]{2,1,0:T(8,128)S(1)} %bitcast.197, ...), custom_call_target="tpu_custom_call" | custom-call | flops 5100273664 | bytes 7471104 | tf_op jit(solution)/shard_map/context_update/pallas_call | solution.py:315
  460.3 3.9 collective-permute-done.78
  471.4 9.2 %update.4.table_ref = f32[304,1024]{1,0:T(8,128)S(1)} custom-call(s32[1]{0:T(128)} %bitcast.base_ref, s32[2,16,3,24,128]{4,3,2,1,0:T(8,128)S(1)} %bitcast.163, f32[304,1024]{1,0:T(8,128)S(1)} %copy-done.103, f32[16,152,128]{2,1,0:T(8,128)S(1)} %bitcast.193, f32[16,152,128]{2,1,0:T(8,128)S(1)} %copy-done.49, f32[16,152,128]{2,1,0:T(8,128)S(1)} %bitcast.190, ...), custom_call_target="tpu_custom_call" | custom-call | flops 5100273664 | bytes 4980736 | tf_op jit(solution)/shard_map/update/pallas_call | solution.py:315
  480.6 7.2 %collective-permute-done.81 = f32[1,1,4,152,128]{4,3,2,1,0:T(8,128)S(1)} collective-permute-done((f32[1,1,4,152,128]{4,3,2,1,0:T(8,128)S(1)}, f32[1,1,4,152,128]{4,3,2,1,0:T(8,128)S(1)}, u32[]{:S(2)}, u32[]{:S(2)}) %collective-permute-start.81) | collective-permute-done | bytes 311328 | tf_op jit(solution)/shard_map/ppermute | solution.py:23
  492.1 10.3 %hot_update.10.refs_0_ = f32[304,256]{1,0:T(8,128)S(1)} custom-call(s32[1]{0:T(128)} %bitcast.36.slice_ref, s32[2,16,3,24,128]{4,3,2,1,0:T(8,128)S(1)} %bitcast.164, f32[4,152,256]{2,1,0:T(8,128)} %bitcast.75.a0.hot_a, f32[4,152,256]{2,1,0:T(8,128)S(1)} %bitcast.225, f32[16,152,128]{2,1,0:T(8,128)S(1)} %bitcast.212, f32[16,152,128]{2,1,0:T(8,128)S(1)} %bitcast.209), custom_call_target="tpu_custom_call" | custom-call | flops 3825205248 | bytes 2490368 | tf_op jit(solution)/shard_map/hot_update/pallas_call | solution.py:489
  502.4 3.0 collective-permute-done.86
  507.0 10.5 %hot_update.11 = (f32[152,256]{1,0:T(8,128)S(1)}, f32[152,256]{1,0:T(8,128)S(1)}) custom-call(s32[1]{0:T(128)} %bitcast.36.slice_ref, s32[2,16,3,24,128]{4,3,2,1,0:T(8,128)S(1)} %bitcast.165, f32[4,152,256]{2,1,0:T(8,128)} %bitcast.75.a0.hot_a, f32[4,152,256]{2,1,0:T(8,128)S(1)} %bitcast.226, f32[16,152,128]{2,1,0:T(8,128)S(1)} %collective-permute-done.83.a.refs_1_, ...), custom_call_target="tpu_custom_call" | custom-call | flops 3825205248 | bytes 2490368 | tf_op jit(solution)/shard_map/hot_update/pallas_call | solution.py:489
  520.2 8.1 %context_update.5 = f32[1024,300]{1,0:T(8,128)S(1)} custom-call(s32[1]{0:T(128)} %bitcast.base_ref, s32[2,16,3,24,128]{4,3,2,1,0:T(8,128)S(1)} %bitcast.166, f32[304,1024]{1,0:T(8,128)S(1)} %context_update.4.table_ref, f32[16,152,128]{2,1,0:T(8,128)S(1)} %bitcast.213, f32[16,152,128]{2,1,0:T(8,128)S(1)} %collective-permute-done.83.a.refs_1_, ...), custom_call_target="tpu_custom_call" | custom-call | flops 5100273664 | bytes 7471104 | tf_op jit(solution)/shard_map/context_update/pallas_call | solution.py:315
  530.0 9.6 %update.5 = f32[1024,300]{1,0:T(8,128)S(1)} custom-call(s32[1]{0:T(128)} %bitcast.base_ref, s32[2,16,3,24,128]{4,3,2,1,0:T(8,128)S(1)} %bitcast.167, f32[304,1024]{1,0:T(8,128)S(1)} %update.4.table_ref, f32[16,152,128]{2,1,0:T(8,128)S(1)} %bitcast.218, f32[16,152,128]{2,1,0:T(8,128)S(1)} %collective-permute-done.87.refs_1_, f32[16,152,128]{2,1,0:T(8,128)S(1)} %bitcast.216, ...), custom_call_target="tpu_custom_call" | custom-call | flops 5100273664 | bytes 4980736 | tf_op jit(solution)/shard_map/update/pallas_call | solution.py:315
  542.2 2.9 copy.100
  545.1 7.8 %collect.1 = f32[2048,300]{1,0:T(8,128)} custom-call(s32[8]{0:T(128)} %copy-done.85, f32[4,152,256]{2,1,0:T(8,128)} %bitcast.287, f32[4,152,256]{2,1,0:T(8,128)} %collective-permute-done.93.a1, f32[4,152,256]{2,1,0:T(8,128)} %bitcast.285, f32[4,152,256]{2,1,0:T(8,128)} %collective-permute-done.94.b1), custom_call_target="tpu_custom_call" | custom-call | flops 1000000 | bytes 4980736 | tf_op jit(solution)/shard_map/collect/pallas_call | solution.py:561
  553.0 3.4 copy.102
  (596 shorter events, 221.8 us)
Async XLA Ops:
  51.9 16.4 %collective-permute-start.8 = (f32[2,1,4,152,128]{4,3,2,1,0:T(8,128)}, f32[2,1,4,152,128]{4,3,2,1,0:T(8,128)}, u32[]{:S(2)}, u32[]{:S(2)}) collective-permute-start(f32[2,1,4,152,128]{4,3,2,1,0:T(8,128)} %slice.273), channel_id=1, source_target_pairs={{0,8},{1,9},{2,10},{3,11},{4,12},{5,13},{6,14},{7,15},{8,0},{9,1},... | collective-permute-start | bytes 1867784 | tf_op jit(solution)/shard_map/ppermute | solution.py:23
  53.5 16.1 %collective-permute-start.7 = (f32[1,2,4,152,128]{4,3,2,1,0:T(8,128)}, f32[1,2,4,152,128]{4,3,2,1,0:T(8,128)}, u32[]{:S(2)}, u32[]{:S(2)}) collective-permute-start(f32[1,2,4,152,128]{4,3,2,1,0:T(8,128)} %bitcast.8), channel_id=1, source_target_pairs={{0,16},{1,17},{2,18},{3,19},{4,20},{5,21},{6,22},{7,23},{8,24},{9,... | collective-permute-start | bytes 1867784 | tf_op jit(solution)/shard_map/ppermute | solution.py:23
  76.2 31.6 %all-to-all-start = ((f32[32,8,300]{2,1,0:T(8,128)}), f32[32,8,300]{2,1,0:T(8,128)}, u32[]{:S(2)}, u32[]{:S(2)}) async-start(f32[32,8,300]{2,1,0:T(8,128)} %slice.213), calls=%async_computation | async-start | bytes 786432 | tf_op jit(solution)/shard_map/all_to_all | solution.py:686
  81.7 15.5 %collective-permute-start.11 = (f32[2,1,304,128]{3,2,1,0:T(8,128)S(1)}, f32[2,1,304,128]{3,2,1,0:T(8,128)S(1)}, u32[]{:S(2)}, u32[]{:S(2)}) collective-permute-start(f32[2,1,304,128]{3,2,1,0:T(8,128)S(1)} %pad_maximum_fusion.38), channel_id=1, source_target_pairs={{0,1},{1,0},{2,3},{3,2},{4,5},{5,4},{6,7},{7,6},{8,9},{9,8},{10,11... | collective-permute-start | bytes 933896 | tf_op jit(solution)/shard_map/ppermute | solution.py:23
  139.4 42.8 %collective-permute-start.27 = (f32[16,152,128]{2,1,0:T(8,128)}, f32[16,152,128]{2,1,0:T(8,128)}, u32[]{:S(2)}, u32[]{:S(2)}) collective-permute-start(f32[16,152,128]{2,1,0:T(8,128)} %get-tuple-element.238), channel_id=1, source_target_pairs={{0,4},{1,5},{2,6},{3,7},{4,0},{5,1},{6,2},{7,3},{8,12},{9,13},{10,... | collective-permute-start | bytes 3735560 | tf_op jit(solution)/shard_map/ppermute | solution.py:23
  153.8 14.9 %collective-permute-start.21 = (f32[1,1,4,152,128]{4,3,2,1,0:T(8,128)S(1)}, f32[1,1,4,152,128]{4,3,2,1,0:T(8,128)S(1)}, u32[]{:S(2)}, u32[]{:S(2)}) collective-permute-start(f32[1,1,4,152,128]{4,3,2,1,0:T(8,128)S(1)} %get-tuple-element.411), channel_id=1, source_target_pairs={{0,8},{1,9},{2,10},{3,11},{4,12},{5,13},{6,14},{7,15},{8,0},{9,1},... | collective-permute-start | bytes 933896 | tf_op jit(solution)/shard_map/ppermute | solution.py:23
  154.9 22.0 %collective-permute-start.20 = (f32[2,1,4,152,128]{4,3,2,1,0:T(8,128)S(1)}, f32[2,1,4,152,128]{4,3,2,1,0:T(8,128)S(1)}, u32[]{:S(2)}, u32[]{:S(2)}) collective-permute-start(f32[2,1,4,152,128]{4,3,2,1,0:T(8,128)S(1)} %pad_maximum_fusion.14), channel_id=1, source_target_pairs={{0,8},{1,9},{2,10},{3,11},{4,12},{5,13},{6,14},{7,15},{8,0},{9,1},... | collective-permute-start | bytes 1867784 | tf_op jit(solution)/shard_map/ppermute | solution.py:23
  156.4 20.8 %collective-permute-start.19 = (f32[1,2,4,152,128]{4,3,2,1,0:T(8,128)S(1)}, f32[1,2,4,152,128]{4,3,2,1,0:T(8,128)S(1)}, u32[]{:S(2)}, u32[]{:S(2)}) collective-permute-start(f32[1,2,4,152,128]{4,3,2,1,0:T(8,128)S(1)} %pad_maximum_fusion.13), channel_id=1, source_target_pairs={{0,16},{1,17},{2,18},{3,19},{4,20},{5,21},{6,22},{7,23},{8,24},{9,... | collective-permute-start | bytes 1867784 | tf_op jit(solution)/shard_map/ppermute | solution.py:23
  168.7 24.1 %collective-permute-start.28 = (f32[16,152,128]{2,1,0:T(8,128)S(1)}, f32[16,152,128]{2,1,0:T(8,128)S(1)}, u32[]{:S(2)}, u32[]{:S(2)}) collective-permute-start(f32[16,152,128]{2,1,0:T(8,128)S(1)} %copy-done.89), channel_id=1, source_target_pairs={{0,4},{1,5},{2,6},{3,7},{4,0},{5,1},{6,2},{7,3},{8,12},{9,13},{10,... | collective-permute-start | bytes 3735560 | tf_op jit(solution)/shard_map/ppermute | solution.py:23
  180.0 18.1 %collective-permute-start.24 = (f32[16,152,128]{2,1,0:T(8,128)S(1)}, f32[16,152,128]{2,1,0:T(8,128)S(1)}, u32[]{:S(2)}, u32[]{:S(2)}) collective-permute-start(f32[16,152,128]{2,1,0:T(8,128)S(1)} %bitcast.177), channel_id=1, source_target_pairs={{0,4},{1,5},{2,6},{3,7},{4,0},{5,1},{6,2},{7,3},{8,12},{9,13},{10,... | collective-permute-start | bytes 3735560 | tf_op jit(solution)/shard_map/ppermute | solution.py:23
  180.1 18.0 %collective-permute-start.23 = (f32[16,152,128]{2,1,0:T(8,128)S(1)}, f32[16,152,128]{2,1,0:T(8,128)S(1)}, u32[]{:S(2)}, u32[]{:S(2)}) collective-permute-start(f32[16,152,128]{2,1,0:T(8,128)S(1)} %bitcast.182), channel_id=1, source_target_pairs={{0,4},{1,5},{2,6},{3,7},{4,0},{5,1},{6,2},{7,3},{8,12},{9,13},{10,... | collective-permute-start | bytes 3735560 | tf_op jit(solution)/shard_map/ppermute | solution.py:23
  180.6 16.1 %collective-permute-start.26 = (f32[2,1,4,152,128]{4,3,2,1,0:T(8,128)S(1)}, f32[2,1,4,152,128]{4,3,2,1,0:T(8,128)S(1)}, u32[]{:S(2)}, u32[]{:S(2)}) collective-permute-start(f32[2,1,4,152,128]{4,3,2,1,0:T(8,128)S(1)} %pad_maximum_fusion.17), channel_id=1, source_target_pairs={{0,8},{1,9},{2,10},{3,11},{4,12},{5,13},{6,14},{7,15},{8,0},{9,1},... | collective-permute-start | bytes 1867784 | tf_op jit(solution)/shard_map/ppermute | solution.py:23
  182.3 15.8 %collective-permute-start.25 = (f32[1,2,4,152,128]{4,3,2,1,0:T(8,128)S(1)}, f32[1,2,4,152,128]{4,3,2,1,0:T(8,128)S(1)}, u32[]{:S(2)}, u32[]{:S(2)}) collective-permute-start(f32[1,2,4,152,128]{4,3,2,1,0:T(8,128)S(1)} %pad_maximum_fusion.16), channel_id=1, source_target_pairs={{0,16},{1,17},{2,18},{3,19},{4,20},{5,21},{6,22},{7,23},{8,24},{9,... | collective-permute-start | bytes 1867784 | tf_op jit(solution)/shard_map/ppermute | solution.py:23
  198.3 20.0 %collective-permute-start.30 = (f32[16,152,128]{2,1,0:T(8,128)S(1)}, f32[16,152,128]{2,1,0:T(8,128)S(1)}, u32[]{:S(2)}, u32[]{:S(2)}) collective-permute-start(f32[16,152,128]{2,1,0:T(8,128)S(1)} %bitcast.168), channel_id=1, source_target_pairs={{0,4},{1,5},{2,6},{3,7},{4,0},{5,1},{6,2},{7,3},{8,12},{9,13},{10,... | collective-permute-start | bytes 3735560 | tf_op jit(solution)/shard_map/ppermute | solution.py:23
  198.4 19.9 %collective-permute-start.29 = (f32[16,152,128]{2,1,0:T(8,128)S(1)}, f32[16,152,128]{2,1,0:T(8,128)S(1)}, u32[]{:S(2)}, u32[]{:S(2)}) collective-permute-start(f32[16,152,128]{2,1,0:T(8,128)S(1)} %bitcast.173), channel_id=1, source_target_pairs={{0,4},{1,5},{2,6},{3,7},{4,0},{5,1},{6,2},{7,3},{8,12},{9,13},{10,... | collective-permute-start | bytes 3735560 | tf_op jit(solution)/shard_map/ppermute | solution.py:23
  200.6 14.9 %collective-permute-start.32 = (f32[2,1,4,152,128]{4,3,2,1,0:T(8,128)S(1)}, f32[2,1,4,152,128]{4,3,2,1,0:T(8,128)S(1)}, u32[]{:S(2)}, u32[]{:S(2)}) collective-permute-start(f32[2,1,4,152,128]{4,3,2,1,0:T(8,128)S(1)} %slice.289), channel_id=1, source_target_pairs={{0,8},{1,9},{2,10},{3,11},{4,12},{5,13},{6,14},{7,15},{8,0},{9,1},... | collective-permute-start | bytes 1867784 | tf_op jit(solution)/shard_map/ppermute | solution.py:23
  203.4 14.9 %collective-permute-start.31 = (f32[1,2,4,152,128]{4,3,2,1,0:T(8,128)S(1)}, f32[1,2,4,152,128]{4,3,2,1,0:T(8,128)S(1)}, u32[]{:S(2)}, u32[]{:S(2)}) collective-permute-start(f32[1,2,4,152,128]{4,3,2,1,0:T(8,128)S(1)} %bitcast.299), channel_id=1, source_target_pairs={{0,16},{1,17},{2,18},{3,19},{4,20},{5,21},{6,22},{7,23},{8,24},{9,... | collective-permute-start | bytes 1867784 | tf_op jit(solution)/shard_map/ppermute | solution.py:23
  221.8 27.1 %collective-permute-start.36 = (f32[1,1,4,152,128]{4,3,2,1,0:T(8,128)}, f32[1,1,4,152,128]{4,3,2,1,0:T(8,128)}, u32[]{:S(2)}, u32[]{:S(2)}) collective-permute-start(f32[1,1,4,152,128]{4,3,2,1,0:T(8,128)} %slice.293), channel_id=1, source_target_pairs={{0,16},{1,17},{2,18},{3,19},{4,20},{5,21},{6,22},{7,23},{8,24},{9,... | collective-permute-start | bytes 933896 | tf_op jit(solution)/shard_map/ppermute | solution.py:23
  222.3 26.6 %collective-permute-start.35 = (f32[1,1,4,152,128]{4,3,2,1,0:T(8,128)}, f32[1,1,4,152,128]{4,3,2,1,0:T(8,128)}, u32[]{:S(2)}, u32[]{:S(2)}) collective-permute-start(f32[1,1,4,152,128]{4,3,2,1,0:T(8,128)} %slice.291), channel_id=1, source_target_pairs={{0,8},{1,9},{2,10},{3,11},{4,12},{5,13},{6,14},{7,15},{8,0},{9,1},... | collective-permute-start | bytes 933896 | tf_op jit(solution)/shard_map/ppermute | solution.py:23
  224.0 33.3 %all-to-all-start.1 = ((f32[32,16,300]{2,1,0:T(8,128)}), f32[32,16,300]{2,1,0:T(8,128)}, u32[]{:S(2)}, u32[]{:S(2)}) async-start(f32[32,16,300]{2,1,0:T(8,128)} %slice.234), calls=%async_computation.1 | async-start | bytes 1572864 | tf_op jit(solution)/shard_map/all_to_all | solution.py:686
  229.0 19.9 %collective-permute-start.33 = (f32[1,1,1,152,256]{4,3,2,1,0:T(8,128)}, f32[1,1,1,152,256]{4,3,2,1,0:T(8,128)S(1)}, u32[]{:S(2)}, u32[]{:S(2)}) collective-permute-start(f32[1,1,1,152,256]{4,3,2,1,0:T(8,128)} %bitcast.227), channel_id=1, source_target_pairs={{0,8},{1,9},{2,10},{3,11},{4,12},{5,13},{6,14},{7,15},{8,0},{9,1},... | collective-permute-start | bytes 466952 | tf_op jit(solution)/shard_map/ppermute | solution.py:23
  230.9 18.0 %collective-permute-start.34 = (f32[1,1,1,152,256]{4,3,2,1,0:T(8,128)}, f32[1,1,1,152,256]{4,3,2,1,0:T(8,128)S(1)}, u32[]{:S(2)}, u32[]{:S(2)}) collective-permute-start(f32[1,1,1,152,256]{4,3,2,1,0:T(8,128)} %bitcast.230), channel_id=1, source_target_pairs={{0,16},{1,17},{2,18},{3,19},{4,20},{5,21},{6,22},{7,23},{8,24},{9,... | collective-permute-start | bytes 466952 | tf_op jit(solution)/shard_map/ppermute | solution.py:23
  252.0 23.6 %collective-permute-start.39 = (f32[2,1,304,128]{3,2,1,0:T(8,128)}, f32[2,1,304,128]{3,2,1,0:T(8,128)}, u32[]{:S(2)}, u32[]{:S(2)}) collective-permute-start(f32[2,1,304,128]{3,2,1,0:T(8,128)} %pad_maximum_fusion.37), channel_id=1, source_target_pairs={{0,1},{1,0},{2,3},{3,2},{4,5},{5,4},{6,7},{7,6},{8,9},{9,8},{10,11... | collective-permute-start | bytes 933896 | tf_op jit(solution)/shard_map/ppermute | solution.py:23
  254.3 21.4 %collective-permute-start.38 = (f32[2,1,1,152,256]{4,3,2,1,0:T(8,128)}, f32[2,1,1,152,256]{4,3,2,1,0:T(8,128)}, u32[]{:S(2)}, u32[]{:S(2)}) collective-permute-start(f32[2,1,1,152,256]{4,3,2,1,0:T(8,128)} %pad_maximum_fusion.42), channel_id=1, source_target_pairs={{0,8},{1,9},{2,10},{3,11},{4,12},{5,13},{6,14},{7,15},{8,0},{9,1},... | collective-permute-start | bytes 933896 | tf_op jit(solution)/shard_map/ppermute | solution.py:23
  255.6 20.1 %collective-permute-start.37 = (f32[1,2,1,152,256]{4,3,2,1,0:T(8,128)}, f32[1,2,1,152,256]{4,3,2,1,0:T(8,128)}, u32[]{:S(2)}, u32[]{:S(2)}) collective-permute-start(f32[1,2,1,152,256]{4,3,2,1,0:T(8,128)} %pad_maximum_fusion.41), channel_id=1, source_target_pairs={{0,16},{1,17},{2,18},{3,19},{4,20},{5,21},{6,22},{7,23},{8,24},{9,... | collective-permute-start | bytes 933896 | tf_op jit(solution)/shard_map/ppermute | solution.py:23
  277.0 16.2 %collective-permute-start.41 = (f32[4,152,256]{2,1,0:T(8,128)S(1)}, f32[4,152,256]{2,1,0:T(8,128)}, u32[]{:S(2)}, u32[]{:S(2)}) collective-permute-start(f32[4,152,256]{2,1,0:T(8,128)S(1)} %bitcast.219), channel_id=1, source_target_pairs={{0,4},{1,5},{2,6},{3,7},{4,0},{5,1},{6,2},{7,3},{8,12},{9,13},{10,... | collective-permute-start | bytes 1867784 | tf_op jit(solution)/shard_map/ppermute | solution.py:23
  321.2 42.6 %collective-permute-start.57 = (f32[16,152,128]{2,1,0:T(8,128)}, f32[16,152,128]{2,1,0:T(8,128)}, u32[]{:S(2)}, u32[]{:S(2)}) collective-permute-start(f32[16,152,128]{2,1,0:T(8,128)} %get-tuple-element.299), channel_id=1, source_target_pairs={{0,4},{1,5},{2,6},{3,7},{4,0},{5,1},{6,2},{7,3},{8,12},{9,13},{10,... | collective-permute-start | bytes 3735560 | tf_op jit(solution)/shard_map/ppermute | solution.py:23
  335.3 23.5 %collective-permute-start.50 = (f32[2,1,4,152,128]{4,3,2,1,0:T(8,128)S(1)}, f32[2,1,4,152,128]{4,3,2,1,0:T(8,128)S(1)}, u32[]{:S(2)}, u32[]{:S(2)}) collective-permute-start(f32[2,1,4,152,128]{4,3,2,1,0:T(8,128)S(1)} %pad_maximum_fusion.22), channel_id=1, source_target_pairs={{0,8},{1,9},{2,10},{3,11},{4,12},{5,13},{6,14},{7,15},{8,0},{9,1},... | collective-permute-start | bytes 1867784 | tf_op jit(solution)/shard_map/ppermute | solution.py:23
  335.9 22.8 %collective-permute-start.49 = (f32[1,2,4,152,128]{4,3,2,1,0:T(8,128)S(1)}, f32[1,2,4,152,128]{4,3,2,1,0:T(8,128)S(1)}, u32[]{:S(2)}, u32[]{:S(2)}) collective-permute-start(f32[1,2,4,152,128]{4,3,2,1,0:T(8,128)S(1)} %pad_maximum_fusion.21), channel_id=1, source_target_pairs={{0,16},{1,17},{2,18},{3,19},{4,20},{5,21},{6,22},{7,23},{8,24},{9,... | collective-permute-start | bytes 1867784 | tf_op jit(solution)/shard_map/ppermute | solution.py:23
  336.3 22.2 %collective-permute-start.51 = (f32[1,1,4,152,128]{4,3,2,1,0:T(8,128)S(1)}, f32[1,1,4,152,128]{4,3,2,1,0:T(8,128)S(1)}, u32[]{:S(2)}, u32[]{:S(2)}) collective-permute-start(f32[1,1,4,152,128]{4,3,2,1,0:T(8,128)S(1)} %get-tuple-element.407), channel_id=1, source_target_pairs={{0,8},{1,9},{2,10},{3,11},{4,12},{5,13},{6,14},{7,15},{8,0},{9,1},... | collective-permute-start | bytes 933896 | tf_op jit(solution)/shard_map/ppermute | solution.py:23
  338.1 20.7 %collective-permute-start.52 = (f32[1,1,4,152,128]{4,3,2,1,0:T(8,128)S(1)}, f32[1,1,4,152,128]{4,3,2,1,0:T(8,128)S(1)}, u32[]{:S(2)}, u32[]{:S(2)}) collective-permute-start(f32[1,1,4,152,128]{4,3,2,1,0:T(8,128)S(1)} %get-tuple-element.406), channel_id=1, source_target_pairs={{0,16},{1,17},{2,18},{3,19},{4,20},{5,21},{6,22},{7,23},{8,24},{9,... | collective-permute-start | bytes 933896 | tf_op jit(solution)/shard_map/ppermute | solution.py:23
  358.5 16.3 %collective-permute-start.58 = (f32[16,152,128]{2,1,0:T(8,128)S(1)}, f32[16,152,128]{2,1,0:T(8,128)S(1)}, u32[]{:S(2)}, u32[]{:S(2)}) collective-permute-start(f32[16,152,128]{2,1,0:T(8,128)S(1)} %copy-done.87), channel_id=1, source_target_pairs={{0,4},{1,5},{2,6},{3,7},{4,0},{5,1},{6,2},{7,3},{8,12},{9,13},{10,... | collective-permute-start | bytes 3735560 | tf_op jit(solution)/shard_map/ppermute | solution.py:23
  361.6 18.0 %collective-permute-start.54 = (f32[16,152,128]{2,1,0:T(8,128)S(1)}, f32[16,152,128]{2,1,0:T(8,128)S(1)}, u32[]{:S(2)}, u32[]{:S(2)}) collective-permute-start(f32[16,152,128]{2,1,0:T(8,128)S(1)} %bitcast.194), channel_id=1, source_target_pairs={{0,4},{1,5},{2,6},{3,7},{4,0},{5,1},{6,2},{7,3},{8,12},{9,13},{10,... | collective-permute-start | bytes 3735560 | tf_op jit(solution)/shard_map/ppermute | solution.py:23
  361.9 17.7 %collective-permute-start.53 = (f32[16,152,128]{2,1,0:T(8,128)S(1)}, f32[16,152,128]{2,1,0:T(8,128)S(1)}, u32[]{:S(2)}, u32[]{:S(2)}) collective-permute-start(f32[16,152,128]{2,1,0:T(8,128)S(1)} %bitcast.198), channel_id=1, source_target_pairs={{0,4},{1,5},{2,6},{3,7},{4,0},{5,1},{6,2},{7,3},{8,12},{9,13},{10,... | collective-permute-start | bytes 3735560 | tf_op jit(solution)/shard_map/ppermute | solution.py:23
  362.2 16.2 %collective-permute-start.56 = (f32[2,1,4,152,128]{4,3,2,1,0:T(8,128)S(1)}, f32[2,1,4,152,128]{4,3,2,1,0:T(8,128)S(1)}, u32[]{:S(2)}, u32[]{:S(2)}) collective-permute-start(f32[2,1,4,152,128]{4,3,2,1,0:T(8,128)S(1)} %pad_maximum_fusion.25), channel_id=1, source_target_pairs={{0,8},{1,9},{2,10},{3,11},{4,12},{5,13},{6,14},{7,15},{8,0},{9,1},... | collective-permute-start | bytes 1867784 | tf_op jit(solution)/shard_map/ppermute | solution.py:23
  363.8 15.8 %collective-permute-start.55 = (f32[1,2,4,152,128]{4,3,2,1,0:T(8,128)S(1)}, f32[1,2,4,152,128]{4,3,2,1,0:T(8,128)S(1)}, u32[]{:S(2)}, u32[]{:S(2)}) collective-permute-start(f32[1,2,4,152,128]{4,3,2,1,0:T(8,128)S(1)} %pad_maximum_fusion.24), channel_id=1, source_target_pairs={{0,16},{1,17},{2,18},{3,19},{4,20},{5,21},{6,22},{7,23},{8,24},{9,... | collective-permute-start | bytes 1867784 | tf_op jit(solution)/shard_map/ppermute | solution.py:23
  379.8 20.0 %collective-permute-start.60 = (f32[16,152,128]{2,1,0:T(8,128)S(1)}, f32[16,152,128]{2,1,0:T(8,128)S(1)}, u32[]{:S(2)}, u32[]{:S(2)}) collective-permute-start(f32[16,152,128]{2,1,0:T(8,128)S(1)} %bitcast.187), channel_id=1, source_target_pairs={{0,4},{1,5},{2,6},{3,7},{4,0},{5,1},{6,2},{7,3},{8,12},{9,13},{10,... | collective-permute-start | bytes 3735560 | tf_op jit(solution)/shard_map/ppermute | solution.py:23
  379.9 19.9 %collective-permute-start.59 = (f32[16,152,128]{2,1,0:T(8,128)S(1)}, f32[16,152,128]{2,1,0:T(8,128)S(1)}, u32[]{:S(2)}, u32[]{:S(2)}) collective-permute-start(f32[16,152,128]{2,1,0:T(8,128)S(1)} %bitcast.191), channel_id=1, source_target_pairs={{0,4},{1,5},{2,6},{3,7},{4,0},{5,1},{6,2},{7,3},{8,12},{9,13},{10,... | collective-permute-start | bytes 3735560 | tf_op jit(solution)/shard_map/ppermute | solution.py:23
  382.1 14.9 %collective-permute-start.62 = (f32[2,1,4,152,128]{4,3,2,1,0:T(8,128)S(1)}, f32[2,1,4,152,128]{4,3,2,1,0:T(8,128)S(1)}, u32[]{:S(2)}, u32[]{:S(2)}) collective-permute-start(f32[2,1,4,152,128]{4,3,2,1,0:T(8,128)S(1)} %slice.306), channel_id=1, source_target_pairs={{0,8},{1,9},{2,10},{3,11},{4,12},{5,13},{6,14},{7,15},{8,0},{9,1},... | collective-permute-start | bytes 1867784 | tf_op jit(solution)/shard_map/ppermute | solution.py:23
  384.9 14.9 %collective-permute-start.61 = (f32[1,2,4,152,128]{4,3,2,1,0:T(8,128)S(1)}, f32[1,2,4,152,128]{4,3,2,1,0:T(8,128)S(1)}, u32[]{:S(2)}, u32[]{:S(2)}) collective-permute-start(f32[1,2,4,152,128]{4,3,2,1,0:T(8,128)S(1)} %bitcast.300), channel_id=1, source_target_pairs={{0,16},{1,17},{2,18},{3,19},{4,20},{5,21},{6,22},{7,23},{8,24},{9,... | collective-permute-start | bytes 1867784 | tf_op jit(solution)/shard_map/ppermute | solution.py:23
  467.2 21.3 %collective-permute-start.80 = (f32[2,1,4,152,128]{4,3,2,1,0:T(8,128)S(1)}, f32[2,1,4,152,128]{4,3,2,1,0:T(8,128)S(1)}, u32[]{:S(2)}, u32[]{:S(2)}) collective-permute-start(f32[2,1,4,152,128]{4,3,2,1,0:T(8,128)S(1)} %pad_maximum_fusion.31), channel_id=1, source_target_pairs={{0,8},{1,9},{2,10},{3,11},{4,12},{5,13},{6,14},{7,15},{8,0},{9,1},... | collective-permute-start | bytes 1867784 | tf_op jit(solution)/shard_map/ppermute | solution.py:23
  468.0 20.4 %collective-permute-start.79 = (f32[1,2,4,152,128]{4,3,2,1,0:T(8,128)S(1)}, f32[1,2,4,152,128]{4,3,2,1,0:T(8,128)S(1)}, u32[]{:S(2)}, u32[]{:S(2)}) collective-permute-start(f32[1,2,4,152,128]{4,3,2,1,0:T(8,128)S(1)} %pad_maximum_fusion.30), channel_id=1, source_target_pairs={{0,16},{1,17},{2,18},{3,19},{4,20},{5,21},{6,22},{7,23},{8,24},{9,... | collective-permute-start | bytes 1867784 | tf_op jit(solution)/shard_map/ppermute | solution.py:23
  469.8 18.0 %collective-permute-start.81 = (f32[1,1,4,152,128]{4,3,2,1,0:T(8,128)S(1)}, f32[1,1,4,152,128]{4,3,2,1,0:T(8,128)S(1)}, u32[]{:S(2)}, u32[]{:S(2)}) collective-permute-start(f32[1,1,4,152,128]{4,3,2,1,0:T(8,128)S(1)} %get-tuple-element.403), channel_id=1, source_target_pairs={{0,8},{1,9},{2,10},{3,11},{4,12},{5,13},{6,14},{7,15},{8,0},{9,1},... | collective-permute-start | bytes 933896 | tf_op jit(solution)/shard_map/ppermute | solution.py:23
  470.9 17.6 %collective-permute-start.82 = (f32[1,1,4,152,128]{4,3,2,1,0:T(8,128)S(1)}, f32[1,1,4,152,128]{4,3,2,1,0:T(8,128)S(1)}, u32[]{:S(2)}, u32[]{:S(2)}) collective-permute-start(f32[1,1,4,152,128]{4,3,2,1,0:T(8,128)S(1)} %get-tuple-element.402), channel_id=1, source_target_pairs={{0,16},{1,17},{2,18},{3,19},{4,20},{5,21},{6,22},{7,23},{8,24},{9,... | collective-permute-start | bytes 933896 | tf_op jit(solution)/shard_map/ppermute | solution.py:23
  488.7 17.6 %collective-permute-start.84 = (f32[16,152,128]{2,1,0:T(8,128)S(1)}, f32[16,152,128]{2,1,0:T(8,128)S(1)}, u32[]{:S(2)}, u32[]{:S(2)}) collective-permute-start(f32[16,152,128]{2,1,0:T(8,128)S(1)} %bitcast.208), channel_id=1, source_target_pairs={{0,4},{1,5},{2,6},{3,7},{4,0},{5,1},{6,2},{7,3},{8,12},{9,13},{10,... | collective-permute-start | bytes 3735560 | tf_op jit(solution)/shard_map/ppermute | solution.py:23
  488.7 17.5 %collective-permute-start.83 = (f32[16,152,128]{2,1,0:T(8,128)S(1)}, f32[16,152,128]{2,1,0:T(8,128)S(1)}, u32[]{:S(2)}, u32[]{:S(2)}) collective-permute-start(f32[16,152,128]{2,1,0:T(8,128)S(1)} %bitcast.211), channel_id=1, source_target_pairs={{0,4},{1,5},{2,6},{3,7},{4,0},{5,1},{6,2},{7,3},{8,12},{9,13},{10,... | collective-permute-start | bytes 3735560 | tf_op jit(solution)/shard_map/ppermute | solution.py:23
  489.3 16.1 %collective-permute-start.86 = (f32[2,1,4,152,128]{4,3,2,1,0:T(8,128)S(1)}, f32[2,1,4,152,128]{4,3,2,1,0:T(8,128)S(1)}, u32[]{:S(2)}, u32[]{:S(2)}) collective-permute-start(f32[2,1,4,152,128]{4,3,2,1,0:T(8,128)S(1)} %pad_maximum_fusion.33), channel_id=1, source_target_pairs={{0,8},{1,9},{2,10},{3,11},{4,12},{5,13},{6,14},{7,15},{8,0},{9,1},... | collective-permute-start | bytes 1867784 | tf_op jit(solution)/shard_map/ppermute | solution.py:23
  490.5 15.7 %collective-permute-start.85 = (f32[1,2,4,152,128]{4,3,2,1,0:T(8,128)S(1)}, f32[1,2,4,152,128]{4,3,2,1,0:T(8,128)S(1)}, u32[]{:S(2)}, u32[]{:S(2)}) collective-permute-start(f32[1,2,4,152,128]{4,3,2,1,0:T(8,128)S(1)} %pad_maximum_fusion.32), channel_id=1, source_target_pairs={{0,16},{1,17},{2,18},{3,19},{4,20},{5,21},{6,22},{7,23},{8,24},{9,... | collective-permute-start | bytes 1867784 | tf_op jit(solution)/shard_map/ppermute | solution.py:23
  (182 other events, 1627.9 us)

commit v6 on v4

--- a/solution.py
+++ b/solution.py
@@ -330,11 +330,13 @@
     )(base, meta, table_t, *arrays)
 
 
-def absorb_kernel(width, ga0, ga1, gb0, gb1, ca0, ca1, cb0, cb1, in_ref, ctx_ref, c_out, x_out):
+def absorb_kernel(width, ga0, ga1, gb0, gb1, ca0, ca1, cb0, cb1, *refs):
+    pairs, outs = refs[:len(refs) // 2], refs[len(refs) // 2:]
+
     @pl.when(pl.program_id(0) == 0)
     def _():
-        c_out[...] = jnp.zeros_like(c_out)
-        x_out[...] = jnp.zeros_like(x_out)
+        for out in outs:
+            out[...] = jnp.zeros_like(out)
 
     group = ga0.shape[0]
     ga, gb = tokens_of(ga0, ga1), tokens_of(gb0, gb1)
@@ -343,29 +345,32 @@
     grad = jnp.concatenate([ga, gb], axis=0)
     centre = jnp.concatenate([tokens_of(ca0, ca1), tokens_of(cb0, cb1)], axis=0) * pos
     feats = grad.shape[0]
-    for value, ref, out in ((grad, in_ref, c_out), (centre, ctx_ref, x_out)):
-        pairs = jnp.concatenate([ref[c, p] for p in range(group) for c in range(2)], axis=1)
+    for k, value in enumerate((grad, centre)):
         parts = jnp.concatenate(split3(value * learn_rate), axis=0)
-        total = lax.dot_general(parts, pairs, NT, preferred_element_type=f32)
-        out[...] += total[:feats] + total[feats:2 * feats] + total[2 * feats:]
-
-
-def absorb(width, g, c, in_pairs, ctx_pairs):
+        for ref, out in zip(pairs[k::2], outs[k::2]):
+            both = jnp.concatenate([ref[c, p] for p in range(group) for c in range(2)], axis=1)
+            total = lax.dot_general(parts, both, NT, preferred_element_type=f32)
+            out[...] += total[:feats] + total[feats:2 * feats] + total[2 * feats:]
+
+
+def absorb(width, g, c, pairs):
     half, feats_half, n = g[0].shape
     piece = pl.BlockSpec((GROUP, feats_half, n), lambda p: (p, 0, 0))
     pair = pl.BlockSpec((2, GROUP, n, n), lambda p: (0, p, 0, 0))
     shape = jax.ShapeDtypeStruct((2 * feats_half, n), f32)
     spec = pl.BlockSpec((2 * feats_half, n), lambda p: (0, 0))
-    return pl.pallas_call(
+    number = 2 * len(pairs)
+    outs = pl.pallas_call(
         functools.partial(absorb_kernel, width),
-        out_shape=(shape, shape),
+        out_shape=(shape,) * number,
         grid=(half // GROUP,),
-        in_specs=[piece] * 8 + [pair] * 2,
-        out_specs=(spec, spec),
+        in_specs=[piece] * 8 + [pair] * number,
+        out_specs=(spec,) * number,
         compiler_params=params("arbitrary"),
-        cost_estimate=cost(2 * 2 * 3 * half * 256 * feats_half * 2 * n, half * 256 * feats_half * 16),
+        cost_estimate=cost(2 * 3 * number * half * 256 * feats_half * 2 * n, half * 256 * feats_half * 16),
         name="absorb",
-    )(*g, *c, in_pairs, ctx_pairs)
+    )(*g, *c, *[array for both in pairs for array in both])
+    return [(outs[k], outs[k + 1]) for k in range(0, number, 2)]
 
 
 def dot6(left, right, dims):
@@ -695,10 +700,11 @@
 
         return fill
 
-    def soak(later, e):
+    def soak(e):
         def fill(gate):
             g, c = held[e]
-            return absorb(width, [gate(g[0])] + g[1:], c, *kept[("pair", later, e)])
+            pairs = [kept[("pair", later, e)] for later in range(e + 1, steps)]
+            return absorb(width, [gate(g[0])] + g[1:], c, pairs)
 
         return fill
 
@@ -720,7 +726,9 @@
             if not last:
                 fills.append((("pair", s + 1, s), pair(s + 1, s)))
             for later in range(s + 2, steps):
-                fills.append((("sums", later), sums(later)) if later == s + 2 else (None, None))
+                fills.append((("pair", later, s), pair(later, s)))
+            if s + 2 < steps:
+                fills.append((("sums", s + 2), sums(s + 2)))
             if s > 0:
                 fills.append((("table", 0), grow(s - 1, 0)))
         if len(fills) == 2:
@@ -729,9 +737,6 @@
         while c_lane.left:
             if c_lane.left == 1:
                 kept.update((name, fill(lambda x: x)) for name, fill in fills if name is not None)
-                for e in range(s):
-                    if not small and not last:
-                        kept[("pair", s + 1, e)] = couple(after(own, c_lane.sent[0]), meta_all, s + 1, e)
                 if not small and not last:
                     r_lane = Lane(tree.reduce(*kept.pop(("sums", s + 1))), span)
                 half_sum = stage(
@@ -756,12 +761,11 @@
             stage([g_lane, r_lane])
         held.append((g_lane.result, c))
         h_lane = Lane(tree.gather_gx(new_a[None], new_b[None]), short)
-        due = [(later, s) for later in range(s + 1, steps)] if small else [(s + 1, e) for e in range(s, -1, -1)]
-        due = [] if last else due
+        due = [(later, s) for later in range(s + 1, steps)]
         if small:
             for later, e in due:
                 kept[("pair", later, e)] = couple(own, meta_all, later, e)
-        fills = [(("soak", later, e), soak(later, e)) for later, e in due]
+        fills = [(("soak", s), soak(s))] if due else []
         if last or small:
             fills += [(("table", 1), grow(s, 1)), (("table", 0), grow(s, 0))]
         run([h_lane, r_lane], fills, kept, h_lane)
@@ -769,8 +773,8 @@
             kept[name] = fill(lambda x: x)
         for which in (0, 1):
             tables[which] = kept.pop(("table", which), tables[which])
-        for later, e in due:
-            added[later].append(kept.pop(("soak", later, e)))
+        for (later, _), both in zip(due, kept.pop(("soak", s), [])):
+            added[later].append(both)
         hot = h_lane.result
         if not last:
             if small:

time: 549 us -> 541 us (0.985)
  local copies, waits for them, and re-layouts: 59.5 us -> 50.1 us
    unnamed x235 -> x221, local copies, waits for them, and re-layouts: 39.3 us -> 31.9 us
    pallas_call x3 -> x2, Pallas kernels: 15.1 us -> 14.9 us  [absorb(): pl.pallas_call(functools.partial(absorb_kernel, width), out_shape=(shape,...]
  transfers between devices with their start and end apart: 96 -> 96, of which waited for: 45 -> 43; matrix products, arithmetic and copies ran while one was open for 8% -> 8% of each run, Pallas kernels for 36% -> 37%
where the time goes in v6:
time: 541 us; the launch traced here: 533 us
  Pallas kernels  212 us (39%)
  waiting for transfers between devices  145 us (27%)
  starting transfers between devices  92.8 us (17%)
  local copies, waits for them, and re-layouts  50.1 us (9%)
  other arithmetic  29.4 us (5%)
    ppermute x95, waiting for transfers between devices, swap(): return lax.ppermute(x, axes, [(d, d ^ bit) for d in range(devices)])  145 us
    ppermute x95, starting transfers between devices, swap(): return lax.ppermute(x, axes, [(d, d ^ bit) for d in range(devices)])  87.5 us
    pallas_call x6, Pallas kernels, hot_update(): pl.pallas_call(functools.partial(hot_kernel, scale), out_shape=sum_shape...  60.9 us
    pallas_call x6, Pallas kernels, update(): pl.pallas_call(functools.partial(update_kernel, rows, width, bool(pos), f...  52.1 us
    unnamed x221, local copies, waits for them, and re-layouts  31.9 us
    pallas_call x3, Pallas kernels, couple(): pl.pallas_call(couple_kernel, out_shape=(shape, shape), grid=(half,), in_...  31 us
    pallas_call x3, Pallas kernels, base_sums(): pl.pallas_call(functools.partial(base_kernel, rows), out_shape=(shape,) *...  28.7 us
    pallas_call x3, Pallas kernels, own_grads(): pl.pallas_call(functools.partial(own_kernel, width, scale), out_shape=jax...  17.8 us
  transfers between devices with their start and end apart: 96, of which 43 were waited for; matrix products, arithmetic and copies ran while one was open for 8% of the time, Pallas kernels for 37%

profile of v6, /device:TPU:0, one launch (start us, length us, event | category | flops | bytes accessed | tf_op | source)
XLA Modules:
  0.0 532.8 jit_solution(2298353294538236881)
XLA Ops:
  3.2 4.1 collective-permute-start
  11.2 2.8 collective-permute-done.1
  15.8 3.4 collective-permute-done.2
  21.1 5.0 collective-permute-done.3
  28.3 9.1 %base_sums.3 = (f32[16,152,128]{2,1,0:T(8,128)S(1)}, f32[16,152,128]{2,1,0:T(8,128)S(1)}, f32[16,152,128]{2,1,0:T(8,128)S(1)}, f32[16,152,128]{2,1,0:T(8,128)S(1)}) custom-call(s32[1]{0:T(128)} %bitcast.base_ref, s32[2,16,3,24,128]{4,3,2,1,0:T(8,128)S(1)} %bitcast.139, f32[304,1024]{1,0:T(8,128)S(1)} %pad.17.table_ref), custom_call_target="tpu_custom_call" | custom-call | flops 7650410496 | bytes 6225920 | tf_op jit(solution)/shard_map/base_sums/pallas_call | solution.py:244
  38.3 9.8 %base_sums.4 = (f32[16,152,128]{2,1,0:T(8,128)S(1)}, f32[16,152,128]{2,1,0:T(8,128)}, f32[16,152,128]{2,1,0:T(8,128)S(1)}, f32[16,152,128]{2,1,0:T(8,128)S(1)}) custom-call(s32[1]{0:T(128)} %bitcast.base_ref, s32[2,16,3,24,128]{4,3,2,1,0:T(8,128)S(1)} %bitcast.140, f32[304,1024]{1,0:T(8,128)S(1)} %pad.17.table_ref), custom_call_target="tpu_custom_call" | custom-call | flops 7650410496 | bytes 6225920 | tf_op jit(solution)/shard_map/base_sums/pallas_call | solution.py:244
  60.1 3.0 gather_fusion.1
  63.1 5.5 %collective-permute-done.8 = f32[2,1,4,152,128]{4,3,2,1,0:T(8,128)} collective-permute-done((f32[2,1,4,152,128]{4,3,2,1,0:T(8,128)}, f32[2,1,4,152,128]{4,3,2,1,0:T(8,128)}, u32[]{:S(2)}, u32[]{:S(2)}) %collective-permute-start.8) | collective-permute-done | bytes 622624 | tf_op jit(solution)/shard_map/ppermute | solution.py:23
  74.8 5.3 all-to-all-start
  83.5 24.7 %collective-permute-done.11 = f32[2,1,304,128]{3,2,1,0:T(8,128)S(1)} collective-permute-done((f32[2,1,304,128]{3,2,1,0:T(8,128)S(1)}, f32[2,1,304,128]{3,2,1,0:T(8,128)S(1)}, u32[]{:S(2)}, u32[]{:S(2)}) %collective-permute-start.11) | collective-permute-done | bytes 311328 | tf_op jit(solution)/shard_map/ppermute | solution.py:23
  122.0 3.2 gather_fusion.2
  128.8 4.9 own_grads.3
  134.5 3.2 collective-permute-start.14
  137.8 10.3 %couple.3 = (bf16[2,16,128,128]{3,2,1,0:T(8,128)(2,1)S(1)}, bf16[2,16,128,128]{3,2,1,0:T(8,128)(2,1)S(1)}) custom-call(s32[3,128,8]{2,1,0:T(8,128)S(1)} %copy.95.own_ref, s32[2,16,3,24,128]{4,3,2,1,0:T(8,128)S(1)} %bitcast.141), custom_call_target="tpu_custom_call" | custom-call | flops 78643200 | bytes 2097152 | tf_op jit(solution)/shard_map/couple/pallas_call | solution.py:192
  154.9 10.3 %couple.4 = (bf16[2,16,128,128]{3,2,1,0:T(8,128)(2,1)S(1)}, bf16[2,16,128,128]{3,2,1,0:T(8,128)(2,1)S(1)}) custom-call(s32[3,128,8]{2,1,0:T(8,128)S(1)} %copy.96.own_ref, s32[2,16,3,24,128]{4,3,2,1,0:T(8,128)S(1)} %bitcast.142), custom_call_target="tpu_custom_call" | custom-call | flops 78643200 | bytes 2097152 | tf_op jit(solution)/shard_map/couple/pallas_call | solution.py:192
  171.4 9.8 %base_sums.5 = (f32[16,152,128]{2,1,0:T(8,128)S(1)}, f32[16,152,128]{2,1,0:T(8,128)}, f32[16,152,128]{2,1,0:T(8,128)S(1)}, f32[16,152,128]{2,1,0:T(8,128)S(1)}) custom-call(s32[1]{0:T(128)} %bitcast.base_ref, s32[2,16,3,24,128]{4,3,2,1,0:T(8,128)S(1)} %bitcast.143, f32[304,1024]{1,0:T(8,128)S(1)} %copy-done.36), custom_call_target="tpu_custom_call" | custom-call | flops 7650410496 | bytes 6225920 | tf_op jit(solution)/shard_map/base_sums/pallas_call | solution.py:244
  182.4 8.0 %collective-permute-done.20 = f32[2,1,4,152,128]{4,3,2,1,0:T(8,128)S(1)} collective-permute-done((f32[2,1,4,152,128]{4,3,2,1,0:T(8,128)S(1)}, f32[2,1,4,152,128]{4,3,2,1,0:T(8,128)S(1)}, u32[]{:S(2)}, u32[]{:S(2)}) %collective-permute-start.20) | collective-permute-done | bytes 622624 | tf_op jit(solution)/shard_map/ppermute | solution.py:23
  194.6 9.9 %hot_update.6.refs_0_ = f32[304,256]{1,0:T(8,128)S(1)} custom-call(s32[1]{0:T(128)} %bitcast.35.slice_ref, s32[2,16,3,24,128]{4,3,2,1,0:T(8,128)S(1)} %bitcast.144, f32[4,152,256]{2,1,0:T(8,128)S(1)} %copy-done.71, f32[4,152,256]{2,1,0:T(8,128)S(1)} %copy-done.74, f32[16,152,128]{2,1,0:T(8,128)S(1)} %bitcast.194, f32[16,152,128]{2,1,0:T(8,128)S(1)} %bitcast.190), custom_call_target="tpu_custom_call" | custom-call | flops 3825205248 | bytes 2490368 | tf_op jit(solution)/shard_map/hot_update/pallas_call | solution.py:494
  204.6 3.9 collective-permute-done.26
  215.8 9.4 %hot_update.7 = (f32[152,256]{1,0:T(8,128)S(1)}, f32[152,256]{1,0:T(8,128)S(1)}) custom-call(s32[1]{0:T(128)} %bitcast.35.slice_ref, s32[2,16,3,24,128]{4,3,2,1,0:T(8,128)S(1)} %bitcast.145, f32[4,152,256]{2,1,0:T(8,128)S(1)} %copy-done.71, f32[4,152,256]{2,1,0:T(8,128)S(1)} %copy-done.74, f32[16,152,128]{2,1,0:T(8,128)S(1)} %collective-permute-done.23.a.ca1.refs_1_, ...), custom_call_target="tpu_custom_call" | custom-call | flops 3825205248 | bytes 2490368 | tf_op jit(solution)/shard_map/hot_update/pallas_call | solution.py:494
  234.5 9.9 %absorb.2 = (f32[304,128]{1,0:T(8,128)S(1)}, f32[304,128]{1,0:T(8,128)S(1)}, f32[304,128]{1,0:T(8,128)S(1)}, f32[304,128]{1,0:T(8,128)S(1)}) custom-call(f32[16,152,128]{2,1,0:T(8,128)S(1)} %bitcast.187, f32[16,152,128]{2,1,0:T(8,128)S(1)} %collective-permute-done.29.ga1.refs_1_, f32[16,152,128]{2,1,0:T(8,128)S(1)} %bitcast.183, ...), custom_call_target="tpu_custom_call" | custom-call | flops 3825205248 | bytes 9961472 | tf_op jit(solution)/shard_map/absorb/pallas_call | solution.py:363
  247.0 5.1 collective-permute-done.39
  258.9 2.9 collective-permute-start.42
  261.9 7.5 %collective-permute-done.42 = f32[1,1,304,128]{3,2,1,0:T(8,128)S(1)} collective-permute-done((f32[1,1,304,128]{3,2,1,0:T(8,128)S(1)}, f32[1,1,304,128]{3,2,1,0:T(8,128)S(1)}, u32[]{:S(2)}, u32[]{:S(2)}) %collective-permute-start.42) | collective-permute-done | bytes 155680 | tf_op jit(solution)/shard_map/ppermute | solution.py:23
  269.7 6.6 %own_grads.4 = f32[304,128]{1,0:T(8,128)S(1)} custom-call(s32[8]{0:T(128)S(1)} %fusion.33.slice_ref, f32[304,128]{1,0:T(8,128)S(1)} %fusion.15.c_ref, f32[304,128]{1,0:T(8,128)S(1)} %pad_subtract_fusion.x_ref, f32[1,128]{1,0:T(1,128)S(1)} %get-tuple-element.421.denom_ref, s32[3,24,128]{2,1,0:T(8,128)S(1)} %pad_add_fusion.6.meta_ref, ...), custom_call_target="tpu_custom_call" | custom-call | flops 1912602624 | bytes 2490368 | tf_op jit(solution)/shard_map/own_grads/pallas_call | solution.py:422
  281.0 7.7 %context_update.3.table_ref = f32[304,1024]{1,0:T(8,128)S(1)} custom-call(s32[1]{0:T(128)} %bitcast.base_ref, s32[2,16,3,24,128]{4,3,2,1,0:T(8,128)S(1)} %bitcast.146, f32[304,1024]{1,0:T(8,128)S(1)} %copy-done.38, f32[16,152,128]{2,1,0:T(8,128)S(1)} %bitcast.196, f32[16,152,128]{2,1,0:T(8,128)S(1)} %copy-done.64, f32[16,152,128]{2,1,0:T(8,128)S(1)} %bitcast.192, ...), custom_call_target="tpu_custom_call" | custom-call | flops 5100273664 | bytes 7471104 | tf_op jit(solution)/shard_map/context_update/pallas_call | solution.py:315
  295.7 10.3 %couple.5 = (bf16[2,16,128,128]{3,2,1,0:T(8,128)(2,1)S(1)}, bf16[2,16,128,128]{3,2,1,0:T(8,128)(2,1)S(1)}) custom-call(s32[3,128,8]{2,1,0:T(8,128)S(1)} %copy.98.own_ref, s32[2,16,3,24,128]{4,3,2,1,0:T(8,128)S(1)} %bitcast.147), custom_call_target="tpu_custom_call" | custom-call | flops 78643200 | bytes 2097152 | tf_op jit(solution)/shard_map/couple/pallas_call | solution.py:192
  314.0 9.2 %update.3.table_ref = f32[304,1024]{1,0:T(8,128)S(1)} custom-call(s32[1]{0:T(128)} %bitcast.base_ref, s32[2,16,3,24,128]{4,3,2,1,0:T(8,128)S(1)} %bitcast.148, f32[304,1024]{1,0:T(8,128)S(1)} %copy-done.37, f32[16,152,128]{2,1,0:T(8,128)S(1)} %bitcast.188, f32[16,152,128]{2,1,0:T(8,128)S(1)} %copy-done.60, f32[16,152,128]{2,1,0:T(8,128)S(1)} %bitcast.185, ...), custom_call_target="tpu_custom_call" | custom-call | flops 5100273664 | bytes 4980736 | tf_op jit(solution)/shard_map/update/pallas_call | solution.py:315
  323.2 9.7 %collective-permute-done.51 = f32[1,1,4,152,128]{4,3,2,1,0:T(8,128)S(1)} collective-permute-done((f32[1,1,4,152,128]{4,3,2,1,0:T(8,128)S(1)}, f32[1,1,4,152,128]{4,3,2,1,0:T(8,128)S(1)}, u32[]{:S(2)}, u32[]{:S(2)}) %collective-permute-start.51) | collective-permute-done | bytes 311328 | tf_op jit(solution)/shard_map/ppermute | solution.py:23
  339.6 10.3 %hot_update.8.refs_0_ = f32[304,256]{1,0:T(8,128)S(1)} custom-call(s32[1]{0:T(128)} %bitcast.35.slice_ref, s32[2,16,3,24,128]{4,3,2,1,0:T(8,128)S(1)} %bitcast.149, f32[4,152,256]{2,1,0:T(8,128)} %bitcast.45.a0.hot_a, f32[4,152,256]{2,1,0:T(8,128)S(1)} %bitcast.210, f32[16,152,128]{2,1,0:T(8,128)S(1)} %bitcast.169, f32[16,152,128]{2,1,0:T(8,128)S(1)} %bitcast.165), custom_call_target="tpu_custom_call" | custom-call | flops 3825205248 | bytes 2490368 | tf_op jit(solution)/shard_map/hot_update/pallas_call | solution.py:494
  349.9 2.9 collective-permute-done.56
  360.7 10.6 %hot_update.9 = (f32[152,256]{1,0:T(8,128)S(1)}, f32[152,256]{1,0:T(8,128)S(1)}) custom-call(s32[1]{0:T(128)} %bitcast.35.slice_ref, s32[2,16,3,24,128]{4,3,2,1,0:T(8,128)S(1)} %bitcast.150, f32[4,152,256]{2,1,0:T(8,128)} %bitcast.45.a0.hot_a, f32[4,152,256]{2,1,0:T(8,128)S(1)} %bitcast.211, f32[16,152,128]{2,1,0:T(8,128)S(1)} %collective-permute-done.53.a.ca1.refs_1_, ...), custom_call_target="tpu_custom_call" | custom-call | flops 3825205248 | bytes 2490368 | tf_op jit(solution)/shard_map/hot_update/pallas_call | solution.py:494
  378.6 5.0 absorb.3
  389.2 4.1 collective-permute-done.69
  401.4 8.9 %collective-permute-done.72 = f32[1,1,304,128]{3,2,1,0:T(8,128)S(1)} collective-permute-done((f32[1,1,304,128]{3,2,1,0:T(8,128)S(1)}, f32[1,1,304,128]{3,2,1,0:T(8,128)S(1)}, u32[]{:S(2)}, u32[]{:S(2)}) %collective-permute-start.72) | collective-permute-done | bytes 155680 | tf_op jit(solution)/shard_map/ppermute | solution.py:23
  410.6 6.3 %own_grads.5 = f32[304,128]{1,0:T(8,128)S(1)} custom-call(s32[8]{0:T(128)S(1)} %fusion.33.slice_ref, f32[304,128]{1,0:T(8,128)S(1)} %fusion.11.c_ref, f32[304,128]{1,0:T(8,128)S(1)} %subtract_subtract_fusion.x_ref, f32[1,128]{1,0:T(1,128)S(1)} %get-tuple-element.417.denom_ref, s32[3,24,128]{2,1,0:T(8,128)S(1)} %pad_add_fusion.6.meta_ref, ...), custom_call_target="tpu_custom_call" | custom-call | flops 1912602624 | bytes 2490368 | tf_op jit(solution)/shard_map/own_grads/pallas_call | solution.py:422
  419.4 3.1 collective-permute-start.75
  422.6 7.7 %context_update.4.table_ref = f32[304,1024]{1,0:T(8,128)S(1)} custom-call(s32[1]{0:T(128)} %bitcast.base_ref, s32[2,16,3,24,128]{4,3,2,1,0:T(8,128)S(1)} %bitcast.151, f32[304,1024]{1,0:T(8,128)S(1)} %copy-done.80, f32[16,152,128]{2,1,0:T(8,128)S(1)} %bitcast.171, f32[16,152,128]{2,1,0:T(8,128)S(1)} %copy-done.34, f32[16,152,128]{2,1,0:T(8,128)S(1)} %bitcast.167, ...), custom_call_target="tpu_custom_call" | custom-call | flops 5100273664 | bytes 7471104 | tf_op jit(solution)/shard_map/context_update/pallas_call | solution.py:315
  435.4 5.2 collective-permute-done.78
  447.5 9.6 %update.4.table_ref = f32[304,1024]{1,0:T(8,128)S(1)} custom-call(s32[1]{0:T(128)} %bitcast.base_ref, s32[2,16,3,24,128]{4,3,2,1,0:T(8,128)S(1)} %bitcast.152, f32[304,1024]{1,0:T(8,128)S(1)} %copy-done.82, f32[16,152,128]{2,1,0:T(8,128)S(1)} %bitcast.163, f32[16,152,128]{2,1,0:T(8,128)S(1)} %copy-done.26, f32[16,152,128]{2,1,0:T(8,128)S(1)} %bitcast.160, ...), custom_call_target="tpu_custom_call" | custom-call | flops 5100273664 | bytes 4980736 | tf_op jit(solution)/shard_map/update/pallas_call | solution.py:315
  457.1 6.8 %collective-permute-done.81 = f32[1,1,4,152,128]{4,3,2,1,0:T(8,128)S(1)} collective-permute-done((f32[1,1,4,152,128]{4,3,2,1,0:T(8,128)S(1)}, f32[1,1,4,152,128]{4,3,2,1,0:T(8,128)S(1)}, u32[]{:S(2)}, u32[]{:S(2)}) %collective-permute-start.81) | collective-permute-done | bytes 311328 | tf_op jit(solution)/shard_map/ppermute | solution.py:23
  467.1 10.3 %hot_update.10.refs_0_ = f32[304,256]{1,0:T(8,128)S(1)} custom-call(s32[1]{0:T(128)} %bitcast.35.slice_ref, s32[2,16,3,24,128]{4,3,2,1,0:T(8,128)S(1)} %bitcast.153, f32[4,152,256]{2,1,0:T(8,128)} %bitcast.70.a0.hot_a, f32[4,152,256]{2,1,0:T(8,128)S(1)} %bitcast.214, f32[16,152,128]{2,1,0:T(8,128)S(1)} %bitcast.201, f32[16,152,128]{2,1,0:T(8,128)S(1)} %bitcast.198), custom_call_target="tpu_custom_call" | custom-call | flops 3825205248 | bytes 2490368 | tf_op jit(solution)/shard_map/hot_update/pallas_call | solution.py:494
  477.5 4.0 collective-permute-done.86
  483.1 10.3 %hot_update.11 = (f32[152,256]{1,0:T(8,128)S(1)}, f32[152,256]{1,0:T(8,128)S(1)}) custom-call(s32[1]{0:T(128)} %bitcast.35.slice_ref, s32[2,16,3,24,128]{4,3,2,1,0:T(8,128)S(1)} %bitcast.154, f32[4,152,256]{2,1,0:T(8,128)} %bitcast.70.a0.hot_a, f32[4,152,256]{2,1,0:T(8,128)S(1)} %bitcast.215, f32[16,152,128]{2,1,0:T(8,128)S(1)} %collective-permute-done.83.a.refs_1_, ...), custom_call_target="tpu_custom_call" | custom-call | flops 3825205248 | bytes 2490368 | tf_op jit(solution)/shard_map/hot_update/pallas_call | solution.py:494
  494.9 8.1 %context_update.5 = f32[1024,300]{1,0:T(8,128)S(1)} custom-call(s32[1]{0:T(128)} %bitcast.base_ref, s32[2,16,3,24,128]{4,3,2,1,0:T(8,128)S(1)} %bitcast.155, f32[304,1024]{1,0:T(8,128)S(1)} %context_update.4.table_ref, f32[16,152,128]{2,1,0:T(8,128)S(1)} %bitcast.202, f32[16,152,128]{2,1,0:T(8,128)S(1)} %collective-permute-done.83.a.refs_1_, ...), custom_call_target="tpu_custom_call" | custom-call | flops 5100273664 | bytes 7471104 | tf_op jit(solution)/shard_map/context_update/pallas_call | solution.py:315
  505.9 9.8 %update.5 = f32[1024,300]{1,0:T(8,128)S(1)} custom-call(s32[1]{0:T(128)} %bitcast.base_ref, s32[2,16,3,24,128]{4,3,2,1,0:T(8,128)S(1)} %bitcast.156, f32[304,1024]{1,0:T(8,128)S(1)} %update.4.table_ref, f32[16,152,128]{2,1,0:T(8,128)S(1)} %bitcast.207, f32[16,152,128]{2,1,0:T(8,128)S(1)} %collective-permute-done.87.refs_1_, f32[16,152,128]{2,1,0:T(8,128)S(1)} %bitcast.205, ...), custom_call_target="tpu_custom_call" | custom-call | flops 5100273664 | bytes 4980736 | tf_op jit(solution)/shard_map/update/pallas_call | solution.py:315
  518.3 2.9 copy.100
  525.3 5.1 collect.1
  (534 shorter events, 183.8 us)
Async XLA Ops:
  52.2 16.4 %collective-permute-start.8 = (f32[2,1,4,152,128]{4,3,2,1,0:T(8,128)}, f32[2,1,4,152,128]{4,3,2,1,0:T(8,128)}, u32[]{:S(2)}, u32[]{:S(2)}) collective-permute-start(f32[2,1,4,152,128]{4,3,2,1,0:T(8,128)} %slice.258), channel_id=1, source_target_pairs={{0,8},{1,9},{2,10},{3,11},{4,12},{5,13},{6,14},{7,15},{8,0},{9,1},... | collective-permute-start | bytes 1867784 | tf_op jit(solution)/shard_map/ppermute | solution.py:23
  53.9 16.1 %collective-permute-start.7 = (f32[1,2,4,152,128]{4,3,2,1,0:T(8,128)}, f32[1,2,4,152,128]{4,3,2,1,0:T(8,128)}, u32[]{:S(2)}, u32[]{:S(2)}) collective-permute-start(f32[1,2,4,152,128]{4,3,2,1,0:T(8,128)} %bitcast.8), channel_id=1, source_target_pairs={{0,16},{1,17},{2,18},{3,19},{4,20},{5,21},{6,22},{7,23},{8,24},{9,... | collective-permute-start | bytes 1867784 | tf_op jit(solution)/shard_map/ppermute | solution.py:23
  74.8 47.2 %all-to-all-start = ((f32[32,24,300]{2,1,0:T(8,128)}), f32[32,24,300]{2,1,0:T(8,128)}, u32[]{:S(2)}, u32[]{:S(2)}) async-start(f32[32,24,300]{2,1,0:T(8,128)} %bitcast.17), calls=%async_computation | async-start | bytes 2359296 | tf_op jit(solution)/shard_map/all_to_all | solution.py:685
  82.1 26.2 %collective-permute-start.11 = (f32[2,1,304,128]{3,2,1,0:T(8,128)S(1)}, f32[2,1,304,128]{3,2,1,0:T(8,128)S(1)}, u32[]{:S(2)}, u32[]{:S(2)}) collective-permute-start(f32[2,1,304,128]{3,2,1,0:T(8,128)S(1)} %pad_maximum_fusion.38), channel_id=1, source_target_pairs={{0,1},{1,0},{2,3},{3,2},{4,5},{5,4},{6,7},{7,6},{8,9},{9,8},{10,11... | collective-permute-start | bytes 933896 | tf_op jit(solution)/shard_map/ppermute | solution.py:23
  134.5 13.7 %collective-permute-start.14 = (f32[2,1,304,128]{3,2,1,0:T(8,128)}, f32[2,1,304,128]{3,2,1,0:T(8,128)}, u32[]{:S(2)}, u32[]{:S(2)}) collective-permute-start(f32[2,1,304,128]{3,2,1,0:T(8,128)} %pad_maximum_fusion.39), channel_id=1, source_target_pairs={{0,1},{1,0},{2,3},{3,2},{4,5},{5,4},{6,7},{7,6},{8,9},{9,8},{10,11... | collective-permute-start | bytes 933896 | tf_op jit(solution)/shard_map/ppermute | solution.py:23
  150.2 15.0 %collective-permute-start.18 = (f32[2,1,304,128]{3,2,1,0:T(8,128)}, f32[2,1,304,128]{3,2,1,0:T(8,128)}, u32[]{:S(2)}, u32[]{:S(2)}) collective-permute-start(f32[2,1,304,128]{3,2,1,0:T(8,128)} %pad_maximum_fusion.40), channel_id=1, source_target_pairs={{0,1},{1,0},{2,3},{3,2},{4,5},{5,4},{6,7},{7,6},{8,9},{9,8},{10,11... | collective-permute-start | bytes 933896 | tf_op jit(solution)/shard_map/ppermute | solution.py:23
  154.7 39.3 %collective-permute-start.27 = (f32[16,152,128]{2,1,0:T(8,128)}, f32[16,152,128]{2,1,0:T(8,128)}, u32[]{:S(2)}, u32[]{:S(2)}) collective-permute-start(f32[16,152,128]{2,1,0:T(8,128)} %get-tuple-element.236), channel_id=1, source_target_pairs={{0,4},{1,5},{2,6},{3,7},{4,0},{5,1},{6,2},{7,3},{8,12},{9,13},{10,... | collective-permute-start | bytes 3735560 | tf_op jit(solution)/shard_map/ppermute | solution.py:23
  167.3 15.0 %collective-permute-start.21 = (f32[1,1,4,152,128]{4,3,2,1,0:T(8,128)S(1)}, f32[1,1,4,152,128]{4,3,2,1,0:T(8,128)S(1)}, u32[]{:S(2)}, u32[]{:S(2)}) collective-permute-start(f32[1,1,4,152,128]{4,3,2,1,0:T(8,128)S(1)} %get-tuple-element.407), channel_id=1, source_target_pairs={{0,8},{1,9},{2,10},{3,11},{4,12},{5,13},{6,14},{7,15},{8,0},{9,1},... | collective-permute-start | bytes 933896 | tf_op jit(solution)/shard_map/ppermute | solution.py:23
  167.9 14.5 %collective-permute-start.22 = (f32[1,1,4,152,128]{4,3,2,1,0:T(8,128)S(1)}, f32[1,1,4,152,128]{4,3,2,1,0:T(8,128)S(1)}, u32[]{:S(2)}, u32[]{:S(2)}) collective-permute-start(f32[1,1,4,152,128]{4,3,2,1,0:T(8,128)S(1)} %get-tuple-element.406), channel_id=1, source_target_pairs={{0,16},{1,17},{2,18},{3,19},{4,20},{5,21},{6,22},{7,23},{8,24},{9,... | collective-permute-start | bytes 933896 | tf_op jit(solution)/shard_map/ppermute | solution.py:23
  168.4 22.0 %collective-permute-start.20 = (f32[2,1,4,152,128]{4,3,2,1,0:T(8,128)S(1)}, f32[2,1,4,152,128]{4,3,2,1,0:T(8,128)S(1)}, u32[]{:S(2)}, u32[]{:S(2)}) collective-permute-start(f32[2,1,4,152,128]{4,3,2,1,0:T(8,128)S(1)} %pad_maximum_fusion.14), channel_id=1, source_target_pairs={{0,8},{1,9},{2,10},{3,11},{4,12},{5,13},{6,14},{7,15},{8,0},{9,1},... | collective-permute-start | bytes 1867784 | tf_op jit(solution)/shard_map/ppermute | solution.py:23
  169.9 20.8 %collective-permute-start.19 = (f32[1,2,4,152,128]{4,3,2,1,0:T(8,128)S(1)}, f32[1,2,4,152,128]{4,3,2,1,0:T(8,128)S(1)}, u32[]{:S(2)}, u32[]{:S(2)}) collective-permute-start(f32[1,2,4,152,128]{4,3,2,1,0:T(8,128)S(1)} %pad_maximum_fusion.13), channel_id=1, source_target_pairs={{0,16},{1,17},{2,18},{3,19},{4,20},{5,21},{6,22},{7,23},{8,24},{9,... | collective-permute-start | bytes 1867784 | tf_op jit(solution)/shard_map/ppermute | solution.py:23
  182.3 22.3 %collective-permute-start.28 = (f32[16,152,128]{2,1,0:T(8,128)S(1)}, f32[16,152,128]{2,1,0:T(8,128)S(1)}, u32[]{:S(2)}, u32[]{:S(2)}) collective-permute-start(f32[16,152,128]{2,1,0:T(8,128)S(1)} %copy-done.55), channel_id=1, source_target_pairs={{0,4},{1,5},{2,6},{3,7},{4,0},{5,1},{6,2},{7,3},{8,12},{9,13},{10,... | collective-permute-start | bytes 3735560 | tf_op jit(solution)/shard_map/ppermute | solution.py:23
  191.8 18.1 %collective-permute-start.24 = (f32[16,152,128]{2,1,0:T(8,128)S(1)}, f32[16,152,128]{2,1,0:T(8,128)S(1)}, u32[]{:S(2)}, u32[]{:S(2)}) collective-permute-start(f32[16,152,128]{2,1,0:T(8,128)S(1)} %bitcast.189), channel_id=1, source_target_pairs={{0,4},{1,5},{2,6},{3,7},{4,0},{5,1},{6,2},{7,3},{8,12},{9,13},{10,... | collective-permute-start | bytes 3735560 | tf_op jit(solution)/shard_map/ppermute | solution.py:23
  191.9 18.0 %collective-permute-start.23 = (f32[16,152,128]{2,1,0:T(8,128)S(1)}, f32[16,152,128]{2,1,0:T(8,128)S(1)}, u32[]{:S(2)}, u32[]{:S(2)}) collective-permute-start(f32[16,152,128]{2,1,0:T(8,128)S(1)} %bitcast.193), channel_id=1, source_target_pairs={{0,4},{1,5},{2,6},{3,7},{4,0},{5,1},{6,2},{7,3},{8,12},{9,13},{10,... | collective-permute-start | bytes 3735560 | tf_op jit(solution)/shard_map/ppermute | solution.py:23
  192.4 16.1 %collective-permute-start.26 = (f32[2,1,4,152,128]{4,3,2,1,0:T(8,128)S(1)}, f32[2,1,4,152,128]{4,3,2,1,0:T(8,128)S(1)}, u32[]{:S(2)}, u32[]{:S(2)}) collective-permute-start(f32[2,1,4,152,128]{4,3,2,1,0:T(8,128)S(1)} %pad_maximum_fusion.17), channel_id=1, source_target_pairs={{0,8},{1,9},{2,10},{3,11},{4,12},{5,13},{6,14},{7,15},{8,0},{9,1},... | collective-permute-start | bytes 1867784 | tf_op jit(solution)/shard_map/ppermute | solution.py:23
  194.0 15.8 %collective-permute-start.25 = (f32[1,2,4,152,128]{4,3,2,1,0:T(8,128)S(1)}, f32[1,2,4,152,128]{4,3,2,1,0:T(8,128)S(1)}, u32[]{:S(2)}, u32[]{:S(2)}) collective-permute-start(f32[1,2,4,152,128]{4,3,2,1,0:T(8,128)S(1)} %pad_maximum_fusion.16), channel_id=1, source_target_pairs={{0,16},{1,17},{2,18},{3,19},{4,20},{5,21},{6,22},{7,23},{8,24},{9,... | collective-permute-start | bytes 1867784 | tf_op jit(solution)/shard_map/ppermute | solution.py:23
  210.1 20.0 %collective-permute-start.30 = (f32[16,152,128]{2,1,0:T(8,128)S(1)}, f32[16,152,128]{2,1,0:T(8,128)S(1)}, u32[]{:S(2)}, u32[]{:S(2)}) collective-permute-start(f32[16,152,128]{2,1,0:T(8,128)S(1)} %bitcast.182), channel_id=1, source_target_pairs={{0,4},{1,5},{2,6},{3,7},{4,0},{5,1},{6,2},{7,3},{8,12},{9,13},{10,... | collective-permute-start | bytes 3735560 | tf_op jit(solution)/shard_map/ppermute | solution.py:23
  210.2 19.9 %collective-permute-start.29 = (f32[16,152,128]{2,1,0:T(8,128)S(1)}, f32[16,152,128]{2,1,0:T(8,128)S(1)}, u32[]{:S(2)}, u32[]{:S(2)}) collective-permute-start(f32[16,152,128]{2,1,0:T(8,128)S(1)} %bitcast.186), channel_id=1, source_target_pairs={{0,4},{1,5},{2,6},{3,7},{4,0},{5,1},{6,2},{7,3},{8,12},{9,13},{10,... | collective-permute-start | bytes 3735560 | tf_op jit(solution)/shard_map/ppermute | solution.py:23
  212.4 14.9 %collective-permute-start.32 = (f32[2,1,4,152,128]{4,3,2,1,0:T(8,128)S(1)}, f32[2,1,4,152,128]{4,3,2,1,0:T(8,128)S(1)}, u32[]{:S(2)}, u32[]{:S(2)}) collective-permute-start(f32[2,1,4,152,128]{4,3,2,1,0:T(8,128)S(1)} %slice.275), channel_id=1, source_target_pairs={{0,8},{1,9},{2,10},{3,11},{4,12},{5,13},{6,14},{7,15},{8,0},{9,1},... | collective-permute-start | bytes 1867784 | tf_op jit(solution)/shard_map/ppermute | solution.py:23
  215.2 14.9 %collective-permute-start.31 = (f32[1,2,4,152,128]{4,3,2,1,0:T(8,128)S(1)}, f32[1,2,4,152,128]{4,3,2,1,0:T(8,128)S(1)}, u32[]{:S(2)}, u32[]{:S(2)}) collective-permute-start(f32[1,2,4,152,128]{4,3,2,1,0:T(8,128)S(1)} %bitcast.282), channel_id=1, source_target_pairs={{0,16},{1,17},{2,18},{3,19},{4,20},{5,21},{6,22},{7,23},{8,24},{9,... | collective-permute-start | bytes 1867784 | tf_op jit(solution)/shard_map/ppermute | solution.py:23
  230.4 14.1 %collective-permute-start.36 = (f32[1,1,4,152,128]{4,3,2,1,0:T(8,128)S(1)}, f32[1,1,4,152,128]{4,3,2,1,0:T(8,128)S(1)}, u32[]{:S(2)}, u32[]{:S(2)}) collective-permute-start(f32[1,1,4,152,128]{4,3,2,1,0:T(8,128)S(1)} %slice.279), channel_id=1, source_target_pairs={{0,16},{1,17},{2,18},{3,19},{4,20},{5,21},{6,22},{7,23},{8,24},{9,... | collective-permute-start | bytes 933896 | tf_op jit(solution)/shard_map/ppermute | solution.py:23
  231.0 13.5 %collective-permute-start.35 = (f32[1,1,4,152,128]{4,3,2,1,0:T(8,128)S(1)}, f32[1,1,4,152,128]{4,3,2,1,0:T(8,128)S(1)}, u32[]{:S(2)}, u32[]{:S(2)}) collective-permute-start(f32[1,1,4,152,128]{4,3,2,1,0:T(8,128)S(1)} %slice.277), channel_id=1, source_target_pairs={{0,8},{1,9},{2,10},{3,11},{4,12},{5,13},{6,14},{7,15},{8,0},{9,1},... | collective-permute-start | bytes 933896 | tf_op jit(solution)/shard_map/ppermute | solution.py:23
  253.3 16.1 %collective-permute-start.41 = (f32[4,152,256]{2,1,0:T(8,128)S(1)}, f32[4,152,256]{2,1,0:T(8,128)}, u32[]{:S(2)}, u32[]{:S(2)}) collective-permute-start(f32[4,152,256]{2,1,0:T(8,128)S(1)} %bitcast.208), channel_id=1, source_target_pairs={{0,4},{1,5},{2,6},{3,7},{4,0},{5,1},{6,2},{7,3},{8,12},{9,13},{10,... | collective-permute-start | bytes 1867784 | tf_op jit(solution)/shard_map/ppermute | solution.py:23
  254.3 15.1 %collective-permute-start.40 = (f32[4,152,256]{2,1,0:T(8,128)}, f32[4,152,256]{2,1,0:T(8,128)}, u32[]{:S(2)}, u32[]{:S(2)}) collective-permute-start(f32[4,152,256]{2,1,0:T(8,128)} %bitcast.45.a0.hot_a), channel_id=1, source_target_pairs={{0,4},{1,5},{2,6},{3,7},{4,0},{5,1},{6,2},{7,3},{8,12},{9,13},{10,... | collective-permute-start | bytes 1867784 | tf_op jit(solution)/shard_map/ppermute | solution.py:23
  295.6 42.6 %collective-permute-start.57 = (f32[16,152,128]{2,1,0:T(8,128)}, f32[16,152,128]{2,1,0:T(8,128)}, u32[]{:S(2)}, u32[]{:S(2)}) collective-permute-start(f32[16,152,128]{2,1,0:T(8,128)} %get-tuple-element.295), channel_id=1, source_target_pairs={{0,4},{1,5},{2,6},{3,7},{4,0},{5,1},{6,2},{7,3},{8,12},{9,13},{10,... | collective-permute-start | bytes 3735560 | tf_op jit(solution)/shard_map/ppermute | solution.py:23
  309.8 23.6 %collective-permute-start.50 = (f32[2,1,4,152,128]{4,3,2,1,0:T(8,128)S(1)}, f32[2,1,4,152,128]{4,3,2,1,0:T(8,128)S(1)}, u32[]{:S(2)}, u32[]{:S(2)}) collective-permute-start(f32[2,1,4,152,128]{4,3,2,1,0:T(8,128)S(1)} %pad_maximum_fusion.22), channel_id=1, source_target_pairs={{0,8},{1,9},{2,10},{3,11},{4,12},{5,13},{6,14},{7,15},{8,0},{9,1},... | collective-permute-start | bytes 1867784 | tf_op jit(solution)/shard_map/ppermute | solution.py:23
  310.5 22.8 %collective-permute-start.49 = (f32[1,2,4,152,128]{4,3,2,1,0:T(8,128)S(1)}, f32[1,2,4,152,128]{4,3,2,1,0:T(8,128)S(1)}, u32[]{:S(2)}, u32[]{:S(2)}) collective-permute-start(f32[1,2,4,152,128]{4,3,2,1,0:T(8,128)S(1)} %pad_maximum_fusion.21), channel_id=1, source_target_pairs={{0,16},{1,17},{2,18},{3,19},{4,20},{5,21},{6,22},{7,23},{8,24},{9,... | collective-permute-start | bytes 1867784 | tf_op jit(solution)/shard_map/ppermute | solution.py:23
  311.9 21.0 %collective-permute-start.51 = (f32[1,1,4,152,128]{4,3,2,1,0:T(8,128)S(1)}, f32[1,1,4,152,128]{4,3,2,1,0:T(8,128)S(1)}, u32[]{:S(2)}, u32[]{:S(2)}) collective-permute-start(f32[1,1,4,152,128]{4,3,2,1,0:T(8,128)S(1)} %get-tuple-element.403), channel_id=1, source_target_pairs={{0,8},{1,9},{2,10},{3,11},{4,12},{5,13},{6,14},{7,15},{8,0},{9,1},... | collective-permute-start | bytes 933896 | tf_op jit(solution)/shard_map/ppermute | solution.py:23
  313.3 20.1 %collective-permute-start.52 = (f32[1,1,4,152,128]{4,3,2,1,0:T(8,128)S(1)}, f32[1,1,4,152,128]{4,3,2,1,0:T(8,128)S(1)}, u32[]{:S(2)}, u32[]{:S(2)}) collective-permute-start(f32[1,1,4,152,128]{4,3,2,1,0:T(8,128)S(1)} %get-tuple-element.402), channel_id=1, source_target_pairs={{0,16},{1,17},{2,18},{3,19},{4,20},{5,21},{6,22},{7,23},{8,24},{9,... | collective-permute-start | bytes 933896 | tf_op jit(solution)/shard_map/ppermute | solution.py:23
  332.9 17.0 %collective-permute-start.58 = (f32[16,152,128]{2,1,0:T(8,128)S(1)}, f32[16,152,128]{2,1,0:T(8,128)S(1)}, u32[]{:S(2)}, u32[]{:S(2)}) collective-permute-start(f32[16,152,128]{2,1,0:T(8,128)S(1)} %copy-done.53), channel_id=1, source_target_pairs={{0,4},{1,5},{2,6},{3,7},{4,0},{5,1},{6,2},{7,3},{8,12},{9,13},{10,... | collective-permute-start | bytes 3735560 | tf_op jit(solution)/shard_map/ppermute | solution.py:23
  336.1 17.9 %collective-permute-start.54 = (f32[16,152,128]{2,1,0:T(8,128)S(1)}, f32[16,152,128]{2,1,0:T(8,128)S(1)}, u32[]{:S(2)}, u32[]{:S(2)}) collective-permute-start(f32[16,152,128]{2,1,0:T(8,128)S(1)} %bitcast.164), channel_id=1, source_target_pairs={{0,4},{1,5},{2,6},{3,7},{4,0},{5,1},{6,2},{7,3},{8,12},{9,13},{10,... | collective-permute-start | bytes 3735560 | tf_op jit(solution)/shard_map/ppermute | solution.py:23
  336.3 17.7 %collective-permute-start.53 = (f32[16,152,128]{2,1,0:T(8,128)S(1)}, f32[16,152,128]{2,1,0:T(8,128)S(1)}, u32[]{:S(2)}, u32[]{:S(2)}) collective-permute-start(f32[16,152,128]{2,1,0:T(8,128)S(1)} %bitcast.168), channel_id=1, source_target_pairs={{0,4},{1,5},{2,6},{3,7},{4,0},{5,1},{6,2},{7,3},{8,12},{9,13},{10,... | collective-permute-start | bytes 3735560 | tf_op jit(solution)/shard_map/ppermute | solution.py:23
  336.8 16.1 %collective-permute-start.56 = (f32[2,1,4,152,128]{4,3,2,1,0:T(8,128)S(1)}, f32[2,1,4,152,128]{4,3,2,1,0:T(8,128)S(1)}, u32[]{:S(2)}, u32[]{:S(2)}) collective-permute-start(f32[2,1,4,152,128]{4,3,2,1,0:T(8,128)S(1)} %pad_maximum_fusion.25), channel_id=1, source_target_pairs={{0,8},{1,9},{2,10},{3,11},{4,12},{5,13},{6,14},{7,15},{8,0},{9,1},... | collective-permute-start | bytes 1867784 | tf_op jit(solution)/shard_map/ppermute | solution.py:23
  338.2 15.8 %collective-permute-start.55 = (f32[1,2,4,152,128]{4,3,2,1,0:T(8,128)S(1)}, f32[1,2,4,152,128]{4,3,2,1,0:T(8,128)S(1)}, u32[]{:S(2)}, u32[]{:S(2)}) collective-permute-start(f32[1,2,4,152,128]{4,3,2,1,0:T(8,128)S(1)} %pad_maximum_fusion.24), channel_id=1, source_target_pairs={{0,16},{1,17},{2,18},{3,19},{4,20},{5,21},{6,22},{7,23},{8,24},{9,... | collective-permute-start | bytes 1867784 | tf_op jit(solution)/shard_map/ppermute | solution.py:23
  354.2 20.0 %collective-permute-start.60 = (f32[16,152,128]{2,1,0:T(8,128)S(1)}, f32[16,152,128]{2,1,0:T(8,128)S(1)}, u32[]{:S(2)}, u32[]{:S(2)}) collective-permute-start(f32[16,152,128]{2,1,0:T(8,128)S(1)} %bitcast.157), channel_id=1, source_target_pairs={{0,4},{1,5},{2,6},{3,7},{4,0},{5,1},{6,2},{7,3},{8,12},{9,13},{10,... | collective-permute-start | bytes 3735560 | tf_op jit(solution)/shard_map/ppermute | solution.py:23
  354.3 19.9 %collective-permute-start.59 = (f32[16,152,128]{2,1,0:T(8,128)S(1)}, f32[16,152,128]{2,1,0:T(8,128)S(1)}, u32[]{:S(2)}, u32[]{:S(2)}) collective-permute-start(f32[16,152,128]{2,1,0:T(8,128)S(1)} %bitcast.161), channel_id=1, source_target_pairs={{0,4},{1,5},{2,6},{3,7},{4,0},{5,1},{6,2},{7,3},{8,12},{9,13},{10,... | collective-permute-start | bytes 3735560 | tf_op jit(solution)/shard_map/ppermute | solution.py:23
  356.5 14.9 %collective-permute-start.62 = (f32[2,1,4,152,128]{4,3,2,1,0:T(8,128)S(1)}, f32[2,1,4,152,128]{4,3,2,1,0:T(8,128)S(1)}, u32[]{:S(2)}, u32[]{:S(2)}) collective-permute-start(f32[2,1,4,152,128]{4,3,2,1,0:T(8,128)S(1)} %slice.292), channel_id=1, source_target_pairs={{0,8},{1,9},{2,10},{3,11},{4,12},{5,13},{6,14},{7,15},{8,0},{9,1},... | collective-permute-start | bytes 1867784 | tf_op jit(solution)/shard_map/ppermute | solution.py:23
  359.3 14.9 %collective-permute-start.61 = (f32[1,2,4,152,128]{4,3,2,1,0:T(8,128)S(1)}, f32[1,2,4,152,128]{4,3,2,1,0:T(8,128)S(1)}, u32[]{:S(2)}, u32[]{:S(2)}) collective-permute-start(f32[1,2,4,152,128]{4,3,2,1,0:T(8,128)S(1)} %bitcast.283), channel_id=1, source_target_pairs={{0,16},{1,17},{2,18},{3,19},{4,20},{5,21},{6,22},{7,23},{8,24},{9,... | collective-permute-start | bytes 1867784 | tf_op jit(solution)/shard_map/ppermute | solution.py:23
  395.6 14.7 %collective-permute-start.71 = (f32[4,152,256]{2,1,0:T(8,128)S(1)}, f32[4,152,256]{2,1,0:T(8,128)}, u32[]{:S(2)}, u32[]{:S(2)}) collective-permute-start(f32[4,152,256]{2,1,0:T(8,128)S(1)} %bitcast.212), channel_id=1, source_target_pairs={{0,4},{1,5},{2,6},{3,7},{4,0},{5,1},{6,2},{7,3},{8,12},{9,13},{10,... | collective-permute-start | bytes 1867784 | tf_op jit(solution)/shard_map/ppermute | solution.py:23
  396.6 13.7 %collective-permute-start.70 = (f32[4,152,256]{2,1,0:T(8,128)}, f32[4,152,256]{2,1,0:T(8,128)}, u32[]{:S(2)}, u32[]{:S(2)}) collective-permute-start(f32[4,152,256]{2,1,0:T(8,128)} %bitcast.70.a0.hot_a), channel_id=1, source_target_pairs={{0,4},{1,5},{2,6},{3,7},{4,0},{5,1},{6,2},{7,3},{8,12},{9,13},{10,... | collective-permute-start | bytes 1867784 | tf_op jit(solution)/shard_map/ppermute | solution.py:23
  443.2 21.3 %collective-permute-start.80 = (f32[2,1,4,152,128]{4,3,2,1,0:T(8,128)S(1)}, f32[2,1,4,152,128]{4,3,2,1,0:T(8,128)S(1)}, u32[]{:S(2)}, u32[]{:S(2)}) collective-permute-start(f32[2,1,4,152,128]{4,3,2,1,0:T(8,128)S(1)} %pad_maximum_fusion.31), channel_id=1, source_target_pairs={{0,8},{1,9},{2,10},{3,11},{4,12},{5,13},{6,14},{7,15},{8,0},{9,1},... | collective-permute-start | bytes 1867784 | tf_op jit(solution)/shard_map/ppermute | solution.py:23
  444.2 20.3 %collective-permute-start.79 = (f32[1,2,4,152,128]{4,3,2,1,0:T(8,128)S(1)}, f32[1,2,4,152,128]{4,3,2,1,0:T(8,128)S(1)}, u32[]{:S(2)}, u32[]{:S(2)}) collective-permute-start(f32[1,2,4,152,128]{4,3,2,1,0:T(8,128)S(1)} %pad_maximum_fusion.30), channel_id=1, source_target_pairs={{0,16},{1,17},{2,18},{3,19},{4,20},{5,21},{6,22},{7,23},{8,24},{9,... | collective-permute-start | bytes 1867784 | tf_op jit(solution)/shard_map/ppermute | solution.py:23
  444.6 19.3 %collective-permute-start.81 = (f32[1,1,4,152,128]{4,3,2,1,0:T(8,128)S(1)}, f32[1,1,4,152,128]{4,3,2,1,0:T(8,128)S(1)}, u32[]{:S(2)}, u32[]{:S(2)}) collective-permute-start(f32[1,1,4,152,128]{4,3,2,1,0:T(8,128)S(1)} %get-tuple-element.399), channel_id=1, source_target_pairs={{0,8},{1,9},{2,10},{3,11},{4,12},{5,13},{6,14},{7,15},{8,0},{9,1},... | collective-permute-start | bytes 933896 | tf_op jit(solution)/shard_map/ppermute | solution.py:23
  445.9 18.6 %collective-permute-start.82 = (f32[1,1,4,152,128]{4,3,2,1,0:T(8,128)S(1)}, f32[1,1,4,152,128]{4,3,2,1,0:T(8,128)S(1)}, u32[]{:S(2)}, u32[]{:S(2)}) collective-permute-start(f32[1,1,4,152,128]{4,3,2,1,0:T(8,128)S(1)} %get-tuple-element.398), channel_id=1, source_target_pairs={{0,16},{1,17},{2,18},{3,19},{4,20},{5,21},{6,22},{7,23},{8,24},{9,... | collective-permute-start | bytes 933896 | tf_op jit(solution)/shard_map/ppermute | solution.py:23
  464.7 17.6 %collective-permute-start.84 = (f32[16,152,128]{2,1,0:T(8,128)S(1)}, f32[16,152,128]{2,1,0:T(8,128)S(1)}, u32[]{:S(2)}, u32[]{:S(2)}) collective-permute-start(f32[16,152,128]{2,1,0:T(8,128)S(1)} %bitcast.197), channel_id=1, source_target_pairs={{0,4},{1,5},{2,6},{3,7},{4,0},{5,1},{6,2},{7,3},{8,12},{9,13},{10,... | collective-permute-start | bytes 3735560 | tf_op jit(solution)/shard_map/ppermute | solution.py:23
  464.8 17.5 %collective-permute-start.83 = (f32[16,152,128]{2,1,0:T(8,128)S(1)}, f32[16,152,128]{2,1,0:T(8,128)S(1)}, u32[]{:S(2)}, u32[]{:S(2)}) collective-permute-start(f32[16,152,128]{2,1,0:T(8,128)S(1)} %bitcast.200), channel_id=1, source_target_pairs={{0,4},{1,5},{2,6},{3,7},{4,0},{5,1},{6,2},{7,3},{8,12},{9,13},{10,... | collective-permute-start | bytes 3735560 | tf_op jit(solution)/shard_map/ppermute | solution.py:23
  465.4 16.1 %collective-permute-start.86 = (f32[2,1,4,152,128]{4,3,2,1,0:T(8,128)S(1)}, f32[2,1,4,152,128]{4,3,2,1,0:T(8,128)S(1)}, u32[]{:S(2)}, u32[]{:S(2)}) collective-permute-start(f32[2,1,4,152,128]{4,3,2,1,0:T(8,128)S(1)} %pad_maximum_fusion.33), channel_id=1, source_target_pairs={{0,8},{1,9},{2,10},{3,11},{4,12},{5,13},{6,14},{7,15},{8,0},{9,1},... | collective-permute-start | bytes 1867784 | tf_op jit(solution)/shard_map/ppermute | solution.py:23
  466.6 15.7 %collective-permute-start.85 = (f32[1,2,4,152,128]{4,3,2,1,0:T(8,128)S(1)}, f32[1,2,4,152,128]{4,3,2,1,0:T(8,128)S(1)}, u32[]{:S(2)}, u32[]{:S(2)}) collective-permute-start(f32[1,2,4,152,128]{4,3,2,1,0:T(8,128)S(1)} %pad_maximum_fusion.32), channel_id=1, source_target_pairs={{0,16},{1,17},{2,18},{3,19},{4,20},{5,21},{6,22},{7,23},{8,24},{9,... | collective-permute-start | bytes 1867784 | tf_op jit(solution)/shard_map/ppermute | solution.py:23
  (155 other events, 1307.6 us)
